TPU v7x, 32 devices: a whole 2x2x4 slice. The times are simulated.
32 devices in a mesh: dp: 8 (over z, x), chan: 4 (over y, core).
Axes of the slice: x: 2, y: 2, z: 4, core: 2. Of those that a mesh axis runs over, the one named last changes fastest.
Arguments:
- block_in: bfloat16 [12544, 2048], P('dp', 'chan'), may hold values from -6 to 6
- weight_in: bfloat16 [2048, 512], P('dp', 'chan'), may hold values from -0.125 to 0.125
- weight_mid: bfloat16 [4608, 512], P('dp', 'chan'), may hold values from -0.09375 to 0.09375
- weight_out: bfloat16 [512, 2048], P('dp', 'chan'), may hold values from -0.25 to 0.25
- gain_in: float32 [512], P('chan'), may hold values from 0.1 to 1.9
- bias_in: float32 [512], P('chan'), may hold values from -3 to 3
- gain_mid: float32 [512], P('chan'), may hold values from 0.1 to 1.9
- bias_mid: float32 [512], P('chan'), may hold values from -3 to 3
- gain_out: float32 [2048], P('chan'), may hold values from 0.1 to 1.9
- bias_out: float32 [2048], P('chan'), may hold values from -3 to 3
- kernel_near: float32 [9, 512], P(None, 'chan'), may hold values from -2 to 2
- kernel_far: float32 [9, 512], P(None, 'chan'), may hold values from -2 to 2
- gate_bias: float32 [512], P('chan'), may hold values from -3 to 3
- same_video: int32 [32, 7], P('dp'), may hold values 0 or 1
- video: bfloat16 [256, 15, 1024], P('dp'), may hold values from -6 to 6
- stem_center: bfloat16 [147, 64], P(None, 'chan'), may hold values from -0.5 to 0.5
- stem_diff: bfloat16 [588, 64], P(None, 'chan'), may hold values from -0.1875 to 0.1875
- stem_gain: float32 [64], P('chan'), may hold values from 0.1 to 1.9
- stem_bias: float32 [64], P('chan'), may hold values from -3 to 3
- block_grad: bfloat16 [12544, 2048], P('dp', 'chan'), may hold values from -6 to 6
- stem_grad: bfloat16 [256, 64, 256], P('dp', 'chan'), may hold values from -6 to 6
Outputs:
- block_out: bfloat16 [12544, 2048], P('dp', 'chan')
- stem_out: bfloat16 [256, 64, 256], P('dp', 'chan')
- grad_block_in: bfloat16 [12544, 2048], P('dp', 'chan')
- grad_weight_in: float32 [2048, 512], P('dp', 'chan')
- grad_weight_mid: float32 [4608, 512], P('dp', 'chan')
- grad_weight_out: float32 [512, 2048], P('dp', 'chan')
- grad_gain_in: float32 [512], P('chan')
- grad_bias_in: float32 [512], P('chan')
- grad_gain_mid: float32 [512], P('chan')
- grad_bias_mid: float32 [512], P('chan')
- grad_gain_out: float32 [2048], P('chan')
- grad_bias_out: float32 [2048], P('chan')
- grad_kernel_near: float32 [9, 512], P(None, 'chan')
- grad_kernel_far: float32 [9, 512], P(None, 'chan')
- grad_gate_bias: float32 [512], P('chan')
- grad_stem_center: float32 [147, 64], P(None, 'chan')
- grad_stem_diff: float32 [588, 64], P(None, 'chan')
- grad_stem_gain: float32 [64], P('chan')
- grad_stem_bias: float32 [64], P('chan')
All inputs are finite; a program needn't handle non-finite values. No bound on the sum of `same_video` on one device may be relied on, other than what follows from the above.
Results may differ from a plain program's by a relative error of at most 0.0085.
Values may be sent and summed in bfloat16 or wider, within the bound.
No kernel may reach another device: no remote copies, remote signals or barrier semaphores. Data moves between devices by JAX's collectives and lax.ppermute only.
A program may use at most 256 MiB of HBM per device.

v0:
```python
import jax
import jax.numpy as jnp
from jax import lax
from jax.sharding import PartitionSpec as P

SEG = 8
SIDE = 7
FRAMES = 5


eps = 1e-05


def silu_slope(value):
    logistic = jax.nn.sigmoid(value)
    return logistic * (1.0 + value * (1.0 - logistic))


def norm_stats(totals, squares, count):
    center = totals / count
    spread = squares / count - center * center
    return (center, lax.rsqrt(spread + eps))


def norm_back(upstream, scaled, gain, rate, bias_grad, gain_grad, count):
    return gain * rate * (upstream - bias_grad / count - scaled * gain_grad / count)


def depthwise(field, kernel, step):
    padded = jnp.pad(field, ((0, 0), (step, step), (step, step), (0, 0)))
    total = jnp.zeros_like(field)
    for tap in range(9):
        row_at = tap // 3 * step
        col_at = tap % 3 * step
        total = total + kernel[tap] * padded[:, row_at : row_at + SIDE, col_at : col_at + SIDE, :]
    return total


def temporal_gate(hidden, same_video, kernel_near, kernel_far, gate_bias):
    clips = same_video.shape[0]
    field = hidden.reshape(clips, SEG, SIDE * SIDE, hidden.shape[1])
    later = (field[:, 1:] - field[:, :-1]) * same_video.astype(jnp.float32)[:, :, None, None]
    change = jnp.concatenate([later, jnp.zeros_like(field[:, :1])], axis=1)
    change = change.reshape(clips * SEG, SIDE, SIDE, hidden.shape[1])
    score = depthwise(change, kernel_near, 1) + depthwise(change, kernel_far, 2) + gate_bias
    gate = jax.nn.sigmoid(score).reshape(hidden.shape)
    return hidden * (1.0 + gate)


def neighbours(values, clips):
    field = values.reshape(clips * SEG, SIDE, SIDE, values.shape[1])
    padded = jnp.pad(field, ((0, 0), (1, 1), (1, 1), (0, 0)))
    taps = [
        padded[:, row : row + SIDE, col : col + SIDE, :] for row in range(3) for col in range(3)
    ]
    return jnp.concatenate(taps, axis=-1).reshape(values.shape[0], 9 * values.shape[1])


def stem_conv(planes, kernel):
    segs, chans = (planes.shape[0], planes.shape[1])
    side = planes.shape[2]
    width = int(round(side**0.5))
    field = planes.reshape(segs, chans, width, width)
    weights = kernel.reshape(chans, 7, 7, kernel.shape[1])
    result = lax.conv_general_dilated(
        field,
        weights,
        (2, 2),
        ((3, 3), (3, 3)),
        dimension_numbers=("NCHW", "IHWO", "NCHW"),
        preferred_element_type=jnp.float32,
    )
    return result.reshape(segs, kernel.shape[1], width // 2 * (width // 2))


def stem_kernel_grad(planes, slopes):
    segs, chans = (planes.shape[0], planes.shape[1])
    width = int(round(planes.shape[2] ** 0.5))
    half = width // 2
    outputs = slopes.shape[1]
    field = planes.reshape(segs, chans, width, width)
    grads = slopes.reshape(segs, outputs, half, half)
    result = lax.conv_general_dilated(
        field,
        grads,
        (1, 1),
        ((3, 2), (3, 2)),
        rhs_dilation=(2, 2),
        dimension_numbers=("CNHW", "IOHW", "NCHW"),
        preferred_element_type=jnp.float32,
    )
    return jnp.transpose(result, (0, 2, 3, 1)).reshape(chans * 49, outputs)


def reduce_weights(parts):
    return (
        lax.psum_scatter(parts[0], "dp", scatter_dimension=0, tiled=True),
        lax.psum_scatter(parts[1], "dp", scatter_dimension=0, tiled=True),
        lax.psum_scatter(parts[2], "dp", scatter_dimension=0, tiled=True),
    )


def transposed(left, right):
    return lax.dot_general(
        left, right, (((1,), (1,)), ((), ())), preferred_element_type=jnp.float32
    )


def weight_grad(left, right):
    return lax.dot_general(
        left, right, (((0,), (0,)), ((), ())), preferred_element_type=jnp.float32
    )


def per_device(
    block_in,
    weight_in,
    weight_mid,
    weight_out,
    gain_in,
    bias_in,
    gain_mid,
    bias_mid,
    gain_out,
    bias_out,
    kernel_near,
    kernel_far,
    gate_bias,
    same_video,
    video,
    stem_center,
    stem_diff,
    stem_gain,
    stem_bias,
    block_grad,
    stem_grad,
):
    groups = lax.axis_size("dp")
    clips = same_video.shape[0]
    rows = block_in.shape[0]
    count = float(rows * groups)
    segs = video.shape[0]
    stem_count = float(segs * stem_grad.shape[2] * groups)
    full_in, full_mid, full_out = (
        lax.all_gather(weight_in, "dp", axis=0, tiled=True),
        lax.all_gather(weight_mid, "dp", axis=0, tiled=True),
        lax.all_gather(weight_out, "dp", axis=0, tiled=True),
    )
    wide_in = lax.all_gather(block_in, "chan", axis=1, tiled=True)
    pre_in = jnp.dot(wide_in, full_in, preferred_element_type=jnp.float32)
    frames = video.reshape(segs, FRAMES, 3, video.shape[2])
    center_frame = frames[:, FRAMES // 2]
    moving = frames[:, 1:].astype(jnp.float32) - frames[:, :-1].astype(jnp.float32)
    diff_frames = moving.reshape(segs, 3 * (FRAMES - 1), video.shape[2]).astype(jnp.bfloat16)
    pre_stem = stem_conv(center_frame, stem_center) + stem_conv(diff_frames, stem_diff)
    sums_in, squares_in, sums_stem, squares_stem = lax.psum(
        (
            jnp.sum(pre_in, 0),
            jnp.sum(pre_in * pre_in, 0),
            jnp.sum(pre_stem, (0, 2)),
            jnp.sum(pre_stem * pre_stem, (0, 2)),
        ),
        "dp",
    )
    center_in, rate_in = norm_stats(sums_in, squares_in, count)
    scaled_in = (pre_in - center_in) * rate_in
    normed_in = scaled_in * gain_in + bias_in
    hidden = jax.nn.silu(normed_in)
    center_stem, rate_stem = norm_stats(sums_stem, squares_stem, stem_count)
    scaled_stem = (pre_stem - center_stem[:, None]) * rate_stem[:, None]
    normed_stem = scaled_stem * stem_gain[:, None] + stem_bias[:, None]
    stem_out = jax.nn.silu(normed_stem).astype(jnp.bfloat16)

    def gate_piece(values, near, far, offset):
        return temporal_gate(values, same_video, near, far, offset)

    mixed, gate_back = jax.vjp(gate_piece, hidden, kernel_near, kernel_far, gate_bias)
    wide_mid = lax.all_gather(mixed.astype(jnp.bfloat16), "chan", axis=1, tiled=True)
    mid_taps = neighbours(wide_mid, clips)
    pre_mid = jnp.dot(mid_taps, full_mid, preferred_element_type=jnp.float32)
    sums_mid, squares_mid = lax.psum((jnp.sum(pre_mid, 0), jnp.sum(pre_mid * pre_mid, 0)), "dp")
    center_mid, rate_mid = norm_stats(sums_mid, squares_mid, count)
    scaled_mid = (pre_mid - center_mid) * rate_mid
    normed_mid = scaled_mid * gain_mid + bias_mid
    second = jax.nn.silu(normed_mid).astype(jnp.bfloat16)
    wide_second = lax.all_gather(second, "chan", axis=1, tiled=True)
    pre_out = jnp.dot(wide_second, full_out, preferred_element_type=jnp.float32)
    sums_out, squares_out = lax.psum((jnp.sum(pre_out, 0), jnp.sum(pre_out * pre_out, 0)), "dp")
    center_out, rate_out = norm_stats(sums_out, squares_out, count)
    scaled_out = (pre_out - center_out) * rate_out
    total = scaled_out * gain_out + bias_out + block_in.astype(jnp.float32)
    block_out = jax.nn.silu(total).astype(jnp.bfloat16)
    grad_total = block_grad.astype(jnp.float32) * silu_slope(total)
    grad_normed_stem = stem_grad.astype(jnp.float32) * silu_slope(normed_stem)
    bias_out_grad, gain_out_grad, stem_bias_grad, stem_gain_grad = lax.psum(
        (
            jnp.sum(grad_total, 0),
            jnp.sum(grad_total * scaled_out, 0),
            jnp.sum(grad_normed_stem, (0, 2)),
            jnp.sum(grad_normed_stem * scaled_stem, (0, 2)),
        ),
        "dp",
    )
    grad_pre_out = norm_back(
        grad_total, scaled_out, gain_out, rate_out, bias_out_grad, gain_out_grad, count
    ).astype(jnp.bfloat16)
    grad_pre_stem = norm_back(
        grad_normed_stem,
        scaled_stem,
        stem_gain[:, None],
        rate_stem[:, None],
        stem_bias_grad[:, None],
        stem_gain_grad[:, None],
        stem_count,
    ).astype(jnp.bfloat16)
    part_center = stem_kernel_grad(center_frame, grad_pre_stem)
    part_diff = stem_kernel_grad(diff_frames, grad_pre_stem)
    part_out = weight_grad(wide_second, grad_pre_out)
    grad_second = lax.psum_scatter(
        transposed(grad_pre_out, full_out), "chan", scatter_dimension=1, tiled=True
    )
    grad_normed_mid = grad_second * silu_slope(normed_mid)
    bias_mid_grad, gain_mid_grad = lax.psum(
        (jnp.sum(grad_normed_mid, 0), jnp.sum(grad_normed_mid * scaled_mid, 0)), "dp"
    )
    grad_pre_mid = norm_back(
        grad_normed_mid, scaled_mid, gain_mid, rate_mid, bias_mid_grad, gain_mid_grad, count
    ).astype(jnp.bfloat16)
    part_mid = weight_grad(mid_taps, grad_pre_mid)
    tap_grads = transposed(grad_pre_mid, full_mid)
    _, tap_adjoint = jax.vjp(
        lambda values: neighbours(values, clips), jnp.zeros(wide_mid.shape, jnp.float32)
    )
    grad_mixed = lax.psum_scatter(
        tap_adjoint(tap_grads)[0], "chan", scatter_dimension=1, tiled=True
    )
    grad_hidden, near_part, far_part, offset_part = gate_back(grad_mixed)
    grad_normed_in = grad_hidden * silu_slope(normed_in)
    bias_in_grad, gain_in_grad, near_grad, far_grad, offset_grad, center_grad, diff_grad = lax.psum(
        (
            jnp.sum(grad_normed_in, 0),
            jnp.sum(grad_normed_in * scaled_in, 0),
            near_part,
            far_part,
            offset_part,
            part_center,
            part_diff,
        ),
        "dp",
    )
    grad_pre_in = norm_back(
        grad_normed_in, scaled_in, gain_in, rate_in, bias_in_grad, gain_in_grad, count
    ).astype(jnp.bfloat16)
    part_in = weight_grad(wide_in, grad_pre_in)
    through_in = lax.psum_scatter(
        transposed(grad_pre_in, full_in), "chan", scatter_dimension=1, tiled=True
    )
    grad_block_in = (through_in + grad_total).astype(jnp.bfloat16)
    sum_in, sum_mid, sum_out = reduce_weights((part_in, part_mid, part_out))
    return (
        block_out,
        stem_out,
        grad_block_in,
        sum_in,
        sum_mid,
        sum_out,
        gain_in_grad,
        bias_in_grad,
        gain_mid_grad,
        bias_mid_grad,
        gain_out_grad,
        bias_out_grad,
        near_grad,
        far_grad,
        offset_grad,
        center_grad,
        diff_grad,
        stem_gain_grad,
        stem_bias_grad,
    )


def solution(mesh):
    placed = (
        P("dp", "chan"),
        P("dp", "chan"),
        P("dp", "chan"),
        P("dp", "chan"),
        P("chan"),
        P("chan"),
        P("chan"),
        P("chan"),
        P("chan"),
        P("chan"),
        P(None, "chan"),
        P(None, "chan"),
        P("chan"),
        P("dp", None),
        P("dp", None, None),
        P(None, "chan"),
        P(None, "chan"),
        P("chan"),
        P("chan"),
        P("dp", "chan"),
        P("dp", "chan", None),
    )
    return jax.shard_map(
        per_device,
        mesh=mesh,
        in_specs=placed,
        out_specs=(
            P("dp", "chan"),
            P("dp", "chan", None),
            P("dp", "chan"),
            P("dp", "chan"),
            P("dp", "chan"),
            P("dp", "chan"),
            P("chan"),
            P("chan"),
            P("chan"),
            P("chan"),
            P("chan"),
            P("chan"),
            P(None, "chan"),
            P(None, "chan"),
            P("chan"),
            P(None, "chan"),
            P(None, "chan"),
            P("chan"),
            P("chan"),
        ),
        check_vma=False,
    )
```

profile of v0, /device:TPU:0, one launch (start us, length us, event | category | flops | bytes accessed | tf_op | source)
XLA Modules:
  0.0 885.6 jit_solution(11460310748672835666)
XLA Ops:
  9.9 33.3 %all_gather.19 = bf16[2048,128]{1,0:T(8,128)(2,1)S(1)} all-gather(bf16[256,128]{1,0:T(8,128)(2,1)} %param.22), channel_id=1, replica_groups=mesh['dp'=8,'chan'=4] {'dp'}, dimensions={0}, use_global_device_ids=true | all-gather | bytes 589824 | tf_op jit(solution)/shard_map/all_gather | solution.py:145
  43.2 16.2 %all-gather.5.cloned.1.call-done = bf16[1568,2048]{1,0:T(8,128)(2,1)} async-done(((bf16[1568,512]{1,0:T(8,128)(2,1)}), bf16[1568,2048]{1,0:T(8,128)(2,1)}) %all-gather.5.cloned.1.call-update) | async-done | bytes 6422544 | tf_op jit(solution)/shard_map/all_gather | solution.py:149
  59.4 4.7 fusion.25
  64.1 21.3 %all-reduce.55 = (f32[128]{0:T(128)S(1)}, f32[128]{0:T(128)S(1)}) all-reduce(f32[128]{0:T(128)S(1)} %get-tuple-element.126, f32[128]{0:T(128)S(1)} %get-tuple-element.125), channel_id=1, replica_groups=mesh['dp'=8,'chan'=4] {'dp'}, use_global_device_ids=true, to_apply=%region_3.0 | all-reduce | flops 256 | bytes 2048 | tf_op jit(solution)/shard_map/psum | solution.py:156
  87.7 2.2 broadcast_add_fusion
  92.4 15.7 %all-gather.7.cloned.1.call-done = bf16[1568,512]{1,0:T(8,128)(2,1)} async-done(((bf16[1568,128]{1,0:T(8,128)(2,1)}), bf16[1568,512]{1,0:T(8,128)(2,1)}) %all-gather.7.cloned.1.call-update) | async-done | bytes 1605648 | tf_op jit(solution)/shard_map/all_gather | solution.py:178
  108.1 3.7 reshape.232
  111.8 10.7 %pad_slice_fusion = (bf16[32,7,7,512]{3,2,1,0:T(8,128)(2,1)}, bf16[32,7,7,512]{3,2,1,0:T(8,128)(2,1)}, bf16[32,7,7,512]{3,2,1,0:T(8,128)(2,1)}, bf16[32,7,7,512]...) fusion(bf16[32,7,7,512]{3,2,1,0:T(8,128)(2,1)} %reshape.232), kind=kLoop, calls=%fused_computation | loop fusion | bytes 14450688 | tf_op jit(solution)/shard_map/slice | solution.py:54
  122.5 2.6 concatenate.25
  125.1 3.7 concatenate.24
  128.8 2.8 constant_dynamic-update-slice_fusion.8
  132.9 2.6 concatenate.31
  135.4 3.7 concatenate.26
  139.1 3.7 concatenate.27
  142.8 3.7 concatenate.28
  146.5 3.7 concatenate.29
  151.7 2.9 constant_dynamic-update-slice_fusion.6
  162.7 7.6 fusion.24
  170.3 21.3 %all-reduce.54 = (f32[128]{0:T(128)S(1)}, f32[128]{0:T(128)S(1)}) all-reduce(f32[128]{0:T(128)S(1)} %get-tuple-element.124, f32[128]{0:T(128)S(1)} %get-tuple-element.123), channel_id=1, replica_groups=mesh['dp'=8,'chan'=4] {'dp'}, use_global_device_ids=true, to_apply=%region_7.0 | all-reduce | flops 256 | bytes 2048 | tf_op jit(solution)/shard_map/psum | solution.py:181
  196.0 3.8 convert_element_type.66
  199.7 6.1 copy.95
  205.8 31.4 %all_gather.23 = bf16[512,512]{1,0:T(8,128)(2,1)S(1)} all-gather(bf16[64,512]{1,0:T(8,128)(2,1)S(1)} %copy-done.20), channel_id=1, replica_groups=mesh['dp'=8,'chan'=4] {'dp'}, dimensions={0}, use_global_device_ids=true | all-gather | bytes 589824 | tf_op jit(solution)/shard_map/all_gather | solution.py:147
  237.3 4.7 fusion.5
  242.0 8.4 fusion.21
  250.5 4.1 fusion.20
  254.5 27.1 %all-reduce.53 = (f32[512]{0:T(512)S(1)}, f32[512]{0:T(512)S(1)}) all-reduce(f32[512]{0:T(512)S(1)} %get-tuple-element.98, f32[512]{0:T(512)S(1)} %get-tuple-element.97), channel_id=1, replica_groups=mesh['dp'=8,'chan'=4] {'dp'}, use_global_device_ids=true, to_apply=%region_11.12 | all-reduce | flops 1024 | bytes 8192 | tf_op jit(solution)/shard_map/psum | solution.py:188
  281.7 5.0 fusion.19
  286.7 19.0 %all-reduce.52 = (f32[16]{0:T(128)S(1)}, f32[16]{0:T(128)S(1)}, f32[512]{0:T(512)S(1)}, f32[512]{0:T(512)S(1)}) all-reduce(f32[16]{0:T(128)S(1)} %get-tuple-element.100, f32[16]{0:T(128)S(1)} %get-tuple-element.99, f32[512]{0:T(512)S(1)} %get-tuple-element.96, f32[512]{0:T(512)S(1)} %get-tuple-element.95), channel_id=1, replica_groups=mesh['dp'=8,'chan'=4] {'dp'}, use_global_device_ids=true, to_apply=%region_15.16 | all-reduce | flops 1056 | bytes 8448 | tf_op jit(solution)/shard_map/psum | solution.py:156
  305.7 2.9 multiply_convert_fusion
  309.7 2.7 fusion.32
  312.6 3.5 copy.98
  316.1 2.5 fusion.26
  318.6 28.8 %reduce-scatter.7.cloned.1.call-done = f32[1568,128]{1,0:T(8,128)} async-done(((f32[1568,512]{1,0:T(8,128)}), f32[1568,128]{1,0:T(8,128)}) %reduce-scatter.7.cloned.1.call-update) | async-done | bytes 802832 | tf_op jit(solution)/shard_map/reduce_scatter | solution.py:219
  347.4 2.7 fusion.23
  350.1 21.3 %all-reduce.51 = (f32[128]{0:T(128)S(1)}, f32[128]{0:T(128)S(1)}, f32[16]{0:T(128)S(1)}, f32[16]{0:T(128)S(1)}) all-reduce(f32[128]{0:T(128)S(1)} %get-tuple-element.122, f32[128]{0:T(128)S(1)} %get-tuple-element.121, f32[16]{0:T(128)S(1)} %get-tuple-element.128, f32[16]{0:T(128)S(1)} %get-tuple-element.127), channel_id=1, replica_groups=mesh['dp'=8,'chan'=4] {'dp'}, use_global_device_ids=true, to_apply=%region_24.25 | all-reduce | flops 288 | bytes 2304 | tf_op jit(solution)/shard_map/psum | solution.py:223
  371.5 1.6 multiply_convert_fusion.3
  373.8 12.7 %fusion.33 = f32[1568,4608]{1,0:T(8,128)} fusion(bf16[1568,128]{1,0:T(8,128)(2,1)S(1)} %multiply_convert_fusion.3, bf16[4608,128]{1,0:T(8,128)(2,1)} %all-gather.9.cloned.1.call-done), kind=kOutput, calls=%fused_computation.195 | convolution fusion | flops 1849688064 | bytes 30482432 | tf_op jit(solution)/shard_map/dot_general | solution.py:104
  386.5 31.1 %reshape.236 = f32[32,7,7,4608]{3,2,1,0:T(8,128)} reshape(f32[1568,4608]{1,0:T(8,128)} %fusion.33) | data formatting | bytes 57802752 | tf_op jit(solution)/shard_map/transpose(jvp())/reshape | solution.py:56
  417.6 22.7 %fusion.29 = (f32[32,7,7,512]{3,2,1,0:T(8,128)}, f32[32,7,7,512]{3,2,1,0:T(8,128)S(1)}, f32[32,7,7,512]{3,2,1,0:T(8,128)}, f32[32,7,7,512]{3,2,1,0:T(8,128)}, f3...) fusion(f32[32,7,7,4608]{3,2,1,0:T(8,128)} %reshape.236), kind=kLoop, calls=%fused_computation.191 | loop fusion | bytes 57802752 | tf_op jit(solution)/shard_map/transpose(jvp())/split | solution.py:56
  440.3 10.1 %pad_add_fusion = f32[32,9,9,512]{3,2,1,0:T(8,128)} fusion(f32[32,7,7,512]{3,2,1,0:T(8,128)} %get-tuple-element.166, f32[32,7,7,512]{3,2,1,0:T(8,128)} %get-tuple-element.167, f32[32,7,7,512]{3,2,1,0:T(8,128)} %get-tuple-element.159), kind=kLoop, calls=%fused_computation.8 | loop fusion | flops 2654208 | bytes 14942208 | tf_op jit(solution)/shard_map/transpose(jvp())/add_any | solution.py:54
  450.4 10.5 %pad_add_fusion.1 = f32[32,7,7,512]{3,2,1,0:T(8,128)} fusion(f32[32,7,7,512]{3,2,1,0:T(8,128)S(1)} %get-tuple-element.160, f32[32,7,7,512]{3,2,1,0:T(8,128)} %get-tuple-element.161, f32[32,7,7,512]{3,2,1,0:T(8,128)} %get-tuple-element.162, f32[32,7,7,512]{3,2,1,0:T(8,128)} %get-tuple-element.163, f32[32,7,7,512]{3,2,1,0:T(8,128)} %get-tuple-element.164, ...), kind=kLoop, calls=%fused_computation.17 | loop fusion | flops 4816896 | bytes 25690112 | tf_op jit(solution)/shard_map/transpose(jvp())/add_any | solution.py:54
  460.9 4.7 reshape.237
  467.3 2.0 copy.112
  469.3 7.6 fusion.31
  477.8 4.1 fusion.30
  482.7 17.7 %reduce-scatter.9.cloned.1.call-done = f32[1568,128]{1,0:T(8,128)} async-done(((f32[1568,512]{1,0:T(8,128)}), f32[1568,128]{1,0:T(8,128)}) %reduce-scatter.9.cloned.1.call-update) | async-done | bytes 802832 | tf_op jit(solution)/shard_map/reduce_scatter | solution.py:234
  500.4 2.6 fusion.61
  503.0 2.2 reshape.238
  505.2 7.2 multiply_reduce_fusion.10
  512.5 1.9 broadcast_multiply_fusion
  517.7 2.2 reshape.240
  520.7 3.8 fusion.22
  524.5 43.5 %all-reduce.50 = (f32[128]{0:T(128)S(1)}, f32[128]{0:T(128)S(1)}, f32[9,128]{1,0:T(8,128)}, f32[9,128]{1,0:T(8,128)}, f32[128]{0:T(128)}, /*index=5*/f32[147,16]{1,0:T(8,128)}, f32[588,16]{1,0:T(8,128)}) all-reduce(f32[128]{0:T(128)} %get-tuple-element.120, f32[128]{0:T(128)S(1)} %get-tuple-element.119, ...), channel_id=1, replica_groups=mesh['dp'=8,'chan'=4] {'dp'}, use_global_device_ids=true, to_apply=%region_29.30 | all-reduce | flops 14448 | bytes 115584 | tf_op jit(solution)/shard_map/psum | solution.py:239
  568.0 1.6 multiply_convert_fusion.2
  570.4 5.0 convolution_bitcast_fusion
  575.4 7.6 fusion.34
  583.1 4.0 fusion.36
  587.2 10.9 %fusion.35 = f32[4608,128]{1,0:T(8,128)} fusion(bf16[1568,4608]{1,0:T(8,128)(2,1)} %constant_dynamic-update-slice_fusion, bf16[1568,128]{1,0:T(8,128)(2,1)} %copy-done.12), kind=kOutput, calls=%fused_computation.197 | convolution fusion | flops 1849688064 | bytes 17211392 | tf_op jit(solution)/shard_map/dot_general | solution.py:110
  600.5 35.2 %reduce-scatter.13.cloned.1.call-done = f32[256,128]{0,1:T(8,128)} async-done(((f32[2048,128]{0,1:T(8,128)}), f32[256,128]{0,1:T(8,128)}) %reduce-scatter.13.cloned.1.call-update) | async-done | bytes 131088 | tf_op jit(solution)/shard_map/reduce_scatter | solution.py:97
  635.7 1.7 copy.107
  637.4 101.0 %reduce-scatter.11.cloned.1.call-done = f32[1568,512]{1,0:T(8,128)} async-done(((f32[1568,2048]{1,0:T(8,128)}), f32[1568,512]{1,0:T(8,128)}) %reduce-scatter.11.cloned.1.call-update) | async-done | bytes 3211280 | tf_op jit(solution)/shard_map/reduce_scatter | solution.py:255
  738.4 3.6 add_convert_fusion
  742.0 64.1 %reduce-scatter.17.cloned.1.call-done = f32[64,512]{1,0:T(8,128)} async-done(((f32[512,512]{1,0:T(8,128)}), f32[64,512]{1,0:T(8,128)}) %reduce-scatter.17.cloned.1.call-update) | async-done | bytes 131088 | tf_op jit(solution)/shard_map/reduce_scatter | solution.py:99
  806.1 72.2 %reduce-scatter.15.cloned.1.call-done = f32[576,128]{1,0:T(8,128)} async-done(((f32[4608,128]{1,0:T(8,128)}), f32[576,128]{1,0:T(8,128)}) %reduce-scatter.15.cloned.1.call-update) | async-done | bytes 294928 | tf_op jit(solution)/shard_map/reduce_scatter | solution.py:98
  (237 shorter events, 34.7 us)
Async XLA Ops:
  7.2 52.3 %all-gather.5.cloned.1.call-start = ((), (), s32[]{:S(2)}) async-start(), calls=%async_computation.6 | async-start | bytes 8028160 | tf_op jit(solution)/shard_map/all_gather | solution.py:149
  7.9 100.2 %all-gather.7.cloned.1.call-start = ((), (), s32[]{:S(2)}) async-start(), calls=%async_computation.7 | async-start | bytes 2007040 | tf_op jit(solution)/shard_map/all_gather | solution.py:178
  8.7 77.7 %copy-start.22 = (f32[4,7]{1,0:T(4,128)}, f32[4,7]{1,0:T(4,128)S(1)}, u32[]{:S(2)}) copy-start(f32[4,7]{1,0:T(4,128)S(1)} %convert_element_type.58) | copy-start | bytes 340
  9.7 77.1 %copy-start.34 = (f32[128]{0:T(128)}, f32[128]{0:T(128)S(1)}, u32[]{:S(2)}) copy-start(f32[128]{0:T(128)S(1)} %get-tuple-element.205) | copy-start | bytes 1540
  9.7 77.1 %copy-start.36 = (f32[128]{0:T(128)}, f32[128]{0:T(128)S(1)}, u32[]{:S(2)}) copy-start(f32[128]{0:T(128)S(1)} %get-tuple-element.206) | copy-start | bytes 1540
  9.7 77.1 %copy-start.38 = (f32[128]{0:T(128)}, f32[128]{0:T(128)S(1)}, u32[]{:S(2)}) copy-start(f32[128]{0:T(128)S(1)} %get-tuple-element.207) | copy-start | bytes 1540
  9.7 77.1 %copy-start.40 = (f32[128]{0:T(128)}, f32[128]{0:T(128)S(1)}, u32[]{:S(2)}) copy-start(f32[128]{0:T(128)S(1)} %get-tuple-element.208) | copy-start | bytes 1540
  9.7 77.1 %copy-start.42 = (f32[128]{0:T(128)}, f32[128]{0:T(128)S(1)}, u32[]{:S(2)}) copy-start(f32[128]{0:T(128)S(1)} %get-tuple-element.209) | copy-start | bytes 1540
  9.7 77.1 %copy-start.44 = (f32[128]{0:T(128)}, f32[128]{0:T(128)S(1)}, u32[]{:S(2)}) copy-start(f32[128]{0:T(128)S(1)} %get-tuple-element.210) | copy-start | bytes 1540
  9.8 77.1 %copy-start.46 = (f32[128]{0:T(128)}, f32[128]{0:T(128)S(1)}, u32[]{:S(2)}) copy-start(f32[128]{0:T(128)S(1)} %get-tuple-element.211) | copy-start | bytes 1540
  9.8 77.1 %copy-start.48 = (f32[128]{0:T(128)}, f32[128]{0:T(128)S(1)}, u32[]{:S(2)}) copy-start(f32[128]{0:T(128)S(1)} %get-tuple-element.212) | copy-start | bytes 1540
  9.8 77.1 %copy-start.50 = (f32[128]{0:T(128)}, f32[128]{0:T(128)S(1)}, u32[]{:S(2)}) copy-start(f32[128]{0:T(128)S(1)} %get-tuple-element.213) | copy-start | bytes 1540
  9.8 77.1 %copy-start.52 = (f32[128]{0:T(128)}, f32[128]{0:T(128)S(1)}, u32[]{:S(2)}) copy-start(f32[128]{0:T(128)S(1)} %get-tuple-element.232) | copy-start | bytes 1540
  9.8 77.1 %copy-start.54 = (f32[128]{0:T(128)}, f32[128]{0:T(128)S(1)}, u32[]{:S(2)}) copy-start(f32[128]{0:T(128)S(1)} %get-tuple-element.233) | copy-start | bytes 1540
  9.8 77.1 %copy-start.56 = (f32[128]{0:T(128)}, f32[128]{0:T(128)S(1)}, u32[]{:S(2)}) copy-start(f32[128]{0:T(128)S(1)} %get-tuple-element.234) | copy-start | bytes 1540
  9.8 77.1 %copy-start.58 = (f32[128]{0:T(128)}, f32[128]{0:T(128)S(1)}, u32[]{:S(2)}) copy-start(f32[128]{0:T(128)S(1)} %get-tuple-element.235) | copy-start | bytes 1540
  9.8 77.1 %copy-start.60 = (f32[128]{0:T(128)}, f32[128]{0:T(128)S(1)}, u32[]{:S(2)}) copy-start(f32[128]{0:T(128)S(1)} %get-tuple-element.236) | copy-start | bytes 1540
  9.8 77.1 %copy-start.62 = (f32[128]{0:T(128)}, f32[128]{0:T(128)S(1)}, u32[]{:S(2)}) copy-start(f32[128]{0:T(128)S(1)} %get-tuple-element.237) | copy-start | bytes 1540
  9.8 77.1 %copy-start.64 = (f32[128]{0:T(128)}, f32[128]{0:T(128)S(1)}, u32[]{:S(2)}) copy-start(f32[128]{0:T(128)S(1)} %get-tuple-element.238) | copy-start | bytes 1540
  9.9 77.1 %copy-start.66 = (f32[128]{0:T(128)}, f32[128]{0:T(128)S(1)}, u32[]{:S(2)}) copy-start(f32[128]{0:T(128)S(1)} %get-tuple-element.239) | copy-start | bytes 1540
  9.9 77.1 %copy-start.68 = (f32[128]{0:T(128)}, f32[128]{0:T(128)S(1)}, u32[]{:S(2)}) copy-start(f32[128]{0:T(128)S(1)} %get-tuple-element.240) | copy-start | bytes 1540
  43.2 42.3 %copy-start.28 = (f32[128]{0:T(128)S(1)}, f32[128]{0:T(128)}, u32[]{:S(2)}) copy-start(f32[128]{0:T(128)} %param.25) | copy-start | bytes 1540
  43.2 42.8 %copy-start.32 = (f32[128]{0:T(128)S(1)}, f32[128]{0:T(128)}, u32[]{:S(2)}) copy-start(f32[128]{0:T(128)} %param.26) | copy-start | bytes 1540
  64.1 26.3 %copy-start.2 = (f32[1568,128]{1,0:T(8,128)}, f32[1568,128]{1,0:T(8,128)S(1)}, u32[]{:S(2)}) copy-start(f32[1568,128]{1,0:T(8,128)S(1)} %get-tuple-element.228) | copy-start | bytes 2408452
  91.6 71.1 %all-gather.9.cloned.1.call-start = ((), (), s32[]{:S(2)}) async-start(), calls=%async_computation.8 | async-start | bytes 1327104 | tf_op jit(solution)/shard_map/all_gather | solution.py:146
  92.3 158.1 %all-gather.11.cloned.1.call-start = ((), (), s32[]{:S(2)}) async-start(), calls=%async_computation.9 | async-start | bytes 2007040 | tf_op jit(solution)/shard_map/all_gather | solution.py:186
  162.6 29.0 %copy-start.70 = (f32[128]{0:T(128)S(1)}, f32[128]{0:T(128)}, u32[]{:S(2)}) copy-start(f32[128]{0:T(128)} %param.27) | copy-start | bytes 1540
  162.6 29.0 %copy-start.72 = (f32[128]{0:T(128)S(1)}, f32[128]{0:T(128)}, u32[]{:S(2)}) copy-start(f32[128]{0:T(128)} %param.28) | copy-start | bytes 1540
  162.6 30.4 %copy-start.31 = (bf16[147,16]{0,1:T(8,128)(2,1)S(1)}, bf16[147,16]{0,1:T(8,128)(2,1)}, u32[]{:S(2)}) copy-start(bf16[147,16]{0,1:T(8,128)(2,1)} %param.36) | copy-start | bytes 14116
  162.6 30.5 %copy-start.21 = (bf16[588,16]{0,1:T(8,128)(2,1)S(1)}, bf16[588,16]{0,1:T(8,128)(2,1)}, u32[]{:S(2)}) copy-start(bf16[588,16]{0,1:T(8,128)(2,1)} %param.37) | copy-start | bytes 56452
  162.6 30.8 %copy-start.13 = (bf16[32,15,1024]{2,0,1:T(8,128)(2,1)S(1)}, bf16[32,15,1024]{2,0,1:T(8,128)(2,1)}, u32[]{:S(2)}) copy-start(bf16[32,15,1024]{2,0,1:T(8,128)(2,1)} %param.35) | copy-start | bytes 2949124
  170.2 24.6 %copy-start.5 = (f32[1568,128]{1,0:T(8,128)}, f32[1568,128]{1,0:T(8,128)S(1)}, u32[]{:S(2)}) copy-start(f32[1568,128]{1,0:T(8,128)S(1)} %get-tuple-element.229) | copy-start | bytes 2408452
  192.7 154.7 %reduce-scatter.7.cloned.1.call-start = ((), (), s32[]{:S(2)}) async-start(), calls=%async_computation.10 | async-start | bytes 4014080 | tf_op jit(solution)/shard_map/reduce_scatter | solution.py:219
  205.8 36.1 %copy-start.1 = (bf16[32,12,32,32]{0,1,3,2:T(8,128)(2,1)S(1)}, bf16[32,12,32,32]{0,1,3,2:T(8,128)(2,1)}, u32[]{:S(2)}) copy-start(bf16[32,12,32,32]{0,1,3,2:T(8,128)(2,1)} %copy.95) | copy-start | bytes 2359300
  250.4 31.3 %copy-start.30 = (f32[512]{0:T(512)S(1)}, f32[512]{0:T(512)}, u32[]{:S(2)}) copy-start(f32[512]{0:T(512)} %param.29) | copy-start | bytes 6148
  250.4 31.3 %copy-start.71 = (f32[512]{0:T(512)S(1)}, f32[512]{0:T(512)}, u32[]{:S(2)}) copy-start(f32[512]{0:T(512)} %param.30) | copy-start | bytes 6148
  312.5 187.9 %reduce-scatter.9.cloned.1.call-start = ((), (), s32[]{:S(2)}) async-start(), calls=%async_computation.11 | async-start | bytes 4014080 | tf_op jit(solution)/shard_map/reduce_scatter | solution.py:234
  371.4 94.4 %copy-start.82 = (f32[16]{0:T(128)}, f32[16]{0:T(128)S(1)}, u32[]{:S(2)}) copy-start(f32[16]{0:T(128)S(1)} %get-tuple-element.139) | copy-start | bytes 196
  371.4 94.4 %copy-start.78 = (f32[16]{0:T(128)}, f32[16]{0:T(128)S(1)}, u32[]{:S(2)}) copy-start(f32[16]{0:T(128)S(1)} %get-tuple-element.138) | copy-start | bytes 196
  465.6 170.1 %reduce-scatter.13.cloned.1.call-start = ((), (), s32[]{:S(2)}) async-start(), calls=%async_computation.13 | async-start | bytes 1179648 | tf_op jit(solution)/shard_map/reduce_scatter | solution.py:97
  477.8 22.6 %copy-start.27 = (f32[128]{0:T(128)S(1)}, f32[128]{0:T(128)}, u32[]{:S(2)}) copy-start(f32[128]{0:T(128)} %copy-done.26) | copy-start | bytes 1540
  477.8 22.6 %copy-start.29 = (f32[128]{0:T(128)S(1)}, f32[128]{0:T(128)}, u32[]{:S(2)}) copy-start(f32[128]{0:T(128)} %param.25) | copy-start | bytes 1540
  477.8 22.6 %copy-start.33 = (f32[128]{0:T(128)S(1)}, f32[128]{0:T(128)}, u32[]{:S(2)}) copy-start(f32[128]{0:T(128)} %param.26) | copy-start | bytes 1540
  482.5 29.8 %copy-start.35 = (f32[128]{0:T(128)S(1)}, f32[128]{0:T(128)}, u32[]{:S(2)}) copy-start(f32[128]{0:T(128)} %copy-done.34) | copy-start | bytes 1540
  482.6 29.8 %copy-start.37 = (f32[128]{0:T(128)S(1)}, f32[128]{0:T(128)}, u32[]{:S(2)}) copy-start(f32[128]{0:T(128)} %copy-done.36) | copy-start | bytes 1540
  482.6 29.8 %copy-start.39 = (f32[128]{0:T(128)S(1)}, f32[128]{0:T(128)}, u32[]{:S(2)}) copy-start(f32[128]{0:T(128)} %copy-done.38) | copy-start | bytes 1540
  482.6 29.8 %copy-start.41 = (f32[128]{0:T(128)S(1)}, f32[128]{0:T(128)}, u32[]{:S(2)}) copy-start(f32[128]{0:T(128)} %copy-done.40) | copy-start | bytes 1540
  482.6 29.8 %copy-start.43 = (f32[128]{0:T(128)S(1)}, f32[128]{0:T(128)}, u32[]{:S(2)}) copy-start(f32[128]{0:T(128)} %copy-done.42) | copy-start | bytes 1540
  482.6 29.8 %copy-start.45 = (f32[128]{0:T(128)S(1)}, f32[128]{0:T(128)}, u32[]{:S(2)}) copy-start(f32[128]{0:T(128)} %copy-done.44) | copy-start | bytes 1540
  482.6 29.8 %copy-start.47 = (f32[128]{0:T(128)S(1)}, f32[128]{0:T(128)}, u32[]{:S(2)}) copy-start(f32[128]{0:T(128)} %copy-done.46) | copy-start | bytes 1540
  482.6 29.8 %copy-start.49 = (f32[128]{0:T(128)S(1)}, f32[128]{0:T(128)}, u32[]{:S(2)}) copy-start(f32[128]{0:T(128)} %copy-done.48) | copy-start | bytes 1540
  482.6 29.8 %copy-start.51 = (f32[128]{0:T(128)S(1)}, f32[128]{0:T(128)}, u32[]{:S(2)}) copy-start(f32[128]{0:T(128)} %copy-done.50) | copy-start | bytes 1540
  482.6 29.8 %copy-start.53 = (f32[128]{0:T(128)S(1)}, f32[128]{0:T(128)}, u32[]{:S(2)}) copy-start(f32[128]{0:T(128)} %copy-done.52) | copy-start | bytes 1540
  482.6 29.8 %copy-start.55 = (f32[128]{0:T(128)S(1)}, f32[128]{0:T(128)}, u32[]{:S(2)}) copy-start(f32[128]{0:T(128)} %copy-done.54) | copy-start | bytes 1540
  482.6 29.8 %copy-start.57 = (f32[128]{0:T(128)S(1)}, f32[128]{0:T(128)}, u32[]{:S(2)}) copy-start(f32[128]{0:T(128)} %copy-done.56) | copy-start | bytes 1540
  482.6 29.8 %copy-start.59 = (f32[128]{0:T(128)S(1)}, f32[128]{0:T(128)}, u32[]{:S(2)}) copy-start(f32[128]{0:T(128)} %copy-done.58) | copy-start | bytes 1540
  482.6 29.8 %copy-start.61 = (f32[128]{0:T(128)S(1)}, f32[128]{0:T(128)}, u32[]{:S(2)}) copy-start(f32[128]{0:T(128)} %copy-done.60) | copy-start | bytes 1540
  482.7 29.8 %copy-start.63 = (f32[128]{0:T(128)S(1)}, f32[128]{0:T(128)}, u32[]{:S(2)}) copy-start(f32[128]{0:T(128)} %copy-done.62) | copy-start | bytes 1540
  482.7 29.8 %copy-start.65 = (f32[128]{0:T(128)S(1)}, f32[128]{0:T(128)}, u32[]{:S(2)}) copy-start(f32[128]{0:T(128)} %copy-done.64) | copy-start | bytes 1540
  482.7 29.8 %copy-start.67 = (f32[128]{0:T(128)S(1)}, f32[128]{0:T(128)}, u32[]{:S(2)}) copy-start(f32[128]{0:T(128)} %copy-done.66) | copy-start | bytes 1540
  482.7 29.8 %copy-start.69 = (f32[128]{0:T(128)S(1)}, f32[128]{0:T(128)}, u32[]{:S(2)}) copy-start(f32[128]{0:T(128)} %copy-done.68) | copy-start | bytes 1540
  575.4 163.0 %reduce-scatter.11.cloned.1.call-start = ((), (), s32[]{:S(2)}) async-start(), calls=%async_computation.12 | async-start | bytes 16056320 | tf_op jit(solution)/shard_map/reduce_scatter | solution.py:255
  583.1 223.1 %reduce-scatter.17.cloned.1.call-start = ((), (), s32[]{:S(2)}) async-start(), calls=%async_computation.15 | async-start | bytes 1179648 | tf_op jit(solution)/shard_map/reduce_scatter | solution.py:99
  587.2 291.1 %reduce-scatter.15.cloned.1.call-start = ((), (), s32[]{:S(2)}) async-start(), calls=%async_computation.14 | async-start | bytes 2654208 | tf_op jit(solution)/shard_map/reduce_scatter | solution.py:98
  (30 other events, 195.7 us)
Sparse Core Ops, SparseCore 0:
  9.6 49.8 all-gather.4
  91.7 16.3 all-gather.6
  110.3 41.0 all-gather.8
  192.8 16.3 all-gather.10
  312.6 34.7 reduce-scatter.6
  465.7 34.6 reduce-scatter.8
  575.5 60.1 reduce-scatter.12
  638.5 99.8 reduce-scatter.10
  742.7 63.3 reduce-scatter.16
  810.0 68.2 reduce-scatter.14
where the time goes:
time: 896 us; the launch traced here: 886 us
  waiting for transfers between devices  353 us (39%)
  blocking collectives  218 us (24%)
  local copies, waits for them, and re-layouts  146 us (16%)
  matrix products  84.1 us (9%)
  other arithmetic  68.3 us (8%)
  between operations  15.7 us (2%)
    reduce_scatter x1, waiting for transfers between devices, per_device(): lax.psum_scatter(transposed(grad_pre_in, full_in), 'chan', scatter_dimens...  101 us
    reduce_scatter x1, waiting for transfers between devices, reduce_weights(): lax.psum_scatter(parts[1], 'dp', scatter_dimension=0, tiled=True)  72.2 us
    reduce_scatter x1, waiting for transfers between devices, reduce_weights(): lax.psum_scatter(parts[2], 'dp', scatter_dimension=0, tiled=True)  64.1 us
    psum x1, blocking collectives, per_device(): lax.psum((jnp.sum(grad_normed_in, 0), jnp.sum(grad_normed_in * scaled_in,...  43.5 us
    psum x2, blocking collectives, per_device(): lax.psum((jnp.sum(pre_in, 0), jnp.sum(pre_in * pre_in, 0), jnp.sum(pre_st...  40.3 us
    reduce_scatter x1, waiting for transfers between devices, reduce_weights(): lax.psum_scatter(parts[0], 'dp', scatter_dimension=0, tiled=True)  35.2 us
    all_gather x1, blocking collectives, per_device(): lax.all_gather(weight_in, 'dp', axis=0, tiled=True)  33.3 us
    all_gather x1, blocking collectives, per_device(): lax.all_gather(weight_out, 'dp', axis=0, tiled=True)  31.4 us
  transfers between devices with their start and end apart: 10, of which 8 were waited for; matrix products, arithmetic and copies ran while one was open for 15% of the time, Pallas kernels for 0%

commit v1 on v0

v1 whole, which is shorter than its diff:
```python
import functools

import jax
import jax.numpy as jnp
from jax import lax
from jax.experimental import pallas as pl
from jax.experimental.pallas import tpu as pltpu
from jax.sharding import PartitionSpec as P

SEG = 8
SIDE = 7
FRAMES = 5
PIXELS = SIDE * SIDE
BLOCK = 16
SPAN = SIDE + 2

eps = 1e-05
vmem_limit = 60 * 1024 * 1024

whole = pl.BlockSpec(memory_space=pltpu.VMEM)
scalars = pl.BlockSpec(memory_space=pltpu.SMEM)


def logistic(value):
    return 0.5 * jnp.tanh(0.5 * value) + 0.5


def silu_slope(value):
    part = logistic(value)
    return part * (1.0 + value * (1.0 - part))


def norm_stats(totals, squares, count):
    center = totals / count
    spread = squares / count - center * center
    return (center, lax.rsqrt(spread + eps))


def kernel_call(body, out_shape, in_specs, scratch=(), flops=0, moved=0):
    return pl.pallas_call(
        body,
        out_shape=out_shape,
        in_specs=in_specs,
        out_specs=jax.tree.map(lambda _: whole, out_shape),
        scratch_shapes=list(scratch),
        compiler_params=pltpu.CompilerParams(vmem_limit_bytes=vmem_limit),
        cost_estimate=pl.CostEstimate(flops=flops, bytes_accessed=moved, transcendentals=0),
    )


PAIRS = SEG // 2
CLIP = SEG * PIXELS


def pair_row(clip, pair):
    return pl.multiple_of(BLOCK * (2 + SPAN * (PAIRS * clip + pair)), BLOCK)


def clip_view(ref, clip, extra=0):
    return ref.at[pl.ds(pl.multiple_of(clip * CLIP, 8), CLIP + extra)]


def lane_mask(width):
    return lax.broadcasted_iota(jnp.int32, (1, 8, width), 1)


def load_map(ref, first, lanes):
    return jnp.stack([ref[pl.ds(first + SIDE * at, 8), lanes] for at in range(SIDE)])


def store_map(ref, first, lanes, value):
    for at in range(SIDE):
        ref[pl.ds(first + SIDE * at, SIDE), lanes] = value[at][:SIDE]


def two_maps(early, late):
    both = jnp.stack([early, late], axis=1)
    return both.reshape(SIDE * BLOCK, early.shape[-1])


def down(value, step):
    zeros = jnp.zeros((abs(step),) + value.shape[1:], value.dtype)
    if step > 0:
        return jnp.concatenate([value[step:], zeros])
    if step < 0:
        return jnp.concatenate([zeros, value[:step]])
    return value


def across(value, step, place):
    if step == 0:
        return value
    moved = pltpu.roll(value, (-step) % 8, 1)
    if step == 2:
        return jnp.where(place < 6, moved, 0.0)
    if step == -2:
        return jnp.where(place > 0, moved, 0.0)
    return moved


def taps_of(near, far):
    for step, kernel in ((1, near), (2, far)):
        for row in range(3):
            yield step, row, [kernel[row * 3 + col] for col in range(3)]


def gate_score(change, near, far, offset, place):
    views = {step: across(change, step, place) for step in (-2, -1, 0, 1, 2)}
    score = jnp.broadcast_to(offset, change.shape)
    for step, row, kernel in taps_of(near, far):
        term = sum(kernel[col] * views[step * (col - 1)] for col in range(3))
        score = score + down(term, step * (row - 1))
    return score, views


def conv_chunk(parts, weights, first, rows, sign):
    total = None
    for col in (1, 0, 2):
        acc = None
        for row in range(3):
            start = pl.multiple_of(first + BLOCK * (1 + sign * (row - 1)), BLOCK)
            for part, weight in zip(parts, weights, strict=True):
                left = part[pl.ds(start, rows), :]
                term = weight(left, row * 3 + col)
                acc = term if acc is None else acc + term
        acc = acc.reshape(rows // 8, 8, acc.shape[-1])
        shift = sign * (col - 1)
        if shift:
            acc = pltpu.roll(acc, (-shift) % 8, 1)
        total = acc if total is None else total + acc
    return total


def gate_mid_body(
    count,
    y_ref,
    same_ref,
    own_ref,
    oth_ref,
    stats_ref,
    par_own_ref,
    par_oth_ref,
    weight_ref,
    mixed_ref,
    mid_ref,
    mid16_ref,
    sums_ref,
    hidden_ref,
    par_ref,
    acc_ref,
):
    rows, width = own_ref.shape
    clips = rows // CLIP
    y = y_ref[0]
    mixed_ref[...] = jnp.zeros_like(mixed_ref)
    hidden_ref[pl.ds(rows, hidden_ref.shape[0] - rows), :] = jnp.zeros(
        (hidden_ref.shape[0] - rows, 2 * width), jnp.float32
    )
    for side, (pre, par) in enumerate(((own_ref, par_own_ref), (oth_ref, par_oth_ref))):
        place = pl.multiple_of(width * (y if side == 0 else 1 - y), width)
        center, rate = norm_stats(
            stats_ref[2 * side : 2 * side + 1], stats_ref[2 * side + 1 : 2 * side + 2], count
        )
        scaled = (pre[...].astype(jnp.float32) - center) * rate
        normed = scaled * par[0:1] + par[1:2]
        hidden_ref[pl.ds(0, rows), pl.ds(place, width)] = normed * logistic(normed)
        par_ref[:, pl.ds(place, width)] = par[...]
    at = lane_mask(128)

    def lanes_step(chunk, _):
        lanes = pl.ds(pl.multiple_of(chunk * 128, 128), 128)
        near = [par_ref[5 + tap : 6 + tap, lanes].reshape(1, 1, 128) for tap in range(9)]
        far = [par_ref[14 + tap : 15 + tap, lanes].reshape(1, 1, 128) for tap in range(9)]
        offset = par_ref[4:5, lanes].reshape(1, 1, 128)

        def clip_step(clip, _):
            view = clip_view(hidden_ref, clip, 56)
            for pair in range(PAIRS):
                maps = [
                    load_map(view, PIXELS * (2 * pair + seg), lanes) for seg in range(3)
                ]
                results = []
                for seg in range(2):
                    same = same_ref[clip, 2 * pair + seg].astype(jnp.float32)
                    change = jnp.where(at < SIDE, same * (maps[seg + 1] - maps[seg]), 0.0)
                    score, _ = gate_score(change, near, far, offset, at)
                    mixed = maps[seg] * (1.0 + logistic(score))
                    results.append(jnp.where(at < SIDE, mixed, 0.0))
                place = pl.ds(pair_row(clip, pair), SIDE * BLOCK)
                mixed_ref[place, lanes] = two_maps(*results).astype(jnp.bfloat16)
            return 0

        return lax.fori_loop(0, clips, clip_step, 0)

    lax.fori_loop(0, 2 * width // 128, lanes_step, 0)
    depth = 2 * width

    def tap_dot(left, tap):
        return jnp.dot(
            left, weight_ref[tap * depth : (tap + 1) * depth], preferred_element_type=jnp.float32
        )

    def conv_step(clip, _):
        span = PAIRS * SPAN * BLOCK
        total = conv_chunk([mixed_ref], [tap_dot], clip * span, span, 1)
        view = clip_view(acc_ref, clip)
        for seg in range(SEG):
            value = [total[2 * (SPAN * (seg // 2) + 1 + row) + seg % 2] for row in range(SIDE)]
            store_map(view, seg * PIXELS, slice(None), value)
        return 0

    lax.fori_loop(0, clips, conv_step, 0)
    result = acc_ref[pl.ds(0, rows), :]
    mid_ref[...] = result
    mid16_ref[...] = result.astype(jnp.bfloat16)
    sums_ref[...] = jnp.zeros_like(sums_ref)
    sums_ref[0:1, :] = jnp.sum(result, 0, keepdims=True)
    sums_ref[1:2, :] = jnp.sum(result * result, 0, keepdims=True)


def map_rows(rows):
    return (rows // (2 * PIXELS) * SPAN + 2) * BLOCK


def gate_mid(count, y, same, own, oth, stats, par_own, par_oth, weight):
    rows, width = own.shape
    spread = map_rows(rows)
    return kernel_call(
        functools.partial(gate_mid_body, count),
        (
            jax.ShapeDtypeStruct((spread, 2 * width), jnp.bfloat16),
            jax.ShapeDtypeStruct((rows, width), jnp.float32),
            jax.ShapeDtypeStruct((rows, width), jnp.bfloat16),
            jax.ShapeDtypeStruct((8, width), jnp.float32),
        ),
        [scalars, scalars] + [whole] * 6,
        (
            pltpu.VMEM((rows + 56, 2 * width), jnp.float32),
            pltpu.VMEM((24, 2 * width), jnp.float32),
            pltpu.VMEM((rows + 8, width), jnp.float32),
        ),
        flops=2 * rows * weight.shape[0] * width,
        moved=weight.size * 2 + rows * width * 12,
    )(y, same, own, oth, stats, par_own, par_oth, weight)


def mid_back_body(
    count,
    y_ref,
    same_ref,
    d_own_ref,
    d_oth_ref,
    mid_own_ref,
    mid_oth_ref,
    stats_ref,
    back_ref,
    pre_ref,
    stats_in_ref,
    par_own_ref,
    par_oth_ref,
    weight_ref,
    weight_oth_ref,
    slopes_ref,
    d_in_ref,
    d_in16_ref,
    sums_ref,
    grads_ref,
    flat_ref,
    oth_ref,
    dmix_ref,
    scaled_ref,
    parts_ref,
):
    rows, width = d_own_ref.shape
    clips = rows // CLIP
    y = y_ref[0]
    everything = slice(None)
    slopes_ref[...] = jnp.zeros_like(slopes_ref)
    oth_ref[...] = jnp.zeros_like(oth_ref)
    flat_ref[pl.ds(rows, flat_ref.shape[0] - rows), :] = jnp.zeros(
        (flat_ref.shape[0] - rows, width), jnp.float32
    )
    at_wide = lane_mask(width)
    for side, (grad, pre, par) in enumerate(
        ((d_own_ref, mid_own_ref, par_own_ref), (d_oth_ref, mid_oth_ref, par_oth_ref))
    ):
        lo = 2 * side
        center, rate = norm_stats(stats_ref[lo : lo + 1], stats_ref[lo + 1 : lo + 2], count)
        scaled = (pre[...].astype(jnp.float32) - center) * rate
        flat_ref[pl.ds(0, rows), :] = (par[2:3] * rate) * (
            grad[...].astype(jnp.float32)
            - back_ref[lo : lo + 1] / count
            - scaled * (back_ref[lo + 1 : lo + 2] / count)
        )

        def spread_step(clip, _, side=side):
            view = clip_view(flat_ref, clip, 8)
            for pair in range(PAIRS):
                maps = [
                    jnp.where(
                        at_wide < SIDE, load_map(view, PIXELS * (2 * pair + seg), everything), 0.0
                    )
                    for seg in range(2)
                ]
                place = pl.ds(pair_row(clip, pair), SIDE * BLOCK)
                if side:
                    oth_ref[place, :] = two_maps(*maps).astype(jnp.bfloat16)
                else:
                    for col in range(3):
                        slopes_ref[col, place, :] = two_maps(
                            *[across(value, 1 - col, at_wide) for value in maps]
                        ).astype(jnp.bfloat16)
            return 0

        lax.fori_loop(0, clips, spread_step, 0)

    depth = 2 * width
    turned = (((1,), (1,)), ((), ()))

    def own_dot(left, tap):
        start = pl.multiple_of(tap * depth + y * width, width)
        return lax.dot_general(
            left, weight_ref[pl.ds(start, width), :], turned, preferred_element_type=jnp.float32
        )

    def oth_dot(left, tap):
        return lax.dot_general(
            left,
            weight_oth_ref[tap * width : (tap + 1) * width],
            turned,
            preferred_element_type=jnp.float32,
        )

    def conv_step(clip, _):
        span = PAIRS * SPAN * BLOCK
        total = conv_chunk([slopes_ref.at[1], oth_ref], [own_dot, oth_dot], clip * span, span, -1)
        dmix_ref[pl.ds(clip * (span // 8), span // 8)] = total
        return 0

    lax.fori_loop(0, clips, conv_step, 0)

    center, rate = norm_stats(stats_in_ref[0:1], stats_in_ref[1:2], count)
    scaled_ref[pl.ds(0, rows), :] = (pre_ref[...] - center) * rate
    scaled_ref[pl.ds(rows, scaled_ref.shape[0] - rows), :] = jnp.zeros(
        (scaled_ref.shape[0] - rows, width), jnp.float32
    )
    parts_ref[...] = jnp.zeros_like(parts_ref)
    at = lane_mask(128)

    def lanes_step(chunk, _):
        lanes = pl.ds(pl.multiple_of(chunk * 128, 128), 128)

        def row_of(index):
            return par_own_ref[index : index + 1, lanes].reshape(1, 1, 128)

        near = [row_of(5 + tap) for tap in range(9)]
        far = [row_of(14 + tap) for tap in range(9)]
        offset, gain, bias = row_of(4), row_of(0), row_of(1)

        def add_part(index, value):
            here = pl.ds(8 * index, 8)
            parts_ref[here, lanes] += jnp.sum(value, 0)

        def clip_step(clip, carry):
            view = clip_view(scaled_ref, clip, 56)
            target = clip_view(flat_ref, clip)
            for pair in range(PAIRS):
                carry = pair_step(clip, pair, carry, view, target)
            return carry

        def pair_step(clip, pair, carry, view, target):
            normed = [
                load_map(view, PIXELS * (2 * pair + seg), lanes) * gain + bias for seg in range(3)
            ]
            parts = [logistic(value) for value in normed]
            hidden = [value * part for value, part in zip(normed, parts, strict=True)]
            for seg in range(2):
                same = same_ref[clip, 2 * pair + seg].astype(jnp.float32)
                change = jnp.where(at < SIDE, same * (hidden[seg + 1] - hidden[seg]), 0.0)
                score, views = gate_score(change, near, far, offset, at)
                gate = logistic(score)
                start = 2 * (SPAN * (PAIRS * clip + pair) + 1) + seg
                d_mixed = jnp.stack([dmix_ref[start + 2 * row, :, lanes] for row in range(SIDE)])
                d_mixed = jnp.where(at < SIDE, d_mixed, 0.0)
                d_score = d_mixed * hidden[seg] * (gate * (1.0 - gate))
                add_part(0, d_score)
                backs = {step: across(d_score, step, at) for step in (-2, -1, 0, 1, 2)}
                d_change = None
                for index, (step, row, kernel) in enumerate(taps_of(near, far)):
                    here = down(d_score, -step * (row - 1))
                    for col in range(3):
                        add_part(1 + 3 * index + col, here * views[step * (col - 1)])
                    term = sum(kernel[col] * backs[-step * (col - 1)] for col in range(3))
                    term = down(term, -step * (row - 1))
                    d_change = term if d_change is None else d_change + term
                d_change = jnp.where(at < SIDE, same * d_change, 0.0)
                d_hidden = d_mixed * (1.0 + gate) - d_change + carry
                carry = d_change
                slope = parts[seg] * (1.0 + normed[seg] * (1.0 - parts[seg]))
                store_map(target, PIXELS * (2 * pair + seg), lanes, d_hidden * slope)
            return carry

        lax.fori_loop(0, clips, clip_step, jnp.zeros((SIDE, 8, 128), jnp.float32))
        return 0

    lax.fori_loop(0, width // 128, lanes_step, 0)
    result = flat_ref[pl.ds(0, rows), :]
    d_in_ref[...] = result
    d_in16_ref[...] = result.astype(jnp.bfloat16)
    sums_ref[...] = jnp.zeros_like(sums_ref)
    sums_ref[0:1, :] = jnp.sum(result, 0, keepdims=True)
    sums_ref[1:2, :] = jnp.sum(result * scaled_ref[pl.ds(0, rows), :], 0, keepdims=True)
    grads_ref[...] = jnp.sum(parts_ref[...].reshape(24, 8, width), 1)


def mid_back(
    count, y, same, d_own, d_oth, mid_own, mid_oth, stats, back, pre, stats_in, par_own, par_oth,
    weight, weight_oth,
):
    rows, width = d_own.shape
    spread = map_rows(rows)
    return kernel_call(
        functools.partial(mid_back_body, count),
        (
            jax.ShapeDtypeStruct((3, spread, width), jnp.bfloat16),
            jax.ShapeDtypeStruct((rows, width), jnp.float32),
            jax.ShapeDtypeStruct((rows, width), jnp.bfloat16),
            jax.ShapeDtypeStruct((8, width), jnp.float32),
            jax.ShapeDtypeStruct((24, width), jnp.float32),
        ),
        [scalars, scalars] + [whole] * 12,
        (
            pltpu.VMEM((rows + 56, width), jnp.float32),
            pltpu.VMEM((spread, width), jnp.bfloat16),
            pltpu.VMEM((spread // 8, 8, width), jnp.float32),
            pltpu.VMEM((rows + 56, width), jnp.float32),
            pltpu.VMEM((24 * 8, width), jnp.float32),
        ),
        flops=2 * rows * weight.shape[0] * width,
        moved=weight.size * 3 + rows * width * 20,
    )(
        y, same, d_own, d_oth, mid_own, mid_oth, stats, back, pre, stats_in, par_own, par_oth,
        weight, weight_oth,
    )


def mid_weight_body(r_ref, mixed_ref, slopes_ref, keep_ref, send_ref, turned_ref):
    spread, depth = mixed_ref.shape
    rows = spread - 2 * BLOCK
    half = keep_ref.shape[1]
    first = r_ref[0] == 0
    turned_ref[...] = mixed_ref[pl.ds(BLOCK, rows), :].T
    for tap in range(9):
        row, col = tap // 3, tap % 3
        right = slopes_ref[col, pl.ds(BLOCK * (2 - row), rows), :]
        value = jnp.dot(turned_ref[...], right, preferred_element_type=jnp.float32)
        low, high = value[:, :half], value[:, half:]
        keep_ref[tap * depth : (tap + 1) * depth] = jnp.where(first, low, high)
        send_ref[tap * depth : (tap + 1) * depth] = jnp.where(first, high, low).astype(jnp.bfloat16)


def mid_weight(r, mixed, slopes):
    spread, depth = mixed.shape
    width = slopes.shape[2]
    return kernel_call(
        mid_weight_body,
        (
            jax.ShapeDtypeStruct((9 * depth, width // 2), jnp.float32),
            jax.ShapeDtypeStruct((9 * depth, width // 2), jnp.bfloat16),
        ),
        [scalars, whole, whole],
        (pltpu.VMEM((depth, spread - 2 * BLOCK), jnp.bfloat16),),
        flops=2 * spread * 9 * depth * width,
        moved=spread * (2 * depth + 6 * width) + 9 * depth * width * 3,
    )(r, mixed, slopes)


def stem_conv(planes, kernel):
    segs, chans = (planes.shape[0], planes.shape[1])
    side = planes.shape[2]
    width = int(round(side**0.5))
    field = planes.reshape(segs, chans, width, width)
    weights = kernel.reshape(chans, 7, 7, kernel.shape[1])
    result = lax.conv_general_dilated(
        field,
        weights,
        (2, 2),
        ((3, 3), (3, 3)),
        dimension_numbers=("NCHW", "IHWO", "NCHW"),
        preferred_element_type=jnp.float32,
    )
    return result.reshape(segs, kernel.shape[1], width // 2 * (width // 2))


def stem_kernel_grad(planes, slopes):
    segs, chans = (planes.shape[0], planes.shape[1])
    width = int(round(planes.shape[2] ** 0.5))
    half = width // 2
    outputs = slopes.shape[1]
    field = planes.reshape(segs, chans, width, width)
    grads = slopes.reshape(segs, outputs, half, half)
    result = lax.conv_general_dilated(
        field,
        grads,
        (1, 1),
        ((3, 2), (3, 2)),
        rhs_dilation=(2, 2),
        dimension_numbers=("CNHW", "IOHW", "NCHW"),
        preferred_element_type=jnp.float32,
    )
    return jnp.transpose(result, (0, 2, 3, 1)).reshape(chans * 49, outputs)


def norm_back(upstream, scaled, gain, rate, bias_grad, gain_grad, count):
    return gain * rate * (upstream - bias_grad / count - scaled * gain_grad / count)


def swap(value, axis, bit):
    size = lax.axis_size(axis)
    return lax.ppermute(value, axis, [(at, at ^ bit) for at in range(size)])


def steps_of(axis):
    size = lax.axis_size(axis)
    assert size & (size - 1) == 0
    return [1 << at for at in range(size.bit_length() - 1)]


def sum_over(value, axis):
    for bit in steps_of(axis):
        value = value + swap(value, axis, bit)
    return value


def ordered(second, own, other, axis=0):
    return jnp.where(
        second, jnp.concatenate([other, own], axis), jnp.concatenate([own, other], axis)
    )


def gather_rows(value, axis):
    index = lax.axis_index(axis)
    full = value[None]
    bits = steps_of(axis)
    for bit in reversed(bits):
        other = swap(full, axis, bit)
        full = ordered((index & bit) != 0, full[None], other[None])
    full = full.reshape([2] * len(bits) + list(value.shape))
    order = list(reversed(range(len(bits))))
    full = full.transpose(order + [len(bits), len(bits) + 1])
    return full.reshape(-1, value.shape[1])


def scatter_rows(keep, send, axis):
    bits = steps_of(axis)
    index = lax.axis_index(axis)
    for place, bit in enumerate(bits):
        total = keep + swap(send, axis, bit).astype(jnp.float32)
        if place + 1 < len(bits):
            keep, send = split_rows(total, (index >> (place + 1)) & 1, len(bits) - place - 1)
        else:
            keep = total
    return keep


def split_rows(value, bit, left):
    rows, width = value.shape
    blocks = value.reshape(1 << (left - 1), 2, rows >> left, width)
    low, high = blocks[:, 0], blocks[:, 1]
    keep = jnp.where(bit == 0, low, high).reshape(-1, width)
    send = jnp.where(bit == 0, high, low).astype(jnp.bfloat16).reshape(-1, width)
    return keep, send


def reduce_rows(value, axis):
    bits = steps_of(axis)
    keep, send = split_rows(value, lax.axis_index(axis) & 1, len(bits))
    return scatter_rows(keep, send, axis)


def transposed(left, right):
    return lax.dot_general(
        left, right, (((1,), (1,)), ((), ())), preferred_element_type=jnp.float32
    )


def weight_grad(left, right):
    return lax.dot_general(
        left, right, (((0,), (0,)), ((), ())), preferred_element_type=jnp.float32
    )


def per_device(
    block_in,
    weight_in,
    weight_mid,
    weight_out,
    gain_in,
    bias_in,
    gain_mid,
    bias_mid,
    gain_out,
    bias_out,
    kernel_near,
    kernel_far,
    gate_bias,
    same_video,
    video,
    stem_center,
    stem_diff,
    stem_gain,
    stem_bias,
    block_grad,
    stem_grad,
):
    groups = lax.axis_size("dp")
    assert lax.axis_size("chan") == 4
    clips = same_video.shape[0]
    rows, quarter = block_in.shape
    half = rows // 2
    narrow = weight_in.shape[1]
    width = 2 * narrow
    count = float(rows * groups)
    segs = video.shape[0]
    stem_count = float(segs * stem_grad.shape[2] * groups)
    chan = lax.axis_index("chan")
    core, y = chan % 2, chan // 2
    y_scalar, core_scalar = y.reshape(1), core.reshape(1)

    def my_rows(value, which):
        return lax.dynamic_slice_in_dim(value, which * half, half, 0)

    mine, others = my_rows(block_in, core), my_rows(block_in, 1 - core)
    pieces = [mine, swap(others, "chan", 1), swap(mine, "chan", 2), swap(others, "chan", 3)]

    own_in = gather_rows(weight_in, "dp")
    full_in = ordered(core == 1, own_in, swap(own_in, "chan", 1), 1)
    packed = jnp.concatenate([weight_mid, weight_out.reshape(-1, narrow)], 0)
    gathered = lax.all_gather(packed, "dp", axis=0)
    own_mid = gathered[:, : weight_mid.shape[0]].reshape(-1, narrow)
    full_out = gathered[:, weight_mid.shape[0] :].reshape(-1, weight_out.shape[1])
    full_mid = ordered(core == 1, own_mid, swap(own_mid, "chan", 1), 1)
    slab = lax.dynamic_slice_in_dim(own_mid.reshape(9, 2, width, narrow), 1 - y, 1, 1)
    slab = swap(slab.reshape(9 * width, narrow), "chan", 2)
    oth_mid = ordered(core == 1, slab, swap(slab, "chan", 1), 1)
    away = lax.dynamic_slice_in_dim(full_in, (chan ^ 2) * quarter, quarter, 0)
    here = lax.dynamic_slice_in_dim(full_in, chan * quarter, quarter, 0)
    rows_in = ordered(y == 1, here, swap(away, "chan", 2), 1)

    params = jnp.concatenate(
        [
            jnp.stack([gain_in, bias_in, gain_mid, bias_mid, gate_bias]),
            kernel_near,
            kernel_far,
            jnp.zeros((1, narrow), jnp.float32),
        ]
    )
    par_own = ordered(core == 1, params, swap(params, "chan", 1), 1)
    par_oth = swap(par_own, "chan", 2)
    same = lax.dynamic_slice_in_dim(same_video, core * (clips // 2), clips // 2, 0)
    same = jnp.concatenate([same, jnp.zeros((clips // 2, 1), jnp.int32)], 1)

    frames = video.reshape(segs, FRAMES, 3, video.shape[2])
    center_frame = frames[:, FRAMES // 2]
    moving = frames[:, 1:].astype(jnp.float32) - frames[:, :-1].astype(jnp.float32)
    diff_frames = moving.reshape(segs, 3 * (FRAMES - 1), video.shape[2]).astype(jnp.bfloat16)
    pre_stem = stem_conv(center_frame, stem_center) + stem_conv(diff_frames, stem_diff)

    pre_in = sum(
        jnp.dot(
            piece,
            lax.dynamic_slice_in_dim(full_in, (chan ^ at) * quarter, quarter, 0),
            preferred_element_type=jnp.float32,
        )
        for at, piece in enumerate(pieces)
    )
    pre_in_oth = swap(pre_in.astype(jnp.bfloat16), "chan", 2)

    def both_sums(first, second, extra):
        own = jnp.stack([first, second])
        own = own + swap(own, "chan", 1)
        packed = jnp.concatenate([own] + extra)
        packed = sum_over(packed, "dp")
        own = packed[:2]
        oth = swap(own, "chan", 2)
        return jnp.concatenate([own, oth, jnp.zeros((4, width), jnp.float32)]), packed[2:]

    def stem_row(first, second):
        row = jnp.concatenate([first, second])
        return [jnp.pad(row, (0, width - row.shape[0]))[None]]

    outs = stem_grad.shape[1]
    stats_in, stem_stats = both_sums(
        jnp.sum(pre_in, 0),
        jnp.sum(pre_in * pre_in, 0),
        stem_row(jnp.sum(pre_stem, (0, 2)), jnp.sum(pre_stem * pre_stem, (0, 2))),
    )
    center_stem, rate_stem = norm_stats(stem_stats[0, :outs], stem_stats[0, outs : 2 * outs], stem_count)
    scaled_stem = (pre_stem - center_stem[:, None]) * rate_stem[:, None]
    normed_stem = scaled_stem * stem_gain[:, None] + stem_bias[:, None]
    stem_out = (normed_stem * logistic(normed_stem)).astype(jnp.bfloat16)
    grad_normed_stem = stem_grad.astype(jnp.float32) * silu_slope(normed_stem)
    stem_sums = stem_row(
        jnp.sum(grad_normed_stem, (0, 2)), jnp.sum(grad_normed_stem * scaled_stem, (0, 2))
    )

    mixed, pre_mid, pre_mid16, sums_mid = gate_mid(
        count, y_scalar, same, pre_in, pre_in_oth, stats_in, par_own, par_oth, full_mid
    )
    pre_mid_oth = swap(pre_mid16, "chan", 2)
    stats_mid, stem_back = both_sums(sums_mid[0], sums_mid[1], stem_sums)

    def mid_norm(value, stats, par):
        center, rate = norm_stats(stats[0], stats[1], count)
        scaled = (value.astype(jnp.float32) - center) * rate
        return scaled, scaled * par[2] + par[3]

    scaled_mid, normed_mid = mid_norm(pre_mid, stats_mid[:2], par_own)
    _, normed_oth = mid_norm(pre_mid_oth, stats_mid[2:4], par_oth)
    second_own = (normed_mid * logistic(normed_mid)).astype(jnp.bfloat16)
    second_oth = (normed_oth * logistic(normed_oth)).astype(jnp.bfloat16)
    second_half = ordered(y == 1, second_own, second_oth, 1)
    second = ordered(core == 1, second_half, swap(second_half, "chan", 1))

    pre_out = jnp.dot(second, full_out, preferred_element_type=jnp.float32)
    stats_out = sum_over(jnp.stack([jnp.sum(pre_out, 0), jnp.sum(pre_out * pre_out, 0)]), "dp")
    center_out, rate_out = norm_stats(stats_out[0], stats_out[1], count)
    scaled_out = (pre_out - center_out) * rate_out
    total = scaled_out * gain_out + bias_out + block_in.astype(jnp.float32)
    part = logistic(total)
    block_out = (total * part).astype(jnp.bfloat16)
    grad_total = block_grad.astype(jnp.float32) * (part * (1.0 + total * (1.0 - part)))
    back_out = sum_over(
        jnp.stack([jnp.sum(grad_total, 0), jnp.sum(grad_total * scaled_out, 0)]), "dp"
    )
    bias_out_grad, gain_out_grad = back_out[0], back_out[1]
    grad_pre_out = norm_back(
        grad_total, scaled_out, gain_out, rate_out, bias_out_grad, gain_out_grad, count
    ).astype(jnp.bfloat16)

    stem_bias_grad, stem_gain_grad = stem_back[0, :outs], stem_back[0, outs : 2 * outs]
    grad_pre_stem = norm_back(
        grad_normed_stem,
        scaled_stem,
        stem_gain[:, None],
        rate_stem[:, None],
        stem_bias_grad[:, None],
        stem_gain_grad[:, None],
        stem_count,
    ).astype(jnp.bfloat16)
    part_center = stem_kernel_grad(center_frame, grad_pre_stem)
    part_diff = stem_kernel_grad(diff_frames, grad_pre_stem)

    grad_second = transposed(grad_pre_out, full_out)
    keep, send = my_rows(grad_second, core), my_rows(grad_second, 1 - core)
    keep = keep + swap(send.astype(jnp.bfloat16), "chan", 1).astype(jnp.float32)
    send = lax.dynamic_slice_in_dim(keep, (1 - y) * width, width, 1)
    keep = lax.dynamic_slice_in_dim(keep, y * width, width, 1)
    grad_second = keep + swap(send.astype(jnp.bfloat16), "chan", 2).astype(jnp.float32)
    grad_normed_mid = grad_second * silu_slope(normed_mid)
    grad_mid_oth = swap(grad_normed_mid.astype(jnp.bfloat16), "chan", 2)
    back_mid, _ = both_sums(
        jnp.sum(grad_normed_mid, 0), jnp.sum(grad_normed_mid * scaled_mid, 0), []
    )
    sum_out = reduce_rows(weight_grad(second, grad_pre_out), "dp")

    slopes, grad_in, grad_in16, sums_in, gate_parts = mid_back(
        count, y_scalar, same, grad_normed_mid, grad_mid_oth, pre_mid, pre_mid_oth, stats_mid,
        back_mid, pre_in, stats_in, par_own, par_oth, full_mid, oth_mid,
    )
    grad_in_oth = swap(grad_in16, "chan", 2)
    back_in, _ = both_sums(sums_in[0], sums_in[1], [])
    keep, send = mid_weight(core_scalar, mixed, slopes)
    part_mid = keep + swap(send, "chan", 1).astype(jnp.float32)
    sum_mid = reduce_rows(part_mid, "dp")

    def in_back(value, pre, stats, par, back):
        center, rate = norm_stats(stats[0], stats[1], count)
        scaled = (pre.astype(jnp.float32) - center) * rate
        return norm_back(
            value.astype(jnp.float32), scaled, par[0], rate, back[0], back[1], count
        ).astype(jnp.bfloat16)

    pre_own = in_back(grad_in, pre_in, stats_in[:2], par_own, back_in[:2])
    pre_oth = in_back(grad_in_oth, pre_in_oth, stats_in[2:4], par_oth, back_in[2:4])
    grad_half = ordered(y == 1, pre_own, pre_oth, 1)
    grad_pre_in = ordered(core == 1, grad_half, swap(grad_half, "chan", 1))
    grad_block_in = (transposed(grad_pre_in, rows_in) + grad_total).astype(jnp.bfloat16)
    blocks = jnp.stack([weight_grad(piece, pre_own) for piece in pieces])
    blocks = jnp.where(core == 1, blocks[jnp.array([1, 0, 3, 2])], blocks)
    blocks = jnp.where(y == 1, blocks[jnp.array([2, 3, 0, 1])], blocks).reshape(-1, width)
    send = lax.dynamic_slice_in_dim(blocks, (1 - core) * narrow, narrow, 1)
    keep = lax.dynamic_slice_in_dim(blocks, core * narrow, narrow, 1)
    part_in = keep + swap(send.astype(jnp.bfloat16), "chan", 1).astype(jnp.float32)
    sum_in = reduce_rows(part_in, "dp")

    gate_parts = gate_parts + swap(gate_parts, "chan", 1)
    stem_flat = jnp.concatenate([part_center, part_diff]).reshape(-1)
    stem_size = stem_flat.shape[0]
    padded = -(-stem_size // width)
    stem_flat = jnp.pad(stem_flat, (0, padded * width - stem_size)).reshape(padded, width)
    small = sum_over(jnp.concatenate([gate_parts, stem_flat]), "dp")
    stem_flat = small[24:].reshape(-1)[:stem_size].reshape(-1, outs)
    split = part_center.shape[0]

    def my_columns(value):
        return lax.dynamic_slice_in_dim(value, core * narrow, narrow, value.ndim - 1)

    gate_grads = my_columns(small[:24])
    mid_grads, in_grads = my_columns(back_mid), my_columns(back_in)
    return (
        block_out,
        stem_out,
        grad_block_in,
        sum_in,
        sum_mid,
        sum_out,
        in_grads[1],
        in_grads[0],
        mid_grads[1],
        mid_grads[0],
        gain_out_grad,
        bias_out_grad,
        gate_grads[1:10],
        gate_grads[10:19],
        gate_grads[0],
        stem_flat[:split],
        stem_flat[split:],
        stem_gain_grad,
        stem_bias_grad,
    )


def solution(mesh):
    placed = (
        P("dp", "chan"),
        P("dp", "chan"),
        P("dp", "chan"),
        P("dp", "chan"),
        P("chan"),
        P("chan"),
        P("chan"),
        P("chan"),
        P("chan"),
        P("chan"),
        P(None, "chan"),
        P(None, "chan"),
        P("chan"),
        P("dp", None),
        P("dp", None, None),
        P(None, "chan"),
        P(None, "chan"),
        P("chan"),
        P("chan"),
        P("dp", "chan"),
        P("dp", "chan", None),
    )
    return jax.shard_map(
        per_device,
        mesh=mesh,
        in_specs=placed,
        out_specs=(
            P("dp", "chan"),
            P("dp", "chan", None),
            P("dp", "chan"),
            P("dp", "chan"),
            P("dp", "chan"),
            P("dp", "chan"),
            P("chan"),
            P("chan"),
            P("chan"),
            P("chan"),
            P("chan"),
            P("chan"),
            P(None, "chan"),
            P(None, "chan"),
            P("chan"),
            P(None, "chan"),
            P(None, "chan"),
            P("chan"),
            P("chan"),
        ),
        check_vma=False,
    )
```

time: 896 us -> 384 us (0.43)
  waiting for transfers between devices: 353 us -> 98.5 us
  blocking collectives: 218 us -> 0 us
  local copies, waits for them, and re-layouts: 146 us -> 66.2 us
  starting transfers between devices: 0.88 us -> 57.3 us
  Pallas kernels: 0 us -> 32.3 us
  matrix products: 84.1 us -> 53.3 us
  other arithmetic: 68.3 us -> 56.8 us
    reduce_scatter x6 -> x0, waiting for transfers between devices: 319 us -> none  [the longest x1 101 us: per_device(): lax.psum_scatter(transposed(grad_pre_in, full_in), 'chan', scatter_dimens...]
    psum x6 -> x0, blocking collectives: 154 us -> none  [the longest x1 43.5 us: per_device(): lax.psum((jnp.sum(grad_normed_in, 0), jnp.sum(grad_normed_in * scaled_in,...]
    ppermute x0 -> x62, waiting for transfers between devices: none -> 98.5 us  [swap(): return lax.ppermute(value, axis, [(at, at ^ bit) for at in range(size)])]
    all_gather x2 -> x0, blocking collectives: 64.8 us -> none  [the longest x1 33.3 us: per_device(): lax.all_gather(weight_in, 'dp', axis=0, tiled=True)]
    ppermute x0 -> x62, starting transfers between devices: none -> 57.3 us  [swap(): return lax.ppermute(value, axis, [(at, at ^ bit) for at in range(size)])]
    reshape x6 -> x4, local copies, waits for them, and re-layouts: 43.9 us -> 2.14 us  [the longest x1 1.14 us: per_device(): stem_flat = jnp.concatenate([part_center, part_diff]).reshape(-1)]
    pallas_call x0 -> x3, Pallas kernels: none -> 32.3 us  [the longest x1 14.4 us: mid_back(): kernel_call(functools.partial(mid_back_body, count), (jax.ShapeDtypeStruc...]
    all_gather x4 -> x1, waiting for transfers between devices: 32 us -> 0.01 us  [per_device(): gathered = lax.all_gather(packed, 'dp', axis=0)]
  transfers between devices with their start and end apart: 10 -> 63, of which waited for: 8 -> 31; matrix products, arithmetic and copies ran while one was open for 15% -> 44% of each run, Pallas kernels for 0% -> 6%
where the time goes in v1:
time: 384 us; the launch traced here: 380 us
  waiting for transfers between devices  98.5 us (26%)
  local copies, waits for them, and re-layouts  66.2 us (17%)
  starting transfers between devices  57.3 us (15%)
  other arithmetic  56.8 us (15%)
  matrix products  53.3 us (14%)
  Pallas kernels  32.3 us (8%)
  between operations  15.6 us (4%)
    ppermute x62, waiting for transfers between devices, swap(): return lax.ppermute(value, axis, [(at, at ^ bit) for at in range(size)])  98.5 us
    ppermute x62, starting transfers between devices, swap(): return lax.ppermute(value, axis, [(at, at ^ bit) for at in range(size)])  57.3 us
    pallas_call x1, Pallas kernels, mid_back(): kernel_call(functools.partial(mid_back_body, count), (jax.ShapeDtypeStruc...  14.4 us
    conv_general_dilated x2, matrix products, stem_conv(): lax.conv_general_dilated(field, weights, (2, 2), ((3, 3), (3, 3)), dimens...  13.6 us
    convert_element_type x2, local copies, waits for them, and re-layouts, per_device(): moving.reshape(segs, 3 * (FRAMES - 1), video.shape[2]).astype(jnp.bfloat16)  13 us
    concatenate x1, local copies, waits for them, and re-layouts, per_device(): jnp.concatenate([jnp.stack([gain_in, bias_in, gain_mid, bias_mid, gate_bi...  12.2 us
    select_n x10, other arithmetic, ordered(): jnp.where(second, jnp.concatenate([other, own], axis), jnp.concatenate([o...  11.4 us
    pallas_call x1, Pallas kernels, gate_mid(): kernel_call(functools.partial(gate_mid_body, count), (jax.ShapeDtypeStruc...  10.8 us
  transfers between devices with their start and end apart: 63, of which 31 were waited for; matrix products, arithmetic and copies ran while one was open for 44% of the time, Pallas kernels for 6%

profile of v1, /device:TPU:0, one launch (start us, length us, event | category | flops | bytes accessed | tf_op | source)
XLA Modules:
  0.0 380.0 jit_solution(13654758752502041641)
XLA Ops:
  7.3 4.1 %collective-permute-start = (bf16[1,256,128]{2,1,0:T(8,128)(2,1)}, bf16[1,256,128]{2,1,0:T(8,128)(2,1)S(1)}, u32[]{:S(2)}, u32[]{:S(2)}) collective-permute-start(bf16[1,256,128]{2,1,0:T(8,128)(2,1)} %bitcast.259), channel_id=1, source_target_pairs={{0,16},{4,20},{8,24},{12,28},{16,0},{20,4},{24,8},{28,12},{1,17},{... | collective-permute-start | bytes 196616 | tf_op jit(solution)/shard_map/ppermute | solution.py:520
  11.4 2.6 constant_dynamic-slice_fusion.6
  15.8 1.6 collective-permute-start.1
  23.5 3.4 fusion.28
  26.9 5.1 %collective-permute-done.2 = bf16[2,2,1,256,128]{4,3,1,2,0:T(8,128)(2,1)} collective-permute-done((bf16[2,2,1,256,128]{4,3,1,2,0:T(8,128)(2,1)}, bf16[2,2,1,256,128]{4,3,1,2,0:T(8,128)(2,1)}, u32[]{:S(2)}, u32[]{:S(2)}) %collective-permute-start.2) | collective-permute-done | bytes 262176 | tf_op jit(solution)/shard_map/ppermute | solution.py:520
  35.2 4.9 %convert_element_type.190 = bf16[32,12,32,32]{3,2,0,1:T(8,128)(2,1)} reshape(bf16[32,4,3,1024]{3,0,2,1:T(8,128)(2,1)} %subtract_convert_fusion) | data formatting | bytes 1572864 | tf_op jit(solution)/shard_map/convert_element_type | solution.py:666
  40.1 8.1 %copy.167 = bf16[32,12,32,32]{0,1,3,2:T(8,128)(2,1)} copy(bf16[32,12,32,32]{3,2,0,1:T(8,128)(2,1)} %convert_element_type.190) | data formatting | bytes 1572864 | tf_op jit(solution)/shard_map/convert_element_type | solution.py:666
  48.2 10.1 %fusion.57 = (f32[16]{0:T(128)S(1)}, f32[16]{0:T(128)S(1)}, f32[32,16,16,16]{0,1,3,2:T(8,128)}) fusion(f32[32,16,16,16]{0,1,3,2:T(8,128)S(1)} %fusion.28, bf16[32,12,32,32]{0,1,3,2:T(8,128)(2,1)} %copy.167, bf16[12,7,7,16]{3,2,1,0:T(8,128)(2,1)S(1)} %reshape.743), kind=kOutput, calls=%fused_computation.205 | convolution fusion | flops 138592224 | bytes 1853952 | tf_op jit(solution)/shard_map/conv_general_dilated | solution.py:484
  58.4 1.8 maximum_select_fusion.5
  61.0 1.6 fusion.18
  65.7 2.6 fusion.59
  72.0 12.2 %concatenate.266 = f32[24,128]{1,0:T(8,128)S(1)} concatenate(f32[1,128]{1,0:T(1,128)S(1)} %bitcast.325, f32[1,128]{1,0:T(1,128)S(1)} %bitcast.326, f32[1,128]{1,0:T(1,128)S(1)} %bitcast.327, f32[1,128]{1,0:T(1,128)S(1)} %bitcast.328, f32[1,128]{1,0:T(1,128)S(1)} %bitcast.329, f32[9,128]{1,0:T(8,128)S(1)} %copy-done.50, f32[9,128]{1,0:T(8,128)S(1)} %copy-done.51, ...), dimensions={0} | concatenate | bytes 24576 | tf_op jit(solution)/shard_map/concatenate | solution.py:650
  87.5 1.5 collective-permute-start.10
  90.8 2.0 copy.170
  95.2 1.6 collective-permute-start.14
  100.1 2.5 fusion.60
  102.6 5.1 %collective-permute-done.12 = f32[2,256]{1,0:T(2,128)S(1)} collective-permute-done((f32[2,256]{1,0:T(2,128)S(1)}, f32[2,256]{1,0:T(2,128)S(1)}, u32[]{:S(2)}, u32[]{:S(2)}) %collective-permute-start.12) | collective-permute-done | bytes 2080 | tf_op jit(solution)/shard_map/ppermute | solution.py:520
  108.4 3.7 maximum_select_fusion.weight_ref
  112.8 10.8 %shard_map.366 = (bf16[1184,512]{1,0:T(8,128)(2,1)}, f32[784,256]{1,0:T(8,128)}, bf16[784,256]{1,0:T(8,128)(2,1)}, f32[8,256]{1,0:T(8,128)}) custom-call(s32[1]{0:T(128)} %bitcast.y_ref, s32[2,8]{1,0:T(2,128)} %concatenate.243.same_ref, f32[784,256]{1,0:T(8,128)} %get-tuple-element.195.own_ref.pre_ref, bf16[784,256]{1,0:T(8,128)(2,1)} %copy-done.31, ...), custom_call_target="tpu_custom_call" | custom-call | flops 1849688064 | bytes 4767744 | tf_op jit(solution)/shard_map/pallas_call | solution.py:228
  126.4 3.6 collective-permute-done.18
  140.3 4.9 %collective-permute-done.21 = f32[2,256]{1,0:T(2,128)S(1)} collective-permute-done((f32[2,256]{1,0:T(2,128)S(1)}, f32[2,256]{1,0:T(2,128)S(1)}, u32[]{:S(2)}, u32[]{:S(2)}) %collective-permute-start.21) | collective-permute-done | bytes 2080 | tf_op jit(solution)/shard_map/ppermute | solution.py:520
  147.6 1.5 collective-permute-start.37
  151.1 12.4 %collective-permute-done.37 = bf16[2304,128]{1,0:T(8,128)(2,1)} collective-permute-done((bf16[2304,128]{1,0:T(8,128)(2,1)}, bf16[2304,128]{1,0:T(8,128)(2,1)}, u32[]{:S(2)}, u32[]{:S(2)}) %collective-permute-start.37) | collective-permute-done | bytes 589856 | tf_op jit(solution)/shard_map/ppermute | solution.py:520
  163.5 4.8 %fusion.56 = (f32[512]{0:T(512)S(1)}, f32[512]{0:T(512)S(1)}, f32[1568,512]{1,0:T(8,128)}) fusion(bf16[512,512]{1,0:T(8,128)(2,1)S(1)} %reshape.746, bf16[784,512]{1,0:T(8,128)(2,1)} %copy-done.29, bf16[784,512]{1,0:T(8,128)(2,1)} %collective-permute-done.22, pred[]{:T(512)S(6)} %eq.12), kind=kOutput, calls=%fused_computation.204 | convolution fusion | flops 831716352 | bytes 5345281 | tf_op jit(solution)/shard_map/dot_general | solution.py:725
  173.2 3.1 maximum_select_fusion.4.weight_oth_ref
  178.3 2.5 collective-permute-done.25
  181.0 4.0 %fusion.55 = (f32[512]{0:T(512)S(1)}, f32[512]{0:T(512)S(1)}) fusion(bf16[1568,512]{1,0:T(8,128)(2,1)S(1)} %copy-done.2, f32[512]{0:T(512)S(1)} %copy-done.52, f32[512]{0:T(512)S(1)} %copy-done.43, f32[512]{0:T(512)S(1)} %bitcast.272, f32[1568,512]{1,0:T(8,128)} %get-tuple-element.197, f32[512]{0:T(512)S(1)} %bitcast.282, bf16[1568,512]{1,0:T(8,128)(2,1)S(1)} %copy-done.12), kind=kLoop, calls=%fused_computation.203 | loop fusion | flops 14449664 | bytes 6434816 | tf_op jit(solution)/shard_map/reduce_sum | solution.py:734
  185.4 3.2 collective-permute-done.26
  189.9 2.0 copy.187
  193.9 7.2 %fusion.65 = f32[12,7,7,16]{3,0,2,1:T(8,128)S(1)} fusion(bf16[32,12,32,32]{0,1,3,2:T(8,128)(2,1)} %copy.167, bf16[32,16,16,16]{0,1,3,2:T(8,128)(2,1)} %bitcast.250), kind=kOutput, calls=%fused_computation.213 | convolution fusion | flops 138067968 | bytes 1086208 | tf_op jit(solution)/shard_map/transpose | solution.py:511
  201.7 3.7 multiply_convert_fusion
  207.7 3.1 fusion.64
  212.7 1.5 copy.179
  215.8 1.7 pad_maximum_fusion.1
  219.2 3.6 fusion.16
  224.3 1.6 collective-permute-start.30
  226.4 9.7 %collective-permute-done.30 = bf16[784,256]{1,0:T(8,128)(2,1)S(1)} collective-permute-done((bf16[784,256]{1,0:T(8,128)(2,1)S(1)}, bf16[784,256]{1,0:T(8,128)(2,1)S(1)}, u32[]{:S(2)}, u32[]{:S(2)}) %collective-permute-start.30) | collective-permute-done | bytes 401440 | tf_op jit(solution)/shard_map/ppermute | solution.py:520
  239.6 1.9 collective-permute-done.33
  242.9 2.3 collective-permute-done.34
  248.0 1.7 collective-permute-done.35
  252.4 3.5 collective-permute-done.36
  257.4 14.4 %shard_map.367 = (bf16[3,1184,256]{2,1,0:T(8,128)(2,1)}, f32[784,256]{1,0:T(8,128)}, bf16[784,256]{1,0:T(8,128)(2,1)}, f32[8,256]{1,0:T(8,128)}, f32[24,256]{1,0:T(8,128)}) custom-call(s32[1]{0:T(128)} %bitcast.y_ref, s32[2,8]{1,0:T(2,128)} %concatenate.243.same_ref, f32[784,256]{1,0:T(8,128)} %copy-done.19, bf16[784,256]{1,0:T(8,128)(2,1)} %copy-done.76, ...), custom_call_target="tpu_custom_call" | custom-call | flops 1849688064 | bytes 7553024 | tf_op jit(solution)/shard_map/pallas_call | solution.py:422
  275.3 2.6 collective-permute-done.41
  279.4 1.6 collective-permute-start.39
  283.0 7.0 %shard_map.368 = (f32[4608,128]{1,0:T(8,128)}, bf16[4608,128]{1,0:T(8,128)(2,1)}) custom-call(s32[1]{0:T(128)} %bitcast.74.r_ref, bf16[1184,512]{1,0:T(8,128)(2,1)} %get-tuple-element.36.mixed_ref, bf16[3,1184,256]{2,1,0:T(8,128)(2,1)} %get-tuple-element.37.slopes_ref), custom_call_target="tpu_custom_call" | custom-call | flops 2793406464 | bytes 6569984 | tf_op jit(solution)/shard_map/pallas_call | solution.py:465
  290.1 1.6 collective-permute-start.44
  291.9 1.6 convolution_bitcast_fusion.3
  293.5 1.6 convolution_bitcast_fusion.1
  295.2 1.6 convolution_bitcast_fusion.2
  296.8 1.8 convolution_bitcast_fusion
  300.9 2.4 gather_fusion
  303.3 2.8 broadcast_select_fusion
  306.1 3.7 gather_fusion.1
  309.8 1.8 broadcast_select_fusion.1
  316.6 2.9 collective-permute-done.59
  320.8 3.1 collective-permute-done.60
  325.8 4.2 %collective-permute-done.61 = f32[70,256]{1,0:T(8,128)S(1)} collective-permute-done((f32[70,256]{1,0:T(8,128)S(1)}, f32[70,256]{1,0:T(8,128)S(1)}, u32[]{:S(2)}, u32[]{:S(2)}) %collective-permute-start.61) | collective-permute-done | bytes 71712 | tf_op jit(solution)/shard_map/ppermute | solution.py:520
  336.9 5.1 %collective-permute-done.48 = bf16[1024,128]{1,0:T(8,128)(2,1)S(1)} collective-permute-done((bf16[1024,128]{1,0:T(8,128)(2,1)S(1)}, bf16[1024,128]{1,0:T(8,128)(2,1)S(1)}, u32[]{:S(2)}, u32[]{:S(2)}) %collective-permute-start.48) | collective-permute-done | bytes 262176 | tf_op jit(solution)/shard_map/ppermute | solution.py:520
  344.9 2.9 collective-permute-done.49
  348.3 6.8 %collective-permute-done.52 = bf16[2304,128]{1,0:T(8,128)(2,1)S(1)} collective-permute-done((bf16[2304,128]{1,0:T(8,128)(2,1)S(1)}, bf16[2304,128]{1,0:T(8,128)(2,1)S(1)}, u32[]{:S(2)}, u32[]{:S(2)}) %collective-permute-start.52) | collective-permute-done | bytes 589856 | tf_op jit(solution)/shard_map/ppermute | solution.py:520
  355.4 1.8 collective-permute-start.53
  358.0 5.8 %collective-permute-done.53 = bf16[1152,128]{1,0:T(8,128)(2,1)S(1)} collective-permute-done((bf16[1152,128]{1,0:T(8,128)(2,1)S(1)}, bf16[1152,128]{1,0:T(8,128)(2,1)S(1)}, u32[]{:S(2)}, u32[]{:S(2)}) %collective-permute-start.53) | collective-permute-done | bytes 294944 | tf_op jit(solution)/shard_map/ppermute | solution.py:520
  363.9 2.2 collective-permute-start.54
  366.1 6.1 %fusion = bf16[1568,512]{1,0:T(8,128)(2,1)} fusion(bf16[784,512]{1,0:T(8,128)(2,1)S(1)} %maximum_select_fusion.7, bf16[784,512]{1,0:T(8,128)(2,1)S(1)} %collective-permute-done.45, pred[]{:T(512)S(6)} %eq.12, bf16[512,256]{1,0:T(8,128)(2,1)S(1)} %copy-done.27, bf16[512,256]{1,0:T(8,128)(2,1)} %collective-permute-done.46, pred[]{:T(512)S(6)} %eq.13, ...), kind=kOutput, calls=%fused_computation.11 | convolution fusion | flops 845316096 | bytes 10166274 | tf_op jit(solution)/shard_map/dot_general | solution.py:582
  (395 shorter events, 109.8 us)
Async XLA Ops:
  7.2 81.9 %copy-start = (s32[4,7]{1,0:T(4,128)S(1)}, s32[4,7]{1,0:T(4,128)}, u32[]{:S(2)}) copy-start(s32[4,7]{1,0:T(4,128)} %param.36) | copy-start | bytes 340
  7.2 77.1 %all-gather.3.cloned.1.call-start = ((), (), s32[]{:S(2)}) async-start(), calls=%async_computation | async-start | bytes 1916928 | tf_op jit(solution)/shard_map/all_gather | solution.py:639
  7.3 8.4 %collective-permute-start = (bf16[1,256,128]{2,1,0:T(8,128)(2,1)}, bf16[1,256,128]{2,1,0:T(8,128)(2,1)S(1)}, u32[]{:S(2)}, u32[]{:S(2)}) collective-permute-start(bf16[1,256,128]{2,1,0:T(8,128)(2,1)} %bitcast.259), channel_id=1, source_target_pairs={{0,16},{4,20},{8,24},{12,28},{16,0},{20,4},{24,8},{28,12},{1,17},{... | collective-permute-start | bytes 196616 | tf_op jit(solution)/shard_map/ppermute | solution.py:520
  14.0 46.9 %collective-permute-start.6 = (bf16[784,512]{1,0:T(8,128)(2,1)}, bf16[784,512]{1,0:T(8,128)(2,1)}, u32[]{:S(2)}, u32[]{:S(2)}) collective-permute-start(bf16[784,512]{1,0:T(8,128)(2,1)} %get-tuple-element.161), channel_id=1, source_target_pairs={{0,3},{1,2},{2,1},{3,0},{4,7},{5,6},{6,5},{7,4},{8,11},{9,10},{10,... | collective-permute-start | bytes 2408456 | tf_op jit(solution)/shard_map/ppermute | solution.py:520
  14.7 47.9 %collective-permute-start.4 = (bf16[784,512]{1,0:T(8,128)(2,1)}, bf16[784,512]{1,0:T(8,128)(2,1)}, u32[]{:S(2)}, u32[]{:S(2)}) collective-permute-start(bf16[784,512]{1,0:T(8,128)(2,1)} %get-tuple-element.161), channel_id=1, source_target_pairs={{0,1},{1,0},{2,3},{3,2},{4,5},{5,4},{6,7},{7,6},{8,9},{9,8},{10,11... | collective-permute-start | bytes 2408456 | tf_op jit(solution)/shard_map/ppermute | solution.py:520
  15.8 5.5 %collective-permute-start.1 = (bf16[2,1,256,128]{3,2,0,1:T(8,128)(2,1)S(1)}, bf16[2,1,256,128]{3,2,0,1:T(8,128)(2,1)S(1)}, u32[]{:S(2)}, u32[]{:S(2)}) collective-permute-start(bf16[2,1,256,128]{3,2,0,1:T(8,128)(2,1)S(1)} %maximum_select_fusion.15), channel_id=1, source_target_pairs={{0,8},{4,12},{8,0},{12,4},{16,24},{20,28},{24,16},{28,20},{1,9},{5... | collective-permute-start | bytes 393224 | tf_op jit(solution)/shard_map/ppermute | solution.py:520
  18.1 47.6 %collective-permute-start.5 = (bf16[784,512]{1,0:T(8,128)(2,1)}, bf16[784,512]{1,0:T(8,128)(2,1)}, u32[]{:S(2)}, u32[]{:S(2)}) collective-permute-start(bf16[784,512]{1,0:T(8,128)(2,1)} %get-tuple-element.160), channel_id=1, source_target_pairs={{0,2},{1,3},{2,0},{3,1},{4,6},{5,7},{6,4},{7,5},{8,10},{9,11},{10,... | collective-permute-start | bytes 2408456 | tf_op jit(solution)/shard_map/ppermute | solution.py:520
  22.0 10.1 %collective-permute-start.2 = (bf16[2,2,1,256,128]{4,3,1,2,0:T(8,128)(2,1)}, bf16[2,2,1,256,128]{4,3,1,2,0:T(8,128)(2,1)}, u32[]{:S(2)}, u32[]{:S(2)}) collective-permute-start(bf16[2,2,1,256,128]{4,3,1,2,0:T(8,128)(2,1)} %maximum_select_fusion.13), channel_id=1, source_target_pairs={{0,4},{4,0},{8,12},{12,8},{16,20},{20,16},{24,28},{28,24},{1,5},{5... | collective-permute-start | bytes 786440 | tf_op jit(solution)/shard_map/ppermute | solution.py:520
  33.9 24.5 %collective-permute-start.3 = (bf16[2048,128]{1,0:T(8,128)(2,1)}, bf16[2048,128]{1,0:T(8,128)(2,1)}, u32[]{:S(2)}, u32[]{:S(2)}) collective-permute-start(bf16[2048,128]{1,0:T(8,128)(2,1)} %bitcast.12), channel_id=1, source_target_pairs={{0,1},{1,0},{2,3},{3,2},{4,5},{5,4},{6,7},{7,6},{8,9},{9,8},{10,11... | collective-permute-start | bytes 1572872 | tf_op jit(solution)/shard_map/ppermute | solution.py:520
  68.4 1.4 collective-permute-start.8
  70.4 15.9 %collective-permute-start.9 = (f32[3,256]{1,0:T(4,128)}, f32[3,256]{1,0:T(4,128)}, u32[]{:S(2)}, u32[]{:S(2)}) collective-permute-start(f32[3,256]{1,0:T(4,128)} %pad_maximum_fusion.4), channel_id=1, source_target_pairs={{0,4},{4,0},{8,12},{12,8},{16,20},{20,16},{24,28},{28,24},{1,5},{5... | collective-permute-start | bytes 9224 | tf_op jit(solution)/shard_map/ppermute | solution.py:520
  84.2 10.2 %collective-permute-start.13 = (f32[24,128]{1,0:T(8,128)S(1)}, f32[24,128]{1,0:T(8,128)}, u32[]{:S(2)}, u32[]{:S(2)}) collective-permute-start(f32[24,128]{1,0:T(8,128)S(1)} %concatenate.266), channel_id=1, source_target_pairs={{0,1},{1,0},{2,3},{3,2},{4,5},{5,4},{6,7},{7,6},{8,9},{9,8},{10,11... | collective-permute-start | bytes 36872 | tf_op jit(solution)/shard_map/ppermute | solution.py:520
  85.7 22.6 %collective-permute-start.15 = (bf16[4608,128]{1,0:T(8,128)(2,1)S(1)}, bf16[4608,128]{1,0:T(8,128)(2,1)}, u32[]{:S(2)}, u32[]{:S(2)}) collective-permute-start(bf16[4608,128]{1,0:T(8,128)(2,1)S(1)} %bitcast.223), channel_id=1, source_target_pairs={{0,1},{1,0},{2,3},{3,2},{4,5},{5,4},{6,7},{7,6},{8,9},{9,8},{10,11... | collective-permute-start | bytes 3538952 | tf_op jit(solution)/shard_map/ppermute | solution.py:520
  87.5 5.4 %collective-permute-start.10 = (f32[3,256]{1,0:T(4,128)}, f32[3,256]{1,0:T(4,128)}, u32[]{:S(2)}, u32[]{:S(2)}) collective-permute-start(f32[3,256]{1,0:T(4,128)} %fusion.49), channel_id=1, source_target_pairs={{0,8},{4,12},{8,0},{12,4},{16,24},{20,28},{24,16},{28,20},{1,9},{5... | collective-permute-start | bytes 9224 | tf_op jit(solution)/shard_map/ppermute | solution.py:520
  93.7 4.5 %collective-permute-start.11 = (f32[3,256]{1,0:T(4,128)S(1)}, f32[3,256]{1,0:T(4,128)S(1)}, u32[]{:S(2)}, u32[]{:S(2)}) collective-permute-start(f32[3,256]{1,0:T(4,128)S(1)} %add.311), channel_id=1, source_target_pairs={{0,16},{4,20},{8,24},{12,28},{16,0},{20,4},{24,8},{28,12},{1,17},{... | collective-permute-start | bytes 9224 | tf_op jit(solution)/shard_map/ppermute | solution.py:520
  95.2 16.8 %collective-permute-start.14 = (f32[24,256]{1,0:T(8,128)S(1)}, f32[24,256]{1,0:T(8,128)S(1)}, u32[]{:S(2)}, u32[]{:S(2)}) collective-permute-start(f32[24,256]{1,0:T(8,128)S(1)} %maximum_select_fusion.16.par_own_ref), channel_id=1, source_target_pairs={{0,2},{1,3},{2,0},{3,1},{4,6},{5,7},{6,4},{7,5},{8,10},{9,11},{10,... | collective-permute-start | bytes 73736 | tf_op jit(solution)/shard_map/ppermute | solution.py:520
  96.8 15.3 %collective-permute-start.7 = (bf16[784,256]{1,0:T(8,128)(2,1)}, bf16[784,256]{1,0:T(8,128)(2,1)S(1)}, u32[]{:S(2)}, u32[]{:S(2)}) collective-permute-start(bf16[784,256]{1,0:T(8,128)(2,1)} %get-tuple-element.164), channel_id=1, source_target_pairs={{0,2},{1,3},{2,0},{3,1},{4,6},{5,7},{6,4},{7,5},{8,10},{9,11},{10,... | collective-permute-start | bytes 1204232 | tf_op jit(solution)/shard_map/ppermute | solution.py:520
  98.2 9.5 %collective-permute-start.12 = (f32[2,256]{1,0:T(2,128)S(1)}, f32[2,256]{1,0:T(2,128)S(1)}, u32[]{:S(2)}, u32[]{:S(2)}) collective-permute-start(f32[2,256]{1,0:T(2,128)S(1)} %slice.283), channel_id=1, source_target_pairs={{0,2},{1,3},{2,0},{3,1},{4,6},{5,7},{6,4},{7,5},{8,10},{9,11},{10,... | collective-permute-start | bytes 6152 | tf_op jit(solution)/shard_map/ppermute | solution.py:520
  124.4 1.2 collective-permute-start.17
  126.3 3.7 collective-permute-start.18
  129.9 3.7 collective-permute-start.19
  133.6 4.5 %collective-permute-start.20 = (f32[3,256]{1,0:T(4,128)S(1)}, f32[3,256]{1,0:T(4,128)S(1)}, u32[]{:S(2)}, u32[]{:S(2)}) collective-permute-start(f32[3,256]{1,0:T(4,128)S(1)} %add.321), channel_id=1, source_target_pairs={{0,16},{4,20},{8,24},{12,28},{16,0},{20,4},{24,8},{28,12},{1,17},{... | collective-permute-start | bytes 9224 | tf_op jit(solution)/shard_map/ppermute | solution.py:520
  136.2 9.1 %collective-permute-start.16 = (bf16[784,256]{1,0:T(8,128)(2,1)}, bf16[784,256]{1,0:T(8,128)(2,1)S(1)}, u32[]{:S(2)}, u32[]{:S(2)}) collective-permute-start(bf16[784,256]{1,0:T(8,128)(2,1)} %get-tuple-element.30), channel_id=1, source_target_pairs={{0,2},{1,3},{2,0},{3,1},{4,6},{5,7},{6,4},{7,5},{8,10},{9,11},{10,... | collective-permute-start | bytes 1204232 | tf_op jit(solution)/shard_map/ppermute | solution.py:520
  138.1 7.1 %collective-permute-start.21 = (f32[2,256]{1,0:T(2,128)S(1)}, f32[2,256]{1,0:T(2,128)S(1)}, u32[]{:S(2)}, u32[]{:S(2)}) collective-permute-start(f32[2,256]{1,0:T(2,128)S(1)} %slice.287), channel_id=1, source_target_pairs={{0,2},{1,3},{2,0},{3,1},{4,6},{5,7},{6,4},{7,5},{8,10},{9,11},{10,... | collective-permute-start | bytes 6152 | tf_op jit(solution)/shard_map/ppermute | solution.py:520
  146.5 17.0 %collective-permute-start.22 = (bf16[784,512]{1,0:T(8,128)(2,1)S(1)}, bf16[784,512]{1,0:T(8,128)(2,1)}, u32[]{:S(2)}, u32[]{:S(2)}) collective-permute-start(bf16[784,512]{1,0:T(8,128)(2,1)S(1)} %maximum_select_fusion.6), channel_id=1, source_target_pairs={{0,1},{1,0},{2,3},{3,2},{4,5},{5,4},{6,7},{7,6},{8,9},{9,8},{10,11... | collective-permute-start | bytes 2408456 | tf_op jit(solution)/shard_map/ppermute | solution.py:520
  147.6 15.9 %collective-permute-start.37 = (bf16[2304,128]{1,0:T(8,128)(2,1)}, bf16[2304,128]{1,0:T(8,128)(2,1)}, u32[]{:S(2)}, u32[]{:S(2)}) collective-permute-start(bf16[2304,128]{1,0:T(8,128)(2,1)} %bitcast.50), channel_id=1, source_target_pairs={{0,2},{1,3},{2,0},{3,1},{4,6},{5,7},{6,4},{7,5},{8,10},{9,11},{10,... | collective-permute-start | bytes 1769480 | tf_op jit(solution)/shard_map/ppermute | solution.py:520
  163.5 9.7 %collective-permute-start.38 = (bf16[2304,128]{1,0:T(8,128)(2,1)}, bf16[2304,128]{1,0:T(8,128)(2,1)}, u32[]{:S(2)}, u32[]{:S(2)}) collective-permute-start(bf16[2304,128]{1,0:T(8,128)(2,1)} %collective-permute-done.37), channel_id=1, source_target_pairs={{0,1},{1,0},{2,3},{3,2},{4,5},{5,4},{6,7},{7,6},{8,9},{9,8},{10,11... | collective-permute-start | bytes 1769480 | tf_op jit(solution)/shard_map/ppermute | solution.py:520
  168.3 3.7 collective-permute-start.23
  169.4 196.7 %collective-permute-start.46 = (bf16[512,256]{1,0:T(8,128)(2,1)}, bf16[512,256]{1,0:T(8,128)(2,1)}, u32[]{:S(2)}, u32[]{:S(2)}) collective-permute-start(bf16[512,256]{1,0:T(8,128)(2,1)} %get-tuple-element.162), channel_id=1, source_target_pairs={{0,2},{1,3},{2,0},{3,1},{4,6},{5,7},{6,4},{7,5},{8,10},{9,11},{10,... | collective-permute-start | bytes 786440 | tf_op jit(solution)/shard_map/ppermute | solution.py:520
  172.0 4.3 %collective-permute-start.24 = (f32[2,512]{1,0:T(2,128)S(1)}, f32[2,512]{1,0:T(2,128)S(1)}, u32[]{:S(2)}, u32[]{:S(2)}) collective-permute-start(f32[2,512]{1,0:T(2,128)S(1)} %fusion.53), channel_id=1, source_target_pairs={{0,8},{4,12},{8,0},{12,4},{16,24},{20,28},{24,16},{28,20},{1,9},{5... | collective-permute-start | bytes 12296 | tf_op jit(solution)/shard_map/ppermute | solution.py:520
  176.3 4.6 %collective-permute-start.25 = (f32[2,512]{1,0:T(2,128)S(1)}, f32[2,512]{1,0:T(2,128)S(1)}, u32[]{:S(2)}, u32[]{:S(2)}) collective-permute-start(f32[2,512]{1,0:T(2,128)S(1)} %fusion.93), channel_id=1, source_target_pairs={{0,16},{4,20},{8,24},{12,28},{16,0},{20,4},{24,8},{28,12},{1,17},{... | collective-permute-start | bytes 12296 | tf_op jit(solution)/shard_map/ppermute | solution.py:520
  185.0 3.7 collective-permute-start.26
  188.7 3.7 collective-permute-start.27
  192.4 8.7 %collective-permute-start.28 = (f32[2,512]{1,0:T(2,128)S(1)}, f32[2,512]{1,0:T(2,128)S(1)}, u32[]{:S(2)}, u32[]{:S(2)}) collective-permute-start(f32[2,512]{1,0:T(2,128)S(1)} %fusion.92), channel_id=1, source_target_pairs={{0,16},{4,20},{8,24},{12,28},{16,0},{20,4},{24,8},{28,12},{1,17},{... | collective-permute-start | bytes 12296 | tf_op jit(solution)/shard_map/ppermute | solution.py:520
  207.7 15.1 %collective-permute-start.29 = (bf16[784,512]{1,0:T(8,128)(2,1)}, bf16[784,512]{1,0:T(8,128)(2,1)}, u32[]{:S(2)}, u32[]{:S(2)}) collective-permute-start(bf16[784,512]{1,0:T(8,128)(2,1)} %dynamic-slice_convert_fusion), channel_id=1, source_target_pairs={{0,1},{1,0},{2,3},{3,2},{4,5},{5,4},{6,7},{7,6},{8,9},{9,8},{10,11... | collective-permute-start | bytes 2408456 | tf_op jit(solution)/shard_map/ppermute | solution.py:520
  224.3 11.8 %collective-permute-start.30 = (bf16[784,256]{1,0:T(8,128)(2,1)S(1)}, bf16[784,256]{1,0:T(8,128)(2,1)S(1)}, u32[]{:S(2)}, u32[]{:S(2)}) collective-permute-start(bf16[784,256]{1,0:T(8,128)(2,1)S(1)} %dynamic-slice_convert_fusion.2), channel_id=1, source_target_pairs={{0,2},{1,3},{2,0},{3,1},{4,6},{5,7},{6,4},{7,5},{8,10},{9,11},{10,... | collective-permute-start | bytes 1204232 | tf_op jit(solution)/shard_map/ppermute | solution.py:520
  226.0 10.7 %collective-permute-start.55 = (bf16[256,512]{1,0:T(8,128)(2,1)S(1)}, bf16[256,512]{1,0:T(8,128)(2,1)S(1)}, u32[]{:S(2)}, u32[]{:S(2)}) collective-permute-start(bf16[256,512]{1,0:T(8,128)(2,1)S(1)} %bitcast.257), channel_id=1, source_target_pairs={{0,4},{4,0},{8,12},{12,8},{16,20},{20,16},{24,28},{28,24},{1,5},{5... | collective-permute-start | bytes 786440 | tf_op jit(solution)/shard_map/ppermute | solution.py:520
  236.6 1.2 collective-permute-start.32
  237.9 3.7 collective-permute-start.33
  238.5 8.2 %collective-permute-start.56 = (bf16[128,512]{1,0:T(8,128)(2,1)S(1)}, bf16[128,512]{1,0:T(8,128)(2,1)S(1)}, u32[]{:S(2)}, u32[]{:S(2)}) collective-permute-start(bf16[128,512]{1,0:T(8,128)(2,1)S(1)} %bitcast.264), channel_id=1, source_target_pairs={{0,8},{4,12},{8,0},{12,4},{16,24},{20,28},{24,16},{28,20},{1,9},{5... | collective-permute-start | bytes 393224 | tf_op jit(solution)/shard_map/ppermute | solution.py:520
  241.5 3.7 collective-permute-start.34
  245.2 4.5 %collective-permute-start.35 = (f32[2,256]{1,0:T(2,128)S(1)}, f32[2,256]{1,0:T(2,128)S(1)}, u32[]{:S(2)}, u32[]{:S(2)}) collective-permute-start(f32[2,256]{1,0:T(2,128)S(1)} %add.355), channel_id=1, source_target_pairs={{0,16},{4,20},{8,24},{12,28},{16,0},{20,4},{24,8},{28,12},{1,17},{... | collective-permute-start | bytes 6152 | tf_op jit(solution)/shard_map/ppermute | solution.py:520
  246.7 9.9 %collective-permute-start.31 = (bf16[784,256]{1,0:T(8,128)(2,1)S(1)}, bf16[784,256]{1,0:T(8,128)(2,1)S(1)}, u32[]{:S(2)}, u32[]{:S(2)}) collective-permute-start(bf16[784,256]{1,0:T(8,128)(2,1)S(1)} %convert_element_type.204), channel_id=1, source_target_pairs={{0,2},{1,3},{2,0},{3,1},{4,6},{5,7},{6,4},{7,5},{8,10},{9,11},{10,... | collective-permute-start | bytes 1204232 | tf_op jit(solution)/shard_map/ppermute | solution.py:520
  249.7 6.3 %collective-permute-start.36 = (f32[2,256]{1,0:T(2,128)S(1)}, f32[2,256]{1,0:T(2,128)S(1)}, u32[]{:S(2)}, u32[]{:S(2)}) collective-permute-start(f32[2,256]{1,0:T(2,128)S(1)} %add.356), channel_id=1, source_target_pairs={{0,2},{1,3},{2,0},{3,1},{4,6},{5,7},{6,4},{7,5},{8,10},{9,11},{10,... | collective-permute-start | bytes 6152 | tf_op jit(solution)/shard_map/ppermute | solution.py:520
  251.2 21.3 %collective-permute-start.57 = (bf16[64,512]{1,0:T(8,128)(2,1)S(1)}, bf16[64,512]{1,0:T(8,128)(2,1)S(1)}, u32[]{:S(2)}, u32[]{:S(2)}) collective-permute-start(bf16[64,512]{1,0:T(8,128)(2,1)S(1)} %fusion.27), channel_id=1, source_target_pairs={{0,16},{4,20},{8,24},{12,28},{16,0},{20,4},{24,8},{28,12},{1,17},{... | collective-permute-start | bytes 196616 | tf_op jit(solution)/shard_map/ppermute | solution.py:520
  272.5 1.2 collective-permute-start.40
  274.4 3.6 collective-permute-start.41
  278.0 3.6 collective-permute-start.42
  279.4 34.4 %collective-permute-start.58 = (f32[24,256]{1,0:T(8,128)}, f32[24,256]{1,0:T(8,128)}, u32[]{:S(2)}, u32[]{:S(2)}) collective-permute-start(f32[24,256]{1,0:T(8,128)} %get-tuple-element.40), channel_id=1, source_target_pairs={{0,1},{1,0},{2,3},{3,2},{4,5},{5,4},{6,7},{7,6},{8,9},{9,8},{10,11... | collective-permute-start | bytes 73736 | tf_op jit(solution)/shard_map/ppermute | solution.py:520
  279.4 53.5 %collective-permute-start.39 = (bf16[784,256]{1,0:T(8,128)(2,1)}, bf16[784,256]{1,0:T(8,128)(2,1)}, u32[]{:S(2)}, u32[]{:S(2)}) collective-permute-start(bf16[784,256]{1,0:T(8,128)(2,1)} %get-tuple-element.33), channel_id=1, source_target_pairs={{0,2},{1,3},{2,0},{3,1},{4,6},{5,7},{6,4},{7,5},{8,10},{9,11},{10,... | collective-permute-start | bytes 1204232 | tf_op jit(solution)/shard_map/ppermute | solution.py:520
  281.6 8.5 %collective-permute-start.43 = (f32[2,256]{1,0:T(2,128)S(1)}, f32[2,256]{1,0:T(2,128)S(1)}, u32[]{:S(2)}, u32[]{:S(2)}) collective-permute-start(f32[2,256]{1,0:T(2,128)S(1)} %add.360), channel_id=1, source_target_pairs={{0,16},{4,20},{8,24},{12,28},{16,0},{20,4},{24,8},{28,12},{1,17},{... | collective-permute-start | bytes 6152 | tf_op jit(solution)/shard_map/ppermute | solution.py:520
  290.0 52.2 %collective-permute-start.51 = (bf16[4608,128]{1,0:T(8,128)(2,1)}, bf16[4608,128]{1,0:T(8,128)(2,1)}, u32[]{:S(2)}, u32[]{:S(2)}) collective-permute-start(bf16[4608,128]{1,0:T(8,128)(2,1)} %get-tuple-element.39), channel_id=1, source_target_pairs={{0,1},{1,0},{2,3},{3,2},{4,5},{5,4},{6,7},{7,6},{8,9},{9,8},{10,11... | collective-permute-start | bytes 3538952 | tf_op jit(solution)/shard_map/ppermute | solution.py:520
  290.1 24.8 %collective-permute-start.44 = (f32[2,256]{1,0:T(2,128)S(1)}, f32[2,256]{1,0:T(2,128)}, u32[]{:S(2)}, u32[]{:S(2)}) collective-permute-start(f32[2,256]{1,0:T(2,128)S(1)} %add.361), channel_id=1, source_target_pairs={{0,2},{1,3},{2,0},{3,1},{4,6},{5,7},{6,4},{7,5},{8,10},{9,11},{10,... | collective-permute-start | bytes 6152 | tf_op jit(solution)/shard_map/ppermute | solution.py:520
  313.8 20.5 %collective-permute-start.47 = (bf16[2048,128]{1,0:T(8,128)(2,1)}, bf16[2048,128]{1,0:T(8,128)(2,1)}, u32[]{:S(2)}, u32[]{:S(2)}) collective-permute-start(bf16[2048,128]{1,0:T(8,128)(2,1)} %dynamic-slice_convert_fusion.1), channel_id=1, source_target_pairs={{0,1},{1,0},{2,3},{3,2},{4,5},{5,4},{6,7},{7,6},{8,9},{9,8},{10,11... | collective-permute-start | bytes 1572872 | tf_op jit(solution)/shard_map/ppermute | solution.py:520
  314.9 4.6 %collective-permute-start.59 = (f32[70,256]{1,0:T(8,128)S(1)}, f32[70,256]{1,0:T(8,128)S(1)}, u32[]{:S(2)}, u32[]{:S(2)}) collective-permute-start(f32[70,256]{1,0:T(8,128)S(1)} %pad_maximum_fusion.3), channel_id=1, source_target_pairs={{0,4},{4,0},{8,12},{12,8},{16,20},{20,16},{24,28},{28,24},{1,5},{5... | collective-permute-start | bytes 215048 | tf_op jit(solution)/shard_map/ppermute | solution.py:520
  319.5 4.4 %collective-permute-start.60 = (f32[70,256]{1,0:T(8,128)S(1)}, f32[70,256]{1,0:T(8,128)S(1)}, u32[]{:S(2)}, u32[]{:S(2)}) collective-permute-start(f32[70,256]{1,0:T(8,128)S(1)} %fusion.54), channel_id=1, source_target_pairs={{0,8},{4,12},{8,0},{12,4},{16,24},{20,28},{24,16},{28,20},{1,9},{5... | collective-permute-start | bytes 215048 | tf_op jit(solution)/shard_map/ppermute | solution.py:520
  323.9 6.1 %collective-permute-start.61 = (f32[70,256]{1,0:T(8,128)S(1)}, f32[70,256]{1,0:T(8,128)S(1)}, u32[]{:S(2)}, u32[]{:S(2)}) collective-permute-start(f32[70,256]{1,0:T(8,128)S(1)} %add.381), channel_id=1, source_target_pairs={{0,16},{4,20},{8,24},{12,28},{16,0},{20,4},{24,8},{28,12},{1,17},{... | collective-permute-start | bytes 215048 | tf_op jit(solution)/shard_map/ppermute | solution.py:520
  335.5 6.4 %collective-permute-start.48 = (bf16[1024,128]{1,0:T(8,128)(2,1)S(1)}, bf16[1024,128]{1,0:T(8,128)(2,1)S(1)}, u32[]{:S(2)}, u32[]{:S(2)}) collective-permute-start(bf16[1024,128]{1,0:T(8,128)(2,1)S(1)} %bitcast.258), channel_id=1, source_target_pairs={{0,4},{4,0},{8,12},{12,8},{16,20},{20,16},{24,28},{28,24},{1,5},{5... | collective-permute-start | bytes 786440 | tf_op jit(solution)/shard_map/ppermute | solution.py:520
  336.8 29.3 %collective-permute-start.45 = (bf16[784,512]{1,0:T(8,128)(2,1)S(1)}, bf16[784,512]{1,0:T(8,128)(2,1)S(1)}, u32[]{:S(2)}, u32[]{:S(2)}) collective-permute-start(bf16[784,512]{1,0:T(8,128)(2,1)S(1)} %maximum_select_fusion.7), channel_id=1, source_target_pairs={{0,1},{1,0},{2,3},{3,2},{4,5},{5,4},{6,7},{7,6},{8,9},{9,8},{10,11... | collective-permute-start | bytes 2408456 | tf_op jit(solution)/shard_map/ppermute | solution.py:520
  342.1 5.7 %collective-permute-start.49 = (bf16[512,128]{1,0:T(8,128)(2,1)S(1)}, bf16[512,128]{1,0:T(8,128)(2,1)S(1)}, u32[]{:S(2)}, u32[]{:S(2)}) collective-permute-start(bf16[512,128]{1,0:T(8,128)(2,1)S(1)} %bitcast.265), channel_id=1, source_target_pairs={{0,8},{4,12},{8,0},{12,4},{16,24},{20,28},{24,16},{28,20},{1,9},{5... | collective-permute-start | bytes 393224 | tf_op jit(solution)/shard_map/ppermute | solution.py:520
  343.9 11.3 %collective-permute-start.52 = (bf16[2304,128]{1,0:T(8,128)(2,1)S(1)}, bf16[2304,128]{1,0:T(8,128)(2,1)S(1)}, u32[]{:S(2)}, u32[]{:S(2)}) collective-permute-start(bf16[2304,128]{1,0:T(8,128)(2,1)S(1)} %bitcast.253), channel_id=1, source_target_pairs={{0,4},{4,0},{8,12},{12,8},{16,20},{20,16},{24,28},{28,24},{1,5},{5... | collective-permute-start | bytes 1769480 | tf_op jit(solution)/shard_map/ppermute | solution.py:520
  347.9 9.4 %collective-permute-start.50 = (bf16[256,128]{1,0:T(8,128)(2,1)S(1)}, bf16[256,128]{1,0:T(8,128)(2,1)S(1)}, u32[]{:S(2)}, u32[]{:S(2)}) collective-permute-start(bf16[256,128]{1,0:T(8,128)(2,1)S(1)} %fusion.26), channel_id=1, source_target_pairs={{0,16},{4,20},{8,24},{12,28},{16,0},{20,4},{24,8},{28,12},{1,17},{... | collective-permute-start | bytes 196616 | tf_op jit(solution)/shard_map/ppermute | solution.py:520
  355.4 8.4 %collective-permute-start.53 = (bf16[1152,128]{1,0:T(8,128)(2,1)S(1)}, bf16[1152,128]{1,0:T(8,128)(2,1)S(1)}, u32[]{:S(2)}, u32[]{:S(2)}) collective-permute-start(bf16[1152,128]{1,0:T(8,128)(2,1)S(1)} %bitcast.256), channel_id=1, source_target_pairs={{0,8},{4,12},{8,0},{12,4},{16,24},{20,28},{24,16},{28,20},{1,9},{5... | collective-permute-start | bytes 884744 | tf_op jit(solution)/shard_map/ppermute | solution.py:520
  363.9 8.3 %collective-permute-start.54 = (bf16[576,128]{1,0:T(8,128)(2,1)S(1)}, bf16[576,128]{1,0:T(8,128)(2,1)S(1)}, u32[]{:S(2)}, u32[]{:S(2)}) collective-permute-start(bf16[576,128]{1,0:T(8,128)(2,1)S(1)} %fusion.24), channel_id=1, source_target_pairs={{0,16},{4,20},{8,24},{12,28},{16,0},{20,4},{24,8},{28,12},{1,17},{... | collective-permute-start | bytes 442376 | tf_op jit(solution)/shard_map/ppermute | solution.py:520
  (76 other events, 700.9 us)
Sparse Core Ops, SparseCore 0:
  18.3 45.3 all-gather.2

commit v2 on v1

v2 whole, which is shorter than its diff:
```python
import functools

import jax
import jax.numpy as jnp
from jax import lax
from jax.experimental import pallas as pl
from jax.experimental.pallas import tpu as pltpu
from jax.sharding import PartitionSpec as P

SEG = 8
SIDE = 7
FRAMES = 5
PIXELS = SIDE * SIDE
BLOCK = 16
SPAN = SIDE + 2

eps = 1e-05
vmem_limit = 24 * 1024 * 1024

whole = pl.BlockSpec(memory_space=pltpu.VMEM)
remote = pl.BlockSpec(memory_space=pltpu.HBM)
scalars = pl.BlockSpec(memory_space=pltpu.SMEM)


def logistic(value):
    return 0.5 * jnp.tanh(0.5 * value) + 0.5


def silu_slope(value):
    part = logistic(value)
    return part * (1.0 + value * (1.0 - part))


def norm_stats(totals, squares, count):
    center = totals / count
    spread = squares / count - center * center
    return (center, lax.rsqrt(spread + eps))


def move(source, target, sems, at):
    copy = pltpu.make_async_copy(source, target, sems.at[at])
    copy.start()
    return copy


def kernel_call(body, out_shape, in_specs, scratch=(), flops=0, moved=0, away=(), held=()):
    several = isinstance(out_shape, tuple)
    shapes = list(out_shape) if several else [out_shape]
    specs = [remote if at in away else whole for at in range(len(shapes))]
    shapes = [
        (pltpu.HBM if at in away else pltpu.VMEM)(shape.shape, shape.dtype)
        if at in away or at in held
        else shape
        for at, shape in enumerate(shapes)
    ]
    call = pl.pallas_call(
        body,
        out_shape=tuple(shapes) if several else shapes[0],
        in_specs=in_specs,
        out_specs=tuple(specs) if several else specs[0],
        scratch_shapes=list(scratch),
        compiler_params=pltpu.CompilerParams(vmem_limit_bytes=vmem_limit),
        cost_estimate=pl.CostEstimate(flops=flops, bytes_accessed=moved, transcendentals=0),
    )

    def run(*args):
        return call(
            *[
                pltpu.with_memory_space_constraint(arg, pltpu.HBM) if spec is remote else arg
                for arg, spec in zip(args, in_specs, strict=True)
            ]
        )

    return run


PAIRS = SEG // 2
CLIP = SEG * PIXELS


def pair_row(clip, pair):
    return pl.multiple_of(BLOCK * (2 + SPAN * (PAIRS * clip + pair)), BLOCK)


def clip_view(ref, clip, extra=0):
    return ref.at[pl.ds(pl.multiple_of(clip * CLIP, 8), CLIP + extra)]


def lane_mask(width):
    return lax.broadcasted_iota(jnp.int32, (1, 8, width), 1)


def load_map(ref, first, lanes):
    return jnp.stack([ref[pl.ds(first + SIDE * at, 8), lanes] for at in range(SIDE)])


def store_map(ref, first, lanes, value):
    for at in range(SIDE):
        ref[pl.ds(first + SIDE * at, SIDE), lanes] = value[at][:SIDE]


def two_maps(early, late):
    both = jnp.stack([early, late], axis=1)
    return both.reshape(SIDE * BLOCK, early.shape[-1])


def down(value, step):
    zeros = jnp.zeros((abs(step),) + value.shape[1:], value.dtype)
    if step > 0:
        return jnp.concatenate([value[step:], zeros])
    if step < 0:
        return jnp.concatenate([zeros, value[:step]])
    return value


def across(value, step, place):
    if step == 0:
        return value
    moved = pltpu.roll(value, (-step) % 8, 1)
    if step == 2:
        return jnp.where(place < 6, moved, 0.0)
    if step == -2:
        return jnp.where(place > 0, moved, 0.0)
    return moved


def taps_of(near, far):
    for step, kernel in ((1, near), (2, far)):
        for row in range(3):
            yield step, row, [kernel[row * 3 + col] for col in range(3)]


def gate_score(change, near, far, offset, place):
    views = {step: across(change, step, place) for step in (-2, -1, 0, 1, 2)}
    score = jnp.broadcast_to(offset, change.shape)
    for step, row, kernel in taps_of(near, far):
        term = sum(kernel[col] * views[step * (col - 1)] for col in range(3))
        score = score + down(term, step * (row - 1))
    return score, views


def conv_chunk(parts, weights, first, rows, sign):
    total = None
    for col in (1, 0, 2):
        acc = None
        for row in range(3):
            start = pl.multiple_of(first + BLOCK * (1 + sign * (row - 1)), BLOCK)
            for part, weight in zip(parts, weights, strict=True):
                left = part[pl.ds(start, rows), :]
                term = weight(left, row * 3 + col)
                acc = term if acc is None else acc + term
        acc = acc.reshape(rows // 8, 8, acc.shape[-1])
        shift = sign * (col - 1)
        if shift:
            acc = pltpu.roll(acc, (-shift) % 8, 1)
        total = acc if total is None else total + acc
    return total


def lane_part(index, width=128):
    return pl.ds(pl.multiple_of(index * width, width), width)


def row_part(index, size):
    return pl.ds(pl.multiple_of(index * size, size), size)


def rows_of(stats_ref):
    return stats_ref[0:1], stats_ref[1:2]


def put_sums(sums_ref, first, second):
    sums_ref[...] = jnp.zeros_like(sums_ref)
    sums_ref[0:1, :] = first
    sums_ref[1:2, :] = second


def gate_mid_body(
    count,
    place_ref,
    same_ref,
    own_ref,
    oth_ref,
    stats_own_ref,
    stats_oth_ref,
    par_own_ref,
    par_oth_ref,
    weight_own_ref,
    weight_peer_ref,
    mixed_out_ref,
    mid_ref,
    mid16_ref,
    sums_ref,
    hidden_ref,
    par_ref,
    acc_ref,
    weight_ref,
    oth_here_ref,
    stats_here_ref,
    mixed_ref,
    sems,
):
    rows, width = own_ref.shape
    clips = rows // CLIP
    core, y = place_ref[0] % 2, place_ref[0] // 2
    arrivals = [
        move(stats_oth_ref, stats_here_ref, sems, 0),
        move(oth_ref, oth_here_ref, sems, 1),
    ]
    weight_moves = [
        move(weight_own_ref, weight_ref.at[:, lane_part(core)], sems, 2),
        move(weight_peer_ref, weight_ref.at[:, lane_part(1 - core)], sems, 3),
    ]
    mixed_ref[...] = jnp.zeros_like(mixed_ref)
    hidden_ref[pl.ds(rows, hidden_ref.shape[0] - rows), :] = jnp.zeros(
        (hidden_ref.shape[0] - rows, 2 * width), jnp.float32
    )
    for side, (pre, stats, par) in enumerate(
        (
            (own_ref, stats_own_ref, par_own_ref),
            (oth_here_ref, stats_here_ref, par_oth_ref),
        )
    ):
        place = pl.multiple_of(width * (y if side == 0 else 1 - y), width)
        if side:
            for copy in arrivals:
                copy.wait()
        center, rate = norm_stats(*rows_of(stats), count)
        scaled = (pre[...].astype(jnp.float32) - center) * rate
        normed = scaled * par[0:1] + par[1:2]
        hidden_ref[pl.ds(0, rows), pl.ds(place, width)] = normed * logistic(normed)
        par_ref[:, pl.ds(place, width)] = par[...]
    at = lane_mask(128)

    def lanes_step(chunk, _):
        lanes = pl.ds(pl.multiple_of(chunk * 128, 128), 128)
        near = [par_ref[5 + tap : 6 + tap, lanes].reshape(1, 1, 128) for tap in range(9)]
        far = [par_ref[14 + tap : 15 + tap, lanes].reshape(1, 1, 128) for tap in range(9)]
        offset = par_ref[4:5, lanes].reshape(1, 1, 128)

        def clip_step(clip, _):
            view = clip_view(hidden_ref, clip, 56)
            for pair in range(PAIRS):
                maps = [
                    load_map(view, PIXELS * (2 * pair + seg), lanes) for seg in range(3)
                ]
                results = []
                for seg in range(2):
                    same = same_ref[clip, 2 * pair + seg].astype(jnp.float32)
                    change = jnp.where(at < SIDE, same * (maps[seg + 1] - maps[seg]), 0.0)
                    score, _ = gate_score(change, near, far, offset, at)
                    mixed = maps[seg] * (1.0 + logistic(score))
                    results.append(jnp.where(at < SIDE, mixed, 0.0))
                place = pl.ds(pair_row(clip, pair), SIDE * BLOCK)
                mixed_ref[place, lanes] = two_maps(*results).astype(jnp.bfloat16)
            return 0

        return lax.fori_loop(0, clips, clip_step, 0)

    lax.fori_loop(0, 2 * width // 128, lanes_step, 0)
    depth = 2 * width
    mixed_move = move(mixed_ref, mixed_out_ref, sems, 4)
    for copy in weight_moves:
        copy.wait()

    def tap_dot(left, tap):
        return jnp.dot(
            left, weight_ref[tap * depth : (tap + 1) * depth], preferred_element_type=jnp.float32
        )

    def conv_step(clip, _):
        span = PAIRS * SPAN * BLOCK
        total = conv_chunk([mixed_ref], [tap_dot], clip * span, span, 1)
        view = clip_view(acc_ref, clip)
        for seg in range(SEG):
            value = [total[2 * (SPAN * (seg // 2) + 1 + row) + seg % 2] for row in range(SIDE)]
            store_map(view, seg * PIXELS, slice(None), value)
        return 0

    lax.fori_loop(0, clips, conv_step, 0)
    mid_move = move(acc_ref.at[pl.ds(0, rows)], mid_ref, sems, 5)
    result = acc_ref[pl.ds(0, rows), :]
    mid16_ref[...] = result.astype(jnp.bfloat16)
    put_sums(
        sums_ref, jnp.sum(result, 0, keepdims=True), jnp.sum(result * result, 0, keepdims=True)
    )
    mixed_move.wait()
    mid_move.wait()


def map_rows(rows):
    return (rows // (2 * PIXELS) * SPAN + 2) * BLOCK


def gate_mid(count, place, same, own, oth, stats_own, stats_oth, par_own, par_oth, weights):
    rows, width = own.shape
    spread = map_rows(rows)
    depth = weights[0].shape[0]
    return kernel_call(
        functools.partial(gate_mid_body, count),
        (
            jax.ShapeDtypeStruct((spread, 2 * width), jnp.bfloat16),
            jax.ShapeDtypeStruct((rows, width), jnp.float32),
            jax.ShapeDtypeStruct((rows, width), jnp.bfloat16),
            jax.ShapeDtypeStruct((8, width), jnp.float32),
        ),
        [scalars, scalars, whole, remote, whole, remote, whole, whole, remote, remote],
        (
            pltpu.VMEM((rows + 56, 2 * width), jnp.float32),
            pltpu.VMEM((24, 2 * width), jnp.float32),
            pltpu.VMEM((rows + 8, width), jnp.float32),
            pltpu.VMEM((depth, width), jnp.bfloat16),
            pltpu.VMEM((rows, width), jnp.bfloat16),
            pltpu.VMEM((8, width), jnp.float32),
            pltpu.VMEM((spread, 2 * width), jnp.bfloat16),
            pltpu.SemaphoreType.DMA((6,)),
        ),
        away=(0, 1),
        flops=2 * rows * depth * width,
        moved=depth * width * 2 + rows * width * 12,
    )(place, same, own, oth, stats_own, stats_oth, par_own, par_oth, *weights)


def mid_back_body(
    count,
    place_ref,
    same_ref,
    d_own_ref,
    d_oth_ref,
    mid_own_ref,
    mid_oth_ref,
    stats_own_ref,
    stats_oth_ref,
    back_own_ref,
    back_oth_ref,
    pre_ref,
    stats_in_ref,
    par_own_ref,
    par_oth_ref,
    weight_own_ref,
    weight_peer_ref,
    away_own_ref,
    away_peer_ref,
    slopes_ref,
    d_in_ref,
    d_in16_ref,
    sums_ref,
    flat_ref,
    oth_ref,
    dmix_ref,
    scaled_ref,
    parts_ref,
    weight_ref,
    weight_oth_ref,
    d_here_ref,
    mid_here_ref,
    back_here_ref,
    pre_here_ref,
    sems,
):
    rows, width = d_own_ref.shape
    clips = rows // CLIP
    core, y = place_ref[0] % 2, place_ref[0] // 2
    arrivals = [
        move(back_oth_ref, back_here_ref, sems, 0),
        move(d_oth_ref, d_here_ref, sems, 1),
        move(mid_oth_ref, mid_here_ref, sems, 2),
    ]
    weight_moves = [
        move(weight_own_ref, weight_ref.at[:, lane_part(core)], sems, 3),
        move(weight_peer_ref, weight_ref.at[:, lane_part(1 - core)], sems, 4),
        move(away_own_ref, weight_oth_ref.at[:, lane_part(core)], sems, 5),
        move(away_peer_ref, weight_oth_ref.at[:, lane_part(1 - core)], sems, 6),
    ]
    pre_move = move(pre_ref, pre_here_ref, sems, 7)
    everything = slice(None)
    slopes_ref[...] = jnp.zeros_like(slopes_ref)
    oth_ref[...] = jnp.zeros_like(oth_ref)
    flat_ref[pl.ds(rows, flat_ref.shape[0] - rows), :] = jnp.zeros(
        (flat_ref.shape[0] - rows, width), jnp.float32
    )
    at_wide = lane_mask(width)
    for side, (grad, pre, stats, back, par) in enumerate(
        (
            (d_own_ref, mid_own_ref, stats_own_ref, back_own_ref, par_own_ref),
            (d_here_ref, mid_here_ref, stats_oth_ref, back_here_ref, par_oth_ref),
        )
    ):
        if side:
            for copy in arrivals:
                copy.wait()
        center, rate = norm_stats(*rows_of(stats), count)
        scaled = (pre[...].astype(jnp.float32) - center) * rate
        flat_ref[pl.ds(0, rows), :] = (par[2:3] * rate) * (
            grad[...].astype(jnp.float32)
            - back[0:1] / count
            - scaled * (back[1:2] / count)
        )

        def spread_step(clip, _, side=side):
            view = clip_view(flat_ref, clip, 8)
            for pair in range(PAIRS):
                maps = [
                    jnp.where(
                        at_wide < SIDE, load_map(view, PIXELS * (2 * pair + seg), everything), 0.0
                    )
                    for seg in range(2)
                ]
                place = pl.ds(pair_row(clip, pair), SIDE * BLOCK)
                if side:
                    oth_ref[place, :] = two_maps(*maps).astype(jnp.bfloat16)
                else:
                    for col in range(3):
                        slopes_ref[col, place, :] = two_maps(
                            *[across(value, 1 - col, at_wide) for value in maps]
                        ).astype(jnp.bfloat16)
            return 0

        lax.fori_loop(0, clips, spread_step, 0)

    depth = 2 * width
    turned = (((1,), (1,)), ((), ()))
    for copy in weight_moves:
        copy.wait()

    def own_dot(left, tap):
        start = pl.multiple_of(tap * depth + y * width, width)
        return lax.dot_general(
            left, weight_ref[pl.ds(start, width), :], turned, preferred_element_type=jnp.float32
        )

    def oth_dot(left, tap):
        return lax.dot_general(
            left,
            weight_oth_ref[tap * width : (tap + 1) * width],
            turned,
            preferred_element_type=jnp.float32,
        )

    def conv_step(clip, _):
        span = PAIRS * SPAN * BLOCK
        total = conv_chunk([slopes_ref.at[1], oth_ref], [own_dot, oth_dot], clip * span, span, -1)
        dmix_ref[pl.ds(clip * (span // 8), span // 8)] = total
        return 0

    lax.fori_loop(0, clips, conv_step, 0)

    center, rate = norm_stats(*rows_of(stats_in_ref), count)
    pre_move.wait()
    scaled_ref[pl.ds(0, rows), :] = (pre_here_ref[...] - center) * rate
    scaled_ref[pl.ds(rows, scaled_ref.shape[0] - rows), :] = jnp.zeros(
        (scaled_ref.shape[0] - rows, width), jnp.float32
    )
    parts_ref[...] = jnp.zeros_like(parts_ref)
    at = lane_mask(128)

    def lanes_step(chunk, _):
        lanes = pl.ds(pl.multiple_of(chunk * 128, 128), 128)

        def row_of(index):
            return par_own_ref[index : index + 1, lanes].reshape(1, 1, 128)

        near = [row_of(5 + tap) for tap in range(9)]
        far = [row_of(14 + tap) for tap in range(9)]
        offset, gain, bias = row_of(4), row_of(0), row_of(1)

        def add_part(index, value):
            here = pl.ds(8 * index, 8)
            parts_ref[here, lanes] += jnp.sum(value, 0)

        def clip_step(clip, carry):
            view = clip_view(scaled_ref, clip, 56)
            target = clip_view(flat_ref, clip)
            for pair in range(PAIRS):
                carry = pair_step(clip, pair, carry, view, target)
            return carry

        def pair_step(clip, pair, carry, view, target):
            normed = [
                load_map(view, PIXELS * (2 * pair + seg), lanes) * gain + bias for seg in range(3)
            ]
            parts = [logistic(value) for value in normed]
            hidden = [value * part for value, part in zip(normed, parts, strict=True)]
            for seg in range(2):
                same = same_ref[clip, 2 * pair + seg].astype(jnp.float32)
                change = jnp.where(at < SIDE, same * (hidden[seg + 1] - hidden[seg]), 0.0)
                score, views = gate_score(change, near, far, offset, at)
                gate = logistic(score)
                start = 2 * (SPAN * (PAIRS * clip + pair) + 1) + seg
                d_mixed = jnp.stack([dmix_ref[start + 2 * row, :, lanes] for row in range(SIDE)])
                d_mixed = jnp.where(at < SIDE, d_mixed, 0.0)
                d_score = d_mixed * hidden[seg] * (gate * (1.0 - gate))
                add_part(0, d_score)
                backs = {step: across(d_score, step, at) for step in (-2, -1, 0, 1, 2)}
                d_change = None
                for index, (step, row, kernel) in enumerate(taps_of(near, far)):
                    here = down(d_score, -step * (row - 1))
                    for col in range(3):
                        add_part(1 + 3 * index + col, here * views[step * (col - 1)])
                    term = sum(kernel[col] * backs[-step * (col - 1)] for col in range(3))
                    term = down(term, -step * (row - 1))
                    d_change = term if d_change is None else d_change + term
                d_change = jnp.where(at < SIDE, same * d_change, 0.0)
                d_hidden = d_mixed * (1.0 + gate) - d_change + carry
                carry = d_change
                slope = parts[seg] * (1.0 + normed[seg] * (1.0 - parts[seg]))
                store_map(target, PIXELS * (2 * pair + seg), lanes, d_hidden * slope)
            return carry

        lax.fori_loop(0, clips, clip_step, jnp.zeros((SIDE, 8, 128), jnp.float32))
        return 0

    lax.fori_loop(0, width // 128, lanes_step, 0)
    result = flat_ref[pl.ds(0, rows), :]
    d_in_ref[...] = result
    d_in16_ref[...] = result.astype(jnp.bfloat16)
    put_sums(
        sums_ref,
        jnp.sum(result, 0, keepdims=True),
        jnp.sum(result * scaled_ref[pl.ds(0, rows), :], 0, keepdims=True),
    )
    sums_ref[8:32, :] = jnp.sum(parts_ref[...].reshape(24, 8, width), 1)


def mid_back(
    count, place, same, d_own, d_oth, mid_own, mid_oth, stats, back, pre, stats_in, pars, weights, aways,
):
    rows, width = d_own.shape
    spread = map_rows(rows)
    depth = weights[0].shape[0]
    return kernel_call(
        functools.partial(mid_back_body, count),
        (
            jax.ShapeDtypeStruct((3, spread, width), jnp.bfloat16),
            jax.ShapeDtypeStruct((rows, width), jnp.float32),
            jax.ShapeDtypeStruct((rows, width), jnp.bfloat16),
            jax.ShapeDtypeStruct((32, width), jnp.float32),
        ),
        [scalars, scalars, whole, remote, whole, remote, whole, whole, whole, remote, remote]
        + [whole] * 3
        + [remote] * 4,
        (
            pltpu.VMEM((rows + 56, width), jnp.float32),
            pltpu.VMEM((spread, width), jnp.bfloat16),
            pltpu.VMEM((spread // 8, 8, width), jnp.float32),
            pltpu.VMEM((rows + 56, width), jnp.float32),
            pltpu.VMEM((24 * 8, width), jnp.float32),
            pltpu.VMEM((depth, width), jnp.bfloat16),
            pltpu.VMEM((depth // 2, width), jnp.bfloat16),
            pltpu.VMEM((rows, width), jnp.bfloat16),
            pltpu.VMEM((rows, width), jnp.bfloat16),
            pltpu.VMEM((8, width), jnp.float32),
            pltpu.VMEM((rows, width), jnp.float32),
            pltpu.SemaphoreType.DMA((8,)),
        ),
        flops=2 * rows * depth * width,
        moved=depth * width * 3 + rows * width * 20,
        held=(0, 1),
    )(
        place, same, d_own, d_oth, mid_own, mid_oth, *stats, *back, pre, stats_in, *pars, *weights, *aways,
    )


def turn_body(mixed_ref, out_ref, mixed_here_ref, sems):
    move(mixed_ref, mixed_here_ref, sems, 0).wait()
    out_ref[...] = mixed_here_ref[pl.ds(BLOCK, out_ref.shape[1]), :].T


def turn(mixed):
    spread, depth = mixed.shape
    return kernel_call(
        turn_body,
        jax.ShapeDtypeStruct((depth, spread - 2 * BLOCK), jnp.bfloat16),
        [remote],
        (pltpu.VMEM(mixed.shape, jnp.bfloat16), pltpu.SemaphoreType.DMA((1,))),
        held=(0,),
    )(mixed)


def mid_weight_body(place_ref, turned_ref, slopes_ref, keep_ref, send_ref):
    depth, rows = turned_ref.shape
    half = keep_ref.shape[1]
    first = place_ref[0] % 2 == 0
    for tap in range(9):
        row, col = tap // 3, tap % 3
        right = slopes_ref[col, pl.ds(BLOCK * (2 - row), rows), :]
        value = jnp.dot(turned_ref[...], right, preferred_element_type=jnp.float32)
        low, high = value[:, :half], value[:, half:]
        here = pl.ds(tap * depth, depth)
        keep_ref[here, :] = jnp.where(first, low, high)
        send_ref[here, :] = jnp.where(first, high, low).astype(jnp.bfloat16)


def mid_weight(place, turned, slopes):
    depth, rows = turned.shape
    width = slopes.shape[2]
    return kernel_call(
        mid_weight_body,
        (
            jax.ShapeDtypeStruct((9 * depth, width // 2), jnp.float32),
            jax.ShapeDtypeStruct((9 * depth, width // 2), jnp.bfloat16),
        ),
        [scalars, whole, whole],
        flops=2 * rows * 9 * depth * width,
        moved=rows * (2 * depth + 6 * width) + 9 * depth * width * 3,
        held=(0,),
    )(place, turned, slopes)


def first_conv_body(
    order,
    place_ref,
    block_ref,
    peer_ref,
    across_ref,
    corner_ref,
    own_ref,
    other_ref,
    extra_ref,
    pre_out_ref,
    pre16_ref,
    sums_ref,
    weight_out_ref,
    pre_ref,
    weight_ref,
    sems,
):
    rows = peer_ref.shape[0]
    quarter = block_ref.shape[1]
    chan, group = place_ref[0], place_ref[1]
    core = chan % 2
    size = own_ref.shape[0] // len(order)
    for at, bits in enumerate(order):
        here = row_part(group ^ bits, size)
        weight_ref[here, lane_part(core)] = own_ref[at * size : (at + 1) * size]
        weight_ref[here, lane_part(1 - core)] = other_ref[at * size : (at + 1) * size]
    weight_move = move(weight_ref, weight_out_ref, sems, 0)
    mine = block_ref[row_part(core, rows), :]
    total = None
    for at, piece in enumerate((mine, peer_ref[...], across_ref[...], corner_ref[...])):
        weight = weight_ref[row_part(chan ^ at, quarter), :]
        term = jnp.dot(piece, weight, preferred_element_type=jnp.float32)
        total = term if total is None else total + term
    pre_ref[...] = total
    pre_move = move(pre_ref, pre_out_ref, sems, 1)
    pre16_ref[...] = total.astype(jnp.bfloat16)
    sums_ref[...] = extra_ref[...]
    sums_ref[0:1, :] = jnp.sum(total, 0, keepdims=True)
    sums_ref[1:2, :] = jnp.sum(total * total, 0, keepdims=True)
    weight_move.wait()
    pre_move.wait()


def first_conv(order, place, block, pieces, weights, extra):
    rows, quarter = pieces[0].shape
    width = 2 * weights[0].shape[1]
    return kernel_call(
        functools.partial(first_conv_body, order),
        (
            jax.ShapeDtypeStruct((rows, width), jnp.float32),
            jax.ShapeDtypeStruct((rows, width), jnp.bfloat16),
            jax.ShapeDtypeStruct((8, width), jnp.float32),
            jax.ShapeDtypeStruct((4 * quarter, width), jnp.bfloat16),
        ),
        [scalars] + [whole] * 7,
        (
            pltpu.VMEM((rows, width), jnp.float32),
            pltpu.VMEM((4 * quarter, width), jnp.bfloat16),
            pltpu.SemaphoreType.DMA((2,)),
        ),
        flops=8 * rows * quarter * width,
        moved=rows * quarter * 8,
        away=(0, 3),
    )(place, block, *pieces, *weights, extra)


def second_body(
    count, place_ref, own_ref, oth_ref, stats_own_ref, stats_oth_ref, par_own_ref, par_oth_ref, out_ref,
    oth_here_ref, stats_here_ref, sems,
):
    width = own_ref.shape[1]
    y = place_ref[0] // 2
    arrivals = [
        move(stats_oth_ref, stats_here_ref, sems, 0),
        move(oth_ref, oth_here_ref, sems, 1),
    ]
    for side, pre, stats, par in (
        (y, own_ref, stats_own_ref, par_own_ref),
        (1 - y, oth_here_ref, stats_here_ref, par_oth_ref),
    ):
        center, rate = norm_stats(*rows_of(stats), count)
        normed = (pre[...].astype(jnp.float32) - center) * rate * par[2:3] + par[3:4]
        out_ref[:, lane_part(side, width)] = (normed * logistic(normed)).astype(jnp.bfloat16)
        for copy in arrivals:
            copy.wait()
        arrivals = []


def second_half(count, place, own, oth, stats, pars):
    rows, width = own.shape
    return kernel_call(
        functools.partial(second_body, count),
        jax.ShapeDtypeStruct((rows, 2 * width), jnp.bfloat16),
        [scalars, whole, remote, whole, remote, whole, whole],
        (
            pltpu.VMEM((rows, width), jnp.bfloat16),
            pltpu.VMEM((8, width), jnp.float32),
            pltpu.SemaphoreType.DMA((2,)),
        ),
        moved=rows * width * 10,
    )(place, own, oth, *stats, *pars)


def last_conv_body(place_ref, mine_ref, peer_ref, weight_ref, extra_ref, out_ref, sums_ref):
    rows = mine_ref.shape[0]
    core = place_ref[0] % 2
    sums = squares = 0.0
    for side, part in ((core, mine_ref), (1 - core, peer_ref)):
        value = jnp.dot(part[...], weight_ref[...], preferred_element_type=jnp.float32)
        out_ref[row_part(side, rows), :] = value
        sums += jnp.sum(value, 0, keepdims=True)
        squares += jnp.sum(value * value, 0, keepdims=True)
    sums_ref[...] = extra_ref[...]
    sums_ref[0:1, :] = sums
    sums_ref[1:2, :] = squares


def last_conv(place, mine, peer, weight, extra):
    rows, depth = mine.shape
    width = weight.shape[1]
    return kernel_call(
        last_conv_body,
        (
            jax.ShapeDtypeStruct((2 * rows, width), jnp.float32),
            jax.ShapeDtypeStruct((8, width), jnp.float32),
        ),
        [scalars] + [whole] * 4,
        flops=4 * rows * depth * width,
        moved=rows * width * 12,
    )(place, mine, peer, weight, extra)


def out_back_body(
    count,
    place_ref,
    pre_ref,
    block_ref,
    grad_ref,
    stats_ref,
    gain_ref,
    bias_ref,
    weight_ref,
    out_ref,
    total_out_ref,
    sums_ref,
    keep_ref,
    send_ref,
    total_ref,
    sems,
):
    rows = keep_ref.shape[0]
    core = place_ref[0] % 2
    center, rate = norm_stats(*rows_of(stats_ref), count)
    gain, bias = gain_ref[...], bias_ref[...]
    step = rows // 7

    def add_step(at, sums):
        here = row_part(at, step)
        scaled = (pre_ref[here, :] - center) * rate
        total = scaled * gain + bias + block_ref[here, :].astype(jnp.float32)
        part = logistic(total)
        out_ref[here, :] = (total * part).astype(jnp.bfloat16)
        value = grad_ref[here, :].astype(jnp.float32) * (part * (1.0 + total * (1.0 - part)))
        total_ref[here, :] = value
        return (
            sums[0] + jnp.sum(value, 0, keepdims=True),
            sums[1] + jnp.sum(value * scaled, 0, keepdims=True),
        )

    zero = jnp.zeros((1, pre_ref.shape[1]), jnp.float32)
    sums, products = lax.fori_loop(0, 14, add_step, (zero, zero))
    put_sums(sums_ref, sums, products)
    total_move = move(total_ref, total_out_ref, sems, 0)
    local = 1.0 / (2 * rows)

    def slope_rows(side):
        here = row_part(side, rows)
        scaled = (pre_ref[here, :] - center) * rate
        value = gain * rate * (total_ref[here, :] - sums * local - scaled * (products * local))
        return lax.dot_general(
            value.astype(jnp.bfloat16),
            weight_ref[...],
            (((1,), (1,)), ((), ())),
            preferred_element_type=jnp.float32,
        )

    send_ref[...] = slope_rows(1 - core).astype(jnp.bfloat16)
    keep_ref[...] = slope_rows(core)
    total_move.wait()


def out_back(count, place, pre, block, grad, stats, gain, bias, weight):
    rows, width = pre.shape
    depth = weight.shape[0]
    return kernel_call(
        functools.partial(out_back_body, count),
        (
            jax.ShapeDtypeStruct((rows, width), jnp.bfloat16),
            jax.ShapeDtypeStruct((rows, width), jnp.float32),
            jax.ShapeDtypeStruct((8, width), jnp.float32),
            jax.ShapeDtypeStruct((rows // 2, depth), jnp.float32),
            jax.ShapeDtypeStruct((rows // 2, depth), jnp.bfloat16),
        ),
        [scalars] + [whole] * 7,
        (pltpu.VMEM((rows, width), jnp.float32), pltpu.SemaphoreType.DMA((1,))),
        flops=2 * rows * width * depth,
        moved=rows * width * 20,
        away=(1,),
    )(place, pre, block, grad, stats, gain, bias, weight)


def cross_body(place_ref, keep_ref, got_ref, own_ref, send_ref):
    width = own_ref.shape[1]
    y = place_ref[0] // 2
    for lanes, ref in ((1 - y, send_ref), (y, own_ref)):
        here = lane_part(lanes, width)
        value = keep_ref[:, here] + got_ref[:, here].astype(jnp.float32)
        ref[...] = value.astype(ref.dtype)


def cross_half(place, keep, got):
    rows, width = keep.shape[0], keep.shape[1] // 2
    return kernel_call(
        cross_body,
        (
            jax.ShapeDtypeStruct((rows, width), jnp.float32),
            jax.ShapeDtypeStruct((rows, width), jnp.bfloat16),
        ),
        [scalars, whole, whole],
        moved=rows * width * 18,
    )(place, keep, got)


def out_delta_body(count, local, stats_ref, sums_ref, back_ref, gain_ref, out_ref):
    center, rate = norm_stats(*rows_of(stats_ref), count)
    scale = gain_ref[...] * rate
    first = scale * (back_ref[0:1] / count - sums_ref[0:1] * local)
    second = scale * rate * (back_ref[1:2] / count - sums_ref[1:2] * local)
    put_sums(out_ref, first - second * center, second)


def out_delta(count, rows, stats, sums, back, gain):
    return kernel_call(
        functools.partial(out_delta_body, count, 1.0 / rows),
        jax.ShapeDtypeStruct(stats.shape, jnp.float32),
        [whole] * 4,
    )(stats, sums, back, gain)


def mid_slope_body(
    count,
    place_ref,
    keep_ref,
    got_ref,
    second_ref,
    mid_ref,
    stats_ref,
    par_ref,
    deltas0_ref,
    deltas1_ref,
    deltas2_ref,
    deltas3_ref,
    weights0_ref,
    weights1_ref,
    weights2_ref,
    weights3_ref,
    out_ref,
    out16_ref,
    sums_ref,
):
    width = mid_ref.shape[1]
    y = place_ref[0] // 2
    turned = (((1,), (1,)), ((), ()))
    factor, offset = None, None
    for deltas, weights in (
        (deltas0_ref, weights0_ref),
        (deltas1_ref, weights1_ref),
        (deltas2_ref, weights2_ref),
        (deltas3_ref, weights3_ref),
    ):
        own = weights[row_part(y, width), :]
        left = (weights[...].astype(jnp.float32) * deltas[1:2]).astype(jnp.bfloat16)
        term = lax.dot_general(left, own, turned, preferred_element_type=jnp.float32)
        factor = term if factor is None else factor + term
        term = lax.dot_general(
            deltas[...], own.astype(jnp.float32), turned, preferred_element_type=jnp.float32
        )[0:1]
        offset = term if offset is None else offset + term
    delta = jnp.dot(
        second_ref[...], factor.astype(jnp.bfloat16), preferred_element_type=jnp.float32
    )
    grad = keep_ref[...] + got_ref[...].astype(jnp.float32) - delta - offset
    center, rate = norm_stats(*rows_of(stats_ref), count)
    scaled = (mid_ref[...] - center) * rate
    normed = scaled * par_ref[2:3] + par_ref[3:4]
    result = grad * silu_slope(normed)
    out_ref[...] = result
    out16_ref[...] = result.astype(jnp.bfloat16)
    put_sums(
        sums_ref, jnp.sum(result, 0, keepdims=True), jnp.sum(result * scaled, 0, keepdims=True)
    )


def mid_slope(count, place, keep, got, second, mid, stats, par, deltas, weights):
    rows, width = mid.shape
    return kernel_call(
        functools.partial(mid_slope_body, count),
        (
            jax.ShapeDtypeStruct((rows, width), jnp.float32),
            jax.ShapeDtypeStruct((rows, width), jnp.bfloat16),
            jax.ShapeDtypeStruct((8, width), jnp.float32),
        ),
        [scalars] + [whole] * 14,
        flops=2 * rows * width * 2 * width,
        moved=rows * width * 20,
        held=(0,),
    )(place, keep, got, second, mid, stats, par, *deltas, *weights)


def out_weight_body(
    count, part, place_ref, rows_ref, pre_ref, total_ref, stats_ref, back_ref, gain_ref, *refs
):
    rows = rows_ref.shape[0]
    core = place_ref[0] % 2
    center, rate = norm_stats(*rows_of(stats_ref), count)
    here = row_part(1 - core if part else core, rows)
    scaled = (pre_ref[here, :] - center) * rate
    value = (gain_ref[...] * rate) * (
        total_ref[here, :] - back_ref[0:1] / count - scaled * (back_ref[1:2] / count)
    )
    result = exact(rows_ref[...], value.astype(jnp.bfloat16), ((0,), (0,)))
    refs[-1][...] = refs[0][...] + result if part else result


def out_weight(count, place, second, pre, total, stats, back, gain, start=None):
    rows, depth = second.shape
    width = pre.shape[1]
    part = 0 if start is None else 1
    return kernel_call(
        functools.partial(out_weight_body, count, part),
        jax.ShapeDtypeStruct((depth, width), jnp.float32),
        [scalars] + [whole] * (6 + part),
        flops=2 * rows * depth * width,
        moved=rows * width * 10,
    )(place, second, pre, total, stats, back, gain, *([start] if part else []))


def in_back_body(
    count,
    place_ref,
    d_own_ref,
    d_oth_ref,
    pre_own_ref,
    pre_oth_ref,
    stats_own_ref,
    stats_oth_ref,
    back_own_ref,
    back_oth_ref,
    par_own_ref,
    par_oth_ref,
    block_ref,
    peer_ref,
    across_ref,
    corner_ref,
    out_ref,
    keep_ref,
    send_ref,
    d_here_ref,
    pre_here_ref,
    back_here_ref,
    sems,
):
    rows, width = d_own_ref.shape
    arrivals = [
        move(back_oth_ref, back_here_ref, sems, 0),
        move(d_oth_ref, d_here_ref, sems, 1),
        move(pre_oth_ref, pre_here_ref, sems, 2),
    ]
    half = width // 2
    quarter = block_ref.shape[1]
    chan = place_ref[0]
    core, y = chan % 2, chan // 2
    own = None
    for side, grad, pre, stats, back, par in (
        (y, d_own_ref, pre_own_ref, stats_own_ref, back_own_ref, par_own_ref),
        (1 - y, d_here_ref, pre_here_ref, stats_oth_ref, back_here_ref, par_oth_ref),
    ):
        center, rate = norm_stats(*rows_of(stats), count)
        scaled = (pre[...].astype(jnp.float32) - center) * rate
        value = (par[0:1] * rate) * (
            grad[...].astype(jnp.float32) - back[0:1] / count - scaled * (back[1:2] / count)
        )
        value = value.astype(jnp.bfloat16)
        out_ref[:, lane_part(side, width)] = value
        own = value if own is None else own
        for copy in arrivals:
            copy.wait()
        arrivals = []
    mine = block_ref[row_part(core, rows), :]
    for at, piece in enumerate((mine, peer_ref[...], across_ref[...], corner_ref[...])):
        value = lax.dot_general(
            piece, own, (((0,), (0,)), ((), ())), preferred_element_type=jnp.float32
        )
        here = row_part(chan ^ at, quarter)
        low, high = value[:, :half], value[:, half:]
        keep_ref[here, :] = jnp.where(core == 0, low, high)
        send_ref[here, :] = jnp.where(core == 0, high, low).astype(jnp.bfloat16)


def in_back(count, place, d_own, d_oth, pre_own, pre_oth, stats, back, pars, block, pieces):
    rows, width = d_own.shape
    full = 4 * block.shape[1]
    return kernel_call(
        functools.partial(in_back_body, count),
        (
            jax.ShapeDtypeStruct((rows, 2 * width), jnp.bfloat16),
            jax.ShapeDtypeStruct((full, width // 2), jnp.float32),
            jax.ShapeDtypeStruct((full, width // 2), jnp.bfloat16),
        ),
        [scalars, whole, remote, whole, remote, whole, whole, whole, remote] + [whole] * 6,
        (
            pltpu.VMEM((rows, width), jnp.bfloat16),
            pltpu.VMEM((rows, width), jnp.bfloat16),
            pltpu.VMEM(back[1].shape, jnp.float32),
            pltpu.SemaphoreType.DMA((3,)),
        ),
        flops=2 * rows * width * full,
        moved=rows * full * 2,
        held=(1,),
    )(place, d_own, d_oth, pre_own, pre_oth, *stats, *back, *pars, block, *pieces)


def input_grad_body(place_ref, mine_ref, peer_ref, near_ref, far_ref, total_ref, out_ref):
    rows = mine_ref.shape[0]
    width = near_ref.shape[1]
    core, y = place_ref[0] % 2, place_ref[0] // 2
    turned = (((1,), (1,)), ((), ()))
    for side, part in ((core, mine_ref), (1 - core, peer_ref)):
        here = row_part(side, rows)
        value = total_ref[here, :]
        for lanes, weight in ((y, near_ref), (1 - y, far_ref)):
            value += lax.dot_general(
                part[:, lane_part(lanes, width)],
                weight[...],
                turned,
                preferred_element_type=jnp.float32,
            )
        out_ref[here, :] = value.astype(jnp.bfloat16)


def input_grad(place, mine, peer, near, far, total):
    rows, quarter = total.shape
    return kernel_call(
        input_grad_body,
        jax.ShapeDtypeStruct((rows, quarter), jnp.bfloat16),
        [scalars] + [whole] * 5,
        flops=2 * rows * quarter * 2 * near.shape[1],
        moved=rows * quarter * 8,
    )(place, mine, peer, near, far, total)


def pack_body(gain_in, bias_in, gain_mid, bias_mid, gate_bias, near, far, out_ref):
    for at, ref in enumerate((gain_in, bias_in, gain_mid, bias_mid, gate_bias)):
        out_ref[at : at + 1, :] = ref[...]
    out_ref[5:14, :] = near[...]
    out_ref[14:23, :] = far[...]
    out_ref[23:24, :] = jnp.zeros_like(out_ref[23:24, :])


def pack_params(rows, near, far):
    width = near.shape[1]
    return kernel_call(
        pack_body, jax.ShapeDtypeStruct((24, width), jnp.float32), [whole] * 7
    )(*[row.reshape(1, width) for row in rows], near, far)


TAPS = 7
LANES = 16


def exact(left, right, contract):
    return lax.dot_general(
        left, right, (contract, ((), ())), preferred_element_type=jnp.float32
    )


def spot(core, outs, width, part):
    lane = lax.broadcasted_iota(jnp.int32, (outs, width), 1)
    channel = lax.broadcasted_iota(jnp.int32, (outs, width), 0)
    return (lane == core * 2 * outs + part * outs + channel).astype(jnp.float32)


def stem_row(core, width, first, second):
    row = None
    for part, value in enumerate((first, second)):
        column = jnp.sum(jnp.sum(value, 0), 1, keepdims=True)
        term = jnp.sum(column * spot(core, value.shape[1], width, part), 0, keepdims=True)
        row = term if row is None else row + term
    at = lax.broadcasted_iota(jnp.int32, (8, width), 0)
    return jnp.where(at == 2, row, 0.0)


def stem_columns(core, outs, stats_ref):
    row = stats_ref[2:3, :]
    return [
        jnp.sum(row * spot(core, outs, row.shape[1], part), 1, keepdims=True) for part in range(2)
    ]


def upright(row_ref):
    size = row_ref.shape[1]
    at = lax.broadcasted_iota(jnp.int32, (size, size), 0)
    same = at == lax.broadcasted_iota(jnp.int32, (size, size), 1)
    return jnp.sum(jnp.where(same, row_ref[...], 0.0), 1, keepdims=True)


def stem_front_body(
    place_ref, video_ref, weight_ref, pre_out_ref, rows_out_ref, pick_out_ref, extra_ref, flat_ref, parts_ref,
    pre_ref, rows_ref, pick_ref, sems,
):
    segs, colours, size = video_ref.shape
    side = 32
    half = size // 2
    quarter = half // 2
    core = place_ref[0] % 2
    at = lax.broadcasted_iota(jnp.int32, (LANES, size), 0)
    zero = jnp.zeros((LANES - colours, size), jnp.float32)

    def plane_step(seg, _):
        value = jnp.concatenate([video_ref[seg].astype(jnp.float32), zero])
        moving = pltpu.roll(value, LANES - 3, 0) - value
        center = pltpu.roll(value, 6, 0)
        plane = jnp.where(at < 12, moving, jnp.where(at < 15, center, 0.0))
        flat_ref[pl.ds(pl.multiple_of(seg * LANES, LANES), LANES), :] = plane.astype(jnp.bfloat16)
        return 0

    lax.fori_loop(0, segs, plane_step, 0, unroll=4)
    source = lax.broadcasted_iota(jnp.int32, (size, half), 0)
    lane = lax.broadcasted_iota(jnp.int32, (size, half), 1)
    lanes = lax.broadcasted_iota(jnp.int32, (segs * LANES, half), 1)
    for parity in range(2):
        hit = source == 2 * side * (lane // side) + side * parity + lane % side
        rows = jnp.dot(
            flat_ref[...],
            jnp.where(hit, 1.0, 0.0).astype(jnp.bfloat16),
            preferred_element_type=jnp.float32,
        )
        for tap in range(TAPS):
            if (tap - 3) % 2 != parity:
                continue
            shift = (tap - 3 - parity) // 2 * side
            value = rows
            if shift:
                value = pltpu.roll(rows, (-shift) % half, 1)
                inside = lanes < half - shift if shift > 0 else lanes >= -shift
                value = jnp.where(inside, value, 0.0)
            value = value.astype(jnp.bfloat16).reshape(segs, LANES, half)
            rows_ref[:, tap * LANES : (tap + 1) * LANES, :] = value
    weight = weight_ref[...]
    moves = [move(rows_ref, rows_out_ref, sems, 0)]

    def seg_step(seg, _):
        value = jnp.dot(weight, rows_ref[seg], preferred_element_type=jnp.float32)
        value = value.astype(jnp.bfloat16)
        here = pl.ds(pl.multiple_of(seg * LANES, LANES), LANES)
        for tap in range(TAPS):
            parts_ref[tap, here, :] = value[tap * LANES : (tap + 1) * LANES]
        return 0

    lax.fori_loop(0, segs, seg_step, 0, unroll=4)
    source = lax.broadcasted_iota(jnp.int32, (half, quarter), 0)
    lane = lax.broadcasted_iota(jnp.int32, (half, quarter), 1)
    total = None
    for tap in range(TAPS):
        column = 2 * (lane % LANES) + tap - 3
        hit = (source == side * (lane // LANES) + column) & (column >= 0) & (column < side)
        pick = jnp.where(hit, 1.0, 0.0).astype(jnp.bfloat16)
        pick_ref[tap] = pick
        term = jnp.dot(parts_ref[tap], pick, preferred_element_type=jnp.float32)
        total = term if total is None else total + term
    total = total.reshape(segs, LANES, quarter)
    pre_ref[...] = total
    moves += [move(pick_ref, pick_out_ref, sems, 1), move(pre_ref, pre_out_ref, sems, 2)]
    extra_ref[...] = stem_row(core, extra_ref.shape[1], total, total * total)
    for copy in moves:
        copy.wait()


def stem_front(place, video, weight, width):
    segs, _, size = video.shape
    return kernel_call(
        stem_front_body,
        (
            jax.ShapeDtypeStruct((segs, LANES, size // 4), jnp.float32),
            jax.ShapeDtypeStruct((segs, TAPS * LANES, size // 2), jnp.bfloat16),
            jax.ShapeDtypeStruct((TAPS, size // 2, size // 4), jnp.bfloat16),
            jax.ShapeDtypeStruct((8, width), jnp.float32),
        ),
        [scalars, whole, whole],
        (
            pltpu.VMEM((segs * LANES, size), jnp.bfloat16),
            pltpu.VMEM((TAPS, segs * LANES, size // 2), jnp.bfloat16),
            pltpu.VMEM((segs, LANES, size // 4), jnp.float32),
            pltpu.VMEM((segs, TAPS * LANES, size // 2), jnp.bfloat16),
            pltpu.VMEM((TAPS, size // 2, size // 4), jnp.bfloat16),
            pltpu.SemaphoreType.DMA((3,)),
        ),
        away=(0, 1, 2),
        flops=4 * segs * TAPS * LANES * TAPS * LANES * size,
        moved=segs * size * 40,
    )(place, video, weight)


def stem_norm(count, core, pre, stats_ref, gain_ref, bias_ref):
    outs = pre.shape[1]
    center, rate = norm_stats(*stem_columns(core, outs, stats_ref), count)
    scaled = (pre - center) * rate
    return scaled, scaled * upright(gain_ref) + upright(bias_ref), upright(gain_ref) * rate


def stem_out_body(count, place_ref, pre_ref, grad_ref, stats_ref, gain_ref, bias_ref, out_ref, extra_ref):
    core = place_ref[0] % 2
    scaled, normed, _ = stem_norm(count, core, pre_ref[...], stats_ref, gain_ref, bias_ref)
    part = logistic(normed)
    out_ref[...] = (normed * part).astype(jnp.bfloat16)
    value = grad_ref[...].astype(jnp.float32) * (part * (1.0 + normed * (1.0 - part)))
    extra_ref[...] = stem_row(core, extra_ref.shape[1], value, value * scaled)


def stem_output(count, place, pre, grad, stats, gain, bias, width):
    return kernel_call(
        functools.partial(stem_out_body, count),
        (
            jax.ShapeDtypeStruct(pre.shape, jnp.bfloat16),
            jax.ShapeDtypeStruct((8, width), jnp.float32),
        ),
        [scalars] + [whole] * 5,
    )(place, pre, grad, stats, gain.reshape(1, -1), bias.reshape(1, -1))


def stem_back_body(
    count, first, place_ref, pre_ref, grad_ref, stats_ref, back_ref, gain_ref, bias_ref, rows_ref, pick_ref, start_ref, out_ref, slopes_ref,
):
    core = place_ref[0] % 2
    segs, outs, pixels = pre_ref.shape
    scaled, normed, scale = stem_norm(count, core, pre_ref[...], stats_ref, gain_ref, bias_ref)
    bias_grad, gain_grad = stem_columns(core, outs, back_ref)
    value = grad_ref[...].astype(jnp.float32) * silu_slope(normed)
    value = scale * (value - bias_grad / count - scaled * (gain_grad / count))
    value = value.astype(jnp.bfloat16).reshape(segs * outs, pixels)
    half = rows_ref.shape[2]
    for tap in range(TAPS):
        spread = exact(value, pick_ref[tap], ((1,), (1,)))
        slopes_ref[:, tap * LANES : (tap + 1) * LANES, :] = spread.astype(jnp.bfloat16).reshape(
            segs, outs, half
        )
    total = None
    for seg in range(segs):
        term = exact(rows_ref[seg], slopes_ref[seg], ((1,), (1,)))
        total = term if total is None else total + term
    size = TAPS * LANES
    rows = size // 2
    if first:
        out_ref[...] = jnp.zeros_like(out_ref)
    else:
        out_ref[...] = start_ref[...]
    out_ref[:, :size] += total[:rows]
    out_ref[:, 128 : 128 + size] += total[rows:]


def stem_back(count, place, pre, grad, stats, back, gain, bias, rows, pick, start, chunk, chunks):
    segs, outs, pixels = pre.shape
    size = segs // chunks

    def part(*tail):
        return pl.BlockSpec((size,) + tail, lambda at: (chunk, 0, 0))

    def all_of(shape):
        return pl.BlockSpec(shape, lambda at: (0,) * len(shape))

    small = (TAPS * LANES // 2, 256)
    first = start is None
    start = jnp.zeros((8, 256), jnp.float32) if first else start
    return pl.pallas_call(
        functools.partial(stem_back_body, count, first),
        grid=(1,),
        out_shape=jax.ShapeDtypeStruct(small, jnp.float32),
        in_specs=[scalars, part(outs, pixels), part(outs, pixels)]
        + [all_of(stats.shape), all_of(back.shape), all_of((1, outs)), all_of((1, outs))]
        + [part(*rows.shape[1:]), all_of(pick.shape), all_of(start.shape)],
        out_specs=all_of(small),
        scratch_shapes=[pltpu.VMEM((size, TAPS * LANES, rows.shape[2]), jnp.bfloat16)],
        compiler_params=pltpu.CompilerParams(vmem_limit_bytes=vmem_limit),
        cost_estimate=pl.CostEstimate(
            flops=4 * size * (TAPS * LANES) ** 2 * rows.shape[2], bytes_accessed=1 << 20, transcendentals=0
        ),
    )(place, pre, grad, stats, back, gain.reshape(1, -1), bias.reshape(1, -1), rows, pick, start)


def stem_weight(center, diff):
    outs = center.shape[1]
    value = jnp.concatenate([diff, center, jnp.zeros((TAPS * TAPS, outs), center.dtype)])
    value = value.reshape(LANES, TAPS, TAPS, outs)
    return value.transpose(2, 3, 1, 0).reshape(TAPS * outs, TAPS * LANES)


def stem_grads_body(packed_ref, center_ref, diff_ref):
    full = jnp.concatenate([packed_ref[:, :128], packed_ref[:, 128:]])
    for row in range(TAPS):
        value = full[row * LANES : (row + 1) * LANES]
        for col in range(TAPS):
            here = value[:, col * LANES : (col + 1) * LANES]
            at = row * TAPS + col
            diff_ref[pl.ds(at, 12, stride=TAPS * TAPS), :] = here[:12]
            center_ref[pl.ds(at, 3, stride=TAPS * TAPS), :] = here[12:15]


def stem_grads(packed, outs):
    return kernel_call(
        stem_grads_body,
        (
            jax.ShapeDtypeStruct((3 * TAPS * TAPS, outs), jnp.float32),
            jax.ShapeDtypeStruct((12 * TAPS * TAPS, outs), jnp.float32),
        ),
        [whole],
    )(packed)


def after(value, *marks):
    return lax.optimization_barrier((value, marks))[0]


def swap(value, axis, bit):
    size = lax.axis_size(axis)
    return lax.ppermute(value, axis, [(at, at ^ bit) for at in range(size)])


def steps_of(axis):
    size = lax.axis_size(axis)
    assert size & (size - 1) == 0
    return [1 << at for at in range(size.bit_length() - 1)]


def sum_over(value, axis, jobs=()):
    jobs = list(jobs)
    for bit in steps_of(axis):
        got = swap(value, axis, bit)
        if jobs:
            got = after(got, jobs.pop(0)(value))
        value = value + got
    for job in jobs:
        value = after(value, job(value))
    return value


def ordered(second, own, other, axis=0):
    return jnp.where(
        second, jnp.concatenate([other, own], axis), jnp.concatenate([own, other], axis)
    )


def gather_rows(value, axis):
    order = [0]
    for bit in reversed(steps_of(axis)):
        value = jnp.concatenate([value, swap(value, axis, bit)])
        order += [at ^ bit for at in order]
    return value, order


def halve_body(bit, place_ref, keep_ref, got_ref, mine_ref, send_ref):
    size = send_ref.shape[1]
    high = (place_ref[1] // bit) % 2
    for block in range(send_ref.shape[0]):
        for ref, side in ((mine_ref, high), (send_ref, 1 - high)):
            here = pl.ds(pl.multiple_of((2 * block + side) * size, size), size)
            value = keep_ref[here, :]
            if got_ref is not None:
                value = value + got_ref[here, :].astype(jnp.float32)
            ref[block] = value.astype(ref.dtype)


def halve(place, keep, got, axis, bits, at):
    rows, width = keep.shape
    left = sorted(bits, reverse=True)
    outer = 1 << left.index(at)
    inner = rows // (2 * outer)
    if inner % BLOCK:
        total = keep if got is None else keep + got.astype(jnp.float32)
        blocks = total.reshape(outer, 2, inner, width)
        low, high = blocks[:, 0].reshape(-1, width), blocks[:, 1].reshape(-1, width)
        mine = (place[1] // at) % 2 == 0
        return jnp.where(mine, low, high), jnp.where(mine, high, low).astype(jnp.bfloat16)
    shape = (outer, inner, width)
    if got is None:

        def body(place_ref, keep_ref, mine_ref, send_ref):
            halve_body(at, place_ref, keep_ref, None, mine_ref, send_ref)
    else:
        body = functools.partial(halve_body, at)
    mine, send = kernel_call(
        body,
        (jax.ShapeDtypeStruct(shape, jnp.float32), jax.ShapeDtypeStruct(shape, jnp.bfloat16)),
        [scalars] + [whole] * (1 if got is None else 2),
        moved=rows * width * 9,
        held=(0,),
    )(place, keep, *([] if got is None else [got]))
    return mine.reshape(-1, width), send.reshape(-1, width)


def reduce_rows(place, keep, got, axis, bits, jobs=()):
    jobs, left = list(jobs), list(bits)
    while left:
        bit = left[0]
        keep, send = halve(place, keep, got, axis, left, bit)
        left.pop(0)
        got = swap(send, axis, bit)
        if jobs:
            got = after(got, jobs.pop(0)(send))
    for job in jobs:
        got = after(got, job(got))
    return keep + got.astype(jnp.float32)


def transposed(left, right):
    return lax.dot_general(
        left, right, (((1,), (1,)), ((), ())), preferred_element_type=jnp.float32
    )


def weight_grad(left, right):
    return lax.dot_general(
        left, right, (((0,), (0,)), ((), ())), preferred_element_type=jnp.float32
    )


def per_device(
    block_in,
    weight_in,
    weight_mid,
    weight_out,
    gain_in,
    bias_in,
    gain_mid,
    bias_mid,
    gain_out,
    bias_out,
    kernel_near,
    kernel_far,
    gate_bias,
    same_video,
    video,
    stem_center,
    stem_diff,
    stem_gain,
    stem_bias,
    block_grad,
    stem_grad,
):
    groups = lax.axis_size("dp")
    assert lax.axis_size("chan") == 4
    clips = same_video.shape[0]
    rows, quarter = block_in.shape
    half = rows // 2
    narrow = weight_in.shape[1]
    width = 2 * narrow
    count = float(rows * groups)
    segs = video.shape[0]
    stem_count = float(segs * stem_grad.shape[2] * groups)
    chan = lax.axis_index("chan")
    core, y = chan % 2, chan // 2
    place = jnp.stack([chan, lax.axis_index("dp")])

    def my_rows(value, which):
        return lax.dynamic_slice_in_dim(value, which * half, half, 0)

    mine, others = my_rows(block_in, core), my_rows(block_in, 1 - core)
    pieces = [swap(others, "chan", 1), swap(mine, "chan", 2), swap(others, "chan", 3)]

    own_in, order = gather_rows(after(weight_in, mine, others), "dp")
    weights_in = [own_in, swap(own_in, "chan", 1)]
    parts_out = [weight_out[:, at * narrow : (at + 1) * narrow] for at in range(4)]
    packed = jnp.concatenate([weight_mid] + parts_out, 0)
    gathered = lax.all_gather(packed, "dp", axis=0)

    params = pack_params([gain_in, bias_in, gain_mid, bias_mid, gate_bias], kernel_near, kernel_far)
    par_own = ordered(core == 1, params, swap(params, "chan", 1), 1)
    pars = [par_own, swap(par_own, "chan", 2)]
    same = lax.dynamic_slice_in_dim(same_video, core * (clips // 2), clips // 2, 0)
    same = jnp.pad(same, ((0, 0), (0, 1)))
    gain_row, bias_row = gain_out.reshape(1, -1), bias_out.reshape(1, -1)

    outs = stem_grad.shape[1]
    pre_stem, stem_rows, stem_pick, extra = stem_front(
        place, video, stem_weight(stem_center, stem_diff), width
    )

    def both_sums(sums, crossing, jobs=()):
        own = sum_over(sums + swap(sums, "chan", 1), "dp", jobs[:3])
        oth = swap(after(own, crossing), "chan", 2)
        for job in jobs[3:]:
            oth = after(oth, job(own))
        return [own, oth]

    made = {}

    def job(name, work):
        def run(mark):
            made[name] = work(mark)
            return made[name]

        return run

    pre_in, pre_in16, sums_in, full_in = first_conv(
        order, place, block_in, pieces, weights_in, after(extra, pars)
    )
    pre_in_oth = swap(pre_in16, "chan", 2)

    def mid_rows(mark):
        own = after(gathered, mark)[:, : weight_mid.shape[0]].reshape(-1, narrow)
        return [own, swap(own, "chan", 1)]

    def out_rows(mark):
        parts, first, size = after(gathered, mark), weight_mid.shape[0], weight_out.shape[0]
        parts = [parts[:, first + at * size : first + (at + 1) * size] for at in range(4)]
        return jnp.concatenate([part.reshape(-1, narrow) for part in parts], 1)

    stats_in = both_sums(
        sums_in, pre_in_oth, [job("weights_mid", mid_rows), job("full_out", out_rows)]
    )
    weights_mid, full_out = made["weights_mid"], made["full_out"]

    out_across = swap(after(full_out, stats_in), "chan", 2)

    mixed, pre_mid, pre_mid16, sums_mid = gate_mid(
        count, place, same, pre_in, pre_in_oth, *stats_in, *pars, weights_mid
    )
    pre_mid_oth = swap(pre_mid16, "chan", 2)
    stats_stem = after(stats_in[0], sums_mid)

    def stem_half(mark):
        return stem_output(
            stem_count, place, after(pre_stem, mark), stem_grad, stats_stem, stem_gain, stem_bias, quarter
        )

    def slab_of(mark):
        slab = after(weights_mid[0], mark).reshape(9, 2, width, narrow)
        return lax.dynamic_slice_in_dim(slab, 1 - y, 1, 1).reshape(9 * width, narrow)

    stats_mid = both_sums(
        after(sums_mid, out_across),
        pre_mid_oth,
        [job("stem", stem_half), job("slab", slab_of), job("turned", lambda mark: turn(after(mixed, mark)))],
    )
    stem_out, extra = made["stem"]

    second = second_half(count, place, pre_mid, pre_mid_oth, stats_mid, pars)
    second_peer = swap(second, "chan", 1)
    pre_out, sums_out = last_conv(place, second, second_peer, full_out, extra)
    slab_across = swap(after(made["slab"], stats_mid), "chan", 2)
    stats_out = sum_over(sums_out, "dp", [
        job("near_in", lambda mark: lax.dynamic_slice_in_dim(after(full_in, mark), chan * quarter, quarter, 0)),
        job("away_in", lambda mark: lax.dynamic_slice_in_dim(after(full_in, mark), (chan ^ 2) * quarter, quarter, 0)),
    ])
    stats_out = after(stats_out, slab_across)
    out_peers = [swap(after(value, stats_out), "chan", 1) for value in (full_out, out_across)]
    weights_out = [full_out, out_peers[0], out_across, out_peers[1]]
    block_out, grad_total, sums_back, keep, send = out_back(
        count, place, pre_out, block_in, block_grad, stats_out, gain_row, bias_row, full_out
    )
    got = swap(send, "chan", 1)

    def cross(mark):
        return cross_half(place, keep, after(got, mark))

    def stem_part(chunk, start):
        def work(mark):
            return stem_back(
                stem_count, place, after(pre_stem, mark), stem_grad, stats_in[0], stats_out, stem_gain,
                stem_bias, stem_rows, stem_pick, start and made[start], chunk, 4,
            )

        return job(f"stem{chunk}", work)

    back_out = sum_over(
        sums_back, "dp", [job("cross", cross), stem_part(0, None), stem_part(1, "stem0")]
    )
    keep, send = made["cross"]
    got = swap(send, "chan", 2)
    delta = out_delta(count, rows, stats_out, sums_back, back_out, gain_row)
    deltas = [delta, swap(delta, "chan", 1)]
    deltas += [swap(value, "chan", 2) for value in deltas]

    grad_mid, grad_mid16, sums_mid_back = mid_slope(
        count, place, keep, got, second, pre_mid, stats_mid[0], pars[0], deltas, weights_out
    )
    grad_mid_oth = swap(grad_mid16, "chan", 2)

    aways_mid = [slab_across, swap(after(slab_across, sums_mid_back), "chan", 1)]

    def out_part(start, rows_of_second):
        def work(mark):
            return out_weight(
                count, place, rows_of_second, pre_out, grad_total, stats_out, after(back_out, mark),
                gain_row, start and made[start],
            )

        return work

    back_mid = both_sums(sums_mid_back, grad_mid_oth, [
        job("out0", out_part(None, second)),
        job("out1", out_part("out0", second_peer)),
        stem_part(2, "stem1"),
        stem_part(3, "stem2"),
    ])
    bits = steps_of("dp")
    sum_out = reduce_rows(place, made["out1"], None, "dp", bits)
    far_in = swap(made["away_in"], "chan", 2)

    slopes, grad_in, grad_in16, sums_in_back = mid_back(
        count, place, same, grad_mid, grad_mid_oth, pre_mid, pre_mid_oth, stats_mid, back_mid,
        pre_in, stats_in[0], pars, weights_mid, aways_mid,
    )
    grad_in_oth = swap(grad_in16, "chan", 2)

    def mid_part(mark):
        return mid_weight(place, made["turned"], after(slopes, mark))

    def mid_rest(mark):
        keep, send = made["mid"]
        return halve(place, keep, after(swap(send, "chan", 1), mark), "dp", mid_bits, mid_bits[0])

    mid_bits = bits[1:2] + bits[:1] + bits[2:]
    back_in = both_sums(sums_in_back, grad_in_oth, [job("mid", mid_part), job("mid0", mid_rest)])
    mid_got = swap(made["mid0"][1], "dp", mid_bits[0])

    grad_pre, keep, send = in_back(
        count, place, grad_in, grad_in_oth, pre_in, pre_in_oth, stats_in, back_in, pars, block_in,
        pieces,
    )
    grad_peer = swap(grad_pre, "chan", 1)
    got = swap(send, "chan", 1)

    def input_job(mark):
        near = after(made["near_in"], mark)
        return input_grad(place, grad_pre, grad_peer, near, far_in, grad_total)

    def mid_job(at):
        def work(mark):
            made["mid_keep"], send = halve(
                place, after(made["mid_keep"], mark), made["mid_got"], "dp", mid_bits[at:], mid_bits[at]
            )
            made["mid_got"] = swap(send, "dp", mid_bits[at])
            return send

        return work

    made["mid_keep"], made["mid_got"] = made["mid0"][0], mid_got
    many = [mid_job(at) for at in range(1, len(mid_bits))]

    def first_job(mark):
        made["input"] = input_job(many[0](mark))
        return made["input"]

    sum_in = reduce_rows(place, keep, got, "dp", bits, [first_job] + many[1:])
    sum_mid = made["mid_keep"] + made["mid_got"].astype(jnp.float32)
    grad_block_in = made["input"]
    stem_sum = sum_over(made["stem3"], "dp")
    center_grad, diff_grad = stem_grads(after(stem_sum, made["input"]), outs)

    def my_columns(value):
        return lax.dynamic_slice_in_dim(value, core * narrow, narrow, value.ndim - 1)

    def my_stem(value):
        row = lax.dynamic_slice(value, (2, core * 2 * outs), (1, 2 * outs))[0]
        return row[:outs], row[outs:]

    gate_grads = my_columns(back_in[0][8:])
    mid_grads, in_grads = my_columns(back_mid[0]), my_columns(back_in[0])
    stem_bias_grad, stem_gain_grad = my_stem(stats_out)
    return (
        block_out,
        stem_out,
        grad_block_in,
        sum_in,
        sum_mid,
        sum_out,
        in_grads[1],
        in_grads[0],
        mid_grads[1],
        mid_grads[0],
        back_out[1],
        back_out[0],
        gate_grads[1:10],
        gate_grads[10:19],
        gate_grads[0],
        center_grad,
        diff_grad,
        stem_gain_grad,
        stem_bias_grad,
    )


def solution(mesh):
    placed = (
        P("dp", "chan"),
        P("dp", "chan"),
        P("dp", "chan"),
        P("dp", "chan"),
        P("chan"),
        P("chan"),
        P("chan"),
        P("chan"),
        P("chan"),
        P("chan"),
        P(None, "chan"),
        P(None, "chan"),
        P("chan"),
        P("dp", None),
        P("dp", None, None),
        P(None, "chan"),
        P(None, "chan"),
        P("chan"),
        P("chan"),
        P("dp", "chan"),
        P("dp", "chan", None),
    )
    return jax.shard_map(
        per_device,
        mesh=mesh,
        in_specs=placed,
        out_specs=(
            P("dp", "chan"),
            P("dp", "chan", None),
            P("dp", "chan"),
            P("dp", "chan"),
            P("dp", "chan"),
            P("dp", "chan"),
            P("chan"),
            P("chan"),
            P("chan"),
            P("chan"),
            P("chan"),
            P("chan"),
            P(None, "chan"),
            P(None, "chan"),
            P("chan"),
            P(None, "chan"),
            P(None, "chan"),
            P("chan"),
            P("chan"),
        ),
        check_vma=False,
    )
```

time: 384 us -> 284 us (0.74)
  other arithmetic: 56.8 us -> 3.22 us
  matrix products: 53.3 us -> 0 us
  Pallas kernels: 32.3 us -> 82.3 us
  local copies, waits for them, and re-layouts: 66.2 us -> 34.4 us
  waiting for transfers between devices: 98.5 us -> 78.6 us
  starting transfers between devices: 57.3 us -> 69.5 us
    pallas_call x3 -> x32, Pallas kernels: 32.3 us -> 82.3 us  [the longest x28 75.4 us: run(): call(*[pltpu.with_memory_space_constraint(arg, pltpu.HBM) if spec is remo...]
    dot_general x12 -> x0, matrix products: 29.4 us -> none  [the longest x5 10.2 us: weight_grad(): lax.dot_general(left, right, (((0,), (0,)), ((), ())), preferred_element_...]
    ppermute x62 -> x67, waiting for transfers between devices: 98.5 us -> 78.6 us  [swap(): return lax.ppermute(value, axis, [(at, at ^ bit) for at in range(size)])]
    convert_element_type x5 -> x0, local copies, waits for them, and re-layouts: 15 us -> none  [the longest x2 13 us: per_device(): moving.reshape(segs, 3 * (FRAMES - 1), video.shape[2]).astype(jnp.bfloat16)]
    conv_general_dilated x2 -> x0, matrix products: 13.6 us -> none  [stem_conv(): lax.conv_general_dilated(field, weights, (2, 2), ((3, 3), (3, 3)), dimens...]
    unnamed x158, local copies, waits for them, and re-layouts: 6.44 us -> 19.9 us
    ppermute x62 -> x67, starting transfers between devices: 57.3 us -> 69.4 us  [swap(): return lax.ppermute(value, axis, [(at, at ^ bit) for at in range(size)])]
    concatenate x3 -> x4, local copies, waits for them, and re-layouts: 13.5 us -> 1.68 us  [the longest x1 0.72 us: per_device(): packed = jnp.concatenate([weight_mid] + parts_out, 0)]
  transfers between devices with their start and end apart: 63 -> 68, of which waited for: 31 -> 35; matrix products, arithmetic and copies ran while one was open for 44% -> 7% of each run, Pallas kernels for 6% -> 19%
where the time goes in v2:
time: 284 us; the launch traced here: 283 us
  Pallas kernels  82.3 us (29%)
  waiting for transfers between devices  78.6 us (28%)
  starting transfers between devices  69.5 us (24%)
  local copies, waits for them, and re-layouts  34.4 us (12%)
  between operations  15 us (5%)
  other arithmetic  3.22 us (1%)
    ppermute x67, waiting for transfers between devices, swap(): return lax.ppermute(value, axis, [(at, at ^ bit) for at in range(size)])  78.6 us
    pallas_call x28, Pallas kernels, run(): call(*[pltpu.with_memory_space_constraint(arg, pltpu.HBM) if spec is remo...  75.4 us
    ppermute x67, starting transfers between devices, swap(): return lax.ppermute(value, axis, [(at, at ^ bit) for at in range(size)])  69.4 us
    unnamed x158, local copies, waits for them, and re-layouts  19.9 us
    pallas_call x4, Pallas kernels, stem_back(): pl.pallas_call(functools.partial(stem_back_body, count, first), grid=(1,)...  6.9 us
  transfers between devices with their start and end apart: 68, of which 35 were waited for; matrix products, arithmetic and copies ran while one was open for 7% of the time, Pallas kernels for 19%

profile of v2, /device:TPU:0, one launch (start us, length us, event | category | flops | bytes accessed | tf_op | source)
XLA Modules:
  0.0 283.1 jit_solution(6920853391445182081)
XLA Ops:
  11.9 2.8 constant_dynamic-slice_fusion.6
  14.7 4.1 %collective-permute-start.3 = (bf16[256,128]{1,0:T(8,128)(2,1)S(1)}, bf16[256,128]{1,0:T(8,128)(2,1)S(1)}, u32[]{:S(2)}, u32[]{:S(2)}) collective-permute-start(bf16[256,128]{1,0:T(8,128)(2,1)S(1)} %copy-done.62), channel_id=1, source_target_pairs={{0,16},{4,20},{8,24},{12,28},{16,0},{20,4},{24,8},{28,12},{1,17},{... | collective-permute-start | bytes 196616 | tf_op jit(solution)/shard_map/ppermute | solution.py:1345
  18.8 3.6 %collective-permute-done.3 = bf16[256,128]{1,0:T(8,128)(2,1)S(1)} collective-permute-done((bf16[256,128]{1,0:T(8,128)(2,1)S(1)}, bf16[256,128]{1,0:T(8,128)(2,1)S(1)}, u32[]{:S(2)}, u32[]{:S(2)}) %collective-permute-start.3) | collective-permute-done | bytes 65568 | tf_op jit(solution)/shard_map/ppermute | solution.py:1345
  23.1 1.5 collective-permute-start.1
  25.3 3.7 %collective-permute-done.4 = bf16[512,128]{1,0:T(8,128)(2,1)S(1)} collective-permute-done((bf16[512,128]{1,0:T(8,128)(2,1)S(1)}, bf16[512,128]{1,0:T(8,128)(2,1)S(1)}, u32[]{:S(2)}, u32[]{:S(2)}) %collective-permute-start.4) | collective-permute-done | bytes 131104 | tf_op jit(solution)/shard_map/ppermute | solution.py:1345
  29.1 1.5 collective-permute-start.5
  32.6 2.9 %collective-permute-done.5 = bf16[1024,128]{1,0:T(8,128)(2,1)S(1)} collective-permute-done((bf16[1024,128]{1,0:T(8,128)(2,1)S(1)}, bf16[1024,128]{1,0:T(8,128)(2,1)S(1)}, u32[]{:S(2)}, u32[]{:S(2)}) %collective-permute-start.5) | collective-permute-done | bytes 262176 | tf_op jit(solution)/shard_map/ppermute | solution.py:1345
  36.4 1.5 copy.47.video_ref
  38.7 1.6 collective-permute-start.8
  41.5 7.5 %shard_map.348 = (f32[32,16,256]{2,1,0:T(8,128)}, bf16[32,112,512]{2,1,0:T(8,128)(2,1)}, bf16[7,512,256]{2,1,0:T(8,128)(2,1)}, f32[8,256]{1,0:T(8,128)S(1)}) custom-call(s32[2]{0:T(128)S(1)} %pad_add_fusion.place_ref, bf16[32,15,1024]{2,1,0:T(8,128)(2,1)S(1)} %copy-done.26, bf16[112,112]{1,0:T(8,128)(2,1)S(1)} %reshape.157.weight_ref), custom_call_target="tpu_custom_call" | custom-call | flops 1644167168 | bytes 1310720 | tf_op jit(solution)/shard_map/pallas_call | solution.py:67
  48.9 12.4 %collective-permute-done.8.par_oth_ref = f32[24,256]{1,0:T(8,128)S(1)} collective-permute-done((f32[24,256]{1,0:T(8,128)S(1)}, f32[24,256]{1,0:T(8,128)S(1)}, u32[]{:S(2)}, u32[]{:S(2)}) %collective-permute-start.8) | collective-permute-done | bytes 24608 | tf_op jit(solution)/shard_map/ppermute | solution.py:1345
  61.4 4.1 %shard_map.350 = (f32[784,256]{1,0:T(8,128)}, bf16[784,256]{1,0:T(8,128)(2,1)S(1)}, f32[8,256]{1,0:T(8,128)S(1)}, bf16[2048,256]{1,0:T(8,128)(2,1)}) custom-call(s32[2]{0:T(128)S(1)} %pad_add_fusion.place_ref, bf16[1568,512]{1,0:T(8,128)(2,1)S(1)} %copy-done.5, bf16[784,512]{1,0:T(8,128)(2,1)S(1)} %collective-permute-done.peer_ref, ...), custom_call_target="tpu_custom_call" | custom-call | flops 822083584 | bytes 3211264 | tf_op jit(solution)/shard_map/pallas_call | solution.py:67
  69.1 1.5 collective-permute-start.9
  72.1 2.2 collective-permute-done.11
  74.3 1.7 collective-permute-start.13
  78.0 3.4 %collective-permute-start.14 = (f32[8,256]{1,0:T(8,128)S(1)}, f32[8,256]{1,0:T(8,128)S(1)}, u32[]{:S(2)}, u32[]{:S(2)}) collective-permute-start(f32[8,256]{1,0:T(8,128)S(1)} %add.124), channel_id=1, source_target_pairs={{0,16},{4,20},{8,24},{12,28},{16,0},{20,4},{24,8},{28,12},{1,17},{... | collective-permute-start | bytes 24584 | tf_op jit(solution)/shard_map/ppermute | solution.py:1345
  81.4 1.6 collective-permute-done.14
  84.3 3.2 %collective-permute-done.15.stats_oth_ref = f32[8,256]{1,0:T(8,128)S(1)} collective-permute-done((f32[8,256]{1,0:T(8,128)S(1)}, f32[8,256]{1,0:T(8,128)S(1)}, u32[]{:S(2)}, u32[]{:S(2)}) %collective-permute-start.15) | collective-permute-done | bytes 8224 | tf_op jit(solution)/shard_map/ppermute | solution.py:1345
  88.2 10.6 %shard_map.351 = (bf16[1184,512]{1,0:T(8,128)(2,1)}, f32[784,256]{1,0:T(8,128)}, bf16[784,256]{1,0:T(8,128)(2,1)}, f32[8,256]{1,0:T(8,128)S(1)}) custom-call(s32[2]{0:T(128)S(1)} %pad_add_fusion.place_ref, s32[2,8]{1,0:T(2,128)S(1)} %pad.4.same_ref, f32[784,256]{1,0:T(8,128)S(1)} %copy-done.27, bf16[784,256]{1,0:T(8,128)(2,1)} %copy-done.64, ...), custom_call_target="tpu_custom_call" | custom-call | flops 1849688064 | bytes 4767744 | tf_op jit(solution)/shard_map/pallas_call | solution.py:67
  98.8 1.5 collective-permute-start.16
  103.0 1.8 shard_map.352
  106.4 2.0 constant_dynamic-slice_fusion.5
  108.8 2.9 %collective-permute-start.21 = (f32[8,256]{1,0:T(8,128)S(1)}, f32[8,256]{1,0:T(8,128)S(1)}, u32[]{:S(2)}, u32[]{:S(2)}) collective-permute-start(f32[8,256]{1,0:T(8,128)S(1)} %add.129), channel_id=1, source_target_pairs={{0,16},{4,20},{8,24},{12,28},{16,0},{20,4},{24,8},{28,12},{1,17},{... | collective-permute-start | bytes 24584 | tf_op jit(solution)/shard_map/ppermute | solution.py:1345
  111.7 1.6 shard_map.353.turned_ref
  115.0 3.1 %collective-permute-done.22.stats_oth_ref = f32[8,256]{1,0:T(8,128)S(1)} collective-permute-done((f32[8,256]{1,0:T(8,128)S(1)}, f32[8,256]{1,0:T(8,128)S(1)}, u32[]{:S(2)}, u32[]{:S(2)}) %collective-permute-start.22) | collective-permute-done | bytes 8224 | tf_op jit(solution)/shard_map/ppermute | solution.py:1345
  118.7 1.9 shard_map.354.mine_ref.second_ref.rows_ref
  121.3 1.8 collective-permute-done.23.peer_ref.rows_ref
  123.1 2.3 shard_map.355
  125.4 1.6 collective-permute-start.24
  127.7 1.5 collective-permute-done.24
  130.4 2.6 collective-permute-done.25
  133.0 1.9 collective-permute-start.26
  134.8 2.8 collective-permute-done.26
  137.7 7.7 %shard_map.356 = (bf16[1568,512]{1,0:T(8,128)(2,1)}, f32[1568,512]{1,0:T(8,128)}, f32[8,512]{1,0:T(8,128)S(1)}, f32[784,512]{1,0:T(8,128)S(1)}, bf16[784,512]{1,0:T(8,128)(2,1)S(1)}) custom-call(s32[2]{0:T(128)S(1)} %pad_add_fusion.place_ref, f32[1568,512]{1,0:T(8,128)S(1)} %get-tuple-element.154.pre_ref, bf16[1568,512]{1,0:T(8,128)(2,1)S(1)} %copy-done.5, ...), custom_call_target="tpu_custom_call" | custom-call | flops 822083584 | bytes 16056320 | tf_op jit(solution)/shard_map/pallas_call | solution.py:67
  146.0 2.1 collective-permute-done.28.got_ref
  150.9 2.2 collective-permute-done.30
  153.6 1.7 shard_map.358.start_ref
  155.3 1.6 collective-permute-done.31
  156.9 1.9 collective-permute-start.32
  158.9 1.7 shard_map.359.start_ref
  161.8 1.6 collective-permute-start.34
  167.1 3.1 %shard_map.361 = (f32[784,256]{1,0:T(8,128)S(1)}, bf16[784,256]{1,0:T(8,128)(2,1)S(1)}, f32[8,256]{1,0:T(8,128)S(1)}) custom-call(s32[2]{0:T(128)S(1)} %pad_add_fusion.place_ref, f32[784,256]{1,0:T(8,128)S(1)} %get-tuple-element.168.keep_ref, bf16[784,256]{1,0:T(8,128)(2,1)S(1)} %collective-permute-done.29.got_ref, bf16[784,512]{1,0:T(8,128)(2,1)S(1)} %copy-done.10, ...), custom_call_target="tpu_custom_call" | custom-call | flops 205520896 | bytes 4014080 | tf_op jit(solution)/shard_map/pallas_call | solution.py:67
  172.6 1.5 collective-permute-start.40
  176.7 2.0 shard_map.363.keep_ref
  180.0 1.9 collective-permute-start.42
  181.9 1.7 shard_map.364.start_ref
  185.6 1.7 shard_map.365
  189.1 12.4 %shard_map.366 = (bf16[3,1184,256]{2,1,0:T(8,128)(2,1)S(1)}, f32[784,256]{1,0:T(8,128)S(1)}, bf16[784,256]{1,0:T(8,128)(2,1)}, f32[32,256]{1,0:T(8,128)S(1)}) custom-call(s32[2]{0:T(128)S(1)} %pad_add_fusion.place_ref, s32[2,8]{1,0:T(2,128)S(1)} %copy-done.51, f32[784,256]{1,0:T(8,128)S(1)} %get-tuple-element.179.d_own_ref, bf16[784,256]{1,0:T(8,128)(2,1)} %copy-done.72, ...), custom_call_target="tpu_custom_call" | custom-call | flops 1849688064 | bytes 7553024 | tf_op jit(solution)/shard_map/pallas_call | solution.py:67
  203.7 4.8 %shard_map.367 = (f32[4608,128]{1,0:T(8,128)S(1)}, bf16[4608,128]{1,0:T(8,128)(2,1)}) custom-call(s32[2]{0:T(128)S(1)} %pad_add_fusion.place_ref, bf16[512,1152]{1,0:T(8,128)(2,1)S(1)} %copy-done.24, bf16[3,1184,256]{2,1,0:T(8,128)(2,1)S(1)} %get-tuple-element.197.slopes_ref), custom_call_target="tpu_custom_call" | custom-call | flops 2717908992 | bytes 6488064 | tf_op jit(solution)/shard_map/pallas_call | solution.py:67
  212.5 2.4 collective-permute-done.47
  217.3 1.6 collective-permute-start.61
  218.9 1.7 copy-done.21
  220.6 1.6 shard_map.368
  222.2 1.9 collective-permute-start.50
  224.2 2.9 %collective-permute-done.50 = f32[32,256]{1,0:T(8,128)S(1)} collective-permute-done((f32[32,256]{1,0:T(8,128)S(1)}, f32[32,256]{1,0:T(8,128)S(1)}, u32[]{:S(2)}, u32[]{:S(2)}) %collective-permute-start.50) | collective-permute-done | bytes 32800 | tf_op jit(solution)/shard_map/ppermute | solution.py:1345
  230.3 1.6 collective-permute-start.62
  233.1 4.0 %shard_map.369 = (bf16[784,512]{1,0:T(8,128)(2,1)S(1)}, f32[2048,128]{1,0:T(8,128)S(1)}, bf16[2048,128]{1,0:T(8,128)(2,1)S(1)}) custom-call(s32[2]{0:T(128)S(1)} %pad_add_fusion.place_ref, f32[784,256]{1,0:T(8,128)S(1)} %copy-done.30, bf16[784,256]{1,0:T(8,128)(2,1)} %collective-permute-done.45.d_oth_ref, f32[784,256]{1,0:T(8,128)S(1)} %copy-done.28, ...), custom_call_target="tpu_custom_call" | custom-call | flops 822083584 | bytes 3211264 | tf_op jit(solution)/shard_map/pallas_call | solution.py:67
  238.3 1.6 collective-permute-start.65
  239.9 7.3 %collective-permute-done.65 = f32[56,256]{1,0:T(8,128)S(1)} collective-permute-done((f32[56,256]{1,0:T(8,128)S(1)}, f32[56,256]{1,0:T(8,128)S(1)}, u32[]{:S(2)}, u32[]{:S(2)}) %collective-permute-start.65) | collective-permute-done | bytes 57376 | tf_op jit(solution)/shard_map/ppermute | solution.py:1345
  247.2 2.1 collective-permute-start.66
  258.7 2.7 shard_map.372
  262.1 1.7 collective-permute-start.57
  264.4 2.5 collective-permute-start.60
  272.9 2.6 collective-permute-done.59
  (323 shorter events, 79.2 us)
Async XLA Ops:
  7.2 60.2 %all-gather.3.cloned.1.call-start = ((), (), s32[]{:S(2)}) async-start(), calls=%async_computation | async-start | bytes 1916928 | tf_op jit(solution)/shard_map/all_gather | solution.py:1493
  14.7 7.8 %collective-permute-start.3 = (bf16[256,128]{1,0:T(8,128)(2,1)S(1)}, bf16[256,128]{1,0:T(8,128)(2,1)S(1)}, u32[]{:S(2)}, u32[]{:S(2)}) collective-permute-start(bf16[256,128]{1,0:T(8,128)(2,1)S(1)} %copy-done.62), channel_id=1, source_target_pairs={{0,16},{4,20},{8,24},{12,28},{16,0},{20,4},{24,8},{28,12},{1,17},{... | collective-permute-start | bytes 196616 | tf_op jit(solution)/shard_map/ppermute | solution.py:1345
  22.4 6.6 %collective-permute-start.4 = (bf16[512,128]{1,0:T(8,128)(2,1)S(1)}, bf16[512,128]{1,0:T(8,128)(2,1)S(1)}, u32[]{:S(2)}, u32[]{:S(2)}) collective-permute-start(bf16[512,128]{1,0:T(8,128)(2,1)S(1)} %pad_maximum_fusion.2), channel_id=1, source_target_pairs={{0,8},{4,12},{8,0},{12,4},{16,24},{20,28},{24,16},{28,20},{1,9},{5... | collective-permute-start | bytes 393224 | tf_op jit(solution)/shard_map/ppermute | solution.py:1345
  23.1 38.3 %collective-permute-start = (bf16[784,512]{1,0:T(8,128)(2,1)}, bf16[784,512]{1,0:T(8,128)(2,1)S(1)}, u32[]{:S(2)}, u32[]{:S(2)}) collective-permute-start(bf16[784,512]{1,0:T(8,128)(2,1)} %get-tuple-element.276), channel_id=1, source_target_pairs={{0,1},{1,0},{2,3},{3,2},{4,5},{5,4},{6,7},{7,6},{8,9},{9,8},{10,11... | collective-permute-start | bytes 2408456 | tf_op jit(solution)/shard_map/ppermute | solution.py:1345
  23.1 38.3 %collective-permute-start.1 = (bf16[784,512]{1,0:T(8,128)(2,1)}, bf16[784,512]{1,0:T(8,128)(2,1)S(1)}, u32[]{:S(2)}, u32[]{:S(2)}) collective-permute-start(bf16[784,512]{1,0:T(8,128)(2,1)} %get-tuple-element.275), channel_id=1, source_target_pairs={{0,2},{1,3},{2,0},{3,1},{4,6},{5,7},{6,4},{7,5},{8,10},{9,11},{10,... | collective-permute-start | bytes 2408456 | tf_op jit(solution)/shard_map/ppermute | solution.py:1345
  24.6 36.8 %collective-permute-start.2 = (bf16[784,512]{1,0:T(8,128)(2,1)}, bf16[784,512]{1,0:T(8,128)(2,1)}, u32[]{:S(2)}, u32[]{:S(2)}) collective-permute-start(bf16[784,512]{1,0:T(8,128)(2,1)} %get-tuple-element.276), channel_id=1, source_target_pairs={{0,3},{1,2},{2,1},{3,0},{4,7},{5,6},{6,5},{7,4},{8,11},{9,10},{10,... | collective-permute-start | bytes 2408456 | tf_op jit(solution)/shard_map/ppermute | solution.py:1345
  25.0 13.6 %collective-permute-start.7 = (f32[24,128]{1,0:T(8,128)S(1)}, f32[24,128]{1,0:T(8,128)S(1)}, u32[]{:S(2)}, u32[]{:S(2)}) collective-permute-start(f32[24,128]{1,0:T(8,128)S(1)} %shard_map.349), channel_id=1, source_target_pairs={{0,1},{1,0},{2,3},{3,2},{4,5},{5,4},{6,7},{7,6},{8,9},{9,8},{10,11... | collective-permute-start | bytes 36872 | tf_op jit(solution)/shard_map/ppermute | solution.py:1345
  29.1 6.4 %collective-permute-start.5 = (bf16[1024,128]{1,0:T(8,128)(2,1)S(1)}, bf16[1024,128]{1,0:T(8,128)(2,1)S(1)}, u32[]{:S(2)}, u32[]{:S(2)}) collective-permute-start(bf16[1024,128]{1,0:T(8,128)(2,1)S(1)} %pad_maximum_fusion.1), channel_id=1, source_target_pairs={{0,4},{4,0},{8,12},{12,8},{16,20},{20,16},{24,28},{28,24},{1,5},{5... | collective-permute-start | bytes 786440 | tf_op jit(solution)/shard_map/ppermute | solution.py:1345
  36.3 25.1 %collective-permute-start.6 = (bf16[2048,128]{1,0:T(8,128)(2,1)}, bf16[2048,128]{1,0:T(8,128)(2,1)}, u32[]{:S(2)}, u32[]{:S(2)}) collective-permute-start(bf16[2048,128]{1,0:T(8,128)(2,1)} %constant_dynamic-update-slice_fusion.own_ref), channel_id=1, source_target_pairs={{0,1},{1,0},{2,3},{3,2},{4,5},{5,4},{6,7},{7,6},{8,9},{9,8},{10,11... | collective-permute-start | bytes 1572872 | tf_op jit(solution)/shard_map/ppermute | solution.py:1345
  38.7 22.7 %collective-permute-start.8 = (f32[24,256]{1,0:T(8,128)S(1)}, f32[24,256]{1,0:T(8,128)S(1)}, u32[]{:S(2)}, u32[]{:S(2)}) collective-permute-start(f32[24,256]{1,0:T(8,128)S(1)} %maximum_select_fusion.par_own_ref.par_ref), channel_id=1, source_target_pairs={{0,2},{1,3},{2,0},{3,1},{4,6},{5,7},{6,4},{7,5},{8,10},{9,11},{10,... | collective-permute-start | bytes 73736 | tf_op jit(solution)/shard_map/ppermute | solution.py:1345
  68.8 5.4 %collective-permute-start.12 = (bf16[4608,128]{1,0:T(8,128)(2,1)S(1)}, bf16[4608,128]{1,0:T(8,128)(2,1)S(1)}, u32[]{:S(2)}, u32[]{:S(2)}) collective-permute-start(bf16[4608,128]{1,0:T(8,128)(2,1)S(1)} %bitcast.94), channel_id=1, source_target_pairs={{0,1},{1,0},{2,3},{3,2},{4,5},{5,4},{6,7},{7,6},{8,9},{9,8},{10,11... | collective-permute-start | bytes 3538952 | tf_op jit(solution)/shard_map/ppermute | solution.py:1345
  69.1 13.9 %collective-permute-start.9 = (bf16[784,256]{1,0:T(8,128)(2,1)S(1)}, bf16[784,256]{1,0:T(8,128)(2,1)S(1)}, u32[]{:S(2)}, u32[]{:S(2)}) collective-permute-start(bf16[784,256]{1,0:T(8,128)(2,1)S(1)} %copy-done.58), channel_id=1, source_target_pairs={{0,2},{1,3},{2,0},{3,1},{4,6},{5,7},{6,4},{7,5},{8,10},{9,11},{10,... | collective-permute-start | bytes 1204232 | tf_op jit(solution)/shard_map/ppermute | solution.py:1345
  70.6 3.7 %collective-permute-start.11 = (f32[8,256]{1,0:T(8,128)S(1)}, f32[8,256]{1,0:T(8,128)S(1)}, u32[]{:S(2)}, u32[]{:S(2)}) collective-permute-start(f32[8,256]{1,0:T(8,128)S(1)} %add.122), channel_id=1, source_target_pairs={{0,4},{4,0},{8,12},{12,8},{16,20},{20,16},{24,28},{28,24},{1,5},{5... | collective-permute-start | bytes 24584 | tf_op jit(solution)/shard_map/ppermute | solution.py:1345
  74.3 3.7 %collective-permute-start.13 = (f32[8,256]{1,0:T(8,128)S(1)}, f32[8,256]{1,0:T(8,128)S(1)}, u32[]{:S(2)}, u32[]{:S(2)}) collective-permute-start(f32[8,256]{1,0:T(8,128)S(1)} %add.123), channel_id=1, source_target_pairs={{0,8},{4,12},{8,0},{12,4},{16,24},{20,28},{24,16},{28,20},{1,9},{5... | collective-permute-start | bytes 24584 | tf_op jit(solution)/shard_map/ppermute | solution.py:1345
  78.0 5.0 %collective-permute-start.14 = (f32[8,256]{1,0:T(8,128)S(1)}, f32[8,256]{1,0:T(8,128)S(1)}, u32[]{:S(2)}, u32[]{:S(2)}) collective-permute-start(f32[8,256]{1,0:T(8,128)S(1)} %add.124), channel_id=1, source_target_pairs={{0,16},{4,20},{8,24},{12,28},{16,0},{20,4},{24,8},{28,12},{1,17},{... | collective-permute-start | bytes 24584 | tf_op jit(solution)/shard_map/ppermute | solution.py:1345
  83.8 3.7 %collective-permute-start.15 = (f32[8,256]{1,0:T(8,128)S(1)}, f32[8,256]{1,0:T(8,128)S(1)}, u32[]{:S(2)}, u32[]{:S(2)}) collective-permute-start(f32[8,256]{1,0:T(8,128)S(1)} %add.125.stats_own_ref.stats_ref.stats_in_ref), channel_id=1, source_target_pairs={{0,2},{1,3},{2,0},{3,1},{4,6},{5,7},{6,4},{7,5},{8,10},{9,11},{10,... | collective-permute-start | bytes 24584 | tf_op jit(solution)/shard_map/ppermute | solution.py:1345
  87.5 12.8 %collective-permute-start.17 = (bf16[512,512]{1,0:T(8,128)(2,1)}, bf16[512,512]{1,0:T(8,128)(2,1)}, u32[]{:S(2)}, u32[]{:S(2)}) collective-permute-start(bf16[512,512]{1,0:T(8,128)(2,1)} %pad_maximum_fusion.weight_ref.weights0_ref), channel_id=1, source_target_pairs={{0,2},{1,3},{2,0},{3,1},{4,6},{5,7},{6,4},{7,5},{8,10},{9,11},{10,... | collective-permute-start | bytes 1572872 | tf_op jit(solution)/shard_map/ppermute | solution.py:1345
  98.8 15.6 %collective-permute-start.16 = (bf16[784,256]{1,0:T(8,128)(2,1)}, bf16[784,256]{1,0:T(8,128)(2,1)S(1)}, u32[]{:S(2)}, u32[]{:S(2)}) collective-permute-start(bf16[784,256]{1,0:T(8,128)(2,1)} %get-tuple-element.138), channel_id=1, source_target_pairs={{0,2},{1,3},{2,0},{3,1},{4,6},{5,7},{6,4},{7,5},{8,10},{9,11},{10,... | collective-permute-start | bytes 1204232 | tf_op jit(solution)/shard_map/ppermute | solution.py:1345
  101.5 3.7 %collective-permute-start.19 = (f32[8,256]{1,0:T(8,128)S(1)}, f32[8,256]{1,0:T(8,128)S(1)}, u32[]{:S(2)}, u32[]{:S(2)}) collective-permute-start(f32[8,256]{1,0:T(8,128)S(1)} %add.126), channel_id=1, source_target_pairs={{0,4},{4,0},{8,12},{12,8},{16,20},{20,16},{24,28},{28,24},{1,5},{5... | collective-permute-start | bytes 24584 | tf_op jit(solution)/shard_map/ppermute | solution.py:1345
  105.1 3.7 %collective-permute-start.20 = (f32[8,256]{1,0:T(8,128)S(1)}, f32[8,256]{1,0:T(8,128)S(1)}, u32[]{:S(2)}, u32[]{:S(2)}) collective-permute-start(f32[8,256]{1,0:T(8,128)S(1)} %add.127), channel_id=1, source_target_pairs={{0,8},{4,12},{8,0},{12,4},{16,24},{20,28},{24,16},{28,20},{1,9},{5... | collective-permute-start | bytes 24584 | tf_op jit(solution)/shard_map/ppermute | solution.py:1345
  108.8 5.6 %collective-permute-start.21 = (f32[8,256]{1,0:T(8,128)S(1)}, f32[8,256]{1,0:T(8,128)S(1)}, u32[]{:S(2)}, u32[]{:S(2)}) collective-permute-start(f32[8,256]{1,0:T(8,128)S(1)} %add.129), channel_id=1, source_target_pairs={{0,16},{4,20},{8,24},{12,28},{16,0},{20,4},{24,8},{28,12},{1,17},{... | collective-permute-start | bytes 24584 | tf_op jit(solution)/shard_map/ppermute | solution.py:1345
  114.4 3.7 %collective-permute-start.22 = (f32[8,256]{1,0:T(8,128)S(1)}, f32[8,256]{1,0:T(8,128)S(1)}, u32[]{:S(2)}, u32[]{:S(2)}) collective-permute-start(f32[8,256]{1,0:T(8,128)S(1)} %add.130.stats_own_ref.stats_ref), channel_id=1, source_target_pairs={{0,2},{1,3},{2,0},{3,1},{4,6},{5,7},{6,4},{7,5},{8,10},{9,11},{10,... | collective-permute-start | bytes 24584 | tf_op jit(solution)/shard_map/ppermute | solution.py:1345
  120.6 2.5 collective-permute-start.23
  120.7 16.9 %collective-permute-start.27 = (bf16[2304,128]{1,0:T(8,128)(2,1)}, bf16[2304,128]{1,0:T(8,128)(2,1)}, u32[]{:S(2)}, u32[]{:S(2)}) collective-permute-start(bf16[2304,128]{1,0:T(8,128)(2,1)} %bitcast.17), channel_id=1, source_target_pairs={{0,2},{1,3},{2,0},{3,1},{4,6},{5,7},{6,4},{7,5},{8,10},{9,11},{10,... | collective-permute-start | bytes 1769480 | tf_op jit(solution)/shard_map/ppermute | solution.py:1345
  125.4 3.8 %collective-permute-start.24 = (f32[8,512]{1,0:T(8,128)S(1)}, f32[8,512]{1,0:T(8,128)S(1)}, u32[]{:S(2)}, u32[]{:S(2)}) collective-permute-start(f32[8,512]{1,0:T(8,128)S(1)} %get-tuple-element.155), channel_id=1, source_target_pairs={{0,4},{4,0},{8,12},{12,8},{16,20},{20,16},{24,28},{28,24},{1,5},{5... | collective-permute-start | bytes 49160 | tf_op jit(solution)/shard_map/ppermute | solution.py:1345
  129.2 3.7 %collective-permute-start.25 = (f32[8,512]{1,0:T(8,128)S(1)}, f32[8,512]{1,0:T(8,128)S(1)}, u32[]{:S(2)}, u32[]{:S(2)}) collective-permute-start(f32[8,512]{1,0:T(8,128)S(1)} %add.132), channel_id=1, source_target_pairs={{0,8},{4,12},{8,0},{12,4},{16,24},{20,28},{24,16},{28,20},{1,9},{5... | collective-permute-start | bytes 49160 | tf_op jit(solution)/shard_map/ppermute | solution.py:1345
  133.0 4.6 %collective-permute-start.26 = (f32[8,512]{1,0:T(8,128)S(1)}, f32[8,512]{1,0:T(8,128)S(1)}, u32[]{:S(2)}, u32[]{:S(2)}) collective-permute-start(f32[8,512]{1,0:T(8,128)S(1)} %add.134), channel_id=1, source_target_pairs={{0,16},{4,20},{8,24},{12,28},{16,0},{20,4},{24,8},{28,12},{1,17},{... | collective-permute-start | bytes 49160 | tf_op jit(solution)/shard_map/ppermute | solution.py:1345
  145.4 2.7 collective-permute-start.28
  145.5 19.0 %collective-permute-start.36 = (bf16[512,512]{1,0:T(8,128)(2,1)}, bf16[512,512]{1,0:T(8,128)(2,1)S(1)}, u32[]{:S(2)}, u32[]{:S(2)}) collective-permute-start(bf16[512,512]{1,0:T(8,128)(2,1)} %pad_maximum_fusion.weight_ref.weights0_ref), channel_id=1, source_target_pairs={{0,1},{1,0},{2,3},{3,2},{4,5},{5,4},{6,7},{7,6},{8,9},{9,8},{10,11... | collective-permute-start | bytes 1572872 | tf_op jit(solution)/shard_map/ppermute | solution.py:1345
  146.0 18.5 %collective-permute-start.37 = (bf16[512,512]{1,0:T(8,128)(2,1)}, bf16[512,512]{1,0:T(8,128)(2,1)S(1)}, u32[]{:S(2)}, u32[]{:S(2)}) collective-permute-start(bf16[512,512]{1,0:T(8,128)(2,1)} %collective-permute-done.17.weights2_ref), channel_id=1, source_target_pairs={{0,1},{1,0},{2,3},{3,2},{4,5},{5,4},{6,7},{7,6},{8,9},{9,8},{10,11... | collective-permute-start | bytes 1572872 | tf_op jit(solution)/shard_map/ppermute | solution.py:1345
  148.8 18.2 %collective-permute-start.29 = (bf16[784,256]{1,0:T(8,128)(2,1)S(1)}, bf16[784,256]{1,0:T(8,128)(2,1)S(1)}, u32[]{:S(2)}, u32[]{:S(2)}) collective-permute-start(bf16[784,256]{1,0:T(8,128)(2,1)S(1)} %get-tuple-element.169), channel_id=1, source_target_pairs={{0,2},{1,3},{2,0},{3,1},{4,6},{5,7},{6,4},{7,5},{8,10},{9,11},{10,... | collective-permute-start | bytes 1204232 | tf_op jit(solution)/shard_map/ppermute | solution.py:1345
  149.4 3.7 %collective-permute-start.30 = (f32[8,512]{1,0:T(8,128)S(1)}, f32[8,512]{1,0:T(8,128)S(1)}, u32[]{:S(2)}, u32[]{:S(2)}) collective-permute-start(f32[8,512]{1,0:T(8,128)S(1)} %get-tuple-element.166.sums_ref), channel_id=1, source_target_pairs={{0,4},{4,0},{8,12},{12,8},{16,20},{20,16},{24,28},{28,24},{1,5},{5... | collective-permute-start | bytes 49160 | tf_op jit(solution)/shard_map/ppermute | solution.py:1345
  153.2 3.7 %collective-permute-start.31 = (f32[8,512]{1,0:T(8,128)S(1)}, f32[8,512]{1,0:T(8,128)S(1)}, u32[]{:S(2)}, u32[]{:S(2)}) collective-permute-start(f32[8,512]{1,0:T(8,128)S(1)} %add.136), channel_id=1, source_target_pairs={{0,8},{4,12},{8,0},{12,4},{16,24},{20,28},{24,16},{28,20},{1,9},{5... | collective-permute-start | bytes 49160 | tf_op jit(solution)/shard_map/ppermute | solution.py:1345
  156.9 4.7 %collective-permute-start.32 = (f32[8,512]{1,0:T(8,128)S(1)}, f32[8,512]{1,0:T(8,128)S(1)}, u32[]{:S(2)}, u32[]{:S(2)}) collective-permute-start(f32[8,512]{1,0:T(8,128)S(1)} %add.137), channel_id=1, source_target_pairs={{0,16},{4,20},{8,24},{12,28},{16,0},{20,4},{24,8},{28,12},{1,17},{... | collective-permute-start | bytes 49160 | tf_op jit(solution)/shard_map/ppermute | solution.py:1345
  161.7 1.6 collective-permute-start.33
  161.8 3.8 %collective-permute-start.34 = (f32[8,512]{1,0:T(8,128)S(1)}, f32[8,512]{1,0:T(8,128)S(1)}, u32[]{:S(2)}, u32[]{:S(2)}) collective-permute-start(f32[8,512]{1,0:T(8,128)S(1)} %shard_map.360.deltas0_ref), channel_id=1, source_target_pairs={{0,2},{1,3},{2,0},{3,1},{4,6},{5,7},{6,4},{7,5},{8,10},{9,11},{10,... | collective-permute-start | bytes 49160 | tf_op jit(solution)/shard_map/ppermute | solution.py:1345
  163.3 3.7 %collective-permute-start.35 = (f32[8,512]{1,0:T(8,128)S(1)}, f32[8,512]{1,0:T(8,128)S(1)}, u32[]{:S(2)}, u32[]{:S(2)}) collective-permute-start(f32[8,512]{1,0:T(8,128)S(1)} %collective-permute-done.33.deltas1_ref), channel_id=1, source_target_pairs={{0,2},{1,3},{2,0},{3,1},{4,6},{5,7},{6,4},{7,5},{8,10},{9,11},{10,... | collective-permute-start | bytes 49160 | tf_op jit(solution)/shard_map/ppermute | solution.py:1345
  170.2 18.1 %collective-permute-start.44 = (bf16[2304,128]{1,0:T(8,128)(2,1)}, bf16[2304,128]{1,0:T(8,128)(2,1)S(1)}, u32[]{:S(2)}, u32[]{:S(2)}) collective-permute-start(bf16[2304,128]{1,0:T(8,128)(2,1)} %collective-permute-done.27.away_own_ref), channel_id=1, source_target_pairs={{0,1},{1,0},{2,3},{3,2},{4,5},{5,4},{6,7},{7,6},{8,9},{9,8},{10,11... | collective-permute-start | bytes 1769480 | tf_op jit(solution)/shard_map/ppermute | solution.py:1345
  170.3 14.3 %collective-permute-start.38 = (bf16[784,256]{1,0:T(8,128)(2,1)S(1)}, bf16[784,256]{1,0:T(8,128)(2,1)S(1)}, u32[]{:S(2)}, u32[]{:S(2)}) collective-permute-start(bf16[784,256]{1,0:T(8,128)(2,1)S(1)} %get-tuple-element.180), channel_id=1, source_target_pairs={{0,2},{1,3},{2,0},{3,1},{4,6},{5,7},{6,4},{7,5},{8,10},{9,11},{10,... | collective-permute-start | bytes 1204232 | tf_op jit(solution)/shard_map/ppermute | solution.py:1345
  172.6 3.7 %collective-permute-start.40 = (f32[8,256]{1,0:T(8,128)S(1)}, f32[8,256]{1,0:T(8,128)S(1)}, u32[]{:S(2)}, u32[]{:S(2)}) collective-permute-start(f32[8,256]{1,0:T(8,128)S(1)} %add.139), channel_id=1, source_target_pairs={{0,4},{4,0},{8,12},{12,8},{16,20},{20,16},{24,28},{28,24},{1,5},{5... | collective-permute-start | bytes 24584 | tf_op jit(solution)/shard_map/ppermute | solution.py:1345
  176.3 3.7 %collective-permute-start.41 = (f32[8,256]{1,0:T(8,128)S(1)}, f32[8,256]{1,0:T(8,128)S(1)}, u32[]{:S(2)}, u32[]{:S(2)}) collective-permute-start(f32[8,256]{1,0:T(8,128)S(1)} %add.140), channel_id=1, source_target_pairs={{0,8},{4,12},{8,0},{12,4},{16,24},{20,28},{24,16},{28,20},{1,9},{5... | collective-permute-start | bytes 24584 | tf_op jit(solution)/shard_map/ppermute | solution.py:1345
  180.0 4.6 %collective-permute-start.42 = (f32[8,256]{1,0:T(8,128)S(1)}, f32[8,256]{1,0:T(8,128)S(1)}, u32[]{:S(2)}, u32[]{:S(2)}) collective-permute-start(f32[8,256]{1,0:T(8,128)S(1)} %add.141), channel_id=1, source_target_pairs={{0,16},{4,20},{8,24},{12,28},{16,0},{20,4},{24,8},{28,12},{1,17},{... | collective-permute-start | bytes 24584 | tf_op jit(solution)/shard_map/ppermute | solution.py:1345
  184.6 3.7 %collective-permute-start.43 = (f32[8,256]{1,0:T(8,128)S(1)}, f32[8,256]{1,0:T(8,128)S(1)}, u32[]{:S(2)}, u32[]{:S(2)}) collective-permute-start(f32[8,256]{1,0:T(8,128)S(1)} %add.142.back_own_ref), channel_id=1, source_target_pairs={{0,2},{1,3},{2,0},{3,1},{4,6},{5,7},{6,4},{7,5},{8,10},{9,11},{10,... | collective-permute-start | bytes 24584 | tf_op jit(solution)/shard_map/ppermute | solution.py:1345
  210.0 8.9 %collective-permute-start.49 = (bf16[4608,128]{1,0:T(8,128)(2,1)}, bf16[4608,128]{1,0:T(8,128)(2,1)}, u32[]{:S(2)}, u32[]{:S(2)}) collective-permute-start(bf16[4608,128]{1,0:T(8,128)(2,1)} %get-tuple-element.199), channel_id=1, source_target_pairs={{0,1},{1,0},{2,3},{3,2},{4,5},{5,4},{6,7},{7,6},{8,9},{9,8},{10,11... | collective-permute-start | bytes 3538952 | tf_op jit(solution)/shard_map/ppermute | solution.py:1345
  210.1 17.0 %collective-permute-start.45 = (bf16[784,256]{1,0:T(8,128)(2,1)}, bf16[784,256]{1,0:T(8,128)(2,1)}, u32[]{:S(2)}, u32[]{:S(2)}) collective-permute-start(bf16[784,256]{1,0:T(8,128)(2,1)} %get-tuple-element.194), channel_id=1, source_target_pairs={{0,2},{1,3},{2,0},{3,1},{4,6},{5,7},{6,4},{7,5},{8,10},{9,11},{10,... | collective-permute-start | bytes 1204232 | tf_op jit(solution)/shard_map/ppermute | solution.py:1345
  211.0 3.9 %collective-permute-start.47 = (f32[32,256]{1,0:T(8,128)S(1)}, f32[32,256]{1,0:T(8,128)S(1)}, u32[]{:S(2)}, u32[]{:S(2)}) collective-permute-start(f32[32,256]{1,0:T(8,128)S(1)} %add.143), channel_id=1, source_target_pairs={{0,4},{4,0},{8,12},{12,8},{16,20},{20,16},{24,28},{28,24},{1,5},{5... | collective-permute-start | bytes 98312 | tf_op jit(solution)/shard_map/ppermute | solution.py:1345
  215.0 7.2 %collective-permute-start.48 = (f32[32,256]{1,0:T(8,128)S(1)}, f32[32,256]{1,0:T(8,128)S(1)}, u32[]{:S(2)}, u32[]{:S(2)}) collective-permute-start(f32[32,256]{1,0:T(8,128)S(1)} %add.144), channel_id=1, source_target_pairs={{0,8},{4,12},{8,0},{12,4},{16,24},{20,28},{24,16},{28,20},{1,9},{5... | collective-permute-start | bytes 98312 | tf_op jit(solution)/shard_map/ppermute | solution.py:1345
  217.3 12.4 %collective-permute-start.61 = (bf16[256,512]{1,0:T(8,128)(2,1)S(1)}, bf16[256,512]{1,0:T(8,128)(2,1)S(1)}, u32[]{:S(2)}, u32[]{:S(2)}) collective-permute-start(bf16[256,512]{1,0:T(8,128)(2,1)S(1)} %bitcast.87), channel_id=1, source_target_pairs={{0,4},{4,0},{8,12},{12,8},{16,20},{20,16},{24,28},{28,24},{1,5},{5... | collective-permute-start | bytes 786440 | tf_op jit(solution)/shard_map/ppermute | solution.py:1345
  222.2 4.9 %collective-permute-start.50 = (f32[32,256]{1,0:T(8,128)S(1)}, f32[32,256]{1,0:T(8,128)S(1)}, u32[]{:S(2)}, u32[]{:S(2)}) collective-permute-start(f32[32,256]{1,0:T(8,128)S(1)} %add.145), channel_id=1, source_target_pairs={{0,16},{4,20},{8,24},{12,28},{16,0},{20,4},{24,8},{28,12},{1,17},{... | collective-permute-start | bytes 98312 | tf_op jit(solution)/shard_map/ppermute | solution.py:1345
  227.1 5.3 %collective-permute-start.51 = (f32[32,256]{1,0:T(8,128)S(1)}, f32[32,256]{1,0:T(8,128)S(1)}, u32[]{:S(2)}, u32[]{:S(2)}) collective-permute-start(f32[32,256]{1,0:T(8,128)S(1)} %add.146.back_own_ref), channel_id=1, source_target_pairs={{0,2},{1,3},{2,0},{3,1},{4,6},{5,7},{6,4},{7,5},{8,10},{9,11},{10,... | collective-permute-start | bytes 98312 | tf_op jit(solution)/shard_map/ppermute | solution.py:1345
  228.8 9.4 %collective-permute-start.64 = (f32[56,256]{1,0:T(8,128)S(1)}, f32[56,256]{1,0:T(8,128)S(1)}, u32[]{:S(2)}, u32[]{:S(2)}) collective-permute-start(f32[56,256]{1,0:T(8,128)S(1)} %copy-done.32), channel_id=1, source_target_pairs={{0,4},{4,0},{8,12},{12,8},{16,20},{20,16},{24,28},{28,24},{1,5},{5... | collective-permute-start | bytes 172040 | tf_op jit(solution)/shard_map/ppermute | solution.py:1345
  230.3 19.0 %collective-permute-start.62 = (bf16[128,512]{1,0:T(8,128)(2,1)S(1)}, bf16[128,512]{1,0:T(8,128)(2,1)S(1)}, u32[]{:S(2)}, u32[]{:S(2)}) collective-permute-start(bf16[128,512]{1,0:T(8,128)(2,1)S(1)} %bitcast.90), channel_id=1, source_target_pairs={{0,8},{4,12},{8,0},{12,4},{16,24},{20,28},{24,16},{28,20},{1,9},{5... | collective-permute-start | bytes 393224 | tf_op jit(solution)/shard_map/ppermute | solution.py:1345
  231.9 23.4 %collective-permute-start.54 = (bf16[2304,128]{1,0:T(8,128)(2,1)S(1)}, bf16[2304,128]{1,0:T(8,128)(2,1)S(1)}, u32[]{:S(2)}, u32[]{:S(2)}) collective-permute-start(bf16[2304,128]{1,0:T(8,128)(2,1)S(1)} %bitcast.85), channel_id=1, source_target_pairs={{0,8},{4,12},{8,0},{12,4},{16,24},{20,28},{24,16},{28,20},{1,9},{5... | collective-permute-start | bytes 1769480 | tf_op jit(solution)/shard_map/ppermute | solution.py:1345
  237.1 21.6 %collective-permute-start.52 = (bf16[784,512]{1,0:T(8,128)(2,1)S(1)}, bf16[784,512]{1,0:T(8,128)(2,1)S(1)}, u32[]{:S(2)}, u32[]{:S(2)}) collective-permute-start(bf16[784,512]{1,0:T(8,128)(2,1)S(1)} %get-tuple-element.206.mine_ref), channel_id=1, source_target_pairs={{0,1},{1,0},{2,3},{3,2},{4,5},{5,4},{6,7},{7,6},{8,9},{9,8},{10,11... | collective-permute-start | bytes 2408456 | tf_op jit(solution)/shard_map/ppermute | solution.py:1345
  237.2 16.1 %collective-permute-start.53 = (bf16[2048,128]{1,0:T(8,128)(2,1)S(1)}, bf16[2048,128]{1,0:T(8,128)(2,1)S(1)}, u32[]{:S(2)}, u32[]{:S(2)}) collective-permute-start(bf16[2048,128]{1,0:T(8,128)(2,1)S(1)} %get-tuple-element.208), channel_id=1, source_target_pairs={{0,1},{1,0},{2,3},{3,2},{4,5},{5,4},{6,7},{7,6},{8,9},{9,8},{10,11... | collective-permute-start | bytes 1572872 | tf_op jit(solution)/shard_map/ppermute | solution.py:1345
  238.3 8.9 %collective-permute-start.65 = (f32[56,256]{1,0:T(8,128)S(1)}, f32[56,256]{1,0:T(8,128)S(1)}, u32[]{:S(2)}, u32[]{:S(2)}) collective-permute-start(f32[56,256]{1,0:T(8,128)S(1)} %add.151), channel_id=1, source_target_pairs={{0,8},{4,12},{8,0},{12,4},{16,24},{20,28},{24,16},{28,20},{1,9},{5... | collective-permute-start | bytes 172040 | tf_op jit(solution)/shard_map/ppermute | solution.py:1345
  247.2 5.1 %collective-permute-start.66 = (f32[56,256]{1,0:T(8,128)S(1)}, f32[56,256]{1,0:T(8,128)S(1)}, u32[]{:S(2)}, u32[]{:S(2)}) collective-permute-start(f32[56,256]{1,0:T(8,128)S(1)} %add.152), channel_id=1, source_target_pairs={{0,16},{4,20},{8,24},{12,28},{16,0},{20,4},{24,8},{28,12},{1,17},{... | collective-permute-start | bytes 172040 | tf_op jit(solution)/shard_map/ppermute | solution.py:1345
  249.8 6.9 %collective-permute-start.63 = (bf16[64,512]{1,0:T(8,128)(2,1)S(1)}, bf16[64,512]{1,0:T(8,128)(2,1)S(1)}, u32[]{:S(2)}, u32[]{:S(2)}) collective-permute-start(bf16[64,512]{1,0:T(8,128)(2,1)S(1)} %bitcast.92), channel_id=1, source_target_pairs={{0,16},{4,20},{8,24},{12,28},{16,0},{20,4},{24,8},{28,12},{1,17},{... | collective-permute-start | bytes 196616 | tf_op jit(solution)/shard_map/ppermute | solution.py:1345
  252.3 6.4 %collective-permute-start.55 = (bf16[512,256]{1,0:T(8,128)(2,1)S(1)}, bf16[512,256]{1,0:T(8,128)(2,1)S(1)}, u32[]{:S(2)}, u32[]{:S(2)}) collective-permute-start(bf16[512,256]{1,0:T(8,128)(2,1)S(1)} %copy-done.66), channel_id=1, source_target_pairs={{0,2},{1,3},{2,0},{3,1},{4,6},{5,7},{6,4},{7,5},{8,10},{9,11},{10,... | collective-permute-start | bytes 786440 | tf_op jit(solution)/shard_map/ppermute | solution.py:1345
  253.9 7.5 %collective-permute-start.56 = (bf16[1024,128]{1,0:T(8,128)(2,1)S(1)}, bf16[1024,128]{1,0:T(8,128)(2,1)S(1)}, u32[]{:S(2)}, u32[]{:S(2)}) collective-permute-start(bf16[1024,128]{1,0:T(8,128)(2,1)S(1)} %bitcast.88), channel_id=1, source_target_pairs={{0,4},{4,0},{8,12},{12,8},{16,20},{20,16},{24,28},{28,24},{1,5},{5... | collective-permute-start | bytes 786440 | tf_op jit(solution)/shard_map/ppermute | solution.py:1345
  256.0 7.8 %collective-permute-start.58 = (bf16[1152,128]{1,0:T(8,128)(2,1)S(1)}, bf16[1152,128]{1,0:T(8,128)(2,1)S(1)}, u32[]{:S(2)}, u32[]{:S(2)}) collective-permute-start(bf16[1152,128]{1,0:T(8,128)(2,1)S(1)} %bitcast.86), channel_id=1, source_target_pairs={{0,4},{4,0},{8,12},{12,8},{16,20},{20,16},{24,28},{28,24},{1,5},{5... | collective-permute-start | bytes 884744 | tf_op jit(solution)/shard_map/ppermute | solution.py:1345
  262.1 7.7 %collective-permute-start.57 = (bf16[512,128]{1,0:T(8,128)(2,1)S(1)}, bf16[512,128]{1,0:T(8,128)(2,1)S(1)}, u32[]{:S(2)}, u32[]{:S(2)}) collective-permute-start(bf16[512,128]{1,0:T(8,128)(2,1)S(1)} %bitcast.91), channel_id=1, source_target_pairs={{0,8},{4,12},{8,0},{12,4},{16,24},{20,28},{24,16},{28,20},{1,9},{5... | collective-permute-start | bytes 393224 | tf_op jit(solution)/shard_map/ppermute | solution.py:1345
  264.4 7.7 %collective-permute-start.60 = (bf16[576,128]{1,0:T(8,128)(2,1)S(1)}, bf16[576,128]{1,0:T(8,128)(2,1)S(1)}, u32[]{:S(2)}, u32[]{:S(2)}) collective-permute-start(bf16[576,128]{1,0:T(8,128)(2,1)S(1)} %bitcast.89), channel_id=1, source_target_pairs={{0,16},{4,20},{8,24},{12,28},{16,0},{20,4},{24,8},{28,12},{1,17},{... | collective-permute-start | bytes 442376 | tf_op jit(solution)/shard_map/ppermute | solution.py:1345
  270.3 5.2 %collective-permute-start.59 = (bf16[256,128]{1,0:T(8,128)(2,1)S(1)}, bf16[256,128]{1,0:T(8,128)(2,1)S(1)}, u32[]{:S(2)}, u32[]{:S(2)}) collective-permute-start(bf16[256,128]{1,0:T(8,128)(2,1)S(1)} %bitcast.93), channel_id=1, source_target_pairs={{0,16},{4,20},{8,24},{12,28},{16,0},{20,4},{24,8},{28,12},{1,17},{... | collective-permute-start | bytes 196616 | tf_op jit(solution)/shard_map/ppermute | solution.py:1345
  (78 other events, 787.0 us)
Sparse Core Ops, SparseCore 0:
  11.9 49.0 all-gather.2

commit v3 on v2

--- a/solution.py
+++ b/solution.py
@@ -16,6 +16,7 @@
 
 eps = 1e-05
 vmem_limit = 24 * 1024 * 1024
+flops_per_us = 0.3e9
 
 whole = pl.BlockSpec(memory_space=pltpu.VMEM)
 remote = pl.BlockSpec(memory_space=pltpu.HBM)
@@ -43,7 +44,7 @@
     return copy
 
 
-def kernel_call(body, out_shape, in_specs, scratch=(), flops=0, moved=0, away=(), held=()):
+def kernel_call(body, out_shape, in_specs, scratch=(), lasts=1.0, away=(), held=()):
     several = isinstance(out_shape, tuple)
     shapes = list(out_shape) if several else [out_shape]
     specs = [remote if at in away else whole for at in range(len(shapes))]
@@ -60,7 +61,9 @@
         out_specs=tuple(specs) if several else specs[0],
         scratch_shapes=list(scratch),
         compiler_params=pltpu.CompilerParams(vmem_limit_bytes=vmem_limit),
-        cost_estimate=pl.CostEstimate(flops=flops, bytes_accessed=moved, transcendentals=0),
+        cost_estimate=pl.CostEstimate(
+            flops=int(lasts * flops_per_us), bytes_accessed=0, transcendentals=0
+        ),
     )
 
     def run(*args):
@@ -130,13 +133,17 @@
             yield step, row, [kernel[row * 3 + col] for col in range(3)]
 
 
+def views_of(value, place):
+    return {step: across(value, step, place) for step in (-2, -1, 0, 1, 2)}
+
+
 def gate_score(change, near, far, offset, place):
-    views = {step: across(change, step, place) for step in (-2, -1, 0, 1, 2)}
+    views = views_of(change, place)
     score = jnp.broadcast_to(offset, change.shape)
     for step, row, kernel in taps_of(near, far):
         term = sum(kernel[col] * views[step * (col - 1)] for col in range(3))
         score = score + down(term, step * (row - 1))
-    return score, views
+    return score
 
 
 def conv_chunk(parts, weights, first, rows, sign):
@@ -175,15 +182,101 @@
     sums_ref[1:2, :] = second
 
 
+def fetch_blocks(sources, core, target_ref, sems, first):
+    moves = []
+    for side, source in enumerate(sources):
+        lanes = lane_part(core if side == 0 else 1 - core)
+        blocks = source.shape[0]
+        size = target_ref.shape[0] // blocks
+        for block in range(blocks):
+            here = pl.ds(block * size, size)
+            moves.append(
+                move(
+                    source.at[block, pl.ds(0, size)],
+                    target_ref.at[here, lanes],
+                    sems,
+                    first + side * blocks + block,
+                )
+            )
+    return moves
+
+
+def gate_half(count, same_ref, pre, stats, par, hidden_ref, mixed_ref, first, gates_ref=None):
+    rows, width = pre.shape
+    hidden_ref[pl.ds(rows, hidden_ref.shape[0] - rows), :] = jnp.zeros(
+        (hidden_ref.shape[0] - rows, width), jnp.float32
+    )
+    center, rate = norm_stats(*rows_of(stats), count)
+    scaled = (pre[...].astype(jnp.float32) - center) * rate
+    normed = scaled * par[0:1] + par[1:2]
+    hidden_ref[pl.ds(0, rows), :] = normed * logistic(normed)
+    at = lane_mask(128)
+
+    def lanes_step(chunk, _):
+        lanes = lane_part(chunk)
+        target = pl.ds(pl.multiple_of(first + chunk * 128, 128), 128)
+        near = [par[5 + tap : 6 + tap, lanes].reshape(1, 1, 128) for tap in range(9)]
+        far = [par[14 + tap : 15 + tap, lanes].reshape(1, 1, 128) for tap in range(9)]
+        offset = par[4:5, lanes].reshape(1, 1, 128)
+
+        def clip_step(clip, _):
+            view = clip_view(hidden_ref, clip, 56)
+            for pair in range(PAIRS):
+                maps = [load_map(view, PIXELS * (2 * pair + seg), lanes) for seg in range(3)]
+                results = []
+                for seg in range(2):
+                    same = same_ref[clip, 2 * pair + seg].astype(jnp.float32)
+                    change = jnp.where(at < SIDE, same * (maps[seg + 1] - maps[seg]), 0.0)
+                    gate = logistic(gate_score(change, near, far, offset, at))
+                    results.append(jnp.where(at < SIDE, maps[seg] * (1.0 + gate), 0.0))
+                    if gates_ref is not None:
+                        gates_ref[SEG * clip + 2 * pair + seg, :, :, lanes] = gate
+                place = pl.ds(pair_row(clip, pair), SIDE * BLOCK)
+                mixed_ref[place, target] = two_maps(*results).astype(jnp.bfloat16)
+            return 0
+
+        return lax.fori_loop(0, rows // CLIP, clip_step, 0)
+
+    lax.fori_loop(0, width // 128, lanes_step, 0)
+
+
+def gate_own_body(
+    count, same_ref, own_ref, stats_ref, par_ref, mixed_out_ref, gates_out_ref, hidden_ref, mixed_ref, gates_ref,
+    sems,
+):
+    mixed_ref[...] = jnp.zeros_like(mixed_ref)
+    gate_half(count, same_ref, own_ref, stats_ref, par_ref, hidden_ref, mixed_ref, 0, gates_ref)
+    moves = [move(mixed_ref, mixed_out_ref, sems, 0), move(gates_ref, gates_out_ref, sems, 1)]
+    for copy in moves:
+        copy.wait()
+
+
+def gate_own(count, same, own, stats, par):
+    rows, width = own.shape
+    shape = (map_rows(rows), width)
+    gates = (rows // PIXELS, SIDE, 8, width)
+    return kernel_call(
+        functools.partial(gate_own_body, count),
+        (jax.ShapeDtypeStruct(shape, jnp.bfloat16), jax.ShapeDtypeStruct(gates, jnp.float32)),
+        [scalars, whole, whole, whole],
+        (
+            pltpu.VMEM((rows + 56, width), jnp.float32),
+            pltpu.VMEM(shape, jnp.bfloat16),
+            pltpu.VMEM(gates, jnp.float32),
+            pltpu.SemaphoreType.DMA((2,)),
+        ),
+        away=(0, 1),
+        lasts=3.9,
+    )(same, own, stats, par)
+
+
 def gate_mid_body(
     count,
     place_ref,
     same_ref,
     own_ref,
     oth_ref,
-    stats_own_ref,
     stats_oth_ref,
-    par_own_ref,
     par_oth_ref,
     weight_own_ref,
     weight_peer_ref,
@@ -192,7 +285,6 @@
     mid16_ref,
     sums_ref,
     hidden_ref,
-    par_ref,
     acc_ref,
     weight_ref,
     oth_here_ref,
@@ -200,68 +292,26 @@
     mixed_ref,
     sems,
 ):
-    rows, width = own_ref.shape
+    rows, width = oth_ref.shape
     clips = rows // CLIP
     core, y = place_ref[0] % 2, place_ref[0] // 2
     arrivals = [
         move(stats_oth_ref, stats_here_ref, sems, 0),
         move(oth_ref, oth_here_ref, sems, 1),
     ]
-    weight_moves = [
-        move(weight_own_ref, weight_ref.at[:, lane_part(core)], sems, 2),
-        move(weight_peer_ref, weight_ref.at[:, lane_part(1 - core)], sems, 3),
-    ]
-    mixed_ref[...] = jnp.zeros_like(mixed_ref)
-    hidden_ref[pl.ds(rows, hidden_ref.shape[0] - rows), :] = jnp.zeros(
-        (hidden_ref.shape[0] - rows, 2 * width), jnp.float32
-    )
-    for side, (pre, stats, par) in enumerate(
-        (
-            (own_ref, stats_own_ref, par_own_ref),
-            (oth_here_ref, stats_here_ref, par_oth_ref),
-        )
-    ):
-        place = pl.multiple_of(width * (y if side == 0 else 1 - y), width)
-        if side:
-            for copy in arrivals:
-                copy.wait()
-        center, rate = norm_stats(*rows_of(stats), count)
-        scaled = (pre[...].astype(jnp.float32) - center) * rate
-        normed = scaled * par[0:1] + par[1:2]
-        hidden_ref[pl.ds(0, rows), pl.ds(place, width)] = normed * logistic(normed)
-        par_ref[:, pl.ds(place, width)] = par[...]
-    at = lane_mask(128)
-
-    def lanes_step(chunk, _):
-        lanes = pl.ds(pl.multiple_of(chunk * 128, 128), 128)
-        near = [par_ref[5 + tap : 6 + tap, lanes].reshape(1, 1, 128) for tap in range(9)]
-        far = [par_ref[14 + tap : 15 + tap, lanes].reshape(1, 1, 128) for tap in range(9)]
-        offset = par_ref[4:5, lanes].reshape(1, 1, 128)
-
-        def clip_step(clip, _):
-            view = clip_view(hidden_ref, clip, 56)
-            for pair in range(PAIRS):
-                maps = [
-                    load_map(view, PIXELS * (2 * pair + seg), lanes) for seg in range(3)
-                ]
-                results = []
-                for seg in range(2):
-                    same = same_ref[clip, 2 * pair + seg].astype(jnp.float32)
-                    change = jnp.where(at < SIDE, same * (maps[seg + 1] - maps[seg]), 0.0)
-                    score, _ = gate_score(change, near, far, offset, at)
-                    mixed = maps[seg] * (1.0 + logistic(score))
-                    results.append(jnp.where(at < SIDE, mixed, 0.0))
-                place = pl.ds(pair_row(clip, pair), SIDE * BLOCK)
-                mixed_ref[place, lanes] = two_maps(*results).astype(jnp.bfloat16)
-            return 0
-
-        return lax.fori_loop(0, clips, clip_step, 0)
-
-    lax.fori_loop(0, 2 * width // 128, lanes_step, 0)
+    weight_moves = [move(own_ref, mixed_ref.at[:, lane_part(y, width)], sems, 2)]
+    weight_moves += fetch_blocks((weight_own_ref, weight_peer_ref), core, weight_ref, sems, 5)
+    mixed_ref[:, lane_part(1 - y, width)] = jnp.zeros((mixed_ref.shape[0], width), jnp.bfloat16)
+    for copy in arrivals:
+        copy.wait()
+    gate_half(
+        count, same_ref, oth_here_ref, stats_here_ref, par_oth_ref, hidden_ref, mixed_ref,
+        pl.multiple_of((1 - y) * width, width),
+    )
     depth = 2 * width
-    mixed_move = move(mixed_ref, mixed_out_ref, sems, 4)
     for copy in weight_moves:
         copy.wait()
+    mixed_move = move(mixed_ref, mixed_out_ref, sems, 3)
 
     def tap_dot(left, tap):
         return jnp.dot(
@@ -278,7 +328,7 @@
         return 0
 
     lax.fori_loop(0, clips, conv_step, 0)
-    mid_move = move(acc_ref.at[pl.ds(0, rows)], mid_ref, sems, 5)
+    mid_move = move(acc_ref.at[pl.ds(0, rows)], mid_ref, sems, 4)
     result = acc_ref[pl.ds(0, rows), :]
     mid16_ref[...] = result.astype(jnp.bfloat16)
     put_sums(
@@ -292,10 +342,10 @@
     return (rows // (2 * PIXELS) * SPAN + 2) * BLOCK
 
 
-def gate_mid(count, place, same, own, oth, stats_own, stats_oth, par_own, par_oth, weights):
-    rows, width = own.shape
+def gate_mid(count, place, same, own, oth, stats_oth, par_oth, weights):
+    rows, width = oth.shape
     spread = map_rows(rows)
-    depth = weights[0].shape[0]
+    depth = 18 * width
     return kernel_call(
         functools.partial(gate_mid_body, count),
         (
@@ -304,36 +354,87 @@
             jax.ShapeDtypeStruct((rows, width), jnp.bfloat16),
             jax.ShapeDtypeStruct((8, width), jnp.float32),
         ),
-        [scalars, scalars, whole, remote, whole, remote, whole, whole, remote, remote],
+        [scalars, scalars, remote, remote, remote, whole, remote, remote],
         (
-            pltpu.VMEM((rows + 56, 2 * width), jnp.float32),
-            pltpu.VMEM((24, 2 * width), jnp.float32),
+            pltpu.VMEM((rows + 56, width), jnp.float32),
             pltpu.VMEM((rows + 8, width), jnp.float32),
             pltpu.VMEM((depth, width), jnp.bfloat16),
-            pltpu.VMEM((rows, width), jnp.bfloat16),
+            pltpu.VMEM((rows, width), oth.dtype),
             pltpu.VMEM((8, width), jnp.float32),
             pltpu.VMEM((spread, 2 * width), jnp.bfloat16),
-            pltpu.SemaphoreType.DMA((6,)),
+            pltpu.SemaphoreType.DMA((5 + 2 * weights[0].shape[0],)),
         ),
         away=(0, 1),
-        flops=2 * rows * depth * width,
-        moved=depth * width * 2 + rows * width * 12,
-    )(place, same, own, oth, stats_own, stats_oth, par_own, par_oth, *weights)
+        lasts=8.0,
+    )(place, same, own, oth, stats_oth, par_oth, *weights)
+
+
+def mid_slopes(count, grad, pre, stats, back, par, flat_ref, store):
+    rows, width = grad.shape
+    flat_ref[pl.ds(rows, flat_ref.shape[0] - rows), :] = jnp.zeros(
+        (flat_ref.shape[0] - rows, width), jnp.float32
+    )
+    center, rate = norm_stats(*rows_of(stats), count)
+    scaled = (pre[...].astype(jnp.float32) - center) * rate
+    flat_ref[pl.ds(0, rows), :] = (par[2:3] * rate) * (
+        grad[...].astype(jnp.float32) - back[0:1] / count - scaled * (back[1:2] / count)
+    )
+    at = lane_mask(width)
+
+    def clip_step(clip, _):
+        view = clip_view(flat_ref, clip, 8)
+        for pair in range(PAIRS):
+            maps = [
+                jnp.where(at < SIDE, load_map(view, PIXELS * (2 * pair + seg), slice(None)), 0.0)
+                for seg in range(2)
+            ]
+            store(pl.ds(pair_row(clip, pair), SIDE * BLOCK), maps, at)
+        return 0
+
+    lax.fori_loop(0, rows // CLIP, clip_step, 0)
+
+
+def mid_own_body(count, d_ref, mid_ref, stats_ref, back_ref, par_ref, slopes_ref, flat_ref, mid_here_ref, sems):
+    arrival = move(mid_ref, mid_here_ref, sems, 0)
+    slopes_ref[...] = jnp.zeros_like(slopes_ref)
+
+    def store(place, maps, at):
+        for col in range(3):
+            slopes_ref[col, place, :] = two_maps(
+                *[across(value, 1 - col, at) for value in maps]
+            ).astype(jnp.bfloat16)
+
+    arrival.wait()
+    mid_slopes(count, d_ref, mid_here_ref, stats_ref, back_ref, par_ref, flat_ref, store)
+
+
+def mid_own(count, d_own, mid, stats, back, par):
+    rows, width = d_own.shape
+    return kernel_call(
+        functools.partial(mid_own_body, count),
+        jax.ShapeDtypeStruct((3, map_rows(rows), width), jnp.bfloat16),
+        [whole, remote, whole, whole, whole],
+        (
+            pltpu.VMEM((rows + 56, width), jnp.float32),
+            pltpu.VMEM((rows, width), jnp.float32),
+            pltpu.SemaphoreType.DMA((1,)),
+        ),
+        held=(0,),
+        lasts=1.7,
+    )(d_own, mid, stats, back, par)
 
 
 def mid_back_body(
     count,
     place_ref,
     same_ref,
-    d_own_ref,
+    slopes_ref,
     d_oth_ref,
-    mid_own_ref,
     mid_oth_ref,
-    stats_own_ref,
     stats_oth_ref,
-    back_own_ref,
     back_oth_ref,
     pre_ref,
+    gates_ref,
     stats_in_ref,
     par_own_ref,
     par_oth_ref,
@@ -341,8 +442,7 @@
     weight_peer_ref,
     away_own_ref,
     away_peer_ref,
-    slopes_ref,
-    d_in_ref,
+    d_in_out_ref,
     d_in16_ref,
     sums_ref,
     flat_ref,
@@ -356,9 +456,10 @@
     mid_here_ref,
     back_here_ref,
     pre_here_ref,
+    gates_here_ref,
     sems,
 ):
-    rows, width = d_own_ref.shape
+    rows, width = d_oth_ref.shape
     clips = rows // CLIP
     core, y = place_ref[0] % 2, place_ref[0] // 2
     arrivals = [
@@ -366,58 +467,23 @@
         move(d_oth_ref, d_here_ref, sems, 1),
         move(mid_oth_ref, mid_here_ref, sems, 2),
     ]
-    weight_moves = [
-        move(weight_own_ref, weight_ref.at[:, lane_part(core)], sems, 3),
-        move(weight_peer_ref, weight_ref.at[:, lane_part(1 - core)], sems, 4),
-        move(away_own_ref, weight_oth_ref.at[:, lane_part(core)], sems, 5),
-        move(away_peer_ref, weight_oth_ref.at[:, lane_part(1 - core)], sems, 6),
+    weight_moves = fetch_blocks((weight_own_ref, weight_peer_ref), core, weight_ref, sems, 10)
+    weight_moves += [
+        move(away_own_ref, weight_oth_ref.at[:, lane_part(core)], sems, 3),
+        move(away_peer_ref, weight_oth_ref.at[:, lane_part(1 - core)], sems, 4),
     ]
-    pre_move = move(pre_ref, pre_here_ref, sems, 7)
-    everything = slice(None)
-    slopes_ref[...] = jnp.zeros_like(slopes_ref)
+    pre_moves = [
+        move(pre_ref, pre_here_ref, sems, 7),
+        move(gates_ref, gates_here_ref, sems, 9),
+    ]
     oth_ref[...] = jnp.zeros_like(oth_ref)
-    flat_ref[pl.ds(rows, flat_ref.shape[0] - rows), :] = jnp.zeros(
-        (flat_ref.shape[0] - rows, width), jnp.float32
-    )
-    at_wide = lane_mask(width)
-    for side, (grad, pre, stats, back, par) in enumerate(
-        (
-            (d_own_ref, mid_own_ref, stats_own_ref, back_own_ref, par_own_ref),
-            (d_here_ref, mid_here_ref, stats_oth_ref, back_here_ref, par_oth_ref),
-        )
-    ):
-        if side:
-            for copy in arrivals:
-                copy.wait()
-        center, rate = norm_stats(*rows_of(stats), count)
-        scaled = (pre[...].astype(jnp.float32) - center) * rate
-        flat_ref[pl.ds(0, rows), :] = (par[2:3] * rate) * (
-            grad[...].astype(jnp.float32)
-            - back[0:1] / count
-            - scaled * (back[1:2] / count)
-        )
-
-        def spread_step(clip, _, side=side):
-            view = clip_view(flat_ref, clip, 8)
-            for pair in range(PAIRS):
-                maps = [
-                    jnp.where(
-                        at_wide < SIDE, load_map(view, PIXELS * (2 * pair + seg), everything), 0.0
-                    )
-                    for seg in range(2)
-                ]
-                place = pl.ds(pair_row(clip, pair), SIDE * BLOCK)
-                if side:
-                    oth_ref[place, :] = two_maps(*maps).astype(jnp.bfloat16)
-                else:
-                    for col in range(3):
-                        slopes_ref[col, place, :] = two_maps(
-                            *[across(value, 1 - col, at_wide) for value in maps]
-                        ).astype(jnp.bfloat16)
-            return 0
-
-        lax.fori_loop(0, clips, spread_step, 0)
-
+
+    def store(place, maps, _):
+        oth_ref[place, :] = two_maps(*maps).astype(jnp.bfloat16)
+
+    for copy in arrivals:
+        copy.wait()
+    mid_slopes(count, d_here_ref, mid_here_ref, stats_oth_ref, back_here_ref, par_oth_ref, flat_ref, store)
     depth = 2 * width
     turned = (((1,), (1,)), ((), ()))
     for copy in weight_moves:
@@ -446,7 +512,8 @@
     lax.fori_loop(0, clips, conv_step, 0)
 
     center, rate = norm_stats(*rows_of(stats_in_ref), count)
-    pre_move.wait()
+    for copy in pre_moves:
+        copy.wait()
     scaled_ref[pl.ds(0, rows), :] = (pre_here_ref[...] - center) * rate
     scaled_ref[pl.ds(rows, scaled_ref.shape[0] - rows), :] = jnp.zeros(
         (scaled_ref.shape[0] - rows, width), jnp.float32
@@ -462,7 +529,7 @@
 
         near = [row_of(5 + tap) for tap in range(9)]
         far = [row_of(14 + tap) for tap in range(9)]
-        offset, gain, bias = row_of(4), row_of(0), row_of(1)
+        gain, bias = row_of(0), row_of(1)
 
         def add_part(index, value):
             here = pl.ds(8 * index, 8)
@@ -484,8 +551,8 @@
             for seg in range(2):
                 same = same_ref[clip, 2 * pair + seg].astype(jnp.float32)
                 change = jnp.where(at < SIDE, same * (hidden[seg + 1] - hidden[seg]), 0.0)
-                score, views = gate_score(change, near, far, offset, at)
-                gate = logistic(score)
+                views = views_of(change, at)
+                gate = gates_here_ref[SEG * clip + 2 * pair + seg, :, :, lanes]
                 start = 2 * (SPAN * (PAIRS * clip + pair) + 1) + seg
                 d_mixed = jnp.stack([dmix_ref[start + 2 * row, :, lanes] for row in range(SIDE)])
                 d_mixed = jnp.where(at < SIDE, d_mixed, 0.0)
@@ -496,7 +563,8 @@
                 for index, (step, row, kernel) in enumerate(taps_of(near, far)):
                     here = down(d_score, -step * (row - 1))
                     for col in range(3):
-                        add_part(1 + 3 * index + col, here * views[step * (col - 1)])
+                        if index != 4 or col != 1:
+                            add_part(1 + 3 * index + col, here * views[step * (col - 1)])
                     term = sum(kernel[col] * backs[-step * (col - 1)] for col in range(3))
                     term = down(term, -step * (row - 1))
                     d_change = term if d_change is None else d_change + term
@@ -511,32 +579,33 @@
         return 0
 
     lax.fori_loop(0, width // 128, lanes_step, 0)
+    d_in_move = move(flat_ref.at[pl.ds(0, rows)], d_in_out_ref, sems, 8)
     result = flat_ref[pl.ds(0, rows), :]
-    d_in_ref[...] = result
     d_in16_ref[...] = result.astype(jnp.bfloat16)
     put_sums(
         sums_ref,
         jnp.sum(result, 0, keepdims=True),
         jnp.sum(result * scaled_ref[pl.ds(0, rows), :], 0, keepdims=True),
     )
+    parts_ref[pl.ds(8 * 14, 8), :] = parts_ref[pl.ds(8 * 5, 8), :]
     sums_ref[8:32, :] = jnp.sum(parts_ref[...].reshape(24, 8, width), 1)
+    d_in_move.wait()
 
 
 def mid_back(
-    count, place, same, d_own, d_oth, mid_own, mid_oth, stats, back, pre, stats_in, pars, weights, aways,
+    count, place, same, slopes, d_oth, mid_oth, stats_oth, back_oth, pre, gates, stats_in, pars, weights, aways
 ):
-    rows, width = d_own.shape
+    rows, width = d_oth.shape
     spread = map_rows(rows)
-    depth = weights[0].shape[0]
+    depth = 18 * width
     return kernel_call(
         functools.partial(mid_back_body, count),
         (
-            jax.ShapeDtypeStruct((3, spread, width), jnp.bfloat16),
             jax.ShapeDtypeStruct((rows, width), jnp.float32),
             jax.ShapeDtypeStruct((rows, width), jnp.bfloat16),
             jax.ShapeDtypeStruct((32, width), jnp.float32),
         ),
-        [scalars, scalars, whole, remote, whole, remote, whole, whole, whole, remote, remote]
+        [scalars, scalars, whole, remote, remote, whole, remote, remote, remote]
         + [whole] * 3
         + [remote] * 4,
         (
@@ -551,13 +620,14 @@
             pltpu.VMEM((rows, width), jnp.bfloat16),
             pltpu.VMEM((8, width), jnp.float32),
             pltpu.VMEM((rows, width), jnp.float32),
-            pltpu.SemaphoreType.DMA((8,)),
-        ),
-        flops=2 * rows * depth * width,
-        moved=depth * width * 3 + rows * width * 20,
-        held=(0, 1),
+            pltpu.VMEM(gates.shape, jnp.float32),
+            pltpu.SemaphoreType.DMA((10 + 2 * weights[0].shape[0],)),
+        ),
+        away=(0,),
+        lasts=11.5,
     )(
-        place, same, d_own, d_oth, mid_own, mid_oth, *stats, *back, pre, stats_in, *pars, *weights, *aways,
+        place, same, slopes, d_oth, mid_oth, stats_oth, back_oth, pre, gates, stats_in, *pars, *weights,
+        *aways,
     )
 
 
@@ -574,36 +644,45 @@
         [remote],
         (pltpu.VMEM(mixed.shape, jnp.bfloat16), pltpu.SemaphoreType.DMA((1,))),
         held=(0,),
+        lasts=1.6,
     )(mixed)
 
 
-def mid_weight_body(place_ref, turned_ref, slopes_ref, keep_ref, send_ref):
+def mid_weight_body(place_ref, turned_ref, slopes_ref, keep_ref, early_ref, late_ref, keep_here_ref, sems):
     depth, rows = turned_ref.shape
     half = keep_ref.shape[1]
+    cut = early_ref.shape[0]
     first = place_ref[0] % 2 == 0
+    moves = []
     for tap in range(9):
         row, col = tap // 3, tap % 3
         right = slopes_ref[col, pl.ds(BLOCK * (2 - row), rows), :]
         value = jnp.dot(turned_ref[...], right, preferred_element_type=jnp.float32)
         low, high = value[:, :half], value[:, half:]
         here = pl.ds(tap * depth, depth)
-        keep_ref[here, :] = jnp.where(first, low, high)
-        send_ref[here, :] = jnp.where(first, high, low).astype(jnp.bfloat16)
+        keep_here_ref[here, :] = jnp.where(first, low, high)
+        moves.append(move(keep_here_ref.at[here], keep_ref.at[here], sems, tap))
+        send = jnp.where(first, high, low).astype(jnp.bfloat16)
+        middle = min(max(cut - tap * depth, 0), depth)
+        if middle > 0:
+            early_ref[tap * depth : tap * depth + middle] = send[:middle]
+        if middle < depth:
+            late_ref[tap * depth + middle - cut : (tap + 1) * depth - cut] = send[middle:]
+    for copy in moves:
+        copy.wait()
 
 
 def mid_weight(place, turned, slopes):
     depth, rows = turned.shape
     width = slopes.shape[2]
+    part = jax.ShapeDtypeStruct((9 * depth // 2, width // 2), jnp.bfloat16)
     return kernel_call(
         mid_weight_body,
-        (
-            jax.ShapeDtypeStruct((9 * depth, width // 2), jnp.float32),
-            jax.ShapeDtypeStruct((9 * depth, width // 2), jnp.bfloat16),
-        ),
+        (jax.ShapeDtypeStruct((9 * depth, width // 2), jnp.float32), part, part),
         [scalars, whole, whole],
-        flops=2 * rows * 9 * depth * width,
-        moved=rows * (2 * depth + 6 * width) + 9 * depth * width * 3,
-        held=(0,),
+        (pltpu.VMEM((9 * depth, width // 2), jnp.float32), pltpu.SemaphoreType.DMA((9,))),
+        away=(0,),
+        lasts=4.8,
     )(place, turned, slopes)
 
 
@@ -618,7 +697,6 @@
     other_ref,
     extra_ref,
     pre_out_ref,
-    pre16_ref,
     sums_ref,
     weight_out_ref,
     pre_ref,
@@ -643,7 +721,6 @@
         total = term if total is None else total + term
     pre_ref[...] = total
     pre_move = move(pre_ref, pre_out_ref, sems, 1)
-    pre16_ref[...] = total.astype(jnp.bfloat16)
     sums_ref[...] = extra_ref[...]
     sums_ref[0:1, :] = jnp.sum(total, 0, keepdims=True)
     sums_ref[1:2, :] = jnp.sum(total * total, 0, keepdims=True)
@@ -658,7 +735,6 @@
         functools.partial(first_conv_body, order),
         (
             jax.ShapeDtypeStruct((rows, width), jnp.float32),
-            jax.ShapeDtypeStruct((rows, width), jnp.bfloat16),
             jax.ShapeDtypeStruct((8, width), jnp.float32),
             jax.ShapeDtypeStruct((4 * quarter, width), jnp.bfloat16),
         ),
@@ -668,9 +744,8 @@
             pltpu.VMEM((4 * quarter, width), jnp.bfloat16),
             pltpu.SemaphoreType.DMA((2,)),
         ),
-        flops=8 * rows * quarter * width,
-        moved=rows * quarter * 8,
-        away=(0, 3),
+        away=(0, 2),
+        lasts=4.0,
     )(place, block, *pieces, *weights, extra)
 
 
@@ -707,7 +782,7 @@
             pltpu.VMEM((8, width), jnp.float32),
             pltpu.SemaphoreType.DMA((2,)),
         ),
-        moved=rows * width * 10,
+        lasts=1.9,
     )(place, own, oth, *stats, *pars)
 
 
@@ -735,8 +810,7 @@
             jax.ShapeDtypeStruct((8, width), jnp.float32),
         ),
         [scalars] + [whole] * 4,
-        flops=4 * rows * depth * width,
-        moved=rows * width * 12,
+        lasts=2.3,
     )(place, mine, peer, weight, extra)
 
 
@@ -813,9 +887,8 @@
         ),
         [scalars] + [whole] * 7,
         (pltpu.VMEM((rows, width), jnp.float32), pltpu.SemaphoreType.DMA((1,))),
-        flops=2 * rows * width * depth,
-        moved=rows * width * 20,
         away=(1,),
+        lasts=7.5,
     )(place, pre, block, grad, stats, gain, bias, weight)
 
 
@@ -837,7 +910,7 @@
             jax.ShapeDtypeStruct((rows, width), jnp.bfloat16),
         ),
         [scalars, whole, whole],
-        moved=rows * width * 18,
+        lasts=0.7,
     )(place, keep, got)
 
 
@@ -892,13 +965,17 @@
         left = (weights[...].astype(jnp.float32) * deltas[1:2]).astype(jnp.bfloat16)
         term = lax.dot_general(left, own, turned, preferred_element_type=jnp.float32)
         factor = term if factor is None else factor + term
+        high = deltas[0:1].astype(jnp.bfloat16).astype(jnp.float32)
+        both = jnp.concatenate([high, deltas[0:1] - high, jnp.zeros_like(deltas[2:8])])
         term = lax.dot_general(
-            deltas[...], own.astype(jnp.float32), turned, preferred_element_type=jnp.float32
-        )[0:1]
+            both.astype(jnp.bfloat16), own, turned, preferred_element_type=jnp.float32
+        )
+        term = term[0:1] + term[1:2]
         offset = term if offset is None else offset + term
-    delta = jnp.dot(
-        second_ref[...], factor.astype(jnp.bfloat16), preferred_element_type=jnp.float32
-    )
+    high = factor.astype(jnp.bfloat16)
+    low = (factor - high.astype(jnp.float32)).astype(jnp.bfloat16)
+    delta = jnp.dot(second_ref[...], high, preferred_element_type=jnp.float32)
+    delta += jnp.dot(second_ref[...], low, preferred_element_type=jnp.float32)
     grad = keep_ref[...] + got_ref[...].astype(jnp.float32) - delta - offset
     center, rate = norm_stats(*rows_of(stats_ref), count)
     scaled = (mid_ref[...] - center) * rate
@@ -921,9 +998,8 @@
             jax.ShapeDtypeStruct((8, width), jnp.float32),
         ),
         [scalars] + [whole] * 14,
-        flops=2 * rows * width * 2 * width,
-        moved=rows * width * 20,
         held=(0,),
+        lasts=3.3,
     )(place, keep, got, second, mid, stats, par, *deltas, *weights)
 
 
@@ -950,94 +1026,107 @@
         functools.partial(out_weight_body, count, part),
         jax.ShapeDtypeStruct((depth, width), jnp.float32),
         [scalars] + [whole] * (6 + part),
-        flops=2 * rows * depth * width,
-        moved=rows * width * 10,
+        lasts=1.7,
     )(place, second, pre, total, stats, back, gain, *([start] if part else []))
 
 
-def in_back_body(
-    count,
-    place_ref,
-    d_own_ref,
-    d_oth_ref,
-    pre_own_ref,
-    pre_oth_ref,
-    stats_own_ref,
-    stats_oth_ref,
-    back_own_ref,
-    back_oth_ref,
-    par_own_ref,
-    par_oth_ref,
-    block_ref,
-    peer_ref,
-    across_ref,
-    corner_ref,
-    out_ref,
-    keep_ref,
-    send_ref,
-    d_here_ref,
-    pre_here_ref,
-    back_here_ref,
-    sems,
+def in_slopes(count, grad, pre, stats, back, par):
+    center, rate = norm_stats(*rows_of(stats), count)
+    scaled = (pre[...].astype(jnp.float32) - center) * rate
+    value = (par[0:1] * rate) * (
+        grad[...].astype(jnp.float32) - back[0:1] / count - scaled * (back[1:2] / count)
+    )
+    return value.astype(jnp.bfloat16)
+
+
+def in_own_body(
+    count, place_ref, d_ref, pre_ref, stats_ref, back_ref, par_ref, block_ref, peer_ref, across_ref, corner_ref,
+    out_ref, keep_ref, send_ref, d_here_ref, pre_here_ref, keep_here_ref, pieces_ref, sems,
 ):
-    rows, width = d_own_ref.shape
-    arrivals = [
-        move(back_oth_ref, back_here_ref, sems, 0),
-        move(d_oth_ref, d_here_ref, sems, 1),
-        move(pre_oth_ref, pre_here_ref, sems, 2),
-    ]
+    rows, width = d_ref.shape
+    arrivals = [move(d_ref, d_here_ref, sems, 0), move(pre_ref, pre_here_ref, sems, 1)]
     half = width // 2
     quarter = block_ref.shape[1]
     chan = place_ref[0]
-    core, y = chan % 2, chan // 2
-    own = None
-    for side, grad, pre, stats, back, par in (
-        (y, d_own_ref, pre_own_ref, stats_own_ref, back_own_ref, par_own_ref),
-        (1 - y, d_here_ref, pre_here_ref, stats_oth_ref, back_here_ref, par_oth_ref),
-    ):
-        center, rate = norm_stats(*rows_of(stats), count)
-        scaled = (pre[...].astype(jnp.float32) - center) * rate
-        value = (par[0:1] * rate) * (
-            grad[...].astype(jnp.float32) - back[0:1] / count - scaled * (back[1:2] / count)
-        )
-        value = value.astype(jnp.bfloat16)
-        out_ref[:, lane_part(side, width)] = value
-        own = value if own is None else own
-        for copy in arrivals:
-            copy.wait()
-        arrivals = []
-    mine = block_ref[row_part(core, rows), :]
-    for at, piece in enumerate((mine, peer_ref[...], across_ref[...], corner_ref[...])):
+    core = chan % 2
+    sources = (block_ref.at[row_part(core, rows)], peer_ref, across_ref, corner_ref)
+    pieces = [
+        move(source, pieces_ref.at[at], sems, 6 + at) for at, source in enumerate(sources)
+    ]
+    for copy in arrivals:
+        copy.wait()
+    own = in_slopes(count, d_here_ref, pre_here_ref, stats_ref, back_ref, par_ref)
+    out_ref[...] = own
+    moves = []
+    for at, arrival in enumerate(pieces):
+        arrival.wait()
         value = lax.dot_general(
-            piece, own, (((0,), (0,)), ((), ())), preferred_element_type=jnp.float32
+            pieces_ref[at], own, (((0,), (0,)), ((), ())), preferred_element_type=jnp.float32
         )
         here = row_part(chan ^ at, quarter)
         low, high = value[:, :half], value[:, half:]
-        keep_ref[here, :] = jnp.where(core == 0, low, high)
+        keep_here_ref[here, :] = jnp.where(core == 0, low, high)
+        moves.append(move(keep_here_ref.at[here], keep_ref.at[here], sems, 2 + at))
         send_ref[here, :] = jnp.where(core == 0, high, low).astype(jnp.bfloat16)
-
-
-def in_back(count, place, d_own, d_oth, pre_own, pre_oth, stats, back, pars, block, pieces):
+    for copy in moves:
+        copy.wait()
+
+
+def in_own(count, place, d_own, pre, stats, back, par, block, pieces):
     rows, width = d_own.shape
     full = 4 * block.shape[1]
     return kernel_call(
-        functools.partial(in_back_body, count),
+        functools.partial(in_own_body, count),
         (
-            jax.ShapeDtypeStruct((rows, 2 * width), jnp.bfloat16),
+            jax.ShapeDtypeStruct((rows, width), jnp.bfloat16),
             jax.ShapeDtypeStruct((full, width // 2), jnp.float32),
             jax.ShapeDtypeStruct((full, width // 2), jnp.bfloat16),
         ),
-        [scalars, whole, remote, whole, remote, whole, whole, whole, remote] + [whole] * 6,
+        [scalars, remote, remote] + [whole] * 3 + [remote] * 4,
         (
-            pltpu.VMEM((rows, width), jnp.bfloat16),
-            pltpu.VMEM((rows, width), jnp.bfloat16),
-            pltpu.VMEM(back[1].shape, jnp.float32),
+            pltpu.VMEM((rows, width), jnp.float32),
+            pltpu.VMEM((rows, width), jnp.float32),
+            pltpu.VMEM((full, width // 2), jnp.float32),
+            pltpu.VMEM((4, rows, block.shape[1]), block.dtype),
+            pltpu.SemaphoreType.DMA((10,)),
+        ),
+        away=(1,),
+        lasts=4.5,
+    )(place, d_own, pre, stats, back, par, block, *pieces)
+
+
+def in_other_body(
+    count, place_ref, own_ref, d_ref, pre_ref, stats_ref, back_ref, par_ref, out_ref,
+    d_here_ref, pre_here_ref, back_here_ref, sems,
+):
+    width = d_ref.shape[1]
+    y = place_ref[0] // 2
+    arrivals = [
+        move(back_ref, back_here_ref, sems, 0),
+        move(d_ref, d_here_ref, sems, 1),
+        move(pre_ref, pre_here_ref, sems, 2),
+    ]
+    out_ref[:, lane_part(y, width)] = own_ref[...]
+    for copy in arrivals:
+        copy.wait()
+    value = in_slopes(count, d_here_ref, pre_here_ref, stats_ref, back_here_ref, par_ref)
+    out_ref[:, lane_part(1 - y, width)] = value
+
+
+def in_other(count, place, own, d_oth, pre_oth, stats, back, par):
+    rows, width = d_oth.shape
+    return kernel_call(
+        functools.partial(in_other_body, count),
+        jax.ShapeDtypeStruct((rows, 2 * width), jnp.bfloat16),
+        [scalars, whole, remote, remote, whole, remote, whole],
+        (
+            pltpu.VMEM((rows, width), d_oth.dtype),
+            pltpu.VMEM((rows, width), pre_oth.dtype),
+            pltpu.VMEM(back.shape, jnp.float32),
             pltpu.SemaphoreType.DMA((3,)),
         ),
-        flops=2 * rows * width * full,
-        moved=rows * full * 2,
-        held=(1,),
-    )(place, d_own, d_oth, pre_own, pre_oth, *stats, *back, *pars, block, *pieces)
+        lasts=2.0,
+    )(place, own, d_oth, pre_oth, stats, back, par)
 
 
 def input_grad_body(place_ref, mine_ref, peer_ref, near_ref, far_ref, total_ref, out_ref):
@@ -1064,9 +1153,31 @@
         input_grad_body,
         jax.ShapeDtypeStruct((rows, quarter), jnp.bfloat16),
         [scalars] + [whole] * 5,
-        flops=2 * rows * quarter * 2 * near.shape[1],
-        moved=rows * quarter * 8,
+        lasts=2.8,
     )(place, mine, peer, near, far, total)
+
+
+def pack_weights_body(mid_ref, out_ref, packed_ref):
+    rows, width = mid_ref.shape
+    size = out_ref.shape[0]
+    packed_ref[0:rows, :] = mid_ref[...]
+    for at in range(4):
+        packed_ref[rows + at * size : rows + (at + 1) * size, :] = out_ref[
+            :, at * width : (at + 1) * width
+        ]
+
+
+def pack_weights(mid, out):
+    rows, width = mid.shape
+    size = out.shape[0]
+    if size % BLOCK or rows % BLOCK:
+        parts = [out[:, at * width : (at + 1) * width] for at in range(4)]
+        return jnp.concatenate([mid] + parts, 0)
+    return kernel_call(
+        pack_weights_body,
+        jax.ShapeDtypeStruct((rows + 4 * size, width), mid.dtype),
+        [whole, whole],
+    )(mid, out)
 
 
 def pack_body(gain_in, bias_in, gain_mid, bias_mid, gate_bias, near, far, out_ref):
@@ -1216,8 +1327,7 @@
             pltpu.SemaphoreType.DMA((3,)),
         ),
         away=(0, 1, 2),
-        flops=4 * segs * TAPS * LANES * TAPS * LANES * size,
-        moved=segs * size * 40,
+        lasts=0.0,
     )(place, video, weight)
 
 
@@ -1245,6 +1355,7 @@
             jax.ShapeDtypeStruct((8, width), jnp.float32),
         ),
         [scalars] + [whole] * 5,
+        lasts=1.8,
     )(place, pre, grad, stats, gain.reshape(1, -1), bias.reshape(1, -1))
 
 
@@ -1302,7 +1413,7 @@
         scratch_shapes=[pltpu.VMEM((size, TAPS * LANES, rows.shape[2]), jnp.bfloat16)],
         compiler_params=pltpu.CompilerParams(vmem_limit_bytes=vmem_limit),
         cost_estimate=pl.CostEstimate(
-            flops=4 * size * (TAPS * LANES) ** 2 * rows.shape[2], bytes_accessed=1 << 20, transcendentals=0
+            flops=int(1.7 * flops_per_us), bytes_accessed=0, transcendentals=0
         ),
     )(place, pre, grad, stats, back, gain.reshape(1, -1), bias.reshape(1, -1), rows, pick, start)
 
@@ -1377,58 +1488,56 @@
     return value, order
 
 
-def halve_body(bit, place_ref, keep_ref, got_ref, mine_ref, send_ref):
-    size = send_ref.shape[1]
+def halve_body(bit, parts, far, place_ref, keep_ref, *refs):
+    got_refs, refs = refs[:parts], refs[parts:]
+    mine_ref, send_ref = refs[:2]
+    count, size = send_ref.shape[:2]
     high = (place_ref[1] // bit) % 2
-    for block in range(send_ref.shape[0]):
-        for ref, side in ((mine_ref, high), (send_ref, 1 - high)):
+    source, places, moves = keep_ref, [], []
+    for block in range(count):
+        for side in (1 - high, high):
             here = pl.ds(pl.multiple_of((2 * block + side) * size, size), size)
-            value = keep_ref[here, :]
-            if got_ref is not None:
-                value = value + got_ref[here, :].astype(jnp.float32)
-            ref[block] = value.astype(ref.dtype)
-
-
-def halve(place, keep, got, axis, bits, at):
+            places.append((block, side, here))
+    if far:
+        source, sems = refs[2:]
+        moves = [
+            move(keep_ref.at[here], source.at[here], sems, at)
+            for at, (_, _, here) in enumerate(places)
+        ]
+    for at, (block, side, here) in enumerate(places):
+        if far:
+            moves[at].wait()
+        value = source[here, :]
+        if parts:
+            part = block * parts // count
+            first = 2 * (block - part * count // parts) + side
+            got = got_refs[part][pl.ds(pl.multiple_of(first * size, size), size), :]
+            value = value + got.astype(jnp.float32)
+        ref = mine_ref if at % 2 else send_ref
+        ref[block] = value.astype(ref.dtype)
+
+
+def halve(place, keep, got, bits, at, far=False):
     rows, width = keep.shape
     left = sorted(bits, reverse=True)
     outer = 1 << left.index(at)
     inner = rows // (2 * outer)
-    if inner % BLOCK:
-        total = keep if got is None else keep + got.astype(jnp.float32)
+    if inner % BLOCK or outer % max(len(got), 1):
+        total = keep + jnp.concatenate(got).astype(jnp.float32) if got else keep
         blocks = total.reshape(outer, 2, inner, width)
         low, high = blocks[:, 0].reshape(-1, width), blocks[:, 1].reshape(-1, width)
         mine = (place[1] // at) % 2 == 0
         return jnp.where(mine, low, high), jnp.where(mine, high, low).astype(jnp.bfloat16)
     shape = (outer, inner, width)
-    if got is None:
-
-        def body(place_ref, keep_ref, mine_ref, send_ref):
-            halve_body(at, place_ref, keep_ref, None, mine_ref, send_ref)
-    else:
-        body = functools.partial(halve_body, at)
+    scratch = [pltpu.VMEM(keep.shape, keep.dtype), pltpu.SemaphoreType.DMA((2 * outer,))]
     mine, send = kernel_call(
-        body,
+        functools.partial(halve_body, at, len(got), far),
         (jax.ShapeDtypeStruct(shape, jnp.float32), jax.ShapeDtypeStruct(shape, jnp.bfloat16)),
-        [scalars] + [whole] * (1 if got is None else 2),
-        moved=rows * width * 9,
-        held=(0,),
-    )(place, keep, *([] if got is None else [got]))
+        [scalars, remote if far else whole] + [whole] * len(got),
+        scratch if far else [],
+        lasts=2.0 if far else 0.7,
+    )(place, keep, *got)
     return mine.reshape(-1, width), send.reshape(-1, width)
-
-
-def reduce_rows(place, keep, got, axis, bits, jobs=()):
-    jobs, left = list(jobs), list(bits)
-    while left:
-        bit = left[0]
-        keep, send = halve(place, keep, got, axis, left, bit)
-        left.pop(0)
-        got = swap(send, axis, bit)
-        if jobs:
-            got = after(got, jobs.pop(0)(send))
-    for job in jobs:
-        got = after(got, job(got))
-    return keep + got.astype(jnp.float32)
 
 
 def transposed(left, right):
@@ -1483,18 +1592,19 @@
     def my_rows(value, which):
         return lax.dynamic_slice_in_dim(value, which * half, half, 0)
 
+    packed = pack_weights(weight_mid, weight_out)
+    block_in = after(block_in, packed)
     mine, others = my_rows(block_in, core), my_rows(block_in, 1 - core)
-    pieces = [swap(others, "chan", 1), swap(mine, "chan", 2), swap(others, "chan", 3)]
+    pieces = [swap(others, "chan", 1), swap(mine, "chan", 2)]
+    pieces.append(swap(after(others, pieces[1]), "chan", 3))
 
     own_in, order = gather_rows(after(weight_in, mine, others), "dp")
     weights_in = [own_in, swap(own_in, "chan", 1)]
-    parts_out = [weight_out[:, at * narrow : (at + 1) * narrow] for at in range(4)]
-    packed = jnp.concatenate([weight_mid] + parts_out, 0)
     gathered = lax.all_gather(packed, "dp", axis=0)
 
     params = pack_params([gain_in, bias_in, gain_mid, bias_mid, gate_bias], kernel_near, kernel_far)
     par_own = ordered(core == 1, params, swap(params, "chan", 1), 1)
-    pars = [par_own, swap(par_own, "chan", 2)]
+    pars = [par_own]
     same = lax.dynamic_slice_in_dim(same_video, core * (clips // 2), clips // 2, 0)
     same = jnp.pad(same, ((0, 0), (0, 1)))
     gain_row, bias_row = gain_out.reshape(1, -1), bias_out.reshape(1, -1)
@@ -1504,14 +1614,27 @@
         place, video, stem_weight(stem_center, stem_diff), width
     )
 
-    def both_sums(sums, crossing, jobs=()):
-        own = sum_over(sums + swap(sums, "chan", 1), "dp", jobs[:3])
-        oth = swap(after(own, crossing), "chan", 2)
-        for job in jobs[3:]:
-            oth = after(oth, job(own))
+    def both_sums(sums, jobs=()):
+        jobs = [run or (lambda mark: mark) for run in jobs]
+        got = swap(sums, "chan", 1)
+        if jobs:
+            got = after(got, jobs[0](sums))
+        own = sum_over(sums + got, "dp", jobs[1:4])
+        oth = swap(own, "chan", 2)
+        for run in jobs[4:]:
+            oth = after(oth, run(own))
         return [own, oth]
 
     made = {}
+
+    def in_turn(*works):
+        def run(mark):
+            results = []
+            for work in works:
+                results.append(work((mark, results) if results else mark))
+            return results
+
+        return run
 
     def job(name, work):
         def run(mark):
@@ -1520,29 +1643,36 @@
 
         return run
 
-    pre_in, pre_in16, sums_in, full_in = first_conv(
-        order, place, block_in, pieces, weights_in, after(extra, pars)
-    )
-    pre_in_oth = swap(pre_in16, "chan", 2)
-
-    def mid_rows(mark):
-        own = after(gathered, mark)[:, : weight_mid.shape[0]].reshape(-1, narrow)
-        return [own, swap(own, "chan", 1)]
+    pre_in, sums_in, full_in = first_conv(
+        order, place, block_in, pieces, weights_in, after(extra, par_own)
+    )
+    pre_in_oth = swap(pre_in, "chan", 2)
+
+    blocks = gathered
+    if weight_mid.shape[0] % BLOCK:
+        blocks = gathered[:, : weight_mid.shape[0]].reshape(1, -1, narrow)
+    blocks = after(blocks, sums_in)
+    weights_mid = [blocks, swap(blocks, "chan", 1)]
 
     def out_rows(mark):
         parts, first, size = after(gathered, mark), weight_mid.shape[0], weight_out.shape[0]
         parts = [parts[:, first + at * size : first + (at + 1) * size] for at in range(4)]
         return jnp.concatenate([part.reshape(-1, narrow) for part in parts], 1)
 
+    def own_gate(mark):
+        return gate_own(count, same, pre_in, mark, pars[0])
+
     stats_in = both_sums(
-        sums_in, pre_in_oth, [job("weights_mid", mid_rows), job("full_out", out_rows)]
-    )
-    weights_mid, full_out = made["weights_mid"], made["full_out"]
+        sums_in,
+        [None, None, job("full_out", out_rows), None, job("own", own_gate)],
+    )
+    pars.append(swap(after(par_own, stats_in[0]), "chan", 2))
+    full_out = made["full_out"]
 
     out_across = swap(after(full_out, stats_in), "chan", 2)
 
     mixed, pre_mid, pre_mid16, sums_mid = gate_mid(
-        count, place, same, pre_in, pre_in_oth, *stats_in, *pars, weights_mid
+        count, place, same, made["own"][0], pre_in_oth, stats_in[1], pars[1], weights_mid
     )
     pre_mid_oth = swap(pre_mid16, "chan", 2)
     stats_stem = after(stats_in[0], sums_mid)
@@ -1553,13 +1683,18 @@
         )
 
     def slab_of(mark):
-        slab = after(weights_mid[0], mark).reshape(9, 2, width, narrow)
+        slab = after(gathered, mark)[:, : weight_mid.shape[0]].reshape(9, 2, width, narrow)
         return lax.dynamic_slice_in_dim(slab, 1 - y, 1, 1).reshape(9 * width, narrow)
 
     stats_mid = both_sums(
-        after(sums_mid, out_across),
-        pre_mid_oth,
-        [job("stem", stem_half), job("slab", slab_of), job("turned", lambda mark: turn(after(mixed, mark)))],
+        sums_mid,
+        [
+            None,
+            job("stem", stem_half),
+            in_turn(job("slab", slab_of), lambda mark: out_across),
+            job("turned", lambda mark: turn(after(mixed, mark))),
+            lambda mark: pre_mid_oth,
+        ],
     )
     stem_out, extra = made["stem"]
 
@@ -1592,13 +1727,12 @@
         return job(f"stem{chunk}", work)
 
     back_out = sum_over(
-        sums_back, "dp", [job("cross", cross), stem_part(0, None), stem_part(1, "stem0")]
+        sums_back, "dp", [stem_part(0, None), job("cross", cross), stem_part(1, "stem0")]
     )
     keep, send = made["cross"]
     got = swap(send, "chan", 2)
     delta = out_delta(count, rows, stats_out, sums_back, back_out, gain_row)
-    deltas = [delta, swap(delta, "chan", 1)]
-    deltas += [swap(value, "chan", 2) for value in deltas]
+    deltas = [delta] + [swap(delta, "chan", at) for at in (1, 2, 3)]
 
     grad_mid, grad_mid16, sums_mid_back = mid_slope(
         count, place, keep, got, second, pre_mid, stats_mid[0], pars[0], deltas, weights_out
@@ -1616,19 +1750,26 @@
 
         return work
 
-    back_mid = both_sums(sums_mid_back, grad_mid_oth, [
+    def own_slopes(mark):
+        return mid_own(count, grad_mid, pre_mid, stats_mid[0], mark, pars[0])
+
+    bits = steps_of("dp")
+
+    back_mid = both_sums(sums_mid_back, [
+        None,
         job("out0", out_part(None, second)),
         job("out1", out_part("out0", second_peer)),
         stem_part(2, "stem1"),
-        stem_part(3, "stem2"),
+        in_turn(job("slopes", own_slopes), stem_part(3, "stem2")),
     ])
-    bits = steps_of("dp")
-    sum_out = reduce_rows(place, made["out1"], None, "dp", bits)
+    slopes = made["slopes"]
+    sum_out = lax.psum_scatter(made["out1"], "dp", scatter_dimension=0, tiled=True)
+    stem_first = swap(made["stem3"], "dp", bits[0])
     far_in = swap(made["away_in"], "chan", 2)
 
-    slopes, grad_in, grad_in16, sums_in_back = mid_back(
-        count, place, same, grad_mid, grad_mid_oth, pre_mid, pre_mid_oth, stats_mid, back_mid,
-        pre_in, stats_in[0], pars, weights_mid, aways_mid,
+    grad_in, grad_in16, sums_in_back = mid_back(
+        count, place, same, slopes, grad_mid_oth, pre_mid_oth, stats_mid[1], back_mid[1], pre_in,
+        made["own"][1], stats_in[0], pars, weights_mid, aways_mid,
     )
     grad_in_oth = swap(grad_in16, "chan", 2)
 
@@ -1636,46 +1777,66 @@
         return mid_weight(place, made["turned"], after(slopes, mark))
 
     def mid_rest(mark):
-        keep, send = made["mid"]
-        return halve(place, keep, after(swap(send, "chan", 1), mark), "dp", mid_bits, mid_bits[0])
-
-    mid_bits = bits[1:2] + bits[:1] + bits[2:]
-    back_in = both_sums(sums_in_back, grad_in_oth, [job("mid", mid_part), job("mid0", mid_rest)])
-    mid_got = swap(made["mid0"][1], "dp", mid_bits[0])
-
-    grad_pre, keep, send = in_back(
-        count, place, grad_in, grad_in_oth, pre_in, pre_in_oth, stats_in, back_in, pars, block_in,
-        pieces,
+        keep, *sends = made["mid"]
+        got = [after(swap(send, "chan", 1), mark) for send in sends]
+        return halve(place, keep, got, mid_bits, mid_bits[0], True)
+
+    mid_bits = bits
+
+    def mid_step(at):
+        def work(mark):
+            keep, got = made["keep"], after(swap(made["send"], "dp", mid_bits[at - 1]), mark)
+            made["keep"], made["send"] = halve(place, keep, [got], mid_bits[at:], mid_bits[at])
+            return made["send"]
+
+        return work
+
+    def mid_first(mark):
+        made["keep"], made["send"] = mid_rest(mark)
+        return made["send"]
+
+    def own_in_back(mark):
+        return in_own(
+            count, place, grad_in, pre_in, stats_in[0], mark, pars[0], block_in, pieces
+        )
+
+    back_in = both_sums(
+        sums_in_back,
+        [
+            lambda mark: stem_first,
+            job("mid", mid_part),
+            None,
+            mid_first,
+            job("in", own_in_back),
+        ],
+    )
+
+    grad_own, keep, send = made["in"]
+    got = swap(send, "chan", 1)
+    grad_pre = in_other(
+        count, place, after(grad_own, send), grad_in_oth, pre_in_oth, stats_in[1], back_in[1], pars[1]
     )
     grad_peer = swap(grad_pre, "chan", 1)
-    got = swap(send, "chan", 1)
-
-    def input_job(mark):
-        near = after(made["near_in"], mark)
-        return input_grad(place, grad_pre, grad_peer, near, far_in, grad_total)
-
-    def mid_job(at):
-        def work(mark):
-            made["mid_keep"], send = halve(
-                place, after(made["mid_keep"], mark), made["mid_got"], "dp", mid_bits[at:], mid_bits[at]
-            )
-            made["mid_got"] = swap(send, "dp", mid_bits[at])
-            return send
-
-        return work
-
-    made["mid_keep"], made["mid_got"] = made["mid0"][0], mid_got
-    many = [mid_job(at) for at in range(1, len(mid_bits))]
-
-    def first_job(mark):
-        made["input"] = input_job(many[0](mark))
-        return made["input"]
-
-    sum_in = reduce_rows(place, keep, got, "dp", bits, [first_job] + many[1:])
-    sum_mid = made["mid_keep"] + made["mid_got"].astype(jnp.float32)
-    grad_block_in = made["input"]
-    stem_sum = sum_over(made["stem3"], "dp")
-    center_grad, diff_grad = stem_grads(after(stem_sum, made["input"]), outs)
+    mark, stem_total, stem_got = grad_pre, made["stem3"], stem_first
+    assert len(bits) > 1
+    last = len(bits) - 1
+    for at, bit in enumerate(bits):
+        got = after(got, mark, sum_out) if at == 1 else after(got, mark)
+        keep, send = halve(place, keep, [got], bits[at:], bit, at == 0)
+        got = swap(send, "dp", bit)
+        if at < last:
+            mark = mid_step(at + 1)(send)
+            if at == 0:
+                near = after(made["near_in"], mark)
+                mark = grad_block_in = input_grad(
+                    place, grad_pre, grad_peer, near, far_in, grad_total
+                )
+            mark = stem_total = after(stem_total, mark) + stem_got
+            stem_got = swap(stem_total, "dp", bits[at + 1])
+    sum_mid = after(made["keep"], send) + swap(made["send"], "dp", bit).astype(jnp.float32)
+    stem_total = after(stem_total, sum_mid) + stem_got
+    sum_in = keep + after(got, stem_total).astype(jnp.float32)
+    center_grad, diff_grad = stem_grads(stem_total, outs)
 
     def my_columns(value):
         return lax.dynamic_slice_in_dim(value, core * narrow, narrow, value.ndim - 1)

time: 284 us -> 264 us (0.930)
  waiting for transfers between devices: 78.6 us -> 55.8 us
  Pallas kernels: 82.3 us -> 88.6 us
    ppermute x67 -> x65, waiting for transfers between devices: 78.6 us -> 54.5 us  [swap(): return lax.ppermute(value, axis, [(at, at ^ bit) for at in range(size)])]
    pallas_call x28 -> x29, Pallas kernels: 75.4 us -> 81.7 us  [run(): call(*[pltpu.with_memory_space_constraint(arg, pltpu.HBM) if spec is remo...]
    unnamed x158 -> x148, local copies, waits for them, and re-layouts: 19.9 us -> 13.8 us
    ppermute x67 -> x65, starting transfers between devices: 69.4 us -> 68.8 us  [swap(): return lax.ppermute(value, axis, [(at, at ^ bit) for at in range(size)])]
  transfers between devices with their start and end apart: 68 -> 67, of which waited for: 35 -> 29; matrix products, arithmetic and copies ran while one was open for 7% -> 9% of each run, Pallas kernels for 19% -> 29%
where the time goes in v3:
time: 264 us; the launch traced here: 263 us
  Pallas kernels  88.6 us (34%)
  starting transfers between devices  68.9 us (26%)
  waiting for transfers between devices  55.8 us (21%)
  local copies, waits for them, and re-layouts  31.7 us (12%)
  between operations  15.1 us (6%)
  other arithmetic  3.09 us (1%)
    pallas_call x29, Pallas kernels, run(): call(*[pltpu.with_memory_space_constraint(arg, pltpu.HBM) if spec is remo...  81.7 us
    ppermute x65, starting transfers between devices, swap(): return lax.ppermute(value, axis, [(at, at ^ bit) for at in range(size)])  68.8 us
    ppermute x65, waiting for transfers between devices, swap(): return lax.ppermute(value, axis, [(at, at ^ bit) for at in range(size)])  54.5 us
    unnamed x148, local copies, waits for them, and re-layouts  13.8 us
    pallas_call x4, Pallas kernels, stem_back(): pl.pallas_call(functools.partial(stem_back_body, count, first), grid=(1,)...  6.89 us
  transfers between devices with their start and end apart: 67, of which 29 were waited for; matrix products, arithmetic and copies ran while one was open for 9% of the time, Pallas kernels for 29%

profile of v3, /device:TPU:0, one launch (start us, length us, event | category | flops | bytes accessed | tf_op | source)
XLA Modules:
  0.0 263.2 jit_solution(18141413145149760121)
XLA Ops:
  9.8 2.4 constant_dynamic-slice_fusion.6
  12.3 3.0 %collective-permute-start.1 = (bf16[784,512]{1,0:T(8,128)(2,1)S(1)}, bf16[784,512]{1,0:T(8,128)(2,1)S(1)}, u32[]{:S(2)}, u32[]{:S(2)}) collective-permute-start(bf16[784,512]{1,0:T(8,128)(2,1)S(1)} %get-tuple-element.293), channel_id=1, source_target_pairs={{0,2},{1,3},{2,0},{3,1},{4,6},{5,7},{6,4},{7,5},{8,10},{9,11},{10,... | collective-permute-start | bytes 2408456 | tf_op jit(solution)/shard_map/ppermute | solution.py:1456
  15.3 2.6 collective-permute-start.3
  17.9 2.9 %collective-permute-done.3 = bf16[256,128]{1,0:T(8,128)(2,1)S(1)} collective-permute-done((bf16[256,128]{1,0:T(8,128)(2,1)S(1)}, bf16[256,128]{1,0:T(8,128)(2,1)S(1)}, u32[]{:S(2)}, u32[]{:S(2)}) %collective-permute-start.3) | collective-permute-done | bytes 65568 | tf_op jit(solution)/shard_map/ppermute | solution.py:1456
  22.2 5.2 %collective-permute-done.4 = bf16[512,128]{1,0:T(8,128)(2,1)S(1)} collective-permute-done((bf16[512,128]{1,0:T(8,128)(2,1)S(1)}, bf16[512,128]{1,0:T(8,128)(2,1)S(1)}, u32[]{:S(2)}, u32[]{:S(2)}) %collective-permute-start.4) | collective-permute-done | bytes 131104 | tf_op jit(solution)/shard_map/ppermute | solution.py:1456
  27.4 1.5 collective-permute-start.5
  29.6 3.7 %collective-permute-done.1.across_ref = bf16[784,512]{1,0:T(8,128)(2,1)S(1)} collective-permute-done((bf16[784,512]{1,0:T(8,128)(2,1)S(1)}, bf16[784,512]{1,0:T(8,128)(2,1)S(1)}, u32[]{:S(2)}, u32[]{:S(2)}) %collective-permute-start.1) | collective-permute-done | bytes 802848 | tf_op jit(solution)/shard_map/ppermute | solution.py:1456
  38.9 1.7 reshape.135
  40.6 1.9 copy.46
  43.6 7.5 %shard_map.349 = (f32[32,16,256]{2,1,0:T(8,128)}, bf16[32,112,512]{2,1,0:T(8,128)(2,1)}, bf16[7,512,256]{2,1,0:T(8,128)(2,1)}, f32[8,256]{1,0:T(8,128)S(1)}) custom-call(s32[2]{0:T(128)S(1)} %pad_add_fusion.place_ref, bf16[32,15,1024]{2,1,0:T(8,128)(2,1)S(1)} %copy.47.video_ref, bf16[112,112]{1,0:T(8,128)(2,1)S(1)} %reshape.136.weight_ref), custom_call_target="tpu_custom_call" | custom-call | tf_op jit(solution)/shard_map/pallas_call | solution.py:70
  51.1 2.4 collective-permute-done.2.corner_ref
  53.5 4.1 %shard_map.351 = (f32[784,256]{1,0:T(8,128)}, f32[8,256]{1,0:T(8,128)S(1)}, bf16[2048,256]{1,0:T(8,128)(2,1)}) custom-call(s32[2]{0:T(128)S(1)} %pad_add_fusion.place_ref, bf16[1568,512]{1,0:T(8,128)(2,1)S(1)} %copy-done.8, bf16[784,512]{1,0:T(8,128)(2,1)} %collective-permute-done.peer_ref, bf16[784,512]{1,0:T(8,128)(2,1)S(1)} %collective-permute-done.1.across_ref, ...), custom_call_target="tpu_custom_call" | custom-call | flops 1200000000 | tf_op jit(solution)/shard_map/pallas_call | solution.py:70
  60.6 1.9 collective-permute-done.8
  63.2 2.9 %collective-permute-done.9 = f32[8,256]{1,0:T(8,128)S(1)} collective-permute-done((f32[8,256]{1,0:T(8,128)S(1)}, f32[8,256]{1,0:T(8,128)S(1)}, u32[]{:S(2)}, u32[]{:S(2)}) %collective-permute-start.9) | collective-permute-done | bytes 8224 | tf_op jit(solution)/shard_map/ppermute | solution.py:1456
  66.1 2.0 collective-permute-start.10
  69.8 2.3 collective-permute-start.11
  72.1 2.2 collective-permute-done.11
  76.4 3.9 %shard_map.352 = (bf16[1184,256]{1,0:T(8,128)(2,1)}, f32[16,7,8,256]{3,2,1,0:T(8,128)}) custom-call(s32[2,8]{1,0:T(2,128)S(1)} %pad.4.same_ref, f32[784,256]{1,0:T(8,128)S(1)} %copy-done.29, f32[8,256]{1,0:T(8,128)S(1)} %add.124.stats_ref.stats_in_ref, f32[24,256]{1,0:T(8,128)S(1)} %maximum_select_fusion.par_ref.par_own_ref), custom_call_target="tpu_custom_call" | custom-call | flops 1170000000 | tf_op jit(solution)/shard_map/pallas_call | solution.py:70
  80.4 1.5 collective-permute-start.20
  82.0 8.9 %shard_map.353 = (bf16[1184,512]{1,0:T(8,128)(2,1)}, f32[784,256]{1,0:T(8,128)}, bf16[784,256]{1,0:T(8,128)(2,1)}, f32[8,256]{1,0:T(8,128)S(1)}) custom-call(s32[2]{0:T(128)S(1)} %pad_add_fusion.place_ref, s32[2,8]{1,0:T(2,128)S(1)} %pad.4.same_ref, bf16[1184,256]{1,0:T(8,128)(2,1)} %get-tuple-element.147.own_ref, ...), custom_call_target="tpu_custom_call" | custom-call | flops 2400000000 | tf_op jit(solution)/shard_map/pallas_call | solution.py:70
  93.4 1.8 shard_map.354
  96.4 2.0 collective-permute-start.19
  100.0 2.3 collective-permute-start.21
  102.3 1.6 shard_map.355.turned_ref
  106.0 2.2 collective-permute-done.22.stats_oth_ref
  108.8 1.9 shard_map.356.mine_ref.second_ref.rows_ref
  113.9 2.2 shard_map.357
  116.9 1.7 constant_dynamic-slice_fusion.4.near_ref
  119.9 2.0 collective-permute-start.25
  122.0 1.7 constant_dynamic-slice_fusion.3
  123.7 2.3 collective-permute-start.26
  126.0 2.4 collective-permute-done.26
  129.4 5.8 %shard_map.358 = (bf16[1568,512]{1,0:T(8,128)(2,1)}, f32[1568,512]{1,0:T(8,128)}, f32[8,512]{1,0:T(8,128)S(1)}, f32[784,512]{1,0:T(8,128)S(1)}, bf16[784,512]{1,0:T(8,128)(2,1)S(1)}) custom-call(s32[2]{0:T(128)S(1)} %pad_add_fusion.place_ref, f32[1568,512]{1,0:T(8,128)S(1)} %get-tuple-element.169.pre_ref, bf16[1568,512]{1,0:T(8,128)(2,1)S(1)} %copy-done.8, ...), custom_call_target="tpu_custom_call" | custom-call | flops 2249999872 | tf_op jit(solution)/shard_map/pallas_call | solution.py:70
  136.6 1.7 shard_map.359.start_ref
  141.9 2.0 collective-permute-start.31
  143.9 1.7 collective-permute-done.31
  145.7 2.3 collective-permute-start.32
  148.0 1.7 shard_map.361.start_ref
  152.4 2.1 collective-permute-done.34.deltas2_ref
  154.5 3.6 %shard_map.363 = (f32[784,256]{1,0:T(8,128)S(1)}, bf16[784,256]{1,0:T(8,128)(2,1)}, f32[8,256]{1,0:T(8,128)S(1)}) custom-call(s32[2]{0:T(128)S(1)} %pad_add_fusion.place_ref, f32[784,256]{1,0:T(8,128)S(1)} %get-tuple-element.187.keep_ref, bf16[784,256]{1,0:T(8,128)(2,1)S(1)} %collective-permute-done.30.got_ref, bf16[784,512]{1,0:T(8,128)(2,1)S(1)} %copy-done.17, ...), custom_call_target="tpu_custom_call" | custom-call | flops 990000000 | tf_op jit(solution)/shard_map/pallas_call | solution.py:70
  162.7 1.7 collective-permute-done.39
  165.0 2.0 collective-permute-start.40
  167.0 2.0 shard_map.365
  172.0 2.0 copy-done.3
  175.4 1.7 shard_map.366.start_ref
  177.9 1.7 shard_map.367.slopes_ref
  179.6 1.7 shard_map.368
  181.4 1.6 collective-permute-start.46
  183.6 11.5 %shard_map.369 = (f32[784,256]{1,0:T(8,128)}, bf16[784,256]{1,0:T(8,128)(2,1)S(1)}, f32[32,256]{1,0:T(8,128)S(1)}) custom-call(s32[2]{0:T(128)S(1)} %pad_add_fusion.place_ref, s32[2,8]{1,0:T(2,128)S(1)} %copy-done.48, bf16[3,1184,256]{2,1,0:T(8,128)(2,1)S(1)} %shard_map.367.slopes_ref, bf16[784,256]{1,0:T(8,128)(2,1)} %collective-permute-done.42.d_oth_ref, ...), custom_call_target="tpu_custom_call" | custom-call | flops 3449999872 | tf_op jit(solution)/shard_map/pallas_call | solution.py:70
  196.4 4.7 %shard_map.370 = (f32[4608,128]{1,0:T(8,128)}, bf16[2304,128]{1,0:T(8,128)(2,1)S(1)}, bf16[2304,128]{1,0:T(8,128)(2,1)S(1)}) custom-call(s32[2]{0:T(128)S(1)} %pad_add_fusion.place_ref, bf16[512,1152]{1,0:T(8,128)(2,1)S(1)} %copy-done.25, bf16[3,1184,256]{2,1,0:T(8,128)(2,1)S(1)} %shard_map.367.slopes_ref), custom_call_target="tpu_custom_call" | custom-call | flops 1440000000 | tf_op jit(solution)/shard_map/pallas_call | solution.py:70
  204.3 2.2 collective-permute-done.47
  207.5 2.9 %collective-permute-done.48 = f32[32,256]{1,0:T(8,128)S(1)} collective-permute-done((f32[32,256]{1,0:T(8,128)S(1)}, f32[32,256]{1,0:T(8,128)S(1)}, u32[]{:S(2)}, u32[]{:S(2)}) %collective-permute-start.48) | collective-permute-done | bytes 32800 | tf_op jit(solution)/shard_map/ppermute | solution.py:1456
  211.6 2.2 shard_map.371
  213.9 1.5 collective-permute-start.55
  216.4 5.8 %shard_map.372 = (bf16[784,256]{1,0:T(8,128)(2,1)S(1)}, f32[2048,128]{1,0:T(8,128)}, bf16[2048,128]{1,0:T(8,128)(2,1)S(1)}) custom-call(s32[2]{0:T(128)S(1)} %pad_add_fusion.place_ref, f32[784,256]{1,0:T(8,128)} %get-tuple-element.208.d_ref, f32[784,256]{1,0:T(8,128)} %get-tuple-element.140.own_ref.pre_ref, f32[8,256]{1,0:T(8,128)S(1)} %add.124.stats_ref.stats_in_ref, ...), custom_call_target="tpu_custom_call" | custom-call | flops 1350000000 | tf_op jit(solution)/shard_map/pallas_call | solution.py:70
  223.0 2.1 shard_map.373.mine_ref
  227.5 2.2 shard_map.374
  232.7 2.7 %shard_map.376 = bf16[1568,512]{1,0:T(8,128)(2,1)} custom-call(s32[2]{0:T(128)S(1)} %pad_add_fusion.place_ref, bf16[784,512]{1,0:T(8,128)(2,1)S(1)} %shard_map.373.mine_ref, bf16[784,512]{1,0:T(8,128)(2,1)S(1)} %collective-permute-done.54.peer_ref, bf16[512,256]{1,0:T(8,128)(2,1)S(1)} %copy-done.26, bf16[512,256]{1,0:T(8,128)(2,1)S(1)} %collective-permute-done.57.far_ref, ...), custom_call_target="tpu_custom_call" | custom-call | flops 840000000 | tf_op jit(solution)/shard_map/pallas_call | solution.py:70
  235.4 2.6 collective-permute-done.58.refs_0_
  240.3 2.2 collective-permute-start.63
  244.7 2.9 %collective-permute-done.61 = f32[56,256]{1,0:T(8,128)S(1)} collective-permute-done((f32[56,256]{1,0:T(8,128)S(1)}, f32[56,256]{1,0:T(8,128)S(1)}, u32[]{:S(2)}, u32[]{:S(2)}) %collective-permute-start.61) | collective-permute-done | bytes 57376 | tf_op jit(solution)/shard_map/ppermute | solution.py:1456
  247.7 1.5 collective-permute-start.64
  249.8 1.5 collective-permute-start.62
  252.1 1.9 collective-permute-done.64
  (310 shorter events, 73.3 us)
Async XLA Ops:
  7.2 51.7 %all-gather.3.cloned.1.call-start = ((), (), s32[]{:S(2)}) async-start(), calls=%async_computation.2 | async-start | bytes 1916928 | tf_op jit(solution)/shard_map/all_gather | solution.py:1603
  9.7 228.3 %reduce-scatter.2.cloned.1.call-start = ((), (), s32[]{:S(2)}) async-start(), calls=%async_computation.1 | async-start | bytes 1179648 | tf_op jit(solution)/shard_map/reduce_scatter | solution.py:1766
  12.3 20.9 %collective-permute-start.1 = (bf16[784,512]{1,0:T(8,128)(2,1)S(1)}, bf16[784,512]{1,0:T(8,128)(2,1)S(1)}, u32[]{:S(2)}, u32[]{:S(2)}) collective-permute-start(bf16[784,512]{1,0:T(8,128)(2,1)S(1)} %get-tuple-element.293), channel_id=1, source_target_pairs={{0,2},{1,3},{2,0},{3,1},{4,6},{5,7},{6,4},{7,5},{8,10},{9,11},{10,... | collective-permute-start | bytes 2408456 | tf_op jit(solution)/shard_map/ppermute | solution.py:1456
  15.3 5.5 %collective-permute-start.3 = (bf16[256,128]{1,0:T(8,128)(2,1)S(1)}, bf16[256,128]{1,0:T(8,128)(2,1)S(1)}, u32[]{:S(2)}, u32[]{:S(2)}) collective-permute-start(bf16[256,128]{1,0:T(8,128)(2,1)S(1)} %copy-done.66), channel_id=1, source_target_pairs={{0,16},{4,20},{8,24},{12,28},{16,0},{20,4},{24,8},{28,12},{1,17},{... | collective-permute-start | bytes 196616 | tf_op jit(solution)/shard_map/ppermute | solution.py:1456
  20.8 6.6 %collective-permute-start.4 = (bf16[512,128]{1,0:T(8,128)(2,1)S(1)}, bf16[512,128]{1,0:T(8,128)(2,1)S(1)}, u32[]{:S(2)}, u32[]{:S(2)}) collective-permute-start(bf16[512,128]{1,0:T(8,128)(2,1)S(1)} %pad_maximum_fusion.2), channel_id=1, source_target_pairs={{0,8},{4,12},{8,0},{12,4},{16,24},{20,28},{24,16},{28,20},{1,9},{5... | collective-permute-start | bytes 393224 | tf_op jit(solution)/shard_map/ppermute | solution.py:1456
  22.2 28.9 %collective-permute-start = (bf16[784,512]{1,0:T(8,128)(2,1)}, bf16[784,512]{1,0:T(8,128)(2,1)}, u32[]{:S(2)}, u32[]{:S(2)}) collective-permute-start(bf16[784,512]{1,0:T(8,128)(2,1)} %get-tuple-element.136), channel_id=1, source_target_pairs={{0,1},{1,0},{2,3},{3,2},{4,5},{5,4},{6,7},{7,6},{8,9},{9,8},{10,11... | collective-permute-start | bytes 2408456 | tf_op jit(solution)/shard_map/ppermute | solution.py:1456
  27.4 7.5 %collective-permute-start.5 = (bf16[1024,128]{1,0:T(8,128)(2,1)S(1)}, bf16[1024,128]{1,0:T(8,128)(2,1)S(1)}, u32[]{:S(2)}, u32[]{:S(2)}) collective-permute-start(bf16[1024,128]{1,0:T(8,128)(2,1)S(1)} %pad_maximum_fusion.1), channel_id=1, source_target_pairs={{0,4},{4,0},{8,12},{12,8},{16,20},{20,16},{24,28},{28,24},{1,5},{5... | collective-permute-start | bytes 786440 | tf_op jit(solution)/shard_map/ppermute | solution.py:1456
  33.2 20.2 %collective-permute-start.2 = (bf16[784,512]{1,0:T(8,128)(2,1)}, bf16[784,512]{1,0:T(8,128)(2,1)}, u32[]{:S(2)}, u32[]{:S(2)}) collective-permute-start(bf16[784,512]{1,0:T(8,128)(2,1)} %get-tuple-element.136), channel_id=1, source_target_pairs={{0,3},{1,2},{2,1},{3,0},{4,7},{5,6},{6,5},{7,4},{8,11},{9,10},{10,... | collective-permute-start | bytes 2408456 | tf_op jit(solution)/shard_map/ppermute | solution.py:1456
  35.7 15.4 %collective-permute-start.6 = (bf16[2048,128]{1,0:T(8,128)(2,1)}, bf16[2048,128]{1,0:T(8,128)(2,1)}, u32[]{:S(2)}, u32[]{:S(2)}) collective-permute-start(bf16[2048,128]{1,0:T(8,128)(2,1)} %constant_dynamic-update-slice_fusion.own_ref), channel_id=1, source_target_pairs={{0,1},{1,0},{2,3},{3,2},{4,5},{5,4},{6,7},{7,6},{8,9},{9,8},{10,11... | collective-permute-start | bytes 1572872 | tf_op jit(solution)/shard_map/ppermute | solution.py:1456
  37.2 13.9 %collective-permute-start.7 = (f32[24,128]{1,0:T(8,128)S(1)}, f32[24,128]{1,0:T(8,128)S(1)}, u32[]{:S(2)}, u32[]{:S(2)}) collective-permute-start(f32[24,128]{1,0:T(8,128)S(1)} %shard_map.350), channel_id=1, source_target_pairs={{0,1},{1,0},{2,3},{3,2},{4,5},{5,4},{6,7},{7,6},{8,9},{9,8},{10,11... | collective-permute-start | bytes 36872 | tf_op jit(solution)/shard_map/ppermute | solution.py:1456
  58.9 23.1 %collective-permute-start.15 = (bf16[8,832,128]{2,1,0:T(8,128)(2,1)}, bf16[8,832,128]{2,1,0:T(8,128)(2,1)}, u32[]{:S(2)}, u32[]{:S(2)}) collective-permute-start(bf16[8,832,128]{2,1,0:T(8,128)(2,1)} %bitcast.82), channel_id=1, source_target_pairs={{0,1},{1,0},{2,3},{3,2},{4,5},{5,4},{6,7},{7,6},{8,9},{9,8},{10,11... | collective-permute-start | bytes 5111816 | tf_op jit(solution)/shard_map/ppermute | solution.py:1456
  58.9 23.1 %collective-permute-start.12 = (f32[784,256]{1,0:T(8,128)}, f32[784,256]{1,0:T(8,128)}, u32[]{:S(2)}, u32[]{:S(2)}) collective-permute-start(f32[784,256]{1,0:T(8,128)} %get-tuple-element.140.own_ref.pre_ref), channel_id=1, source_target_pairs={{0,2},{1,3},{2,0},{3,1},{4,6},{5,7},{6,4},{7,5},{8,10},{9,11},{10,... | collective-permute-start | bytes 2408456 | tf_op jit(solution)/shard_map/ppermute | solution.py:1456
  60.3 2.1 collective-permute-start.8
  62.5 3.7 %collective-permute-start.9 = (f32[8,256]{1,0:T(8,128)S(1)}, f32[8,256]{1,0:T(8,128)S(1)}, u32[]{:S(2)}, u32[]{:S(2)}) collective-permute-start(f32[8,256]{1,0:T(8,128)S(1)} %add.121), channel_id=1, source_target_pairs={{0,4},{4,0},{8,12},{12,8},{16,20},{20,16},{24,28},{28,24},{1,5},{5... | collective-permute-start | bytes 24584 | tf_op jit(solution)/shard_map/ppermute | solution.py:1456
  66.1 3.7 %collective-permute-start.10 = (f32[8,256]{1,0:T(8,128)S(1)}, f32[8,256]{1,0:T(8,128)S(1)}, u32[]{:S(2)}, u32[]{:S(2)}) collective-permute-start(f32[8,256]{1,0:T(8,128)S(1)} %add.122), channel_id=1, source_target_pairs={{0,8},{4,12},{8,0},{12,4},{16,24},{20,28},{24,16},{28,20},{1,9},{5... | collective-permute-start | bytes 24584 | tf_op jit(solution)/shard_map/ppermute | solution.py:1456
  69.8 4.5 %collective-permute-start.11 = (f32[8,256]{1,0:T(8,128)S(1)}, f32[8,256]{1,0:T(8,128)S(1)}, u32[]{:S(2)}, u32[]{:S(2)}) collective-permute-start(f32[8,256]{1,0:T(8,128)S(1)} %add.123), channel_id=1, source_target_pairs={{0,16},{4,20},{8,24},{12,28},{16,0},{20,4},{24,8},{28,12},{1,17},{... | collective-permute-start | bytes 24584 | tf_op jit(solution)/shard_map/ppermute | solution.py:1456
  74.4 6.0 %collective-permute-start.13 = (f32[8,256]{1,0:T(8,128)S(1)}, f32[8,256]{1,0:T(8,128)S(1)}, u32[]{:S(2)}, u32[]{:S(2)}) collective-permute-start(f32[8,256]{1,0:T(8,128)S(1)} %add.124.stats_ref.stats_in_ref), channel_id=1, source_target_pairs={{0,2},{1,3},{2,0},{3,1},{4,6},{5,7},{6,4},{7,5},{8,10},{9,11},{10,... | collective-permute-start | bytes 24584 | tf_op jit(solution)/shard_map/ppermute | solution.py:1456
  75.8 6.1 %collective-permute-start.14 = (f32[24,256]{1,0:T(8,128)S(1)}, f32[24,256]{1,0:T(8,128)S(1)}, u32[]{:S(2)}, u32[]{:S(2)}) collective-permute-start(f32[24,256]{1,0:T(8,128)S(1)} %maximum_select_fusion.par_ref.par_own_ref), channel_id=1, source_target_pairs={{0,2},{1,3},{2,0},{3,1},{4,6},{5,7},{6,4},{7,5},{8,10},{9,11},{10,... | collective-permute-start | bytes 73736 | tf_op jit(solution)/shard_map/ppermute | solution.py:1456
  80.4 19.0 %collective-permute-start.20 = (bf16[512,512]{1,0:T(8,128)(2,1)S(1)}, bf16[512,512]{1,0:T(8,128)(2,1)S(1)}, u32[]{:S(2)}, u32[]{:S(2)}) collective-permute-start(bf16[512,512]{1,0:T(8,128)(2,1)S(1)} %pad_maximum_fusion.weight_ref.weights0_ref), channel_id=1, source_target_pairs={{0,2},{1,3},{2,0},{3,1},{4,6},{5,7},{6,4},{7,5},{8,10},{9,11},{10,... | collective-permute-start | bytes 1572872 | tf_op jit(solution)/shard_map/ppermute | solution.py:1456
  90.9 17.3 %collective-permute-start.16 = (bf16[784,256]{1,0:T(8,128)(2,1)}, bf16[784,256]{1,0:T(8,128)(2,1)}, u32[]{:S(2)}, u32[]{:S(2)}) collective-permute-start(bf16[784,256]{1,0:T(8,128)(2,1)} %get-tuple-element.153), channel_id=1, source_target_pairs={{0,2},{1,3},{2,0},{3,1},{4,6},{5,7},{6,4},{7,5},{8,10},{9,11},{10,... | collective-permute-start | bytes 1204232 | tf_op jit(solution)/shard_map/ppermute | solution.py:1456
  92.7 3.7 %collective-permute-start.18 = (f32[8,256]{1,0:T(8,128)S(1)}, f32[8,256]{1,0:T(8,128)S(1)}, u32[]{:S(2)}, u32[]{:S(2)}) collective-permute-start(f32[8,256]{1,0:T(8,128)S(1)} %add.125), channel_id=1, source_target_pairs={{0,4},{4,0},{8,12},{12,8},{16,20},{20,16},{24,28},{28,24},{1,5},{5... | collective-permute-start | bytes 24584 | tf_op jit(solution)/shard_map/ppermute | solution.py:1456
  96.4 3.7 %collective-permute-start.19 = (f32[8,256]{1,0:T(8,128)S(1)}, f32[8,256]{1,0:T(8,128)S(1)}, u32[]{:S(2)}, u32[]{:S(2)}) collective-permute-start(f32[8,256]{1,0:T(8,128)S(1)} %add.126), channel_id=1, source_target_pairs={{0,8},{4,12},{8,0},{12,4},{16,24},{20,28},{24,16},{28,20},{1,9},{5... | collective-permute-start | bytes 24584 | tf_op jit(solution)/shard_map/ppermute | solution.py:1456
  100.0 4.5 %collective-permute-start.21 = (f32[8,256]{1,0:T(8,128)S(1)}, f32[8,256]{1,0:T(8,128)S(1)}, u32[]{:S(2)}, u32[]{:S(2)}) collective-permute-start(f32[8,256]{1,0:T(8,128)S(1)} %add.128), channel_id=1, source_target_pairs={{0,16},{4,20},{8,24},{12,28},{16,0},{20,4},{24,8},{28,12},{1,17},{... | collective-permute-start | bytes 24584 | tf_op jit(solution)/shard_map/ppermute | solution.py:1456
  104.6 3.7 %collective-permute-start.22 = (f32[8,256]{1,0:T(8,128)S(1)}, f32[8,256]{1,0:T(8,128)S(1)}, u32[]{:S(2)}, u32[]{:S(2)}) collective-permute-start(f32[8,256]{1,0:T(8,128)S(1)} %add.129.stats_own_ref.stats_ref), channel_id=1, source_target_pairs={{0,2},{1,3},{2,0},{3,1},{4,6},{5,7},{6,4},{7,5},{8,10},{9,11},{10,... | collective-permute-start | bytes 24584 | tf_op jit(solution)/shard_map/ppermute | solution.py:1456
  110.7 2.5 collective-permute-start.23
  110.8 17.5 %collective-permute-start.27 = (bf16[2304,128]{1,0:T(8,128)(2,1)}, bf16[2304,128]{1,0:T(8,128)(2,1)}, u32[]{:S(2)}, u32[]{:S(2)}) collective-permute-start(bf16[2304,128]{1,0:T(8,128)(2,1)} %bitcast.16), channel_id=1, source_target_pairs={{0,2},{1,3},{2,0},{3,1},{4,6},{5,7},{6,4},{7,5},{8,10},{9,11},{10,... | collective-permute-start | bytes 1769480 | tf_op jit(solution)/shard_map/ppermute | solution.py:1456
  116.1 3.8 %collective-permute-start.24 = (f32[8,512]{1,0:T(8,128)S(1)}, f32[8,512]{1,0:T(8,128)S(1)}, u32[]{:S(2)}, u32[]{:S(2)}) collective-permute-start(f32[8,512]{1,0:T(8,128)S(1)} %get-tuple-element.170), channel_id=1, source_target_pairs={{0,4},{4,0},{8,12},{12,8},{16,20},{20,16},{24,28},{28,24},{1,5},{5... | collective-permute-start | bytes 49160 | tf_op jit(solution)/shard_map/ppermute | solution.py:1456
  119.9 3.7 %collective-permute-start.25 = (f32[8,512]{1,0:T(8,128)S(1)}, f32[8,512]{1,0:T(8,128)S(1)}, u32[]{:S(2)}, u32[]{:S(2)}) collective-permute-start(f32[8,512]{1,0:T(8,128)S(1)} %add.131), channel_id=1, source_target_pairs={{0,8},{4,12},{8,0},{12,4},{16,24},{20,28},{24,16},{28,20},{1,9},{5... | collective-permute-start | bytes 49160 | tf_op jit(solution)/shard_map/ppermute | solution.py:1456
  123.7 4.7 %collective-permute-start.26 = (f32[8,512]{1,0:T(8,128)S(1)}, f32[8,512]{1,0:T(8,128)S(1)}, u32[]{:S(2)}, u32[]{:S(2)}) collective-permute-start(f32[8,512]{1,0:T(8,128)S(1)} %add.133), channel_id=1, source_target_pairs={{0,16},{4,20},{8,24},{12,28},{16,0},{20,4},{24,8},{28,12},{1,17},{... | collective-permute-start | bytes 49160 | tf_op jit(solution)/shard_map/ppermute | solution.py:1456
  135.3 4.4 %collective-permute-start.28 = (bf16[784,512]{1,0:T(8,128)(2,1)S(1)}, bf16[784,512]{1,0:T(8,128)(2,1)S(1)}, u32[]{:S(2)}, u32[]{:S(2)}) collective-permute-start(bf16[784,512]{1,0:T(8,128)(2,1)S(1)} %get-tuple-element.180), channel_id=1, source_target_pairs={{0,1},{1,0},{2,3},{3,2},{4,5},{5,4},{6,7},{7,6},{8,9},{9,8},{10,11... | collective-permute-start | bytes 2408456 | tf_op jit(solution)/shard_map/ppermute | solution.py:1456
  135.4 15.8 %collective-permute-start.36 = (bf16[512,512]{1,0:T(8,128)(2,1)S(1)}, bf16[512,512]{1,0:T(8,128)(2,1)S(1)}, u32[]{:S(2)}, u32[]{:S(2)}) collective-permute-start(bf16[512,512]{1,0:T(8,128)(2,1)S(1)} %copy-done.22), channel_id=1, source_target_pairs={{0,1},{1,0},{2,3},{3,2},{4,5},{5,4},{6,7},{7,6},{8,9},{9,8},{10,11... | collective-permute-start | bytes 1572872 | tf_op jit(solution)/shard_map/ppermute | solution.py:1456
  135.9 16.5 %collective-permute-start.37 = (bf16[512,512]{1,0:T(8,128)(2,1)S(1)}, bf16[512,512]{1,0:T(8,128)(2,1)S(1)}, u32[]{:S(2)}, u32[]{:S(2)}) collective-permute-start(bf16[512,512]{1,0:T(8,128)(2,1)S(1)} %copy-done.31), channel_id=1, source_target_pairs={{0,1},{1,0},{2,3},{3,2},{4,5},{5,4},{6,7},{7,6},{8,9},{9,8},{10,11... | collective-permute-start | bytes 1572872 | tf_op jit(solution)/shard_map/ppermute | solution.py:1456
  135.9 3.7 %collective-permute-start.29 = (f32[8,512]{1,0:T(8,128)S(1)}, f32[8,512]{1,0:T(8,128)S(1)}, u32[]{:S(2)}, u32[]{:S(2)}) collective-permute-start(f32[8,512]{1,0:T(8,128)S(1)} %get-tuple-element.181.sums_ref), channel_id=1, source_target_pairs={{0,4},{4,0},{8,12},{12,8},{16,20},{20,16},{24,28},{28,24},{1,5},{5... | collective-permute-start | bytes 49160 | tf_op jit(solution)/shard_map/ppermute | solution.py:1456
  140.4 14.1 %collective-permute-start.30 = (bf16[784,256]{1,0:T(8,128)(2,1)S(1)}, bf16[784,256]{1,0:T(8,128)(2,1)S(1)}, u32[]{:S(2)}, u32[]{:S(2)}) collective-permute-start(bf16[784,256]{1,0:T(8,128)(2,1)S(1)} %get-tuple-element.188), channel_id=1, source_target_pairs={{0,2},{1,3},{2,0},{3,1},{4,6},{5,7},{6,4},{7,5},{8,10},{9,11},{10,... | collective-permute-start | bytes 1204232 | tf_op jit(solution)/shard_map/ppermute | solution.py:1456
  141.9 3.7 %collective-permute-start.31 = (f32[8,512]{1,0:T(8,128)S(1)}, f32[8,512]{1,0:T(8,128)S(1)}, u32[]{:S(2)}, u32[]{:S(2)}) collective-permute-start(f32[8,512]{1,0:T(8,128)S(1)} %add.135), channel_id=1, source_target_pairs={{0,8},{4,12},{8,0},{12,4},{16,24},{20,28},{24,16},{28,20},{1,9},{5... | collective-permute-start | bytes 49160 | tf_op jit(solution)/shard_map/ppermute | solution.py:1456
  145.7 4.7 %collective-permute-start.32 = (f32[8,512]{1,0:T(8,128)S(1)}, f32[8,512]{1,0:T(8,128)S(1)}, u32[]{:S(2)}, u32[]{:S(2)}) collective-permute-start(f32[8,512]{1,0:T(8,128)S(1)} %add.136), channel_id=1, source_target_pairs={{0,16},{4,20},{8,24},{12,28},{16,0},{20,4},{24,8},{28,12},{1,17},{... | collective-permute-start | bytes 49160 | tf_op jit(solution)/shard_map/ppermute | solution.py:1456
  150.4 2.0 collective-permute-start.33
  150.5 4.0 %collective-permute-start.34 = (f32[8,512]{1,0:T(8,128)S(1)}, f32[8,512]{1,0:T(8,128)S(1)}, u32[]{:S(2)}, u32[]{:S(2)}) collective-permute-start(f32[8,512]{1,0:T(8,128)S(1)} %shard_map.362.deltas0_ref), channel_id=1, source_target_pairs={{0,2},{1,3},{2,0},{3,1},{4,6},{5,7},{6,4},{7,5},{8,10},{9,11},{10,... | collective-permute-start | bytes 49160 | tf_op jit(solution)/shard_map/ppermute | solution.py:1456
  151.2 3.3 %collective-permute-start.35 = (f32[8,512]{1,0:T(8,128)S(1)}, f32[8,512]{1,0:T(8,128)S(1)}, u32[]{:S(2)}, u32[]{:S(2)}) collective-permute-start(f32[8,512]{1,0:T(8,128)S(1)} %shard_map.362.deltas0_ref), channel_id=1, source_target_pairs={{0,3},{1,2},{2,1},{3,0},{4,7},{5,6},{6,5},{7,4},{8,11},{9,10},{10,... | collective-permute-start | bytes 49160 | tf_op jit(solution)/shard_map/ppermute | solution.py:1456
  158.2 24.8 %collective-permute-start.44 = (bf16[2304,128]{1,0:T(8,128)(2,1)}, bf16[2304,128]{1,0:T(8,128)(2,1)}, u32[]{:S(2)}, u32[]{:S(2)}) collective-permute-start(bf16[2304,128]{1,0:T(8,128)(2,1)} %collective-permute-done.27.away_own_ref), channel_id=1, source_target_pairs={{0,1},{1,0},{2,3},{3,2},{4,5},{5,4},{6,7},{7,6},{8,9},{9,8},{10,11... | collective-permute-start | bytes 1769480 | tf_op jit(solution)/shard_map/ppermute | solution.py:1456
  158.3 24.7 %collective-permute-start.42 = (bf16[784,256]{1,0:T(8,128)(2,1)}, bf16[784,256]{1,0:T(8,128)(2,1)}, u32[]{:S(2)}, u32[]{:S(2)}) collective-permute-start(bf16[784,256]{1,0:T(8,128)(2,1)} %get-tuple-element.204), channel_id=1, source_target_pairs={{0,2},{1,3},{2,0},{3,1},{4,6},{5,7},{6,4},{7,5},{8,10},{9,11},{10,... | collective-permute-start | bytes 1204232 | tf_op jit(solution)/shard_map/ppermute | solution.py:1456
  160.8 3.7 %collective-permute-start.39 = (f32[8,256]{1,0:T(8,128)S(1)}, f32[8,256]{1,0:T(8,128)S(1)}, u32[]{:S(2)}, u32[]{:S(2)}) collective-permute-start(f32[8,256]{1,0:T(8,128)S(1)} %add.138), channel_id=1, source_target_pairs={{0,4},{4,0},{8,12},{12,8},{16,20},{20,16},{24,28},{28,24},{1,5},{5... | collective-permute-start | bytes 24584 | tf_op jit(solution)/shard_map/ppermute | solution.py:1456
  165.0 5.0 %collective-permute-start.40 = (f32[8,256]{1,0:T(8,128)}, f32[8,256]{1,0:T(8,128)}, u32[]{:S(2)}, u32[]{:S(2)}) collective-permute-start(f32[8,256]{1,0:T(8,128)} %add.139), channel_id=1, source_target_pairs={{0,8},{4,12},{8,0},{12,4},{16,24},{20,28},{24,16},{28,20},{1,9},{5... | collective-permute-start | bytes 24584 | tf_op jit(solution)/shard_map/ppermute | solution.py:1456
  170.8 6.3 %collective-permute-start.41 = (f32[8,256]{1,0:T(8,128)S(1)}, f32[8,256]{1,0:T(8,128)S(1)}, u32[]{:S(2)}, u32[]{:S(2)}) collective-permute-start(f32[8,256]{1,0:T(8,128)S(1)} %add.140), channel_id=1, source_target_pairs={{0,16},{4,20},{8,24},{12,28},{16,0},{20,4},{24,8},{28,12},{1,17},{... | collective-permute-start | bytes 24584 | tf_op jit(solution)/shard_map/ppermute | solution.py:1456
  177.1 5.9 %collective-permute-start.43 = (f32[8,256]{1,0:T(8,128)S(1)}, f32[8,256]{1,0:T(8,128)S(1)}, u32[]{:S(2)}, u32[]{:S(2)}) collective-permute-start(f32[8,256]{1,0:T(8,128)S(1)} %add.141.back_ref), channel_id=1, source_target_pairs={{0,2},{1,3},{2,0},{3,1},{4,6},{5,7},{6,4},{7,5},{8,10},{9,11},{10,... | collective-permute-start | bytes 24584 | tf_op jit(solution)/shard_map/ppermute | solution.py:1456
  181.4 13.9 %collective-permute-start.46 = (f32[56,256]{1,0:T(8,128)S(1)}, f32[56,256]{1,0:T(8,128)S(1)}, u32[]{:S(2)}, u32[]{:S(2)}) collective-permute-start(f32[56,256]{1,0:T(8,128)S(1)} %shard_map.368), channel_id=1, source_target_pairs={{0,4},{4,0},{8,12},{12,8},{16,20},{20,16},{24,28},{28,24},{1,5},{5... | collective-permute-start | bytes 172040 | tf_op jit(solution)/shard_map/ppermute | solution.py:1456
  201.2 10.5 %collective-permute-start.50 = (bf16[2304,128]{1,0:T(8,128)(2,1)S(1)}, bf16[2304,128]{1,0:T(8,128)(2,1)S(1)}, u32[]{:S(2)}, u32[]{:S(2)}) collective-permute-start(bf16[2304,128]{1,0:T(8,128)(2,1)S(1)} %get-tuple-element.213), channel_id=1, source_target_pairs={{0,1},{1,0},{2,3},{3,2},{4,5},{5,4},{6,7},{7,6},{8,9},{9,8},{10,11... | collective-permute-start | bytes 1769480 | tf_op jit(solution)/shard_map/ppermute | solution.py:1456
  201.4 10.2 %collective-permute-start.51 = (bf16[2304,128]{1,0:T(8,128)(2,1)S(1)}, bf16[2304,128]{1,0:T(8,128)(2,1)S(1)}, u32[]{:S(2)}, u32[]{:S(2)}) collective-permute-start(bf16[2304,128]{1,0:T(8,128)(2,1)S(1)} %get-tuple-element.214), channel_id=1, source_target_pairs={{0,1},{1,0},{2,3},{3,2},{4,5},{5,4},{6,7},{7,6},{8,9},{9,8},{10,11... | collective-permute-start | bytes 1769480 | tf_op jit(solution)/shard_map/ppermute | solution.py:1456
  201.7 20.6 %collective-permute-start.52 = (bf16[784,256]{1,0:T(8,128)(2,1)S(1)}, bf16[784,256]{1,0:T(8,128)(2,1)}, u32[]{:S(2)}, u32[]{:S(2)}) collective-permute-start(bf16[784,256]{1,0:T(8,128)(2,1)S(1)} %get-tuple-element.224), channel_id=1, source_target_pairs={{0,2},{1,3},{2,0},{3,1},{4,6},{5,7},{6,4},{7,5},{8,10},{9,11},{10,... | collective-permute-start | bytes 1204232 | tf_op jit(solution)/shard_map/ppermute | solution.py:1456
  202.6 3.9 %collective-permute-start.47 = (f32[32,256]{1,0:T(8,128)S(1)}, f32[32,256]{1,0:T(8,128)S(1)}, u32[]{:S(2)}, u32[]{:S(2)}) collective-permute-start(f32[32,256]{1,0:T(8,128)S(1)} %add.142), channel_id=1, source_target_pairs={{0,4},{4,0},{8,12},{12,8},{16,20},{20,16},{24,28},{28,24},{1,5},{5... | collective-permute-start | bytes 98312 | tf_op jit(solution)/shard_map/ppermute | solution.py:1456
  203.5 29.1 %collective-permute-start.57 = (bf16[512,256]{1,0:T(8,128)(2,1)}, bf16[512,256]{1,0:T(8,128)(2,1)S(1)}, u32[]{:S(2)}, u32[]{:S(2)}) collective-permute-start(bf16[512,256]{1,0:T(8,128)(2,1)} %constant_dynamic-slice_fusion.3), channel_id=1, source_target_pairs={{0,2},{1,3},{2,0},{3,1},{4,6},{5,7},{6,4},{7,5},{8,10},{9,11},{10,... | collective-permute-start | bytes 786440 | tf_op jit(solution)/shard_map/ppermute | solution.py:1456
  206.5 3.9 %collective-permute-start.48 = (f32[32,256]{1,0:T(8,128)S(1)}, f32[32,256]{1,0:T(8,128)S(1)}, u32[]{:S(2)}, u32[]{:S(2)}) collective-permute-start(f32[32,256]{1,0:T(8,128)S(1)} %add.143), channel_id=1, source_target_pairs={{0,8},{4,12},{8,0},{12,4},{16,24},{20,28},{24,16},{28,20},{1,9},{5... | collective-permute-start | bytes 98312 | tf_op jit(solution)/shard_map/ppermute | solution.py:1456
  210.4 5.0 %collective-permute-start.49 = (f32[32,256]{1,0:T(8,128)S(1)}, f32[32,256]{1,0:T(8,128)S(1)}, u32[]{:S(2)}, u32[]{:S(2)}) collective-permute-start(f32[32,256]{1,0:T(8,128)S(1)} %add.144), channel_id=1, source_target_pairs={{0,16},{4,20},{8,24},{12,28},{16,0},{20,4},{24,8},{28,12},{1,17},{... | collective-permute-start | bytes 98312 | tf_op jit(solution)/shard_map/ppermute | solution.py:1456
  213.9 16.5 %collective-permute-start.55 = (bf16[2304,128]{1,0:T(8,128)(2,1)S(1)}, bf16[2304,128]{1,0:T(8,128)(2,1)S(1)}, u32[]{:S(2)}, u32[]{:S(2)}) collective-permute-start(bf16[2304,128]{1,0:T(8,128)(2,1)S(1)} %bitcast.68), channel_id=1, source_target_pairs={{0,4},{4,0},{8,12},{12,8},{16,20},{20,16},{24,28},{28,24},{1,5},{5... | collective-permute-start | bytes 1769480 | tf_op jit(solution)/shard_map/ppermute | solution.py:1456
  215.4 6.9 %collective-permute-start.53 = (f32[32,256]{1,0:T(8,128)S(1)}, f32[32,256]{1,0:T(8,128)S(1)}, u32[]{:S(2)}, u32[]{:S(2)}) collective-permute-start(f32[32,256]{1,0:T(8,128)S(1)} %add.145.back_ref), channel_id=1, source_target_pairs={{0,2},{1,3},{2,0},{3,1},{4,6},{5,7},{6,4},{7,5},{8,10},{9,11},{10,... | collective-permute-start | bytes 98312 | tf_op jit(solution)/shard_map/ppermute | solution.py:1456
  222.2 5.3 %collective-permute-start.56 = (bf16[2048,128]{1,0:T(8,128)(2,1)S(1)}, bf16[2048,128]{1,0:T(8,128)(2,1)S(1)}, u32[]{:S(2)}, u32[]{:S(2)}) collective-permute-start(bf16[2048,128]{1,0:T(8,128)(2,1)S(1)} %get-tuple-element.222), channel_id=1, source_target_pairs={{0,1},{1,0},{2,3},{3,2},{4,5},{5,4},{6,7},{7,6},{8,9},{9,8},{10,11... | collective-permute-start | bytes 1572872 | tf_op jit(solution)/shard_map/ppermute | solution.py:1456
  225.0 7.6 %collective-permute-start.54 = (bf16[784,512]{1,0:T(8,128)(2,1)S(1)}, bf16[784,512]{1,0:T(8,128)(2,1)S(1)}, u32[]{:S(2)}, u32[]{:S(2)}) collective-permute-start(bf16[784,512]{1,0:T(8,128)(2,1)S(1)} %shard_map.373.mine_ref), channel_id=1, source_target_pairs={{0,1},{1,0},{2,3},{3,2},{4,5},{5,4},{6,7},{7,6},{8,9},{9,8},{10,11... | collective-permute-start | bytes 2408456 | tf_op jit(solution)/shard_map/ppermute | solution.py:1456
  229.8 8.3 %collective-permute-start.58 = (bf16[1024,128]{1,0:T(8,128)(2,1)S(1)}, bf16[1024,128]{1,0:T(8,128)(2,1)S(1)}, u32[]{:S(2)}, u32[]{:S(2)}) collective-permute-start(bf16[1024,128]{1,0:T(8,128)(2,1)S(1)} %bitcast.71), channel_id=1, source_target_pairs={{0,4},{4,0},{8,12},{12,8},{16,20},{20,16},{24,28},{28,24},{1,5},{5... | collective-permute-start | bytes 786440 | tf_op jit(solution)/shard_map/ppermute | solution.py:1456
  231.0 8.7 %collective-permute-start.60 = (bf16[1152,128]{1,0:T(8,128)(2,1)S(1)}, bf16[1152,128]{1,0:T(8,128)(2,1)S(1)}, u32[]{:S(2)}, u32[]{:S(2)}) collective-permute-start(bf16[1152,128]{1,0:T(8,128)(2,1)S(1)} %bitcast.69), channel_id=1, source_target_pairs={{0,8},{4,12},{8,0},{12,4},{16,24},{20,28},{24,16},{28,20},{1,9},{5... | collective-permute-start | bytes 884744 | tf_op jit(solution)/shard_map/ppermute | solution.py:1456
  238.7 10.5 %collective-permute-start.59 = (bf16[512,128]{1,0:T(8,128)(2,1)S(1)}, bf16[512,128]{1,0:T(8,128)(2,1)S(1)}, u32[]{:S(2)}, u32[]{:S(2)}) collective-permute-start(bf16[512,128]{1,0:T(8,128)(2,1)S(1)} %bitcast.73), channel_id=1, source_target_pairs={{0,8},{4,12},{8,0},{12,4},{16,24},{20,28},{24,16},{28,20},{1,9},{5... | collective-permute-start | bytes 393224 | tf_op jit(solution)/shard_map/ppermute | solution.py:1456
  240.3 11.0 %collective-permute-start.63 = (bf16[576,128]{1,0:T(8,128)(2,1)S(1)}, bf16[576,128]{1,0:T(8,128)(2,1)S(1)}, u32[]{:S(2)}, u32[]{:S(2)}) collective-permute-start(bf16[576,128]{1,0:T(8,128)(2,1)S(1)} %bitcast.72), channel_id=1, source_target_pairs={{0,16},{4,20},{8,24},{12,28},{16,0},{20,4},{24,8},{28,12},{1,17},{... | collective-permute-start | bytes 442376 | tf_op jit(solution)/shard_map/ppermute | solution.py:1456
  243.2 4.4 %collective-permute-start.61 = (f32[56,256]{1,0:T(8,128)S(1)}, f32[56,256]{1,0:T(8,128)S(1)}, u32[]{:S(2)}, u32[]{:S(2)}) collective-permute-start(f32[56,256]{1,0:T(8,128)S(1)} %add.146), channel_id=1, source_target_pairs={{0,8},{4,12},{8,0},{12,4},{16,24},{20,28},{24,16},{28,20},{1,9},{5... | collective-permute-start | bytes 172040 | tf_op jit(solution)/shard_map/ppermute | solution.py:1456
  247.7 6.3 %collective-permute-start.64 = (f32[56,256]{1,0:T(8,128)S(1)}, f32[56,256]{1,0:T(8,128)S(1)}, u32[]{:S(2)}, u32[]{:S(2)}) collective-permute-start(f32[56,256]{1,0:T(8,128)S(1)} %add.147), channel_id=1, source_target_pairs={{0,16},{4,20},{8,24},{12,28},{16,0},{20,4},{24,8},{28,12},{1,17},{... | collective-permute-start | bytes 172040 | tf_op jit(solution)/shard_map/ppermute | solution.py:1456
  249.8 5.9 %collective-permute-start.62 = (bf16[256,128]{1,0:T(8,128)(2,1)S(1)}, bf16[256,128]{1,0:T(8,128)(2,1)S(1)}, u32[]{:S(2)}, u32[]{:S(2)}) collective-permute-start(bf16[256,128]{1,0:T(8,128)(2,1)S(1)} %bitcast.74), channel_id=1, source_target_pairs={{0,16},{4,20},{8,24},{12,28},{16,0},{20,4},{24,8},{28,12},{1,17},{... | collective-permute-start | bytes 196616 | tf_op jit(solution)/shard_map/ppermute | solution.py:1456
  (74 other events, 823.0 us)
Sparse Core Ops, SparseCore 0:
  10.2 48.5 all-gather.2
  170.2 62.3 reduce-scatter.1

commit v4 on v3

--- a/solution.py
+++ b/solution.py
@@ -172,8 +172,12 @@
     return pl.ds(pl.multiple_of(index * size, size), size)
 
 
-def rows_of(stats_ref):
-    return stats_ref[0:1], stats_ref[1:2]
+def after_sums(ref):
+    return ref.at[pl.ds(8, 24)]
+
+
+def rows_of(stats_ref, first=0):
+    return stats_ref[first : first + 1], stats_ref[first + 1 : first + 2]
 
 
 def put_sums(sums_ref, first, second):
@@ -206,7 +210,7 @@
     hidden_ref[pl.ds(rows, hidden_ref.shape[0] - rows), :] = jnp.zeros(
         (hidden_ref.shape[0] - rows, width), jnp.float32
     )
-    center, rate = norm_stats(*rows_of(stats), count)
+    center, rate = norm_stats(*stats, count)
     scaled = (pre[...].astype(jnp.float32) - center) * rate
     normed = scaled * par[0:1] + par[1:2]
     hidden_ref[pl.ds(0, rows), :] = normed * logistic(normed)
@@ -240,72 +244,44 @@
     lax.fori_loop(0, width // 128, lanes_step, 0)
 
 
-def gate_own_body(
-    count, same_ref, own_ref, stats_ref, par_ref, mixed_out_ref, gates_out_ref, hidden_ref, mixed_ref, gates_ref,
-    sems,
-):
-    mixed_ref[...] = jnp.zeros_like(mixed_ref)
-    gate_half(count, same_ref, own_ref, stats_ref, par_ref, hidden_ref, mixed_ref, 0, gates_ref)
-    moves = [move(mixed_ref, mixed_out_ref, sems, 0), move(gates_ref, gates_out_ref, sems, 1)]
-    for copy in moves:
-        copy.wait()
-
-
-def gate_own(count, same, own, stats, par):
-    rows, width = own.shape
-    shape = (map_rows(rows), width)
-    gates = (rows // PIXELS, SIDE, 8, width)
-    return kernel_call(
-        functools.partial(gate_own_body, count),
-        (jax.ShapeDtypeStruct(shape, jnp.bfloat16), jax.ShapeDtypeStruct(gates, jnp.float32)),
-        [scalars, whole, whole, whole],
-        (
-            pltpu.VMEM((rows + 56, width), jnp.float32),
-            pltpu.VMEM(shape, jnp.bfloat16),
-            pltpu.VMEM(gates, jnp.float32),
-            pltpu.SemaphoreType.DMA((2,)),
-        ),
-        away=(0, 1),
-        lasts=3.9,
-    )(same, own, stats, par)
-
-
 def gate_mid_body(
     count,
     place_ref,
     same_ref,
     own_ref,
     oth_ref,
-    stats_oth_ref,
+    stats_ref,
+    par_own_ref,
     par_oth_ref,
     weight_own_ref,
     weight_peer_ref,
     mixed_out_ref,
+    gates_out_ref,
     mid_ref,
     mid16_ref,
     sums_ref,
     hidden_ref,
     acc_ref,
     weight_ref,
-    oth_here_ref,
-    stats_here_ref,
+    own_here_ref,
     mixed_ref,
+    gates_ref,
     sems,
 ):
     rows, width = oth_ref.shape
     clips = rows // CLIP
     core, y = place_ref[0] % 2, place_ref[0] // 2
-    arrivals = [
-        move(stats_oth_ref, stats_here_ref, sems, 0),
-        move(oth_ref, oth_here_ref, sems, 1),
-    ]
-    weight_moves = [move(own_ref, mixed_ref.at[:, lane_part(y, width)], sems, 2)]
-    weight_moves += fetch_blocks((weight_own_ref, weight_peer_ref), core, weight_ref, sems, 5)
-    mixed_ref[:, lane_part(1 - y, width)] = jnp.zeros((mixed_ref.shape[0], width), jnp.bfloat16)
-    for copy in arrivals:
-        copy.wait()
+    arrival = move(own_ref, own_here_ref, sems, 0)
+    weight_moves = fetch_blocks((weight_own_ref, weight_peer_ref), core, weight_ref, sems, 5)
+    mixed_ref[...] = jnp.zeros_like(mixed_ref)
+    arrival.wait()
     gate_half(
-        count, same_ref, oth_here_ref, stats_here_ref, par_oth_ref, hidden_ref, mixed_ref,
+        count, same_ref, own_here_ref, rows_of(stats_ref), par_own_ref, hidden_ref, mixed_ref,
+        pl.multiple_of(y * width, width), gates_ref,
+    )
+    gates_move = move(gates_ref, gates_out_ref, sems, 2)
+    gate_half(
+        count, same_ref, oth_ref, rows_of(stats_ref, 4), after_sums(par_oth_ref), hidden_ref, mixed_ref,
         pl.multiple_of((1 - y) * width, width),
     )
     depth = 2 * width
@@ -334,39 +310,41 @@
     put_sums(
         sums_ref, jnp.sum(result, 0, keepdims=True), jnp.sum(result * result, 0, keepdims=True)
     )
-    mixed_move.wait()
-    mid_move.wait()
+    for copy in (gates_move, mixed_move, mid_move):
+        copy.wait()
 
 
 def map_rows(rows):
     return (rows // (2 * PIXELS) * SPAN + 2) * BLOCK
 
 
-def gate_mid(count, place, same, own, oth, stats_oth, par_oth, weights):
+def gate_mid(count, place, same, own, oth, stats, pars, weights):
     rows, width = oth.shape
     spread = map_rows(rows)
     depth = 18 * width
+    gates = (rows // PIXELS, SIDE, 8, width)
     return kernel_call(
         functools.partial(gate_mid_body, count),
         (
             jax.ShapeDtypeStruct((spread, 2 * width), jnp.bfloat16),
+            jax.ShapeDtypeStruct(gates, jnp.float32),
             jax.ShapeDtypeStruct((rows, width), jnp.float32),
             jax.ShapeDtypeStruct((rows, width), jnp.bfloat16),
             jax.ShapeDtypeStruct((8, width), jnp.float32),
         ),
-        [scalars, scalars, remote, remote, remote, whole, remote, remote],
+        [scalars, scalars, remote, whole, whole, whole, whole, remote, remote],
         (
             pltpu.VMEM((rows + 56, width), jnp.float32),
             pltpu.VMEM((rows + 8, width), jnp.float32),
             pltpu.VMEM((depth, width), jnp.bfloat16),
-            pltpu.VMEM((rows, width), oth.dtype),
-            pltpu.VMEM((8, width), jnp.float32),
+            pltpu.VMEM((rows, width), own.dtype),
             pltpu.VMEM((spread, 2 * width), jnp.bfloat16),
+            pltpu.VMEM(gates, jnp.float32),
             pltpu.SemaphoreType.DMA((5 + 2 * weights[0].shape[0],)),
         ),
-        away=(0, 1),
-        lasts=8.0,
-    )(place, same, own, oth, stats_oth, par_oth, *weights)
+        away=(0, 1, 2),
+        lasts=12.0,
+    )(place, same, own, oth, stats, *pars, *weights)
 
 
 def mid_slopes(count, grad, pre, stats, back, par, flat_ref, store):
@@ -394,8 +372,8 @@
     lax.fori_loop(0, rows // CLIP, clip_step, 0)
 
 
-def mid_own_body(count, d_ref, mid_ref, stats_ref, back_ref, par_ref, slopes_ref, flat_ref, mid_here_ref, sems):
-    arrival = move(mid_ref, mid_here_ref, sems, 0)
+def mid_own_body(count, d_ref, mid_ref, stats_ref, back_ref, par_ref, slopes_ref, flat_ref, mid_here_ref, d_here_ref, sems):
+    arrivals = [move(mid_ref, mid_here_ref, sems, 0), move(d_ref, d_here_ref, sems, 1)]
     slopes_ref[...] = jnp.zeros_like(slopes_ref)
 
     def store(place, maps, at):
@@ -404,8 +382,9 @@
                 *[across(value, 1 - col, at) for value in maps]
             ).astype(jnp.bfloat16)
 
-    arrival.wait()
-    mid_slopes(count, d_ref, mid_here_ref, stats_ref, back_ref, par_ref, flat_ref, store)
+    for copy in arrivals:
+        copy.wait()
+    mid_slopes(count, d_here_ref, mid_here_ref, stats_ref, back_ref, par_ref, flat_ref, store)
 
 
 def mid_own(count, d_own, mid, stats, back, par):
@@ -413,11 +392,12 @@
     return kernel_call(
         functools.partial(mid_own_body, count),
         jax.ShapeDtypeStruct((3, map_rows(rows), width), jnp.bfloat16),
-        [whole, remote, whole, whole, whole],
+        [remote, remote, whole, whole, whole],
         (
             pltpu.VMEM((rows + 56, width), jnp.float32),
             pltpu.VMEM((rows, width), jnp.float32),
-            pltpu.SemaphoreType.DMA((1,)),
+            pltpu.VMEM((rows, width), jnp.float32),
+            pltpu.SemaphoreType.DMA((2,)),
         ),
         held=(0,),
         lasts=1.7,
@@ -454,7 +434,6 @@
     weight_oth_ref,
     d_here_ref,
     mid_here_ref,
-    back_here_ref,
     pre_here_ref,
     gates_here_ref,
     sems,
@@ -463,7 +442,6 @@
     clips = rows // CLIP
     core, y = place_ref[0] % 2, place_ref[0] // 2
     arrivals = [
-        move(back_oth_ref, back_here_ref, sems, 0),
         move(d_oth_ref, d_here_ref, sems, 1),
         move(mid_oth_ref, mid_here_ref, sems, 2),
     ]
@@ -483,7 +461,7 @@
 
     for copy in arrivals:
         copy.wait()
-    mid_slopes(count, d_here_ref, mid_here_ref, stats_oth_ref, back_here_ref, par_oth_ref, flat_ref, store)
+    mid_slopes(count, d_here_ref, mid_here_ref, stats_oth_ref, back_oth_ref, after_sums(par_oth_ref), flat_ref, store)
     depth = 2 * width
     turned = (((1,), (1,)), ((), ()))
     for copy in weight_moves:
@@ -605,7 +583,7 @@
             jax.ShapeDtypeStruct((rows, width), jnp.bfloat16),
             jax.ShapeDtypeStruct((32, width), jnp.float32),
         ),
-        [scalars, scalars, whole, remote, remote, whole, remote, remote, remote]
+        [scalars, scalars, whole, remote, remote, whole, whole, remote, remote]
         + [whole] * 3
         + [remote] * 4,
         (
@@ -618,7 +596,6 @@
             pltpu.VMEM((depth // 2, width), jnp.bfloat16),
             pltpu.VMEM((rows, width), jnp.bfloat16),
             pltpu.VMEM((rows, width), jnp.bfloat16),
-            pltpu.VMEM((8, width), jnp.float32),
             pltpu.VMEM((rows, width), jnp.float32),
             pltpu.VMEM(gates.shape, jnp.float32),
             pltpu.SemaphoreType.DMA((10 + 2 * weights[0].shape[0],)),
@@ -696,72 +673,93 @@
     own_ref,
     other_ref,
     extra_ref,
+    par_ref,
     pre_out_ref,
+    pre16_ref,
     sums_ref,
-    weight_out_ref,
+    cross_ref,
+    near_ref,
+    away_ref,
     pre_ref,
     weight_ref,
+    pieces_ref,
     sems,
 ):
     rows = peer_ref.shape[0]
     quarter = block_ref.shape[1]
     chan, group = place_ref[0], place_ref[1]
     core = chan % 2
+    sources = (block_ref.at[row_part(core, rows)], peer_ref, across_ref)
+    arrivals = [
+        move(source, pieces_ref.at[at], sems, 3 + at) for at, source in enumerate(sources)
+    ]
     size = own_ref.shape[0] // len(order)
     for at, bits in enumerate(order):
         here = row_part(group ^ bits, size)
         weight_ref[here, lane_part(core)] = own_ref[at * size : (at + 1) * size]
         weight_ref[here, lane_part(1 - core)] = other_ref[at * size : (at + 1) * size]
-    weight_move = move(weight_ref, weight_out_ref, sems, 0)
-    mine = block_ref[row_part(core, rows), :]
+    weight_moves = [
+        move(weight_ref.at[row_part(chan, quarter)], near_ref, sems, 0),
+        move(weight_ref.at[row_part(chan ^ 2, quarter)], away_ref, sems, 2),
+    ]
     total = None
-    for at, piece in enumerate((mine, peer_ref[...], across_ref[...], corner_ref[...])):
+    for at in range(4):
+        if at < 3:
+            arrivals[at].wait()
+        piece = pieces_ref[at] if at < 3 else corner_ref[...]
         weight = weight_ref[row_part(chan ^ at, quarter), :]
         term = jnp.dot(piece, weight, preferred_element_type=jnp.float32)
         total = term if total is None else total + term
     pre_ref[...] = total
     pre_move = move(pre_ref, pre_out_ref, sems, 1)
+    pre16_ref[...] = total.astype(jnp.bfloat16)
     sums_ref[...] = extra_ref[...]
-    sums_ref[0:1, :] = jnp.sum(total, 0, keepdims=True)
-    sums_ref[1:2, :] = jnp.sum(total * total, 0, keepdims=True)
-    weight_move.wait()
+    cross_ref[0:8, :] = jnp.zeros((8, cross_ref.shape[1]), jnp.float32)
+    cross_ref[8:32, :] = par_ref[...]
+    for at, value in enumerate((total, total * total)):
+        row = jnp.sum(value, 0, keepdims=True)
+        sums_ref[at : at + 1, :] = row
+        cross_ref[4 + at : 5 + at, :] = row
+    for copy in weight_moves:
+        copy.wait()
     pre_move.wait()
 
 
-def first_conv(order, place, block, pieces, weights, extra):
+def first_conv(order, place, block, pieces, weights, extra, par):
     rows, quarter = pieces[0].shape
     width = 2 * weights[0].shape[1]
     return kernel_call(
         functools.partial(first_conv_body, order),
         (
             jax.ShapeDtypeStruct((rows, width), jnp.float32),
+            jax.ShapeDtypeStruct((rows, width), jnp.bfloat16),
             jax.ShapeDtypeStruct((8, width), jnp.float32),
-            jax.ShapeDtypeStruct((4 * quarter, width), jnp.bfloat16),
-        ),
-        [scalars] + [whole] * 7,
+            jax.ShapeDtypeStruct((32, width), jnp.float32),
+            jax.ShapeDtypeStruct((quarter, width), jnp.bfloat16),
+            jax.ShapeDtypeStruct((quarter, width), jnp.bfloat16),
+        ),
+        [scalars, remote, remote, remote] + [whole] * 5,
         (
             pltpu.VMEM((rows, width), jnp.float32),
             pltpu.VMEM((4 * quarter, width), jnp.bfloat16),
-            pltpu.SemaphoreType.DMA((2,)),
-        ),
-        away=(0, 2),
+            pltpu.VMEM((3, rows, quarter), jnp.bfloat16),
+            pltpu.SemaphoreType.DMA((6,)),
+        ),
+        away=(0, 4, 5),
         lasts=4.0,
-    )(place, block, *pieces, *weights, extra)
+    )(place, block, *pieces, *weights, extra, par)
 
 
 def second_body(
     count, place_ref, own_ref, oth_ref, stats_own_ref, stats_oth_ref, par_own_ref, par_oth_ref, out_ref,
-    oth_here_ref, stats_here_ref, sems,
+    oth_here_ref, sems,
 ):
     width = own_ref.shape[1]
     y = place_ref[0] // 2
-    arrivals = [
-        move(stats_oth_ref, stats_here_ref, sems, 0),
-        move(oth_ref, oth_here_ref, sems, 1),
-    ]
+    arrivals = [move(oth_ref, oth_here_ref, sems, 0)]
     for side, pre, stats, par in (
         (y, own_ref, stats_own_ref, par_own_ref),
-        (1 - y, oth_here_ref, stats_here_ref, par_oth_ref),
+        (1 - y, oth_here_ref, stats_oth_ref, after_sums(par_oth_ref)),
     ):
         center, rate = norm_stats(*rows_of(stats), count)
         normed = (pre[...].astype(jnp.float32) - center) * rate * par[2:3] + par[3:4]
@@ -776,11 +774,10 @@
     return kernel_call(
         functools.partial(second_body, count),
         jax.ShapeDtypeStruct((rows, 2 * width), jnp.bfloat16),
-        [scalars, whole, remote, whole, remote, whole, whole],
+        [scalars, whole, remote, whole, whole, whole, whole],
         (
             pltpu.VMEM((rows, width), jnp.bfloat16),
-            pltpu.VMEM((8, width), jnp.float32),
-            pltpu.SemaphoreType.DMA((2,)),
+            pltpu.SemaphoreType.DMA((1,)),
         ),
         lasts=1.9,
     )(place, own, oth, *stats, *pars)
@@ -830,9 +827,11 @@
     keep_ref,
     send_ref,
     total_ref,
+    weight_here_ref,
     sems,
 ):
     rows = keep_ref.shape[0]
+    weight_move = move(weight_ref, weight_here_ref, sems, 1)
     core = place_ref[0] % 2
     center, rate = norm_stats(*rows_of(stats_ref), count)
     gain, bias = gain_ref[...], bias_ref[...]
@@ -856,6 +855,7 @@
     put_sums(sums_ref, sums, products)
     total_move = move(total_ref, total_out_ref, sems, 0)
     local = 1.0 / (2 * rows)
+    weight_move.wait()
 
     def slope_rows(side):
         here = row_part(side, rows)
@@ -863,7 +863,7 @@
         value = gain * rate * (total_ref[here, :] - sums * local - scaled * (products * local))
         return lax.dot_general(
             value.astype(jnp.bfloat16),
-            weight_ref[...],
+            weight_here_ref[...],
             (((1,), (1,)), ((), ())),
             preferred_element_type=jnp.float32,
         )
@@ -885,8 +885,12 @@
             jax.ShapeDtypeStruct((rows // 2, depth), jnp.float32),
             jax.ShapeDtypeStruct((rows // 2, depth), jnp.bfloat16),
         ),
-        [scalars] + [whole] * 7,
-        (pltpu.VMEM((rows, width), jnp.float32), pltpu.SemaphoreType.DMA((1,))),
+        [scalars] + [whole] * 6 + [remote],
+        (
+            pltpu.VMEM((rows, width), jnp.float32),
+            pltpu.VMEM(weight.shape, weight.dtype),
+            pltpu.SemaphoreType.DMA((2,)),
+        ),
         away=(1,),
         lasts=7.5,
     )(place, pre, block, grad, stats, gain, bias, weight)
@@ -950,6 +954,8 @@
     out_ref,
     out16_ref,
     sums_ref,
+    here_ref,
+    sems,
 ):
     width = mid_ref.shape[1]
     y = place_ref[0] // 2
@@ -981,11 +987,13 @@
     scaled = (mid_ref[...] - center) * rate
     normed = scaled * par_ref[2:3] + par_ref[3:4]
     result = grad * silu_slope(normed)
-    out_ref[...] = result
+    here_ref[...] = result
+    out_move = move(here_ref, out_ref, sems, 0)
     out16_ref[...] = result.astype(jnp.bfloat16)
     put_sums(
         sums_ref, jnp.sum(result, 0, keepdims=True), jnp.sum(result * scaled, 0, keepdims=True)
     )
+    out_move.wait()
 
 
 def mid_slope(count, place, keep, got, second, mid, stats, par, deltas, weights):
@@ -998,7 +1006,8 @@
             jax.ShapeDtypeStruct((8, width), jnp.float32),
         ),
         [scalars] + [whole] * 14,
-        held=(0,),
+        (pltpu.VMEM((rows, width), jnp.float32), pltpu.SemaphoreType.DMA((1,))),
+        away=(0,),
         lasts=3.3,
     )(place, keep, got, second, mid, stats, par, *deltas, *weights)
 
@@ -1015,7 +1024,12 @@
         total_ref[here, :] - back_ref[0:1] / count - scaled * (back_ref[1:2] / count)
     )
     result = exact(rows_ref[...], value.astype(jnp.bfloat16), ((0,), (0,)))
-    refs[-1][...] = refs[0][...] + result if part else result
+    if part:
+        start_ref, out_ref, here_ref, sems = refs
+        here_ref[...] = start_ref[...] + result
+        move(here_ref, out_ref, sems, 0).wait()
+    else:
+        refs[0][...] = result
 
 
 def out_weight(count, place, second, pre, total, stats, back, gain, start=None):
@@ -1026,12 +1040,14 @@
         functools.partial(out_weight_body, count, part),
         jax.ShapeDtypeStruct((depth, width), jnp.float32),
         [scalars] + [whole] * (6 + part),
+        (pltpu.VMEM((depth, width), jnp.float32), pltpu.SemaphoreType.DMA((1,))) if part else (),
+        away=(0,) if part else (),
         lasts=1.7,
     )(place, second, pre, total, stats, back, gain, *([start] if part else []))
 
 
 def in_slopes(count, grad, pre, stats, back, par):
-    center, rate = norm_stats(*rows_of(stats), count)
+    center, rate = norm_stats(*stats, count)
     scaled = (pre[...].astype(jnp.float32) - center) * rate
     value = (par[0:1] * rate) * (
         grad[...].astype(jnp.float32) - back[0:1] / count - scaled * (back[1:2] / count)
@@ -1055,7 +1071,7 @@
     ]
     for copy in arrivals:
         copy.wait()
-    own = in_slopes(count, d_here_ref, pre_here_ref, stats_ref, back_ref, par_ref)
+    own = in_slopes(count, d_here_ref, pre_here_ref, rows_of(stats_ref), back_ref, par_ref)
     out_ref[...] = own
     moves = []
     for at, arrival in enumerate(pieces):
@@ -1096,20 +1112,14 @@
 
 
 def in_other_body(
-    count, place_ref, own_ref, d_ref, pre_ref, stats_ref, back_ref, par_ref, out_ref,
-    d_here_ref, pre_here_ref, back_here_ref, sems,
+    count, place_ref, own_ref, d_ref, pre_ref, stats_ref, back_ref, par_ref, out_ref, pre_here_ref, sems
 ):
     width = d_ref.shape[1]
     y = place_ref[0] // 2
-    arrivals = [
-        move(back_ref, back_here_ref, sems, 0),
-        move(d_ref, d_here_ref, sems, 1),
-        move(pre_ref, pre_here_ref, sems, 2),
-    ]
+    arrival = move(pre_ref, pre_here_ref, sems, 0)
     out_ref[:, lane_part(y, width)] = own_ref[...]
-    for copy in arrivals:
-        copy.wait()
-    value = in_slopes(count, d_here_ref, pre_here_ref, stats_ref, back_here_ref, par_ref)
+    arrival.wait()
+    value = in_slopes(count, d_ref, pre_here_ref, rows_of(stats_ref, 4), back_ref, after_sums(par_ref))
     out_ref[:, lane_part(1 - y, width)] = value
 
 
@@ -1118,13 +1128,8 @@
     return kernel_call(
         functools.partial(in_other_body, count),
         jax.ShapeDtypeStruct((rows, 2 * width), jnp.bfloat16),
-        [scalars, whole, remote, remote, whole, remote, whole],
-        (
-            pltpu.VMEM((rows, width), d_oth.dtype),
-            pltpu.VMEM((rows, width), pre_oth.dtype),
-            pltpu.VMEM(back.shape, jnp.float32),
-            pltpu.SemaphoreType.DMA((3,)),
-        ),
+        [scalars, whole, whole, remote, whole, whole, whole],
+        (pltpu.VMEM((rows, width), pre_oth.dtype), pltpu.SemaphoreType.DMA((1,))),
         lasts=2.0,
     )(place, own, d_oth, pre_oth, stats, back, par)
 
@@ -1157,30 +1162,59 @@
     )(place, mine, peer, near, far, total)
 
 
-def pack_weights_body(mid_ref, out_ref, packed_ref):
-    rows, width = mid_ref.shape
+def opening_body(
+    place_ref, block_ref, mid_ref, out_ref, mine_ref, others_ref, packed_ref, rows_ref, small_ref, sems
+):
+    rows = mine_ref.shape[0]
+    core = place_ref[0] % 2
+    count, width = mid_ref.shape
     size = out_ref.shape[0]
-    packed_ref[0:rows, :] = mid_ref[...]
+    sources = [(block_ref.at[row_part(side, rows)], rows_ref.at[at]) for at, side in ((0, core), (1, 1 - core))]
+    sources.append((mid_ref, small_ref.at[pl.ds(0, count)]))
     for at in range(4):
-        packed_ref[rows + at * size : rows + (at + 1) * size, :] = out_ref[
-            :, at * width : (at + 1) * width
-        ]
-
-
-def pack_weights(mid, out):
+        here = small_ref.at[pl.ds(count + at * size, size)]
+        sources.append((out_ref.at[:, pl.ds(at * width, width)], here))
+    arrivals = [move(*pair, sems, at) for at, pair in enumerate(sources)]
+    moves = []
+    for at, target in enumerate((mine_ref, others_ref)):
+        arrivals[at].wait()
+        moves.append(move(rows_ref.at[at], target, sems, 7 + at))
+    for copy in arrivals[2:]:
+        copy.wait()
+    moves.append(move(small_ref, packed_ref, sems, 9))
+    for copy in moves:
+        copy.wait()
+
+
+def opening(place, block, mid, out):
+    half = block.shape[0] // 2
     rows, width = mid.shape
     size = out.shape[0]
     if size % BLOCK or rows % BLOCK:
         parts = [out[:, at * width : (at + 1) * width] for at in range(4)]
-        return jnp.concatenate([mid] + parts, 0)
-    return kernel_call(
-        pack_weights_body,
-        jax.ShapeDtypeStruct((rows + 4 * size, width), mid.dtype),
-        [whole, whole],
-    )(mid, out)
-
-
-def pack_body(gain_in, bias_in, gain_mid, bias_mid, gate_bias, near, far, out_ref):
+        core = place[0] % 2
+        halves = [
+            lax.dynamic_slice_in_dim(block, side * half, half, 0) for side in (core, 1 - core)
+        ]
+        return (*halves, jnp.concatenate([mid] + parts, 0))
+    rows_shape = jax.ShapeDtypeStruct((half, block.shape[1]), block.dtype)
+    return kernel_call(
+        opening_body,
+        (rows_shape, rows_shape, jax.ShapeDtypeStruct((rows + 4 * size, width), mid.dtype)),
+        [scalars, remote, remote, remote],
+        (
+            pltpu.VMEM((2, half, block.shape[1]), block.dtype),
+            pltpu.VMEM((rows + 4 * size, width), mid.dtype),
+            pltpu.SemaphoreType.DMA((10,)),
+        ),
+        away=(0, 1, 2),
+    )(place, block, mid, out)
+
+
+def pack_body(gain_in, bias_in, gain_mid, bias_mid, gate_bias, near, far, stem_gain, stem_bias, out_ref, stem_ref):
+    stem_ref[...] = jnp.zeros_like(stem_ref)
+    stem_ref[0:1, :] = stem_gain[...]
+    stem_ref[1:2, :] = stem_bias[...]
     for at, ref in enumerate((gain_in, bias_in, gain_mid, bias_mid, gate_bias)):
         out_ref[at : at + 1, :] = ref[...]
     out_ref[5:14, :] = near[...]
@@ -1188,11 +1222,16 @@
     out_ref[23:24, :] = jnp.zeros_like(out_ref[23:24, :])
 
 
-def pack_params(rows, near, far):
-    width = near.shape[1]
-    return kernel_call(
-        pack_body, jax.ShapeDtypeStruct((24, width), jnp.float32), [whole] * 7
-    )(*[row.reshape(1, width) for row in rows], near, far)
+def pack_params(rows, near, far, stem):
+    width, outs = near.shape[1], stem[0].shape[0]
+    return kernel_call(
+        pack_body,
+        (
+            jax.ShapeDtypeStruct((24, width), jnp.float32),
+            jax.ShapeDtypeStruct((8, outs), jnp.float32),
+        ),
+        [whole] * 9,
+    )(*[row.reshape(1, width) for row in rows], near, far, *[row.reshape(1, outs) for row in stem])
 
 
 TAPS = 7
@@ -1228,11 +1267,11 @@
     ]
 
 
-def upright(row_ref):
-    size = row_ref.shape[1]
+def upright(row):
+    size = row.shape[1]
     at = lax.broadcasted_iota(jnp.int32, (size, size), 0)
     same = at == lax.broadcasted_iota(jnp.int32, (size, size), 1)
-    return jnp.sum(jnp.where(same, row_ref[...], 0.0), 1, keepdims=True)
+    return jnp.sum(jnp.where(same, row, 0.0), 1, keepdims=True)
 
 
 def stem_front_body(
@@ -1331,40 +1370,41 @@
     )(place, video, weight)
 
 
-def stem_norm(count, core, pre, stats_ref, gain_ref, bias_ref):
+def stem_norm(count, core, pre, stats_ref, par_ref):
     outs = pre.shape[1]
     center, rate = norm_stats(*stem_columns(core, outs, stats_ref), count)
     scaled = (pre - center) * rate
-    return scaled, scaled * upright(gain_ref) + upright(bias_ref), upright(gain_ref) * rate
-
-
-def stem_out_body(count, place_ref, pre_ref, grad_ref, stats_ref, gain_ref, bias_ref, out_ref, extra_ref):
+    gain, bias = upright(par_ref[0:1]), upright(par_ref[1:2])
+    return scaled, scaled * gain + bias, gain * rate
+
+
+def stem_out_body(count, place_ref, pre_ref, grad_ref, stats_ref, par_ref, out_ref, extra_ref):
     core = place_ref[0] % 2
-    scaled, normed, _ = stem_norm(count, core, pre_ref[...], stats_ref, gain_ref, bias_ref)
+    scaled, normed, _ = stem_norm(count, core, pre_ref[...], stats_ref, par_ref)
     part = logistic(normed)
     out_ref[...] = (normed * part).astype(jnp.bfloat16)
     value = grad_ref[...].astype(jnp.float32) * (part * (1.0 + normed * (1.0 - part)))
     extra_ref[...] = stem_row(core, extra_ref.shape[1], value, value * scaled)
 
 
-def stem_output(count, place, pre, grad, stats, gain, bias, width):
+def stem_output(count, place, pre, grad, stats, par, width):
     return kernel_call(
         functools.partial(stem_out_body, count),
         (
             jax.ShapeDtypeStruct(pre.shape, jnp.bfloat16),
             jax.ShapeDtypeStruct((8, width), jnp.float32),
         ),
-        [scalars] + [whole] * 5,
+        [scalars] + [whole] * 4,
         lasts=1.8,
-    )(place, pre, grad, stats, gain.reshape(1, -1), bias.reshape(1, -1))
+    )(place, pre, grad, stats, par)
 
 
 def stem_back_body(
-    count, first, place_ref, pre_ref, grad_ref, stats_ref, back_ref, gain_ref, bias_ref, rows_ref, pick_ref, start_ref, out_ref, slopes_ref,
+    count, first, place_ref, pre_ref, grad_ref, stats_ref, back_ref, par_ref, rows_ref, pick_ref, start_ref, out_ref, slopes_ref,
 ):
     core = place_ref[0] % 2
     segs, outs, pixels = pre_ref.shape
-    scaled, normed, scale = stem_norm(count, core, pre_ref[...], stats_ref, gain_ref, bias_ref)
+    scaled, normed, scale = stem_norm(count, core, pre_ref[...], stats_ref, par_ref)
     bias_grad, gain_grad = stem_columns(core, outs, back_ref)
     value = grad_ref[...].astype(jnp.float32) * silu_slope(normed)
     value = scale * (value - bias_grad / count - scaled * (gain_grad / count))
@@ -1389,7 +1429,7 @@
     out_ref[:, 128 : 128 + size] += total[rows:]
 
 
-def stem_back(count, place, pre, grad, stats, back, gain, bias, rows, pick, start, chunk, chunks):
+def stem_back(count, place, pre, grad, stats, back, par, rows, pick, start, chunk, chunks):
     segs, outs, pixels = pre.shape
     size = segs // chunks
 
@@ -1407,7 +1447,7 @@
         grid=(1,),
         out_shape=jax.ShapeDtypeStruct(small, jnp.float32),
         in_specs=[scalars, part(outs, pixels), part(outs, pixels)]
-        + [all_of(stats.shape), all_of(back.shape), all_of((1, outs)), all_of((1, outs))]
+        + [all_of(stats.shape), all_of(back.shape), all_of(par.shape)]
         + [part(*rows.shape[1:]), all_of(pick.shape), all_of(start.shape)],
         out_specs=all_of(small),
         scratch_shapes=[pltpu.VMEM((size, TAPS * LANES, rows.shape[2]), jnp.bfloat16)],
@@ -1415,7 +1455,7 @@
         cost_estimate=pl.CostEstimate(
             flops=int(1.7 * flops_per_us), bytes_accessed=0, transcendentals=0
         ),
-    )(place, pre, grad, stats, back, gain.reshape(1, -1), bias.reshape(1, -1), rows, pick, start)
+    )(place, pre, grad, stats, back, par, pltpu.with_memory_space_constraint(rows, pltpu.HBM), pick, start)
 
 
 def stem_weight(center, diff):
@@ -1464,6 +1504,7 @@
 
 def sum_over(value, axis, jobs=()):
     jobs = list(jobs)
+    jobs = [job or (lambda mark: mark) for job in jobs]
     for bit in steps_of(axis):
         got = swap(value, axis, bit)
         if jobs:
@@ -1589,12 +1630,7 @@
     core, y = chan % 2, chan // 2
     place = jnp.stack([chan, lax.axis_index("dp")])
 
-    def my_rows(value, which):
-        return lax.dynamic_slice_in_dim(value, which * half, half, 0)
-
-    packed = pack_weights(weight_mid, weight_out)
-    block_in = after(block_in, packed)
-    mine, others = my_rows(block_in, core), my_rows(block_in, 1 - core)
+    mine, others, packed = opening(place, block_in, weight_mid, weight_out)
     pieces = [swap(others, "chan", 1), swap(mine, "chan", 2)]
     pieces.append(swap(after(others, pieces[1]), "chan", 3))
 
@@ -1602,7 +1638,12 @@
     weights_in = [own_in, swap(own_in, "chan", 1)]
     gathered = lax.all_gather(packed, "dp", axis=0)
 
-    params = pack_params([gain_in, bias_in, gain_mid, bias_mid, gate_bias], kernel_near, kernel_far)
+    params, stem_par = pack_params(
+        [gain_in, bias_in, gain_mid, bias_mid, gate_bias],
+        kernel_near,
+        kernel_far,
+        [stem_gain, stem_bias],
+    )
     par_own = ordered(core == 1, params, swap(params, "chan", 1), 1)
     pars = [par_own]
     same = lax.dynamic_slice_in_dim(same_video, core * (clips // 2), clips // 2, 0)
@@ -1643,43 +1684,50 @@
 
         return run
 
-    pre_in, sums_in, full_in = first_conv(
-        order, place, block_in, pieces, weights_in, after(extra, par_own)
-    )
-    pre_in_oth = swap(pre_in, "chan", 2)
+    pre_in, pre_in16, sums_in, cross_in, near_in, away_in = first_conv(
+        order, place, block_in, pieces, weights_in, extra, par_own
+    )
 
     blocks = gathered
     if weight_mid.shape[0] % BLOCK:
         blocks = gathered[:, : weight_mid.shape[0]].reshape(1, -1, narrow)
-    blocks = after(blocks, sums_in)
-    weights_mid = [blocks, swap(blocks, "chan", 1)]
+
+    def mid_blocks(mark):
+        own = after(blocks, mark)
+        return [own, swap(own, "chan", 1)]
+
 
     def out_rows(mark):
         parts, first, size = after(gathered, mark), weight_mid.shape[0], weight_out.shape[0]
         parts = [parts[:, first + at * size : first + (at + 1) * size] for at in range(4)]
         return jnp.concatenate([part.reshape(-1, narrow) for part in parts], 1)
 
-    def own_gate(mark):
-        return gate_own(count, same, pre_in, mark, pars[0])
-
-    stats_in = both_sums(
-        sums_in,
-        [None, None, job("full_out", out_rows), None, job("own", own_gate)],
-    )
-    pars.append(swap(after(par_own, stats_in[0]), "chan", 2))
+    cross_got = swap(cross_in, "chan", 2)
+    pre_in_oth = swap(after(pre_in16, cross_got), "chan", 2)
+    sums_in = sums_in + cross_got[:8]
+    stats_in = sum_over(
+        sums_in + swap(sums_in, "chan", 1),
+        "dp",
+        [
+            None,
+            in_turn(job("weights_mid", mid_blocks), job("full_out", out_rows)),
+        ],
+    )
+    pars.append(cross_got)
+    weights_mid = made["weights_mid"]
     full_out = made["full_out"]
 
     out_across = swap(after(full_out, stats_in), "chan", 2)
 
-    mixed, pre_mid, pre_mid16, sums_mid = gate_mid(
-        count, place, same, made["own"][0], pre_in_oth, stats_in[1], pars[1], weights_mid
+    mixed, gates, pre_mid, pre_mid16, sums_mid = gate_mid(
+        count, place, same, pre_in, pre_in_oth, stats_in, pars, weights_mid
     )
     pre_mid_oth = swap(pre_mid16, "chan", 2)
-    stats_stem = after(stats_in[0], sums_mid)
+    stats_stem = after(stats_in, sums_mid)
 
     def stem_half(mark):
         return stem_output(
-            stem_count, place, after(pre_stem, mark), stem_grad, stats_stem, stem_gain, stem_bias, quarter
+            stem_count, place, after(pre_stem, mark), stem_grad, stats_stem, stem_par, quarter
         )
 
     def slab_of(mark):
@@ -1702,10 +1750,7 @@
     second_peer = swap(second, "chan", 1)
     pre_out, sums_out = last_conv(place, second, second_peer, full_out, extra)
     slab_across = swap(after(made["slab"], stats_mid), "chan", 2)
-    stats_out = sum_over(sums_out, "dp", [
-        job("near_in", lambda mark: lax.dynamic_slice_in_dim(after(full_in, mark), chan * quarter, quarter, 0)),
-        job("away_in", lambda mark: lax.dynamic_slice_in_dim(after(full_in, mark), (chan ^ 2) * quarter, quarter, 0)),
-    ])
+    stats_out = sum_over(sums_out, "dp")
     stats_out = after(stats_out, slab_across)
     out_peers = [swap(after(value, stats_out), "chan", 1) for value in (full_out, out_across)]
     weights_out = [full_out, out_peers[0], out_across, out_peers[1]]
@@ -1720,8 +1765,8 @@
     def stem_part(chunk, start):
         def work(mark):
             return stem_back(
-                stem_count, place, after(pre_stem, mark), stem_grad, stats_in[0], stats_out, stem_gain,
-                stem_bias, stem_rows, stem_pick, start and made[start], chunk, 4,
+                stem_count, place, after(pre_stem, mark), stem_grad, stats_in, stats_out,
+                stem_par, stem_rows, stem_pick, start and made[start], chunk, 4,
             )
 
         return job(f"stem{chunk}", work)
@@ -1765,11 +1810,11 @@
     slopes = made["slopes"]
     sum_out = lax.psum_scatter(made["out1"], "dp", scatter_dimension=0, tiled=True)
     stem_first = swap(made["stem3"], "dp", bits[0])
-    far_in = swap(made["away_in"], "chan", 2)
+    far_in = swap(after(away_in, sums_mid_back), "chan", 2)
 
     grad_in, grad_in16, sums_in_back = mid_back(
         count, place, same, slopes, grad_mid_oth, pre_mid_oth, stats_mid[1], back_mid[1], pre_in,
-        made["own"][1], stats_in[0], pars, weights_mid, aways_mid,
+        gates, stats_in, pars, weights_mid, aways_mid,
     )
     grad_in_oth = swap(grad_in16, "chan", 2)
 
@@ -1797,16 +1842,19 @@
 
     def own_in_back(mark):
         return in_own(
-            count, place, grad_in, pre_in, stats_in[0], mark, pars[0], block_in, pieces
+            count, place, grad_in, pre_in, stats_in, mark, pars[0], block_in, pieces
         )
+
+    def stem_next(mark):
+        return made["stem3"] + after(stem_first, mark)
 
     back_in = both_sums(
         sums_in_back,
         [
-            lambda mark: stem_first,
+            None,
             job("mid", mid_part),
-            None,
-            mid_first,
+            job("stem_total", stem_next),
+            in_turn(mid_first, lambda mark: grad_in_oth),
             job("in", own_in_back),
         ],
     )
@@ -1814,28 +1862,28 @@
     grad_own, keep, send = made["in"]
     got = swap(send, "chan", 1)
     grad_pre = in_other(
-        count, place, after(grad_own, send), grad_in_oth, pre_in_oth, stats_in[1], back_in[1], pars[1]
+        count, place, after(grad_own, send), grad_in_oth, pre_in_oth, stats_in, back_in[1], pars[1]
     )
     grad_peer = swap(grad_pre, "chan", 1)
-    mark, stem_total, stem_got = grad_pre, made["stem3"], stem_first
+    mark, stem_total = grad_pre, made["stem_total"]
     assert len(bits) > 1
     last = len(bits) - 1
     for at, bit in enumerate(bits):
         got = after(got, mark, sum_out) if at == 1 else after(got, mark)
         keep, send = halve(place, keep, [got], bits[at:], bit, at == 0)
         got = swap(send, "dp", bit)
+        mark = send
         if at < last:
-            mark = mid_step(at + 1)(send)
+            mark = mid_step(at + 1)(mark)
             if at == 0:
-                near = after(made["near_in"], mark)
+                near = after(near_in, mark)
                 mark = grad_block_in = input_grad(
                     place, grad_pre, grad_peer, near, far_in, grad_total
                 )
+            stem_got = swap(stem_total, "dp", bits[at + 1])
             mark = stem_total = after(stem_total, mark) + stem_got
-            stem_got = swap(stem_total, "dp", bits[at + 1])
     sum_mid = after(made["keep"], send) + swap(made["send"], "dp", bit).astype(jnp.float32)
-    stem_total = after(stem_total, sum_mid) + stem_got
-    sum_in = keep + after(got, stem_total).astype(jnp.float32)
+    sum_in = keep + after(got, sum_mid).astype(jnp.float32)
     center_grad, diff_grad = stem_grads(stem_total, outs)
 
     def my_columns(value):

time: 264 us -> 252 us (0.955)
  local copies, waits for them, and re-layouts: 31.7 us -> 10 us
  waiting for transfers between devices: 55.8 us -> 60.8 us
  starting transfers between devices: 68.9 us -> 72.3 us
  Pallas kernels: 88.6 us -> 91.9 us
    unnamed x148 -> x88, local copies, waits for them, and re-layouts: 13.8 us -> 4.42 us
    ppermute x65 -> x64, waiting for transfers between devices: 54.5 us -> 60.8 us  [swap(): return lax.ppermute(value, axis, [(at, at ^ bit) for at in range(size)])]
    dynamic_slice x3 -> x0, local copies, waits for them, and re-layouts: 5.74 us -> none  [the longest x1 2.41 us: my_rows(): return lax.dynamic_slice_in_dim(value, which * half, half, 0)]
    ppermute x65 -> x64, starting transfers between devices: 68.8 us -> 72.2 us  [swap(): return lax.ppermute(value, axis, [(at, at ^ bit) for at in range(size)])]
    pallas_call x29 -> x28, Pallas kernels: 81.7 us -> 82.4 us  [run(): call(*[pltpu.with_memory_space_constraint(arg, pltpu.HBM) if spec is remo...]
  transfers between devices with their start and end apart: 67 -> 66, of which waited for: 29 -> 32; matrix products, arithmetic and copies ran while one was open for 9% -> 4% of each run, Pallas kernels for 29% -> 31%
where the time goes in v4:
time: 252 us
  Pallas kernels  91.9 us (36%)
  starting transfers between devices  72.3 us (29%)
  waiting for transfers between devices  60.8 us (24%)
  between operations  14.9 us (6%)
  local copies, waits for them, and re-layouts  10 us (4%)
    pallas_call x28, Pallas kernels, run(): call(*[pltpu.with_memory_space_constraint(arg, pltpu.HBM) if spec is remo...  82.4 us
    ppermute x64, starting transfers between devices, swap(): return lax.ppermute(value, axis, [(at, at ^ bit) for at in range(size)])  72.2 us
    ppermute x64, waiting for transfers between devices, swap(): return lax.ppermute(value, axis, [(at, at ^ bit) for at in range(size)])  60.8 us
    pallas_call x4, Pallas kernels, stem_back(): pl.pallas_call(functools.partial(stem_back_body, count, first), grid=(1,)...  9.45 us
  transfers between devices with their start and end apart: 66, of which 32 were waited for; matrix products, arithmetic and copies ran while one was open for 4% of the time, Pallas kernels for 31%

profile of v4, /device:TPU:0, one launch (start us, length us, event | category | flops | bytes accessed | tf_op | source)
XLA Modules:
  0.0 251.7 jit_solution(240131203793485941)
XLA Ops:
  7.4 3.0 %shard_map.348 = (bf16[784,512]{1,0:T(8,128)(2,1)}, bf16[784,512]{1,0:T(8,128)(2,1)}, bf16[832,128]{1,0:T(8,128)(2,1)}) custom-call(s32[2]{0:T(128)S(1)} %pad_add_fusion.place_ref, bf16[1568,512]{1,0:T(8,128)(2,1)} %block_ref.7, bf16[576,128]{1,0:T(8,128)(2,1)} %mid_ref.1, bf16[64,512]{1,0:T(8,128)(2,1)} %out_ref.1), custom_call_target="tpu_custom_call" | custom-call | flops 300000000 | tf_op jit(solution)/shard_map/pallas_call | solution.py:70
  10.5 3.0 %collective-permute-start.1 = (bf16[784,512]{1,0:T(8,128)(2,1)}, bf16[784,512]{1,0:T(8,128)(2,1)S(1)}, u32[]{:S(2)}, u32[]{:S(2)}) collective-permute-start(bf16[784,512]{1,0:T(8,128)(2,1)} %get-tuple-element.135), channel_id=1, source_target_pairs={{0,2},{1,3},{2,0},{3,1},{4,6},{5,7},{6,4},{7,5},{8,10},{9,11},{10,... | collective-permute-start | bytes 2408456 | tf_op jit(solution)/shard_map/ppermute | solution.py:1496
  13.5 2.6 %collective-permute-start.3 = (bf16[256,128]{1,0:T(8,128)(2,1)S(1)}, bf16[256,128]{1,0:T(8,128)(2,1)S(1)}, u32[]{:S(2)}, u32[]{:S(2)}) collective-permute-start(bf16[256,128]{1,0:T(8,128)(2,1)S(1)} %copy-done.36), channel_id=1, source_target_pairs={{0,16},{4,20},{8,24},{12,28},{16,0},{20,4},{24,8},{28,12},{1,17},{... | collective-permute-start | bytes 196616 | tf_op jit(solution)/shard_map/ppermute | solution.py:1496
  16.1 2.9 %collective-permute-done.3 = bf16[256,128]{1,0:T(8,128)(2,1)S(1)} collective-permute-done((bf16[256,128]{1,0:T(8,128)(2,1)S(1)}, bf16[256,128]{1,0:T(8,128)(2,1)S(1)}, u32[]{:S(2)}, u32[]{:S(2)}) %collective-permute-start.3) | collective-permute-done | bytes 65568 | tf_op jit(solution)/shard_map/ppermute | solution.py:1496
  20.4 4.1 %collective-permute-done.4 = bf16[512,128]{1,0:T(8,128)(2,1)S(1)} collective-permute-done((bf16[512,128]{1,0:T(8,128)(2,1)S(1)}, bf16[512,128]{1,0:T(8,128)(2,1)S(1)}, u32[]{:S(2)}, u32[]{:S(2)}) %collective-permute-start.4) | collective-permute-done | bytes 131104 | tf_op jit(solution)/shard_map/ppermute | solution.py:1496
  25.6 6.0 %collective-permute-done.1.across_ref = bf16[784,512]{1,0:T(8,128)(2,1)S(1)} collective-permute-done((bf16[784,512]{1,0:T(8,128)(2,1)}, bf16[784,512]{1,0:T(8,128)(2,1)S(1)}, u32[]{:S(2)}, u32[]{:S(2)}) %collective-permute-start.1) | collective-permute-done | bytes 802848 | tf_op jit(solution)/shard_map/ppermute | solution.py:1496
  32.2 1.5 collective-permute-start.6
  34.0 1.7 copy.47.video_ref
  36.5 7.4 %shard_map.349 = (f32[32,16,256]{2,1,0:T(8,128)}, bf16[32,112,512]{2,1,0:T(8,128)(2,1)}, bf16[7,512,256]{2,1,0:T(8,128)(2,1)}, f32[8,256]{1,0:T(8,128)S(1)}) custom-call(s32[2]{0:T(128)S(1)} %pad_add_fusion.place_ref, bf16[32,15,1024]{2,1,0:T(8,128)(2,1)S(1)} %copy.47.video_ref, bf16[112,112]{1,0:T(8,128)(2,1)S(1)} %reshape.128.weight_ref), custom_call_target="tpu_custom_call" | custom-call | tf_op jit(solution)/shard_map/pallas_call | solution.py:70
  44.0 7.8 %collective-permute-done.2.corner_ref = bf16[784,512]{1,0:T(8,128)(2,1)S(1)} collective-permute-done((bf16[784,512]{1,0:T(8,128)(2,1)}, bf16[784,512]{1,0:T(8,128)(2,1)S(1)}, u32[]{:S(2)}, u32[]{:S(2)}) %collective-permute-start.2) | collective-permute-done | bytes 802848 | tf_op jit(solution)/shard_map/ppermute | solution.py:1496
  51.8 5.2 %shard_map.351 = (f32[784,256]{1,0:T(8,128)}, bf16[784,256]{1,0:T(8,128)(2,1)S(1)}, f32[8,256]{1,0:T(8,128)S(1)}, f32[32,256]{1,0:T(8,128)S(1)}, bf16[512,256]{1,0:T(8,128)(2,1)}, /*index=5*/bf16[512,256]{1,0:T(8,128)(2,1)}) custom-call(s32[2]{0:T(128)S(1)} %pad_add_fusion.place_ref, bf16[1568,512]{1,0:T(8,128)(2,1)} %block_ref.7, ...), custom_call_target="tpu_custom_call" | custom-call | flops 1200000000 | tf_op jit(solution)/shard_map/pallas_call | solution.py:70
  57.0 1.4 collective-permute-start.8
  58.3 2.6 %collective-permute-done.8.par_oth_ref.par_ref = f32[32,256]{1,0:T(8,128)S(1)} collective-permute-done((f32[32,256]{1,0:T(8,128)S(1)}, f32[32,256]{1,0:T(8,128)S(1)}, u32[]{:S(2)}, u32[]{:S(2)}) %collective-permute-start.8) | collective-permute-done | bytes 32800 | tf_op jit(solution)/shard_map/ppermute | solution.py:1496
  62.1 1.9 collective-permute-start.11
  64.1 1.7 collective-permute-done.11
  67.2 1.6 collective-permute-start.12
  71.0 3.1 %collective-permute-start.14 = (f32[8,256]{1,0:T(8,128)S(1)}, f32[8,256]{1,0:T(8,128)S(1)}, u32[]{:S(2)}, u32[]{:S(2)}) collective-permute-start(f32[8,256]{1,0:T(8,128)S(1)} %add.113), channel_id=1, source_target_pairs={{0,16},{4,20},{8,24},{12,28},{16,0},{20,4},{24,8},{28,12},{1,17},{... | collective-permute-start | bytes 24584 | tf_op jit(solution)/shard_map/ppermute | solution.py:1496
  74.1 1.6 collective-permute-done.14
  77.5 10.4 %shard_map.352 = (bf16[1184,512]{1,0:T(8,128)(2,1)}, f32[16,7,8,256]{3,2,1,0:T(8,128)}, f32[784,256]{1,0:T(8,128)}, bf16[784,256]{1,0:T(8,128)(2,1)S(1)}, f32[8,256]{1,0:T(8,128)S(1)}) custom-call(s32[2]{0:T(128)S(1)} %pad_add_fusion.place_ref, s32[2,8]{1,0:T(2,128)S(1)} %pad.4.same_ref, f32[784,256]{1,0:T(8,128)} %get-tuple-element.140.own_ref.pre_ref, ...), custom_call_target="tpu_custom_call" | custom-call | flops 3600000000 | tf_op jit(solution)/shard_map/pallas_call | solution.py:70
  87.9 1.6 collective-permute-start.15
  90.7 1.5 collective-permute-start.17
  92.2 1.8 shard_map.353
  94.4 1.6 collective-permute-start.18
  96.1 1.9 collective-permute-done.18
  98.0 2.6 %collective-permute-start.20 = (f32[8,256]{1,0:T(8,128)S(1)}, f32[8,256]{1,0:T(8,128)S(1)}, u32[]{:S(2)}, u32[]{:S(2)}) collective-permute-start(f32[8,256]{1,0:T(8,128)S(1)} %add.118), channel_id=1, source_target_pairs={{0,16},{4,20},{8,24},{12,28},{16,0},{20,4},{24,8},{28,12},{1,17},{... | collective-permute-start | bytes 24584 | tf_op jit(solution)/shard_map/ppermute | solution.py:1496
  100.6 1.6 shard_map.354.turned_ref
  104.5 2.4 collective-permute-done.21.stats_oth_ref
  106.9 1.8 shard_map.355.mine_ref.second_ref.rows_ref
  111.2 1.6 shard_map.356
  112.7 1.5 collective-permute-start.23
  114.3 2.3 collective-permute-done.23
  116.5 1.7 collective-permute-start.24
  118.2 2.1 collective-permute-done.24
  120.3 1.9 collective-permute-start.25
  122.2 2.8 %collective-permute-done.25 = f32[8,512]{1,0:T(8,128)S(1)} collective-permute-done((f32[8,512]{1,0:T(8,128)S(1)}, f32[8,512]{1,0:T(8,128)S(1)}, u32[]{:S(2)}, u32[]{:S(2)}) %collective-permute-start.25) | collective-permute-done | bytes 16416 | tf_op jit(solution)/shard_map/ppermute | solution.py:1496
  125.0 5.9 %shard_map.357 = (bf16[1568,512]{1,0:T(8,128)(2,1)}, f32[1568,512]{1,0:T(8,128)}, f32[8,512]{1,0:T(8,128)S(1)}, f32[784,512]{1,0:T(8,128)S(1)}, bf16[784,512]{1,0:T(8,128)(2,1)S(1)}) custom-call(s32[2]{0:T(128)S(1)} %pad_add_fusion.place_ref, f32[1568,512]{1,0:T(8,128)S(1)} %get-tuple-element.168.pre_ref, bf16[1568,512]{1,0:T(8,128)(2,1)S(1)} %copy-done.5, ...), custom_call_target="tpu_custom_call" | custom-call | flops 2249999872 | tf_op jit(solution)/shard_map/pallas_call | solution.py:70
  131.6 1.5 collective-permute-start.28
  133.0 2.4 shard_map.358.start_ref
  137.5 1.6 collective-permute-start.30
  139.1 2.2 collective-permute-done.30
  141.3 1.9 collective-permute-start.31
  143.2 2.4 shard_map.360.start_ref
  147.9 1.9 collective-permute-done.33.deltas2_ref
  150.0 3.8 %shard_map.362 = (f32[784,256]{1,0:T(8,128)}, bf16[784,256]{1,0:T(8,128)(2,1)S(1)}, f32[8,256]{1,0:T(8,128)S(1)}) custom-call(s32[2]{0:T(128)S(1)} %pad_add_fusion.place_ref, f32[784,256]{1,0:T(8,128)S(1)} %get-tuple-element.181.keep_ref, bf16[784,256]{1,0:T(8,128)(2,1)S(1)} %collective-permute-done.29.got_ref, ...), custom_call_target="tpu_custom_call" | custom-call | flops 990000000 | tf_op jit(solution)/shard_map/pallas_call | solution.py:70
  160.1 1.6 collective-permute-start.39
  161.8 2.3 shard_map.364
  164.2 2.0 collective-permute-start.40
  166.2 2.4 shard_map.365.start_ref
  169.7 1.9 shard_map.366.slopes_ref
  171.6 2.4 shard_map.367
  174.0 11.5 %shard_map.368 = (f32[784,256]{1,0:T(8,128)}, bf16[784,256]{1,0:T(8,128)(2,1)S(1)}, f32[32,256]{1,0:T(8,128)S(1)}) custom-call(s32[2]{0:T(128)S(1)} %pad_add_fusion.place_ref, s32[2,8]{1,0:T(2,128)S(1)} %pad.4.same_ref, bf16[3,1184,256]{2,1,0:T(8,128)(2,1)S(1)} %shard_map.366.slopes_ref, bf16[784,256]{1,0:T(8,128)(2,1)} %collective-permute-done.41.d_oth_ref, ...), custom_call_target="tpu_custom_call" | custom-call | flops 3449999872 | tf_op jit(solution)/shard_map/pallas_call | solution.py:70
  186.8 4.7 %shard_map.369 = (f32[4608,128]{1,0:T(8,128)}, bf16[2304,128]{1,0:T(8,128)(2,1)S(1)}, bf16[2304,128]{1,0:T(8,128)(2,1)S(1)}) custom-call(s32[2]{0:T(128)S(1)} %pad_add_fusion.place_ref, bf16[512,1152]{1,0:T(8,128)(2,1)S(1)} %copy-done.17, bf16[3,1184,256]{2,1,0:T(8,128)(2,1)S(1)} %shard_map.366.slopes_ref), custom_call_target="tpu_custom_call" | custom-call | flops 1440000000 | tf_op jit(solution)/shard_map/pallas_call | solution.py:70
  195.4 2.3 collective-permute-done.45
  199.5 2.1 collective-permute-done.46
  201.6 2.0 collective-permute-start.48
  203.7 2.2 shard_map.370
  207.8 5.8 %shard_map.371 = (bf16[784,256]{1,0:T(8,128)(2,1)S(1)}, f32[2048,128]{1,0:T(8,128)}, bf16[2048,128]{1,0:T(8,128)(2,1)S(1)}) custom-call(s32[2]{0:T(128)S(1)} %pad_add_fusion.place_ref, f32[784,256]{1,0:T(8,128)} %get-tuple-element.203.d_ref, f32[784,256]{1,0:T(8,128)} %get-tuple-element.140.own_ref.pre_ref, f32[8,256]{1,0:T(8,128)S(1)} %add.114.stats_ref.stats_in_ref, ...), custom_call_target="tpu_custom_call" | custom-call | flops 1350000000 | tf_op jit(solution)/shard_map/pallas_call | solution.py:70
  213.7 1.8 shard_map.372.mine_ref
  216.6 1.5 collective-permute-start.56
  219.8 2.2 shard_map.373
  225.8 2.7 %shard_map.375 = bf16[1568,512]{1,0:T(8,128)(2,1)} custom-call(s32[2]{0:T(128)S(1)} %pad_add_fusion.place_ref, bf16[784,512]{1,0:T(8,128)(2,1)S(1)} %shard_map.372.mine_ref, bf16[784,512]{1,0:T(8,128)(2,1)S(1)} %collective-permute-done.53.peer_ref, bf16[512,256]{1,0:T(8,128)(2,1)S(1)} %copy-done.20, bf16[512,256]{1,0:T(8,128)(2,1)S(1)} %collective-permute-done.56.far_ref, ...), custom_call_target="tpu_custom_call" | custom-call | flops 840000000 | tf_op jit(solution)/shard_map/pallas_call | solution.py:70
  228.6 1.7 collective-permute-start.61
  233.2 2.0 collective-permute-start.63
  239.3 3.5 %collective-permute-done.63 = bf16[576,128]{1,0:T(8,128)(2,1)S(1)} collective-permute-done((bf16[576,128]{1,0:T(8,128)(2,1)S(1)}, bf16[576,128]{1,0:T(8,128)(2,1)S(1)}, u32[]{:S(2)}, u32[]{:S(2)}) %collective-permute-start.63) | collective-permute-done | bytes 147488 | tf_op jit(solution)/shard_map/ppermute | solution.py:1496
  (246 shorter events, 54.7 us)
Async XLA Ops:
  7.2 58.6 %all-gather.3.cloned.1.call-start = ((), (), s32[]{:S(2)}) async-start(), calls=%async_computation.2 | async-start | bytes 1916928 | tf_op jit(solution)/shard_map/all_gather | solution.py:1639
  10.5 219.9 %reduce-scatter.2.cloned.1.call-start = ((), (), s32[]{:S(2)}) async-start(), calls=%async_computation.1 | async-start | bytes 1179648 | tf_op jit(solution)/shard_map/reduce_scatter | solution.py:1811
  10.5 21.1 %collective-permute-start.1 = (bf16[784,512]{1,0:T(8,128)(2,1)}, bf16[784,512]{1,0:T(8,128)(2,1)S(1)}, u32[]{:S(2)}, u32[]{:S(2)}) collective-permute-start(bf16[784,512]{1,0:T(8,128)(2,1)} %get-tuple-element.135), channel_id=1, source_target_pairs={{0,2},{1,3},{2,0},{3,1},{4,6},{5,7},{6,4},{7,5},{8,10},{9,11},{10,... | collective-permute-start | bytes 2408456 | tf_op jit(solution)/shard_map/ppermute | solution.py:1496
  13.5 5.5 %collective-permute-start.3 = (bf16[256,128]{1,0:T(8,128)(2,1)S(1)}, bf16[256,128]{1,0:T(8,128)(2,1)S(1)}, u32[]{:S(2)}, u32[]{:S(2)}) collective-permute-start(bf16[256,128]{1,0:T(8,128)(2,1)S(1)} %copy-done.36), channel_id=1, source_target_pairs={{0,16},{4,20},{8,24},{12,28},{16,0},{20,4},{24,8},{28,12},{1,17},{... | collective-permute-start | bytes 196616 | tf_op jit(solution)/shard_map/ppermute | solution.py:1496
  19.0 5.4 %collective-permute-start.4 = (bf16[512,128]{1,0:T(8,128)(2,1)S(1)}, bf16[512,128]{1,0:T(8,128)(2,1)S(1)}, u32[]{:S(2)}, u32[]{:S(2)}) collective-permute-start(bf16[512,128]{1,0:T(8,128)(2,1)S(1)} %pad_maximum_fusion.2), channel_id=1, source_target_pairs={{0,8},{4,12},{8,0},{12,4},{16,24},{20,28},{24,16},{28,20},{1,9},{5... | collective-permute-start | bytes 393224 | tf_op jit(solution)/shard_map/ppermute | solution.py:1496
  20.4 23.6 %collective-permute-start = (bf16[784,512]{1,0:T(8,128)(2,1)}, bf16[784,512]{1,0:T(8,128)(2,1)}, u32[]{:S(2)}, u32[]{:S(2)}) collective-permute-start(bf16[784,512]{1,0:T(8,128)(2,1)} %get-tuple-element.136), channel_id=1, source_target_pairs={{0,1},{1,0},{2,3},{3,2},{4,5},{5,4},{6,7},{7,6},{8,9},{9,8},{10,11... | collective-permute-start | bytes 2408456 | tf_op jit(solution)/shard_map/ppermute | solution.py:1496
  24.4 7.7 %collective-permute-start.5 = (bf16[1024,128]{1,0:T(8,128)(2,1)S(1)}, bf16[1024,128]{1,0:T(8,128)(2,1)S(1)}, u32[]{:S(2)}, u32[]{:S(2)}) collective-permute-start(bf16[1024,128]{1,0:T(8,128)(2,1)S(1)} %pad_maximum_fusion.1), channel_id=1, source_target_pairs={{0,4},{4,0},{8,12},{12,8},{16,20},{20,16},{24,28},{28,24},{1,5},{5... | collective-permute-start | bytes 786440 | tf_op jit(solution)/shard_map/ppermute | solution.py:1496
  31.6 20.1 %collective-permute-start.2 = (bf16[784,512]{1,0:T(8,128)(2,1)}, bf16[784,512]{1,0:T(8,128)(2,1)S(1)}, u32[]{:S(2)}, u32[]{:S(2)}) collective-permute-start(bf16[784,512]{1,0:T(8,128)(2,1)} %get-tuple-element.136), channel_id=1, source_target_pairs={{0,3},{1,2},{2,1},{3,0},{4,7},{5,6},{6,5},{7,4},{8,11},{9,10},{10,... | collective-permute-start | bytes 2408456 | tf_op jit(solution)/shard_map/ppermute | solution.py:1496
  32.2 11.8 %collective-permute-start.6 = (bf16[2048,128]{1,0:T(8,128)(2,1)S(1)}, bf16[2048,128]{1,0:T(8,128)(2,1)S(1)}, u32[]{:S(2)}, u32[]{:S(2)}) collective-permute-start(bf16[2048,128]{1,0:T(8,128)(2,1)S(1)} %constant_dynamic-update-slice_fusion.own_ref), channel_id=1, source_target_pairs={{0,1},{1,0},{2,3},{3,2},{4,5},{5,4},{6,7},{7,6},{8,9},{9,8},{10,11... | collective-permute-start | bytes 1572872 | tf_op jit(solution)/shard_map/ppermute | solution.py:1496
  33.7 10.2 %collective-permute-start.7 = (f32[24,128]{1,0:T(8,128)S(1)}, f32[24,128]{1,0:T(8,128)S(1)}, u32[]{:S(2)}, u32[]{:S(2)}) collective-permute-start(f32[24,128]{1,0:T(8,128)S(1)} %get-tuple-element.139), channel_id=1, source_target_pairs={{0,1},{1,0},{2,3},{3,2},{4,5},{5,4},{6,7},{7,6},{8,9},{9,8},{10,11... | collective-permute-start | bytes 36872 | tf_op jit(solution)/shard_map/ppermute | solution.py:1496
  57.0 4.0 %collective-permute-start.8 = (f32[32,256]{1,0:T(8,128)S(1)}, f32[32,256]{1,0:T(8,128)S(1)}, u32[]{:S(2)}, u32[]{:S(2)}) collective-permute-start(f32[32,256]{1,0:T(8,128)S(1)} %get-tuple-element.142), channel_id=1, source_target_pairs={{0,2},{1,3},{2,0},{3,1},{4,6},{5,7},{6,4},{7,5},{8,10},{9,11},{10,... | collective-permute-start | bytes 98312 | tf_op jit(solution)/shard_map/ppermute | solution.py:1496
  60.9 1.2 collective-permute-start.10
  62.1 3.7 %collective-permute-start.11 = (f32[8,256]{1,0:T(8,128)S(1)}, f32[8,256]{1,0:T(8,128)S(1)}, u32[]{:S(2)}, u32[]{:S(2)}) collective-permute-start(f32[8,256]{1,0:T(8,128)S(1)} %add.111), channel_id=1, source_target_pairs={{0,4},{4,0},{8,12},{12,8},{16,20},{20,16},{24,28},{28,24},{1,5},{5... | collective-permute-start | bytes 24584 | tf_op jit(solution)/shard_map/ppermute | solution.py:1496
  65.8 3.9 %collective-permute-start.13 = (bf16[8,832,128]{2,1,0:T(8,128)(2,1)}, bf16[8,832,128]{2,1,0:T(8,128)(2,1)}, u32[]{:S(2)}, u32[]{:S(2)}) collective-permute-start(bf16[8,832,128]{2,1,0:T(8,128)(2,1)} %bitcast.74), channel_id=1, source_target_pairs={{0,1},{1,0},{2,3},{3,2},{4,5},{5,4},{6,7},{7,6},{8,9},{9,8},{10,11... | collective-permute-start | bytes 5111816 | tf_op jit(solution)/shard_map/ppermute | solution.py:1496
  65.8 11.7 %collective-permute-start.9 = (bf16[784,256]{1,0:T(8,128)(2,1)S(1)}, bf16[784,256]{1,0:T(8,128)(2,1)S(1)}, u32[]{:S(2)}, u32[]{:S(2)}) collective-permute-start(bf16[784,256]{1,0:T(8,128)(2,1)S(1)} %get-tuple-element.143), channel_id=1, source_target_pairs={{0,2},{1,3},{2,0},{3,1},{4,6},{5,7},{6,4},{7,5},{8,10},{9,11},{10,... | collective-permute-start | bytes 1204232 | tf_op jit(solution)/shard_map/ppermute | solution.py:1496
  67.2 3.8 %collective-permute-start.12 = (f32[8,256]{1,0:T(8,128)S(1)}, f32[8,256]{1,0:T(8,128)S(1)}, u32[]{:S(2)}, u32[]{:S(2)}) collective-permute-start(f32[8,256]{1,0:T(8,128)S(1)} %add.112), channel_id=1, source_target_pairs={{0,8},{4,12},{8,0},{12,4},{16,24},{20,28},{24,16},{28,20},{1,9},{5... | collective-permute-start | bytes 24584 | tf_op jit(solution)/shard_map/ppermute | solution.py:1496
  71.0 4.7 %collective-permute-start.14 = (f32[8,256]{1,0:T(8,128)S(1)}, f32[8,256]{1,0:T(8,128)S(1)}, u32[]{:S(2)}, u32[]{:S(2)}) collective-permute-start(f32[8,256]{1,0:T(8,128)S(1)} %add.113), channel_id=1, source_target_pairs={{0,16},{4,20},{8,24},{12,28},{16,0},{20,4},{24,8},{28,12},{1,17},{... | collective-permute-start | bytes 24584 | tf_op jit(solution)/shard_map/ppermute | solution.py:1496
  75.7 22.3 %collective-permute-start.19 = (bf16[512,512]{1,0:T(8,128)(2,1)S(1)}, bf16[512,512]{1,0:T(8,128)(2,1)S(1)}, u32[]{:S(2)}, u32[]{:S(2)}) collective-permute-start(bf16[512,512]{1,0:T(8,128)(2,1)S(1)} %pad_maximum_fusion.weight_ref.weights0_ref), channel_id=1, source_target_pairs={{0,2},{1,3},{2,0},{3,1},{4,6},{5,7},{6,4},{7,5},{8,10},{9,11},{10,... | collective-permute-start | bytes 1572872 | tf_op jit(solution)/shard_map/ppermute | solution.py:1496
  87.9 16.6 %collective-permute-start.15 = (bf16[784,256]{1,0:T(8,128)(2,1)S(1)}, bf16[784,256]{1,0:T(8,128)(2,1)S(1)}, u32[]{:S(2)}, u32[]{:S(2)}) collective-permute-start(bf16[784,256]{1,0:T(8,128)(2,1)S(1)} %get-tuple-element.151), channel_id=1, source_target_pairs={{0,2},{1,3},{2,0},{3,1},{4,6},{5,7},{6,4},{7,5},{8,10},{9,11},{10,... | collective-permute-start | bytes 1204232 | tf_op jit(solution)/shard_map/ppermute | solution.py:1496
  90.7 3.7 %collective-permute-start.17 = (f32[8,256]{1,0:T(8,128)S(1)}, f32[8,256]{1,0:T(8,128)S(1)}, u32[]{:S(2)}, u32[]{:S(2)}) collective-permute-start(f32[8,256]{1,0:T(8,128)S(1)} %add.115), channel_id=1, source_target_pairs={{0,4},{4,0},{8,12},{12,8},{16,20},{20,16},{24,28},{28,24},{1,5},{5... | collective-permute-start | bytes 24584 | tf_op jit(solution)/shard_map/ppermute | solution.py:1496
  94.4 3.7 %collective-permute-start.18 = (f32[8,256]{1,0:T(8,128)S(1)}, f32[8,256]{1,0:T(8,128)S(1)}, u32[]{:S(2)}, u32[]{:S(2)}) collective-permute-start(f32[8,256]{1,0:T(8,128)S(1)} %add.116), channel_id=1, source_target_pairs={{0,8},{4,12},{8,0},{12,4},{16,24},{20,28},{24,16},{28,20},{1,9},{5... | collective-permute-start | bytes 24584 | tf_op jit(solution)/shard_map/ppermute | solution.py:1496
  98.0 5.2 %collective-permute-start.20 = (f32[8,256]{1,0:T(8,128)S(1)}, f32[8,256]{1,0:T(8,128)S(1)}, u32[]{:S(2)}, u32[]{:S(2)}) collective-permute-start(f32[8,256]{1,0:T(8,128)S(1)} %add.118), channel_id=1, source_target_pairs={{0,16},{4,20},{8,24},{12,28},{16,0},{20,4},{24,8},{28,12},{1,17},{... | collective-permute-start | bytes 24584 | tf_op jit(solution)/shard_map/ppermute | solution.py:1496
  103.2 3.7 %collective-permute-start.21 = (f32[8,256]{1,0:T(8,128)S(1)}, f32[8,256]{1,0:T(8,128)S(1)}, u32[]{:S(2)}, u32[]{:S(2)}) collective-permute-start(f32[8,256]{1,0:T(8,128)S(1)} %add.119.stats_own_ref.stats_ref), channel_id=1, source_target_pairs={{0,2},{1,3},{2,0},{3,1},{4,6},{5,7},{6,4},{7,5},{8,10},{9,11},{10,... | collective-permute-start | bytes 24584 | tf_op jit(solution)/shard_map/ppermute | solution.py:1496
  108.8 2.4 collective-permute-start.22
  108.9 16.1 %collective-permute-start.26 = (bf16[2304,128]{1,0:T(8,128)(2,1)S(1)}, bf16[2304,128]{1,0:T(8,128)(2,1)}, u32[]{:S(2)}, u32[]{:S(2)}) collective-permute-start(bf16[2304,128]{1,0:T(8,128)(2,1)S(1)} %bitcast.80), channel_id=1, source_target_pairs={{0,2},{1,3},{2,0},{3,1},{4,6},{5,7},{6,4},{7,5},{8,10},{9,11},{10,... | collective-permute-start | bytes 1769480 | tf_op jit(solution)/shard_map/ppermute | solution.py:1496
  112.7 3.8 %collective-permute-start.23 = (f32[8,512]{1,0:T(8,128)S(1)}, f32[8,512]{1,0:T(8,128)S(1)}, u32[]{:S(2)}, u32[]{:S(2)}) collective-permute-start(f32[8,512]{1,0:T(8,128)S(1)} %get-tuple-element.169), channel_id=1, source_target_pairs={{0,4},{4,0},{8,12},{12,8},{16,20},{20,16},{24,28},{28,24},{1,5},{5... | collective-permute-start | bytes 49160 | tf_op jit(solution)/shard_map/ppermute | solution.py:1496
  116.5 3.7 %collective-permute-start.24 = (f32[8,512]{1,0:T(8,128)S(1)}, f32[8,512]{1,0:T(8,128)S(1)}, u32[]{:S(2)}, u32[]{:S(2)}) collective-permute-start(f32[8,512]{1,0:T(8,128)S(1)} %add.120), channel_id=1, source_target_pairs={{0,8},{4,12},{8,0},{12,4},{16,24},{20,28},{24,16},{28,20},{1,9},{5... | collective-permute-start | bytes 49160 | tf_op jit(solution)/shard_map/ppermute | solution.py:1496
  120.3 4.6 %collective-permute-start.25 = (f32[8,512]{1,0:T(8,128)S(1)}, f32[8,512]{1,0:T(8,128)S(1)}, u32[]{:S(2)}, u32[]{:S(2)}) collective-permute-start(f32[8,512]{1,0:T(8,128)S(1)} %add.121), channel_id=1, source_target_pairs={{0,16},{4,20},{8,24},{12,28},{16,0},{20,4},{24,8},{28,12},{1,17},{... | collective-permute-start | bytes 49160 | tf_op jit(solution)/shard_map/ppermute | solution.py:1496
  130.9 4.6 %collective-permute-start.27 = (bf16[784,512]{1,0:T(8,128)(2,1)S(1)}, bf16[784,512]{1,0:T(8,128)(2,1)S(1)}, u32[]{:S(2)}, u32[]{:S(2)}) collective-permute-start(bf16[784,512]{1,0:T(8,128)(2,1)S(1)} %get-tuple-element.174), channel_id=1, source_target_pairs={{0,1},{1,0},{2,3},{3,2},{4,5},{5,4},{6,7},{7,6},{8,9},{9,8},{10,11... | collective-permute-start | bytes 2408456 | tf_op jit(solution)/shard_map/ppermute | solution.py:1496
  131.0 15.9 %collective-permute-start.35 = (bf16[512,512]{1,0:T(8,128)(2,1)S(1)}, bf16[512,512]{1,0:T(8,128)(2,1)S(1)}, u32[]{:S(2)}, u32[]{:S(2)}) collective-permute-start(bf16[512,512]{1,0:T(8,128)(2,1)S(1)} %copy-done.15), channel_id=1, source_target_pairs={{0,1},{1,0},{2,3},{3,2},{4,5},{5,4},{6,7},{7,6},{8,9},{9,8},{10,11... | collective-permute-start | bytes 1572872 | tf_op jit(solution)/shard_map/ppermute | solution.py:1496
  131.5 16.4 %collective-permute-start.36 = (bf16[512,512]{1,0:T(8,128)(2,1)S(1)}, bf16[512,512]{1,0:T(8,128)(2,1)S(1)}, u32[]{:S(2)}, u32[]{:S(2)}) collective-permute-start(bf16[512,512]{1,0:T(8,128)(2,1)S(1)} %copy-done.19), channel_id=1, source_target_pairs={{0,1},{1,0},{2,3},{3,2},{4,5},{5,4},{6,7},{7,6},{8,9},{9,8},{10,11... | collective-permute-start | bytes 1572872 | tf_op jit(solution)/shard_map/ppermute | solution.py:1496
  131.6 3.9 %collective-permute-start.28 = (f32[8,512]{1,0:T(8,128)S(1)}, f32[8,512]{1,0:T(8,128)S(1)}, u32[]{:S(2)}, u32[]{:S(2)}) collective-permute-start(f32[8,512]{1,0:T(8,128)S(1)} %get-tuple-element.175.sums_ref), channel_id=1, source_target_pairs={{0,4},{4,0},{8,12},{12,8},{16,20},{20,16},{24,28},{28,24},{1,5},{5... | collective-permute-start | bytes 49160 | tf_op jit(solution)/shard_map/ppermute | solution.py:1496
  136.2 13.8 %collective-permute-start.29 = (bf16[784,256]{1,0:T(8,128)(2,1)S(1)}, bf16[784,256]{1,0:T(8,128)(2,1)S(1)}, u32[]{:S(2)}, u32[]{:S(2)}) collective-permute-start(bf16[784,256]{1,0:T(8,128)(2,1)S(1)} %get-tuple-element.182), channel_id=1, source_target_pairs={{0,2},{1,3},{2,0},{3,1},{4,6},{5,7},{6,4},{7,5},{8,10},{9,11},{10,... | collective-permute-start | bytes 1204232 | tf_op jit(solution)/shard_map/ppermute | solution.py:1496
  137.5 3.7 %collective-permute-start.30 = (f32[8,512]{1,0:T(8,128)S(1)}, f32[8,512]{1,0:T(8,128)S(1)}, u32[]{:S(2)}, u32[]{:S(2)}) collective-permute-start(f32[8,512]{1,0:T(8,128)S(1)} %add.123), channel_id=1, source_target_pairs={{0,8},{4,12},{8,0},{12,4},{16,24},{20,28},{24,16},{28,20},{1,9},{5... | collective-permute-start | bytes 49160 | tf_op jit(solution)/shard_map/ppermute | solution.py:1496
  141.3 4.6 %collective-permute-start.31 = (f32[8,512]{1,0:T(8,128)S(1)}, f32[8,512]{1,0:T(8,128)S(1)}, u32[]{:S(2)}, u32[]{:S(2)}) collective-permute-start(f32[8,512]{1,0:T(8,128)S(1)} %add.124), channel_id=1, source_target_pairs={{0,16},{4,20},{8,24},{12,28},{16,0},{20,4},{24,8},{28,12},{1,17},{... | collective-permute-start | bytes 49160 | tf_op jit(solution)/shard_map/ppermute | solution.py:1496
  146.0 2.0 collective-permute-start.32
  146.0 3.8 %collective-permute-start.33 = (f32[8,512]{1,0:T(8,128)S(1)}, f32[8,512]{1,0:T(8,128)S(1)}, u32[]{:S(2)}, u32[]{:S(2)}) collective-permute-start(f32[8,512]{1,0:T(8,128)S(1)} %shard_map.361.deltas0_ref), channel_id=1, source_target_pairs={{0,2},{1,3},{2,0},{3,1},{4,6},{5,7},{6,4},{7,5},{8,10},{9,11},{10,... | collective-permute-start | bytes 49160 | tf_op jit(solution)/shard_map/ppermute | solution.py:1496
  146.9 3.2 %collective-permute-start.34 = (f32[8,512]{1,0:T(8,128)S(1)}, f32[8,512]{1,0:T(8,128)S(1)}, u32[]{:S(2)}, u32[]{:S(2)}) collective-permute-start(f32[8,512]{1,0:T(8,128)S(1)} %shard_map.361.deltas0_ref), channel_id=1, source_target_pairs={{0,3},{1,2},{2,1},{3,0},{4,7},{5,6},{6,5},{7,4},{8,11},{9,10},{10,... | collective-permute-start | bytes 49160 | tf_op jit(solution)/shard_map/ppermute | solution.py:1496
  153.8 20.2 %collective-permute-start.43 = (bf16[2304,128]{1,0:T(8,128)(2,1)}, bf16[2304,128]{1,0:T(8,128)(2,1)}, u32[]{:S(2)}, u32[]{:S(2)}) collective-permute-start(bf16[2304,128]{1,0:T(8,128)(2,1)} %collective-permute-done.26.away_own_ref), channel_id=1, source_target_pairs={{0,1},{1,0},{2,3},{3,2},{4,5},{5,4},{6,7},{7,6},{8,9},{9,8},{10,11... | collective-permute-start | bytes 1769480 | tf_op jit(solution)/shard_map/ppermute | solution.py:1496
  154.0 19.9 %collective-permute-start.41 = (bf16[784,256]{1,0:T(8,128)(2,1)S(1)}, bf16[784,256]{1,0:T(8,128)(2,1)}, u32[]{:S(2)}, u32[]{:S(2)}) collective-permute-start(bf16[784,256]{1,0:T(8,128)(2,1)S(1)} %get-tuple-element.198), channel_id=1, source_target_pairs={{0,2},{1,3},{2,0},{3,1},{4,6},{5,7},{6,4},{7,5},{8,10},{9,11},{10,... | collective-permute-start | bytes 1204232 | tf_op jit(solution)/shard_map/ppermute | solution.py:1496
  156.5 3.7 %collective-permute-start.38 = (f32[8,256]{1,0:T(8,128)S(1)}, f32[8,256]{1,0:T(8,128)S(1)}, u32[]{:S(2)}, u32[]{:S(2)}) collective-permute-start(f32[8,256]{1,0:T(8,128)S(1)} %add.126), channel_id=1, source_target_pairs={{0,4},{4,0},{8,12},{12,8},{16,20},{20,16},{24,28},{28,24},{1,5},{5... | collective-permute-start | bytes 24584 | tf_op jit(solution)/shard_map/ppermute | solution.py:1496
  160.1 4.0 %collective-permute-start.39 = (f32[8,256]{1,0:T(8,128)S(1)}, f32[8,256]{1,0:T(8,128)S(1)}, u32[]{:S(2)}, u32[]{:S(2)}) collective-permute-start(f32[8,256]{1,0:T(8,128)S(1)} %add.127), channel_id=1, source_target_pairs={{0,8},{4,12},{8,0},{12,4},{16,24},{20,28},{24,16},{28,20},{1,9},{5... | collective-permute-start | bytes 24584 | tf_op jit(solution)/shard_map/ppermute | solution.py:1496
  164.2 4.6 %collective-permute-start.40 = (f32[8,256]{1,0:T(8,128)S(1)}, f32[8,256]{1,0:T(8,128)S(1)}, u32[]{:S(2)}, u32[]{:S(2)}) collective-permute-start(f32[8,256]{1,0:T(8,128)S(1)} %add.128), channel_id=1, source_target_pairs={{0,16},{4,20},{8,24},{12,28},{16,0},{20,4},{24,8},{28,12},{1,17},{... | collective-permute-start | bytes 24584 | tf_op jit(solution)/shard_map/ppermute | solution.py:1496
  168.8 5.2 %collective-permute-start.42 = (f32[8,256]{1,0:T(8,128)S(1)}, f32[8,256]{1,0:T(8,128)S(1)}, u32[]{:S(2)}, u32[]{:S(2)}) collective-permute-start(f32[8,256]{1,0:T(8,128)S(1)} %add.129.back_ref), channel_id=1, source_target_pairs={{0,2},{1,3},{2,0},{3,1},{4,6},{5,7},{6,4},{7,5},{8,10},{9,11},{10,... | collective-permute-start | bytes 24584 | tf_op jit(solution)/shard_map/ppermute | solution.py:1496
  185.5 1.3 collective-permute-start.44
  191.5 12.1 %collective-permute-start.49 = (bf16[2304,128]{1,0:T(8,128)(2,1)S(1)}, bf16[2304,128]{1,0:T(8,128)(2,1)S(1)}, u32[]{:S(2)}, u32[]{:S(2)}) collective-permute-start(bf16[2304,128]{1,0:T(8,128)(2,1)S(1)} %get-tuple-element.208), channel_id=1, source_target_pairs={{0,1},{1,0},{2,3},{3,2},{4,5},{5,4},{6,7},{7,6},{8,9},{9,8},{10,11... | collective-permute-start | bytes 1769480 | tf_op jit(solution)/shard_map/ppermute | solution.py:1496
  191.8 11.9 %collective-permute-start.50 = (bf16[2304,128]{1,0:T(8,128)(2,1)S(1)}, bf16[2304,128]{1,0:T(8,128)(2,1)S(1)}, u32[]{:S(2)}, u32[]{:S(2)}) collective-permute-start(bf16[2304,128]{1,0:T(8,128)(2,1)S(1)} %get-tuple-element.209), channel_id=1, source_target_pairs={{0,1},{1,0},{2,3},{3,2},{4,5},{5,4},{6,7},{7,6},{8,9},{9,8},{10,11... | collective-permute-start | bytes 1769480 | tf_op jit(solution)/shard_map/ppermute | solution.py:1496
  192.1 15.0 %collective-permute-start.51 = (bf16[784,256]{1,0:T(8,128)(2,1)S(1)}, bf16[784,256]{1,0:T(8,128)(2,1)S(1)}, u32[]{:S(2)}, u32[]{:S(2)}) collective-permute-start(bf16[784,256]{1,0:T(8,128)(2,1)S(1)} %get-tuple-element.216), channel_id=1, source_target_pairs={{0,2},{1,3},{2,0},{3,1},{4,6},{5,7},{6,4},{7,5},{8,10},{9,11},{10,... | collective-permute-start | bytes 1204232 | tf_op jit(solution)/shard_map/ppermute | solution.py:1496
  193.3 4.4 %collective-permute-start.45 = (f32[32,256]{1,0:T(8,128)S(1)}, f32[32,256]{1,0:T(8,128)S(1)}, u32[]{:S(2)}, u32[]{:S(2)}) collective-permute-start(f32[32,256]{1,0:T(8,128)S(1)} %add.130), channel_id=1, source_target_pairs={{0,4},{4,0},{8,12},{12,8},{16,20},{20,16},{24,28},{28,24},{1,5},{5... | collective-permute-start | bytes 98312 | tf_op jit(solution)/shard_map/ppermute | solution.py:1496
  194.7 4.8 %collective-permute-start.47 = (f32[56,256]{1,0:T(8,128)S(1)}, f32[56,256]{1,0:T(8,128)S(1)}, u32[]{:S(2)}, u32[]{:S(2)}) collective-permute-start(f32[56,256]{1,0:T(8,128)S(1)} %shard_map.367), channel_id=1, source_target_pairs={{0,4},{4,0},{8,12},{12,8},{16,20},{20,16},{24,28},{28,24},{1,5},{5... | collective-permute-start | bytes 172040 | tf_op jit(solution)/shard_map/ppermute | solution.py:1496
  197.7 3.9 %collective-permute-start.46 = (f32[32,256]{1,0:T(8,128)S(1)}, f32[32,256]{1,0:T(8,128)S(1)}, u32[]{:S(2)}, u32[]{:S(2)}) collective-permute-start(f32[32,256]{1,0:T(8,128)S(1)} %add.131), channel_id=1, source_target_pairs={{0,8},{4,12},{8,0},{12,4},{16,24},{20,28},{24,16},{28,20},{1,9},{5... | collective-permute-start | bytes 98312 | tf_op jit(solution)/shard_map/ppermute | solution.py:1496
  201.6 5.5 %collective-permute-start.48 = (f32[32,256]{1,0:T(8,128)S(1)}, f32[32,256]{1,0:T(8,128)S(1)}, u32[]{:S(2)}, u32[]{:S(2)}) collective-permute-start(f32[32,256]{1,0:T(8,128)S(1)} %add.133), channel_id=1, source_target_pairs={{0,16},{4,20},{8,24},{12,28},{16,0},{20,4},{24,8},{28,12},{1,17},{... | collective-permute-start | bytes 98312 | tf_op jit(solution)/shard_map/ppermute | solution.py:1496
  205.9 16.9 %collective-permute-start.54 = (bf16[2304,128]{1,0:T(8,128)(2,1)S(1)}, bf16[2304,128]{1,0:T(8,128)(2,1)S(1)}, u32[]{:S(2)}, u32[]{:S(2)}) collective-permute-start(bf16[2304,128]{1,0:T(8,128)(2,1)S(1)} %bitcast.58), channel_id=1, source_target_pairs={{0,4},{4,0},{8,12},{12,8},{16,20},{20,16},{24,28},{28,24},{1,5},{5... | collective-permute-start | bytes 1769480 | tf_op jit(solution)/shard_map/ppermute | solution.py:1496
  207.2 6.5 %collective-permute-start.52 = (f32[32,256]{1,0:T(8,128)S(1)}, f32[32,256]{1,0:T(8,128)S(1)}, u32[]{:S(2)}, u32[]{:S(2)}) collective-permute-start(f32[32,256]{1,0:T(8,128)S(1)} %add.134.back_ref), channel_id=1, source_target_pairs={{0,2},{1,3},{2,0},{3,1},{4,6},{5,7},{6,4},{7,5},{8,10},{9,11},{10,... | collective-permute-start | bytes 98312 | tf_op jit(solution)/shard_map/ppermute | solution.py:1496
  213.6 6.2 %collective-permute-start.55 = (bf16[2048,128]{1,0:T(8,128)(2,1)S(1)}, bf16[2048,128]{1,0:T(8,128)(2,1)S(1)}, u32[]{:S(2)}, u32[]{:S(2)}) collective-permute-start(bf16[2048,128]{1,0:T(8,128)(2,1)S(1)} %get-tuple-element.219), channel_id=1, source_target_pairs={{0,1},{1,0},{2,3},{3,2},{4,5},{5,4},{6,7},{7,6},{8,9},{9,8},{10,11... | collective-permute-start | bytes 1572872 | tf_op jit(solution)/shard_map/ppermute | solution.py:1496
  215.5 10.3 %collective-permute-start.53 = (bf16[784,512]{1,0:T(8,128)(2,1)S(1)}, bf16[784,512]{1,0:T(8,128)(2,1)S(1)}, u32[]{:S(2)}, u32[]{:S(2)}) collective-permute-start(bf16[784,512]{1,0:T(8,128)(2,1)S(1)} %shard_map.372.mine_ref), channel_id=1, source_target_pairs={{0,1},{1,0},{2,3},{3,2},{4,5},{5,4},{6,7},{7,6},{8,9},{9,8},{10,11... | collective-permute-start | bytes 2408456 | tf_op jit(solution)/shard_map/ppermute | solution.py:1496
  216.6 9.2 %collective-permute-start.56 = (bf16[512,256]{1,0:T(8,128)(2,1)S(1)}, bf16[512,256]{1,0:T(8,128)(2,1)S(1)}, u32[]{:S(2)}, u32[]{:S(2)}) collective-permute-start(bf16[512,256]{1,0:T(8,128)(2,1)S(1)} %copy-done.40), channel_id=1, source_target_pairs={{0,2},{1,3},{2,0},{3,1},{4,6},{5,7},{6,4},{7,5},{8,10},{9,11},{10,... | collective-permute-start | bytes 786440 | tf_op jit(solution)/shard_map/ppermute | solution.py:1496
  218.6 9.9 %collective-permute-start.58 = (f32[56,256]{1,0:T(8,128)S(1)}, f32[56,256]{1,0:T(8,128)S(1)}, u32[]{:S(2)}, u32[]{:S(2)}) collective-permute-start(f32[56,256]{1,0:T(8,128)S(1)} %add.132), channel_id=1, source_target_pairs={{0,8},{4,12},{8,0},{12,4},{16,24},{20,28},{24,16},{28,20},{1,9},{5... | collective-permute-start | bytes 172040 | tf_op jit(solution)/shard_map/ppermute | solution.py:1496
  222.0 8.3 %collective-permute-start.57 = (bf16[1024,128]{1,0:T(8,128)(2,1)S(1)}, bf16[1024,128]{1,0:T(8,128)(2,1)S(1)}, u32[]{:S(2)}, u32[]{:S(2)}) collective-permute-start(bf16[1024,128]{1,0:T(8,128)(2,1)S(1)} %bitcast.60), channel_id=1, source_target_pairs={{0,4},{4,0},{8,12},{12,8},{16,20},{20,16},{24,28},{28,24},{1,5},{5... | collective-permute-start | bytes 786440 | tf_op jit(solution)/shard_map/ppermute | solution.py:1496
  223.4 9.1 %collective-permute-start.60 = (bf16[1152,128]{1,0:T(8,128)(2,1)S(1)}, bf16[1152,128]{1,0:T(8,128)(2,1)S(1)}, u32[]{:S(2)}, u32[]{:S(2)}) collective-permute-start(bf16[1152,128]{1,0:T(8,128)(2,1)S(1)} %bitcast.59), channel_id=1, source_target_pairs={{0,8},{4,12},{8,0},{12,4},{16,24},{20,28},{24,16},{28,20},{1,9},{5... | collective-permute-start | bytes 884744 | tf_op jit(solution)/shard_map/ppermute | solution.py:1496
  228.6 7.1 %collective-permute-start.61 = (f32[56,256]{1,0:T(8,128)S(1)}, f32[56,256]{1,0:T(8,128)S(1)}, u32[]{:S(2)}, u32[]{:S(2)}) collective-permute-start(f32[56,256]{1,0:T(8,128)S(1)} %add.135), channel_id=1, source_target_pairs={{0,16},{4,20},{8,24},{12,28},{16,0},{20,4},{24,8},{28,12},{1,17},{... | collective-permute-start | bytes 172040 | tf_op jit(solution)/shard_map/ppermute | solution.py:1496
  230.9 6.6 %collective-permute-start.59 = (bf16[512,128]{1,0:T(8,128)(2,1)S(1)}, bf16[512,128]{1,0:T(8,128)(2,1)S(1)}, u32[]{:S(2)}, u32[]{:S(2)}) collective-permute-start(bf16[512,128]{1,0:T(8,128)(2,1)S(1)} %bitcast.63), channel_id=1, source_target_pairs={{0,8},{4,12},{8,0},{12,4},{16,24},{20,28},{24,16},{28,20},{1,9},{5... | collective-permute-start | bytes 393224 | tf_op jit(solution)/shard_map/ppermute | solution.py:1496
  233.2 9.6 %collective-permute-start.63 = (bf16[576,128]{1,0:T(8,128)(2,1)S(1)}, bf16[576,128]{1,0:T(8,128)(2,1)S(1)}, u32[]{:S(2)}, u32[]{:S(2)}) collective-permute-start(bf16[576,128]{1,0:T(8,128)(2,1)S(1)} %bitcast.62), channel_id=1, source_target_pairs={{0,16},{4,20},{8,24},{12,28},{16,0},{20,4},{24,8},{28,12},{1,17},{... | collective-permute-start | bytes 442376 | tf_op jit(solution)/shard_map/ppermute | solution.py:1496
  238.1 6.1 %collective-permute-start.62 = (bf16[256,128]{1,0:T(8,128)(2,1)S(1)}, bf16[256,128]{1,0:T(8,128)(2,1)S(1)}, u32[]{:S(2)}, u32[]{:S(2)}) collective-permute-start(bf16[256,128]{1,0:T(8,128)(2,1)S(1)} %bitcast.64), channel_id=1, source_target_pairs={{0,16},{4,20},{8,24},{12,28},{16,0},{20,4},{24,8},{28,12},{1,17},{... | collective-permute-start | bytes 196616 | tf_op jit(solution)/shard_map/ppermute | solution.py:1496
  (43 other events, 642.7 us)
Sparse Core Ops, SparseCore 0:
  10.8 48.4 all-gather.2
  164.3 62.6 reduce-scatter.1

commit v5 on v4

--- a/solution.py
+++ b/solution.py
@@ -15,7 +15,7 @@
 SPAN = SIDE + 2
 
 eps = 1e-05
-vmem_limit = 24 * 1024 * 1024
+vmem_limit = 32 * 1024 * 1024
 flops_per_us = 0.3e9
 
 whole = pl.BlockSpec(memory_space=pltpu.VMEM)
@@ -107,13 +107,13 @@
     return both.reshape(SIDE * BLOCK, early.shape[-1])
 
 
-def down(value, step):
-    zeros = jnp.zeros((abs(step),) + value.shape[1:], value.dtype)
-    if step > 0:
-        return jnp.concatenate([value[step:], zeros])
-    if step < 0:
-        return jnp.concatenate([zeros, value[:step]])
-    return value
+def load_rows(ref, first, lanes):
+    return [ref[pl.ds(first + SIDE * at, 8), lanes] for at in range(SIDE)]
+
+
+def store_rows(ref, first, lanes, rows):
+    for at in range(SIDE):
+        ref[pl.ds(first + SIDE * at, SIDE), lanes] = rows[at][:SIDE]
 
 
 def across(value, step, place):
@@ -133,17 +133,31 @@
             yield step, row, [kernel[row * 3 + col] for col in range(3)]
 
 
-def views_of(value, place):
-    return {step: across(value, step, place) for step in (-2, -1, 0, 1, 2)}
-
-
-def gate_score(change, near, far, offset, place):
-    views = views_of(change, place)
-    score = jnp.broadcast_to(offset, change.shape)
-    for step, row, kernel in taps_of(near, far):
-        term = sum(kernel[col] * views[step * (col - 1)] for col in range(3))
-        score = score + down(term, step * (row - 1))
-    return score
+def row_views(value, place):
+    views = {0: value}
+    for step in (-2, -1, 1, 2):
+        moved = pltpu.roll(value, (-step) % 8, 0)
+        if step == 2:
+            moved = jnp.where(place < 6, moved, 0.0)
+        if step == -2:
+            moved = jnp.where(place > 0, moved, 0.0)
+        views[step] = moved
+    return views
+
+
+def weighted(kernel, views, step):
+    return sum(kernel[col] * views[step * (col - 1)] for col in range(3))
+
+
+def gate_scores(change, near, far, offset, place):
+    scores = [offset] * SIDE
+    for at in range(SIDE):
+        views = row_views(change[at], place)
+        for step, row, kernel in taps_of(near, far):
+            target = at - step * (row - 1)
+            if 0 <= target < SIDE:
+                scores[target] = scores[target] + weighted(kernel, views, step)
+    return scores
 
 
 def conv_chunk(parts, weights, first, rows, sign):
@@ -214,29 +228,40 @@
     scaled = (pre[...].astype(jnp.float32) - center) * rate
     normed = scaled * par[0:1] + par[1:2]
     hidden_ref[pl.ds(0, rows), :] = normed * logistic(normed)
-    at = lane_mask(128)
+    place = lax.broadcasted_iota(jnp.int32, (8, 128), 0)
 
     def lanes_step(chunk, _):
         lanes = lane_part(chunk)
         target = pl.ds(pl.multiple_of(first + chunk * 128, 128), 128)
-        near = [par[5 + tap : 6 + tap, lanes].reshape(1, 1, 128) for tap in range(9)]
-        far = [par[14 + tap : 15 + tap, lanes].reshape(1, 1, 128) for tap in range(9)]
-        offset = par[4:5, lanes].reshape(1, 1, 128)
+        near = [par[5 + tap : 6 + tap, lanes] for tap in range(9)]
+        far = [par[14 + tap : 15 + tap, lanes] for tap in range(9)]
+        offset = par[4:5, lanes]
 
         def clip_step(clip, _):
             view = clip_view(hidden_ref, clip, 56)
             for pair in range(PAIRS):
-                maps = [load_map(view, PIXELS * (2 * pair + seg), lanes) for seg in range(3)]
+                maps = [load_rows(view, PIXELS * (2 * pair + seg), lanes) for seg in range(3)]
                 results = []
                 for seg in range(2):
                     same = same_ref[clip, 2 * pair + seg].astype(jnp.float32)
-                    change = jnp.where(at < SIDE, same * (maps[seg + 1] - maps[seg]), 0.0)
-                    gate = logistic(gate_score(change, near, far, offset, at))
-                    results.append(jnp.where(at < SIDE, maps[seg] * (1.0 + gate), 0.0))
+                    change = [
+                        jnp.where(place < SIDE, same * (later - now), 0.0)
+                        for now, later in zip(maps[seg], maps[seg + 1], strict=True)
+                    ]
+                    scores = gate_scores(change, near, far, offset, place)
+                    gates = [logistic(score) for score in scores]
+                    results.append(
+                        [
+                            jnp.where(place < SIDE, now * (1.0 + gate), 0.0)
+                            for now, gate in zip(maps[seg], gates, strict=True)
+                        ]
+                    )
                     if gates_ref is not None:
-                        gates_ref[SEG * clip + 2 * pair + seg, :, :, lanes] = gate
-                place = pl.ds(pair_row(clip, pair), SIDE * BLOCK)
-                mixed_ref[place, target] = two_maps(*results).astype(jnp.bfloat16)
+                        for row in range(SIDE):
+                            gates_ref[SEG * clip + 2 * pair + seg, row, :, lanes] = gates[row]
+                here = pl.ds(pair_row(clip, pair), SIDE * BLOCK)
+                blocks = [results[seg][row] for row in range(SIDE) for seg in range(2)]
+                mixed_ref[here, target] = jnp.concatenate(blocks).astype(jnp.bfloat16)
             return 0
 
         return lax.fori_loop(0, rows // CLIP, clip_step, 0)
@@ -250,7 +275,8 @@
     same_ref,
     own_ref,
     oth_ref,
-    stats_ref,
+    first_ref,
+    second_ref,
     par_own_ref,
     par_oth_ref,
     weight_own_ref,
@@ -272,18 +298,19 @@
     clips = rows // CLIP
     core, y = place_ref[0] % 2, place_ref[0] // 2
     arrival = move(own_ref, own_here_ref, sems, 0)
+    stats = first_ref[...] + second_ref[...]
     weight_moves = fetch_blocks((weight_own_ref, weight_peer_ref), core, weight_ref, sems, 5)
     mixed_ref[...] = jnp.zeros_like(mixed_ref)
+    gate_half(
+        count, same_ref, oth_ref, rows_of(stats, 4), after_sums(par_oth_ref), hidden_ref, mixed_ref,
+        pl.multiple_of((1 - y) * width, width),
+    )
     arrival.wait()
     gate_half(
-        count, same_ref, own_here_ref, rows_of(stats_ref), par_own_ref, hidden_ref, mixed_ref,
+        count, same_ref, own_here_ref, rows_of(stats), par_own_ref, hidden_ref, mixed_ref,
         pl.multiple_of(y * width, width), gates_ref,
     )
     gates_move = move(gates_ref, gates_out_ref, sems, 2)
-    gate_half(
-        count, same_ref, oth_ref, rows_of(stats_ref, 4), after_sums(par_oth_ref), hidden_ref, mixed_ref,
-        pl.multiple_of((1 - y) * width, width),
-    )
     depth = 2 * width
     for copy in weight_moves:
         copy.wait()
@@ -332,7 +359,7 @@
             jax.ShapeDtypeStruct((rows, width), jnp.bfloat16),
             jax.ShapeDtypeStruct((8, width), jnp.float32),
         ),
-        [scalars, scalars, remote, whole, whole, whole, whole, remote, remote],
+        [scalars, scalars, remote] + [whole] * 5 + [remote, remote],
         (
             pltpu.VMEM((rows + 56, width), jnp.float32),
             pltpu.VMEM((rows + 8, width), jnp.float32),
@@ -344,7 +371,7 @@
         ),
         away=(0, 1, 2),
         lasts=12.0,
-    )(place, same, own, oth, stats, *pars, *weights)
+    )(place, same, own, oth, *stats, *pars, *weights)
 
 
 def mid_slopes(count, grad, pre, stats, back, par, flat_ref, store):
@@ -441,10 +468,7 @@
     rows, width = d_oth_ref.shape
     clips = rows // CLIP
     core, y = place_ref[0] % 2, place_ref[0] // 2
-    arrivals = [
-        move(d_oth_ref, d_here_ref, sems, 1),
-        move(mid_oth_ref, mid_here_ref, sems, 2),
-    ]
+    arrivals = [move(d_oth_ref, d_here_ref, sems, 1), move(mid_oth_ref, mid_here_ref, sems, 2)]
     weight_moves = fetch_blocks((weight_own_ref, weight_peer_ref), core, weight_ref, sems, 10)
     weight_moves += [
         move(away_own_ref, weight_oth_ref.at[:, lane_part(core)], sems, 3),
@@ -497,21 +521,21 @@
         (scaled_ref.shape[0] - rows, width), jnp.float32
     )
     parts_ref[...] = jnp.zeros_like(parts_ref)
-    at = lane_mask(128)
+    place = lax.broadcasted_iota(jnp.int32, (8, 128), 0)
+    inside = place < SIDE
 
     def lanes_step(chunk, _):
-        lanes = pl.ds(pl.multiple_of(chunk * 128, 128), 128)
+        lanes = lane_part(chunk)
 
         def row_of(index):
-            return par_own_ref[index : index + 1, lanes].reshape(1, 1, 128)
+            return par_own_ref[index : index + 1, lanes]
 
         near = [row_of(5 + tap) for tap in range(9)]
         far = [row_of(14 + tap) for tap in range(9)]
         gain, bias = row_of(0), row_of(1)
 
         def add_part(index, value):
-            here = pl.ds(8 * index, 8)
-            parts_ref[here, lanes] += jnp.sum(value, 0)
+            parts_ref[pl.ds(8 * index, 8), lanes] += value
 
         def clip_step(clip, carry):
             view = clip_view(scaled_ref, clip, 56)
@@ -522,38 +546,59 @@
 
         def pair_step(clip, pair, carry, view, target):
             normed = [
-                load_map(view, PIXELS * (2 * pair + seg), lanes) * gain + bias for seg in range(3)
+                [value * gain + bias for value in load_rows(view, PIXELS * (2 * pair + seg), lanes)]
+                for seg in range(3)
             ]
-            parts = [logistic(value) for value in normed]
-            hidden = [value * part for value, part in zip(normed, parts, strict=True)]
+            parts = [[logistic(value) for value in rows] for rows in normed]
+            hidden = [
+                [value * part for value, part in zip(*both, strict=True)]
+                for both in zip(normed, parts, strict=True)
+            ]
             for seg in range(2):
                 same = same_ref[clip, 2 * pair + seg].astype(jnp.float32)
-                change = jnp.where(at < SIDE, same * (hidden[seg + 1] - hidden[seg]), 0.0)
-                views = views_of(change, at)
-                gate = gates_here_ref[SEG * clip + 2 * pair + seg, :, :, lanes]
                 start = 2 * (SPAN * (PAIRS * clip + pair) + 1) + seg
-                d_mixed = jnp.stack([dmix_ref[start + 2 * row, :, lanes] for row in range(SIDE)])
-                d_mixed = jnp.where(at < SIDE, d_mixed, 0.0)
-                d_score = d_mixed * hidden[seg] * (gate * (1.0 - gate))
-                add_part(0, d_score)
-                backs = {step: across(d_score, step, at) for step in (-2, -1, 0, 1, 2)}
-                d_change = None
-                for index, (step, row, kernel) in enumerate(taps_of(near, far)):
-                    here = down(d_score, -step * (row - 1))
-                    for col in range(3):
-                        if index != 4 or col != 1:
-                            add_part(1 + 3 * index + col, here * views[step * (col - 1)])
-                    term = sum(kernel[col] * backs[-step * (col - 1)] for col in range(3))
-                    term = down(term, -step * (row - 1))
-                    d_change = term if d_change is None else d_change + term
-                d_change = jnp.where(at < SIDE, same * d_change, 0.0)
-                d_hidden = d_mixed * (1.0 + gate) - d_change + carry
+                d_mixed, gates, d_score = [], [], []
+                for row in range(SIDE):
+                    gate = gates_here_ref[SEG * clip + 2 * pair + seg, row, :, lanes]
+                    grad = jnp.where(inside, dmix_ref[start + 2 * row, :, lanes], 0.0)
+                    gates.append(gate)
+                    d_mixed.append(grad)
+                    d_score.append(grad * hidden[seg][row] * (gate * (1.0 - gate)))
+                add_part(0, sum(d_score[1:], d_score[0]))
+                sums = [None] * 18
+                d_change = [None] * SIDE
+                for row in range(SIDE):
+                    change = hidden[seg + 1][row] - hidden[seg][row]
+                    views = row_views(jnp.where(inside, same * change, 0.0), place)
+                    backs = row_views(d_score[row], place)
+                    for index, (step, tap_row, kernel) in enumerate(taps_of(near, far)):
+                        other = row - step * (tap_row - 1)
+                        if 0 <= other < SIDE:
+                            for col in range(3):
+                                if index == 4 and col == 1:
+                                    continue
+                                term = d_score[other] * views[step * (col - 1)]
+                                at = 3 * index + col
+                                sums[at] = term if sums[at] is None else sums[at] + term
+                        other = row + step * (tap_row - 1)
+                        if 0 <= other < SIDE:
+                            term = weighted(kernel, backs, -step)
+                            before = d_change[other]
+                            d_change[other] = term if before is None else before + term
+                for at, value in enumerate(sums):
+                    if value is not None:
+                        add_part(1 + at, value)
+                d_change = [jnp.where(inside, same * value, 0.0) for value in d_change]
+                results = []
+                for row in range(SIDE):
+                    d_hidden = d_mixed[row] * (1.0 + gates[row]) - d_change[row] + carry[row]
+                    part, value = parts[seg][row], normed[seg][row]
+                    results.append(d_hidden * (part * (1.0 + value * (1.0 - part))))
                 carry = d_change
-                slope = parts[seg] * (1.0 + normed[seg] * (1.0 - parts[seg]))
-                store_map(target, PIXELS * (2 * pair + seg), lanes, d_hidden * slope)
+                store_rows(target, PIXELS * (2 * pair + seg), lanes, results)
             return carry
 
-        lax.fori_loop(0, clips, clip_step, jnp.zeros((SIDE, 8, 128), jnp.float32))
+        lax.fori_loop(0, clips, clip_step, [jnp.zeros((8, 128), jnp.float32)] * SIDE)
         return 0
 
     lax.fori_loop(0, width // 128, lanes_step, 0)
@@ -703,7 +748,7 @@
         move(weight_ref.at[row_part(chan ^ 2, quarter)], away_ref, sems, 2),
     ]
     total = None
-    for at in range(4):
+    for at in (3, 0, 1, 2):
         if at < 3:
             arrivals[at].wait()
         piece = pieces_ref[at] if at < 3 else corner_ref[...]
@@ -817,7 +862,8 @@
     pre_ref,
     block_ref,
     grad_ref,
-    stats_ref,
+    first_ref,
+    second_ref,
     gain_ref,
     bias_ref,
     weight_ref,
@@ -833,7 +879,7 @@
     rows = keep_ref.shape[0]
     weight_move = move(weight_ref, weight_here_ref, sems, 1)
     core = place_ref[0] % 2
-    center, rate = norm_stats(*rows_of(stats_ref), count)
+    center, rate = norm_stats(*rows_of(first_ref[...] + second_ref[...]), count)
     gain, bias = gain_ref[...], bias_ref[...]
     step = rows // 7
 
@@ -856,11 +902,13 @@
     total_move = move(total_ref, total_out_ref, sems, 0)
     local = 1.0 / (2 * rows)
     weight_move.wait()
+    scale = gain * rate
+    factor = scale * rate * (products * local)
+    offset = scale * (sums * local) - factor * center
 
     def slope_rows(side):
         here = row_part(side, rows)
-        scaled = (pre_ref[here, :] - center) * rate
-        value = gain * rate * (total_ref[here, :] - sums * local - scaled * (products * local))
+        value = scale * total_ref[here, :] - (factor * pre_ref[here, :] + offset)
         return lax.dot_general(
             value.astype(jnp.bfloat16),
             weight_here_ref[...],
@@ -885,7 +933,7 @@
             jax.ShapeDtypeStruct((rows // 2, depth), jnp.float32),
             jax.ShapeDtypeStruct((rows // 2, depth), jnp.bfloat16),
         ),
-        [scalars] + [whole] * 6 + [remote],
+        [scalars] + [whole] * 7 + [remote],
         (
             pltpu.VMEM((rows, width), jnp.float32),
             pltpu.VMEM(weight.shape, weight.dtype),
@@ -893,7 +941,7 @@
         ),
         away=(1,),
         lasts=7.5,
-    )(place, pre, block, grad, stats, gain, bias, weight)
+    )(place, pre, block, grad, *stats, gain, bias, weight)
 
 
 def cross_body(place_ref, keep_ref, got_ref, own_ref, send_ref):
@@ -918,11 +966,12 @@
     )(place, keep, got)
 
 
-def out_delta_body(count, local, stats_ref, sums_ref, back_ref, gain_ref, out_ref):
+def out_delta_body(count, local, stats_ref, sums_ref, first_ref, second_ref, gain_ref, out_ref):
     center, rate = norm_stats(*rows_of(stats_ref), count)
+    back = first_ref[...] + second_ref[...]
     scale = gain_ref[...] * rate
-    first = scale * (back_ref[0:1] / count - sums_ref[0:1] * local)
-    second = scale * rate * (back_ref[1:2] / count - sums_ref[1:2] * local)
+    first = scale * (back[0:1] / count - sums_ref[0:1] * local)
+    second = scale * rate * (back[1:2] / count - sums_ref[1:2] * local)
     put_sums(out_ref, first - second * center, second)
 
 
@@ -930,8 +979,8 @@
     return kernel_call(
         functools.partial(out_delta_body, count, 1.0 / rows),
         jax.ShapeDtypeStruct(stats.shape, jnp.float32),
-        [whole] * 4,
-    )(stats, sums, back, gain)
+        [whole] * 5,
+    )(stats, sums, *back, gain)
 
 
 def mid_slope_body(
@@ -1504,15 +1553,22 @@
 
 def sum_over(value, axis, jobs=()):
     jobs = list(jobs)
+    value, got = open_sum(value, axis, jobs)
+    return value + got
+
+
+def open_sum(value, axis, jobs=()):
     jobs = [job or (lambda mark: mark) for job in jobs]
-    for bit in steps_of(axis):
+    bits = steps_of(axis)
+    for bit in bits:
         got = swap(value, axis, bit)
         if jobs:
             got = after(got, jobs.pop(0)(value))
-        value = value + got
+        if bit != bits[-1]:
+            value = value + got
     for job in jobs:
-        value = after(value, job(value))
-    return value
+        got = after(got, job(value))
+    return value, got
 
 
 def ordered(second, own, other, axis=0):
@@ -1703,27 +1759,24 @@
         return jnp.concatenate([part.reshape(-1, narrow) for part in parts], 1)
 
     cross_got = swap(cross_in, "chan", 2)
+    corner_got = swap(cross_in[:8], "chan", 3)
     pre_in_oth = swap(after(pre_in16, cross_got), "chan", 2)
-    sums_in = sums_in + cross_got[:8]
-    stats_in = sum_over(
-        sums_in + swap(sums_in, "chan", 1),
-        "dp",
-        [
-            None,
-            in_turn(job("weights_mid", mid_blocks), job("full_out", out_rows)),
-        ],
+    sums_in = sums_in + swap(sums_in, "chan", 1) + cross_got[:8] + corner_got
+    open_in = open_sum(
+        sums_in, "dp", [None, in_turn(job("weights_mid", mid_blocks), job("full_out", out_rows))]
     )
     pars.append(cross_got)
     weights_mid = made["weights_mid"]
     full_out = made["full_out"]
 
-    out_across = swap(after(full_out, stats_in), "chan", 2)
+    out_across = swap(after(full_out, open_in), "chan", 2)
 
     mixed, gates, pre_mid, pre_mid16, sums_mid = gate_mid(
-        count, place, same, pre_in, pre_in_oth, stats_in, pars, weights_mid
+        count, place, same, pre_in, pre_in_oth, open_in, pars, weights_mid
     )
     pre_mid_oth = swap(pre_mid16, "chan", 2)
-    stats_stem = after(stats_in, sums_mid)
+    first, second_part = after(open_in, sums_mid)
+    stats_stem = stats_in = first + second_part
 
     def stem_half(mark):
         return stem_output(
@@ -1750,13 +1803,14 @@
     second_peer = swap(second, "chan", 1)
     pre_out, sums_out = last_conv(place, second, second_peer, full_out, extra)
     slab_across = swap(after(made["slab"], stats_mid), "chan", 2)
-    stats_out = sum_over(sums_out, "dp")
-    stats_out = after(stats_out, slab_across)
-    out_peers = [swap(after(value, stats_out), "chan", 1) for value in (full_out, out_across)]
+    open_out = after(open_sum(sums_out, "dp"), slab_across)
+    out_peers = [swap(after(value, open_out), "chan", 1) for value in (full_out, out_across)]
     weights_out = [full_out, out_peers[0], out_across, out_peers[1]]
     block_out, grad_total, sums_back, keep, send = out_back(
-        count, place, pre_out, block_in, block_grad, stats_out, gain_row, bias_row, full_out
-    )
+        count, place, pre_out, block_in, block_grad, open_out, gain_row, bias_row, full_out
+    )
+    first, second_part = after(open_out, sums_back)
+    stats_out = first + second_part
     got = swap(send, "chan", 1)
 
     def cross(mark):
@@ -1771,18 +1825,20 @@
 
         return job(f"stem{chunk}", work)
 
-    back_out = sum_over(
+    open_back = open_sum(
         sums_back, "dp", [stem_part(0, None), job("cross", cross), stem_part(1, "stem0")]
     )
     keep, send = made["cross"]
     got = swap(send, "chan", 2)
-    delta = out_delta(count, rows, stats_out, sums_back, back_out, gain_row)
+    delta = out_delta(count, rows, stats_out, sums_back, open_back, gain_row)
     deltas = [delta] + [swap(delta, "chan", at) for at in (1, 2, 3)]
 
     grad_mid, grad_mid16, sums_mid_back = mid_slope(
         count, place, keep, got, second, pre_mid, stats_mid[0], pars[0], deltas, weights_out
     )
     grad_mid_oth = swap(grad_mid16, "chan", 2)
+    first, second_part = after(open_back, sums_mid_back)
+    back_out = first + second_part
 
     aways_mid = [slab_across, swap(after(slab_across, sums_mid_back), "chan", 1)]
 

time: 252 us -> 250 us (level)
    ppermute x64 -> x65, waiting for transfers between devices: 60.8 us -> 59.3 us  [swap(): return lax.ppermute(value, axis, [(at, at ^ bit) for at in range(size)])]
    ppermute x64 -> x65, starting transfers between devices: 72.2 us -> 73.1 us  [swap(): return lax.ppermute(value, axis, [(at, at ^ bit) for at in range(size)])]
  transfers between devices with their start and end apart: 66 -> 67, of which waited for: 32 -> 29; matrix products, arithmetic and copies ran while one was open for 4% -> 4% of each run, Pallas kernels for 31% -> 31%
where the time goes in v5:
time: 250 us
  Pallas kernels  91.3 us (37%)
  starting transfers between devices  73.2 us (29%)
  waiting for transfers between devices  59.3 us (24%)
  between operations  15 us (6%)
  local copies, waits for them, and re-layouts  9.02 us (4%)
    pallas_call x28, Pallas kernels, run(): call(*[pltpu.with_memory_space_constraint(arg, pltpu.HBM) if spec is remo...  81.9 us
    ppermute x65, starting transfers between devices, swap(): return lax.ppermute(value, axis, [(at, at ^ bit) for at in range(size)])  73.1 us
    ppermute x65, waiting for transfers between devices, swap(): return lax.ppermute(value, axis, [(at, at ^ bit) for at in range(size)])  59.3 us
    pallas_call x4, Pallas kernels, stem_back(): pl.pallas_call(functools.partial(stem_back_body, count, first), grid=(1,)...  9.45 us
  transfers between devices with their start and end apart: 67, of which 29 were waited for; matrix products, arithmetic and copies ran while one was open for 4% of the time, Pallas kernels for 31%

profile of v5, /device:TPU:0, one launch (start us, length us, event | category | flops | bytes accessed | tf_op | source)
XLA Modules:
  0.0 249.6 jit_solution(1528750669290989157)
XLA Ops:
  7.4 3.0 %shard_map.348 = (bf16[784,512]{1,0:T(8,128)(2,1)}, bf16[784,512]{1,0:T(8,128)(2,1)}, bf16[832,128]{1,0:T(8,128)(2,1)}) custom-call(s32[2]{0:T(128)S(1)} %pad_add_fusion.place_ref, bf16[1568,512]{1,0:T(8,128)(2,1)} %block_ref.7, bf16[576,128]{1,0:T(8,128)(2,1)} %mid_ref.1, bf16[64,512]{1,0:T(8,128)(2,1)} %out_ref.1), custom_call_target="tpu_custom_call" | custom-call | flops 300000000 | tf_op jit(solution)/shard_map/pallas_call | solution.py:70
  10.5 3.0 %collective-permute-start.1 = (bf16[784,512]{1,0:T(8,128)(2,1)}, bf16[784,512]{1,0:T(8,128)(2,1)S(1)}, u32[]{:S(2)}, u32[]{:S(2)}) collective-permute-start(bf16[784,512]{1,0:T(8,128)(2,1)} %get-tuple-element.141), channel_id=1, source_target_pairs={{0,2},{1,3},{2,0},{3,1},{4,6},{5,7},{6,4},{7,5},{8,10},{9,11},{10,... | collective-permute-start | bytes 2408456 | tf_op jit(solution)/shard_map/ppermute | solution.py:1545
  13.5 2.6 %collective-permute-start.3 = (bf16[256,128]{1,0:T(8,128)(2,1)S(1)}, bf16[256,128]{1,0:T(8,128)(2,1)S(1)}, u32[]{:S(2)}, u32[]{:S(2)}) collective-permute-start(bf16[256,128]{1,0:T(8,128)(2,1)S(1)} %copy-done.36), channel_id=1, source_target_pairs={{0,16},{4,20},{8,24},{12,28},{16,0},{20,4},{24,8},{28,12},{1,17},{... | collective-permute-start | bytes 196616 | tf_op jit(solution)/shard_map/ppermute | solution.py:1545
  16.1 2.9 %collective-permute-done.3 = bf16[256,128]{1,0:T(8,128)(2,1)S(1)} collective-permute-done((bf16[256,128]{1,0:T(8,128)(2,1)S(1)}, bf16[256,128]{1,0:T(8,128)(2,1)S(1)}, u32[]{:S(2)}, u32[]{:S(2)}) %collective-permute-start.3) | collective-permute-done | bytes 65568 | tf_op jit(solution)/shard_map/ppermute | solution.py:1545
  19.0 1.3 collective-permute-start.4
  20.4 4.1 %collective-permute-done.4 = bf16[512,128]{1,0:T(8,128)(2,1)S(1)} collective-permute-done((bf16[512,128]{1,0:T(8,128)(2,1)S(1)}, bf16[512,128]{1,0:T(8,128)(2,1)S(1)}, u32[]{:S(2)}, u32[]{:S(2)}) %collective-permute-start.4) | collective-permute-done | bytes 131104 | tf_op jit(solution)/shard_map/ppermute | solution.py:1545
  25.6 6.0 %collective-permute-done.1.across_ref = bf16[784,512]{1,0:T(8,128)(2,1)S(1)} collective-permute-done((bf16[784,512]{1,0:T(8,128)(2,1)}, bf16[784,512]{1,0:T(8,128)(2,1)S(1)}, u32[]{:S(2)}, u32[]{:S(2)}) %collective-permute-start.1) | collective-permute-done | bytes 802848 | tf_op jit(solution)/shard_map/ppermute | solution.py:1545
  32.2 1.5 collective-permute-start.6
  34.0 1.7 copy.47.video_ref
  36.5 7.4 %shard_map.349 = (f32[32,16,256]{2,1,0:T(8,128)}, bf16[32,112,512]{2,1,0:T(8,128)(2,1)}, bf16[7,512,256]{2,1,0:T(8,128)(2,1)}, f32[8,256]{1,0:T(8,128)S(1)}) custom-call(s32[2]{0:T(128)S(1)} %pad_add_fusion.place_ref, bf16[32,15,1024]{2,1,0:T(8,128)(2,1)S(1)} %copy.47.video_ref, bf16[112,112]{1,0:T(8,128)(2,1)S(1)} %reshape.128.weight_ref), custom_call_target="tpu_custom_call" | custom-call | tf_op jit(solution)/shard_map/pallas_call | solution.py:70
  44.0 7.8 %collective-permute-done.2.corner_ref = bf16[784,512]{1,0:T(8,128)(2,1)S(1)} collective-permute-done((bf16[784,512]{1,0:T(8,128)(2,1)}, bf16[784,512]{1,0:T(8,128)(2,1)S(1)}, u32[]{:S(2)}, u32[]{:S(2)}) %collective-permute-start.2) | collective-permute-done | bytes 802848 | tf_op jit(solution)/shard_map/ppermute | solution.py:1545
  51.8 4.8 %shard_map.351 = (f32[784,256]{1,0:T(8,128)}, bf16[784,256]{1,0:T(8,128)(2,1)S(1)}, f32[8,256]{1,0:T(8,128)S(1)}, f32[32,256]{1,0:T(8,128)S(1)}, bf16[512,256]{1,0:T(8,128)(2,1)}, /*index=5*/bf16[512,256]{1,0:T(8,128)(2,1)}) custom-call(s32[2]{0:T(128)S(1)} %pad_add_fusion.place_ref, bf16[1568,512]{1,0:T(8,128)(2,1)} %block_ref.7, ...), custom_call_target="tpu_custom_call" | custom-call | flops 1200000000 | tf_op jit(solution)/shard_map/pallas_call | solution.py:70
  56.6 1.4 collective-permute-start.8
  58.8 2.3 collective-permute-done.11
  61.1 1.5 collective-permute-start.12
  62.6 2.2 collective-permute-done.12
  65.7 1.8 collective-permute-start.13
  70.0 2.6 %collective-permute-start.15 = (f32[8,256]{1,0:T(8,128)S(1)}, f32[8,256]{1,0:T(8,128)S(1)}, u32[]{:S(2)}, u32[]{:S(2)}) collective-permute-start(f32[8,256]{1,0:T(8,128)S(1)} %add.117.first_ref), channel_id=1, source_target_pairs={{0,16},{4,20},{8,24},{12,28},{16,0},{20,4},{24,8},{28,12},{1,17},{... | collective-permute-start | bytes 24584 | tf_op jit(solution)/shard_map/ppermute | solution.py:1545
  72.6 2.0 collective-permute-done.15.second_ref
  75.4 1.4 collective-permute-done.9.oth_ref.pre_ref
  76.8 9.1 %shard_map.352 = (bf16[1184,512]{1,0:T(8,128)(2,1)}, f32[16,7,8,256]{3,2,1,0:T(8,128)}, f32[784,256]{1,0:T(8,128)}, bf16[784,256]{1,0:T(8,128)(2,1)S(1)}, f32[8,256]{1,0:T(8,128)S(1)}) custom-call(s32[2]{0:T(128)S(1)} %pad_add_fusion.place_ref, s32[2,8]{1,0:T(2,128)S(1)} %pad.4.same_ref, f32[784,256]{1,0:T(8,128)} %get-tuple-element.146.own_ref.pre_ref, ...), custom_call_target="tpu_custom_call" | custom-call | flops 3600000000 | tf_op jit(solution)/shard_map/pallas_call | solution.py:70
  87.8 2.0 collective-permute-start.18
  89.8 1.8 shard_map.353
  91.6 1.9 collective-permute-start.19
  93.7 1.6 collective-permute-done.19
  95.2 3.1 %collective-permute-start.21 = (f32[8,256]{1,0:T(8,128)S(1)}, f32[8,256]{1,0:T(8,128)S(1)}, u32[]{:S(2)}, u32[]{:S(2)}) collective-permute-start(f32[8,256]{1,0:T(8,128)S(1)} %add.122), channel_id=1, source_target_pairs={{0,16},{4,20},{8,24},{12,28},{16,0},{20,4},{24,8},{28,12},{1,17},{... | collective-permute-start | bytes 24584 | tf_op jit(solution)/shard_map/ppermute | solution.py:1545
  98.3 1.6 shard_map.354.turned_ref
  101.1 2.6 %collective-permute-done.22.stats_oth_ref = f32[8,256]{1,0:T(8,128)S(1)} collective-permute-done((f32[8,256]{1,0:T(8,128)S(1)}, f32[8,256]{1,0:T(8,128)S(1)}, u32[]{:S(2)}, u32[]{:S(2)}) %collective-permute-start.22) | collective-permute-done | bytes 8224 | tf_op jit(solution)/shard_map/ppermute | solution.py:1545
  103.7 1.8 shard_map.355.mine_ref.second_ref.rows_ref
  108.0 1.5 shard_map.356
  109.5 1.7 collective-permute-start.24
  111.3 2.1 collective-permute-done.24
  113.4 1.7 collective-permute-start.25
  115.1 2.0 collective-permute-done.25
  117.1 2.8 %collective-permute-start.26 = (f32[8,512]{1,0:T(8,128)S(1)}, f32[8,512]{1,0:T(8,128)S(1)}, u32[]{:S(2)}, u32[]{:S(2)}) collective-permute-start(f32[8,512]{1,0:T(8,128)S(1)} %add.125.first_ref), channel_id=1, source_target_pairs={{0,16},{4,20},{8,24},{12,28},{16,0},{20,4},{24,8},{28,12},{1,17},{... | collective-permute-start | bytes 49160 | tf_op jit(solution)/shard_map/ppermute | solution.py:1545
  119.9 1.6 collective-permute-done.27.away_own_ref
  121.8 5.8 %shard_map.357 = (bf16[1568,512]{1,0:T(8,128)(2,1)}, f32[1568,512]{1,0:T(8,128)}, f32[8,512]{1,0:T(8,128)S(1)}, f32[784,512]{1,0:T(8,128)S(1)}, bf16[784,512]{1,0:T(8,128)(2,1)S(1)}) custom-call(s32[2]{0:T(128)S(1)} %pad_add_fusion.place_ref, f32[1568,512]{1,0:T(8,128)S(1)} %get-tuple-element.175.pre_ref, bf16[1568,512]{1,0:T(8,128)(2,1)S(1)} %copy-done.5, ...), custom_call_target="tpu_custom_call" | custom-call | flops 2249999872 | tf_op jit(solution)/shard_map/pallas_call | solution.py:70
  128.3 1.6 collective-permute-start.29
  130.0 2.4 shard_map.358.start_ref
  134.1 1.6 collective-permute-start.31
  135.7 2.2 collective-permute-done.31
  137.9 2.5 %collective-permute-start.32 = (f32[8,512]{1,0:T(8,128)S(1)}, f32[8,512]{1,0:T(8,128)S(1)}, u32[]{:S(2)}, u32[]{:S(2)}) collective-permute-start(f32[8,512]{1,0:T(8,128)S(1)} %add.128.first_ref), channel_id=1, source_target_pairs={{0,16},{4,20},{8,24},{12,28},{16,0},{20,4},{24,8},{28,12},{1,17},{... | collective-permute-start | bytes 49160 | tf_op jit(solution)/shard_map/ppermute | solution.py:1545
  140.4 2.4 shard_map.360.start_ref
  144.8 1.9 collective-permute-done.34.deltas2_ref
  147.3 3.8 %shard_map.362 = (f32[784,256]{1,0:T(8,128)}, bf16[784,256]{1,0:T(8,128)(2,1)S(1)}, f32[8,256]{1,0:T(8,128)S(1)}) custom-call(s32[2]{0:T(128)S(1)} %pad_add_fusion.place_ref, f32[784,256]{1,0:T(8,128)S(1)} %get-tuple-element.191.keep_ref, bf16[784,256]{1,0:T(8,128)(2,1)S(1)} %collective-permute-done.30.got_ref, ...), custom_call_target="tpu_custom_call" | custom-call | flops 990000000 | tf_op jit(solution)/shard_map/pallas_call | solution.py:70
  154.7 1.4 shard_map.363.refs_0_
  157.0 1.7 collective-permute-start.40
  158.7 2.3 shard_map.364
  161.1 2.3 collective-permute-start.41
  163.4 2.4 shard_map.365.start_ref
  167.1 1.9 shard_map.366.slopes_ref
  169.0 2.4 shard_map.367
  171.4 12.1 %shard_map.368 = (f32[784,256]{1,0:T(8,128)}, bf16[784,256]{1,0:T(8,128)(2,1)}, f32[32,256]{1,0:T(8,128)S(1)}) custom-call(s32[2]{0:T(128)S(1)} %pad_add_fusion.place_ref, s32[2,8]{1,0:T(2,128)S(1)} %pad.4.same_ref, bf16[3,1184,256]{2,1,0:T(8,128)(2,1)S(1)} %shard_map.366.slopes_ref, bf16[784,256]{1,0:T(8,128)(2,1)} %collective-permute-done.42.d_oth_ref, ...), custom_call_target="tpu_custom_call" | custom-call | flops 3449999872 | tf_op jit(solution)/shard_map/pallas_call | solution.py:70
  184.8 4.8 %shard_map.369 = (f32[4608,128]{1,0:T(8,128)}, bf16[2304,128]{1,0:T(8,128)(2,1)S(1)}, bf16[2304,128]{1,0:T(8,128)(2,1)S(1)}) custom-call(s32[2]{0:T(128)S(1)} %pad_add_fusion.place_ref, bf16[512,1152]{1,0:T(8,128)(2,1)S(1)} %copy-done.17, bf16[3,1184,256]{2,1,0:T(8,128)(2,1)S(1)} %shard_map.366.slopes_ref), custom_call_target="tpu_custom_call" | custom-call | flops 1440000000 | tf_op jit(solution)/shard_map/pallas_call | solution.py:70
  193.1 2.4 collective-permute-done.46
  199.4 2.0 collective-permute-start.49
  201.4 2.2 shard_map.370
  206.2 5.8 %shard_map.371 = (bf16[784,256]{1,0:T(8,128)(2,1)S(1)}, f32[2048,128]{1,0:T(8,128)}, bf16[2048,128]{1,0:T(8,128)(2,1)S(1)}) custom-call(s32[2]{0:T(128)S(1)} %pad_add_fusion.place_ref, f32[784,256]{1,0:T(8,128)} %get-tuple-element.215.d_ref, f32[784,256]{1,0:T(8,128)} %get-tuple-element.146.own_ref.pre_ref, f32[8,256]{1,0:T(8,128)S(1)} %add.119.stats_ref.stats_in_ref, ...), custom_call_target="tpu_custom_call" | custom-call | flops 1350000000 | tf_op jit(solution)/shard_map/pallas_call | solution.py:70
  212.1 2.2 shard_map.372.mine_ref
  217.2 2.2 shard_map.373
  223.3 2.7 %shard_map.375 = bf16[1568,512]{1,0:T(8,128)(2,1)} custom-call(s32[2]{0:T(128)S(1)} %pad_add_fusion.place_ref, bf16[784,512]{1,0:T(8,128)(2,1)S(1)} %shard_map.372.mine_ref, bf16[784,512]{1,0:T(8,128)(2,1)S(1)} %collective-permute-done.54.peer_ref, bf16[512,256]{1,0:T(8,128)(2,1)S(1)} %copy-done.20, bf16[512,256]{1,0:T(8,128)(2,1)S(1)} %collective-permute-done.57.far_ref, ...), custom_call_target="tpu_custom_call" | custom-call | flops 840000000 | tf_op jit(solution)/shard_map/pallas_call | solution.py:70
  226.1 1.6 collective-permute-start.62
  231.1 1.7 collective-permute-start.64
  236.9 3.8 %collective-permute-done.64 = bf16[576,128]{1,0:T(8,128)(2,1)S(1)} collective-permute-done((bf16[576,128]{1,0:T(8,128)(2,1)S(1)}, bf16[576,128]{1,0:T(8,128)(2,1)S(1)}, u32[]{:S(2)}, u32[]{:S(2)}) %collective-permute-start.64) | collective-permute-done | bytes 147488 | tf_op jit(solution)/shard_map/ppermute | solution.py:1545
  (246 shorter events, 52.0 us)
Async XLA Ops:
  7.2 57.6 %all-gather.3.cloned.1.call-start = ((), (), s32[]{:S(2)}) async-start(), calls=%async_computation.2 | async-start | bytes 1916928 | tf_op jit(solution)/shard_map/all_gather | solution.py:1695
  10.5 217.3 %reduce-scatter.2.cloned.1.call-start = ((), (), s32[]{:S(2)}) async-start(), calls=%async_computation.1 | async-start | bytes 1179648 | tf_op jit(solution)/shard_map/reduce_scatter | solution.py:1867
  10.5 21.1 %collective-permute-start.1 = (bf16[784,512]{1,0:T(8,128)(2,1)}, bf16[784,512]{1,0:T(8,128)(2,1)S(1)}, u32[]{:S(2)}, u32[]{:S(2)}) collective-permute-start(bf16[784,512]{1,0:T(8,128)(2,1)} %get-tuple-element.141), channel_id=1, source_target_pairs={{0,2},{1,3},{2,0},{3,1},{4,6},{5,7},{6,4},{7,5},{8,10},{9,11},{10,... | collective-permute-start | bytes 2408456 | tf_op jit(solution)/shard_map/ppermute | solution.py:1545
  13.5 5.5 %collective-permute-start.3 = (bf16[256,128]{1,0:T(8,128)(2,1)S(1)}, bf16[256,128]{1,0:T(8,128)(2,1)S(1)}, u32[]{:S(2)}, u32[]{:S(2)}) collective-permute-start(bf16[256,128]{1,0:T(8,128)(2,1)S(1)} %copy-done.36), channel_id=1, source_target_pairs={{0,16},{4,20},{8,24},{12,28},{16,0},{20,4},{24,8},{28,12},{1,17},{... | collective-permute-start | bytes 196616 | tf_op jit(solution)/shard_map/ppermute | solution.py:1545
  19.0 5.4 %collective-permute-start.4 = (bf16[512,128]{1,0:T(8,128)(2,1)S(1)}, bf16[512,128]{1,0:T(8,128)(2,1)S(1)}, u32[]{:S(2)}, u32[]{:S(2)}) collective-permute-start(bf16[512,128]{1,0:T(8,128)(2,1)S(1)} %pad_maximum_fusion.2), channel_id=1, source_target_pairs={{0,8},{4,12},{8,0},{12,4},{16,24},{20,28},{24,16},{28,20},{1,9},{5... | collective-permute-start | bytes 393224 | tf_op jit(solution)/shard_map/ppermute | solution.py:1545
  20.4 23.6 %collective-permute-start = (bf16[784,512]{1,0:T(8,128)(2,1)}, bf16[784,512]{1,0:T(8,128)(2,1)}, u32[]{:S(2)}, u32[]{:S(2)}) collective-permute-start(bf16[784,512]{1,0:T(8,128)(2,1)} %get-tuple-element.142), channel_id=1, source_target_pairs={{0,1},{1,0},{2,3},{3,2},{4,5},{5,4},{6,7},{7,6},{8,9},{9,8},{10,11... | collective-permute-start | bytes 2408456 | tf_op jit(solution)/shard_map/ppermute | solution.py:1545
  24.4 7.7 %collective-permute-start.5 = (bf16[1024,128]{1,0:T(8,128)(2,1)S(1)}, bf16[1024,128]{1,0:T(8,128)(2,1)S(1)}, u32[]{:S(2)}, u32[]{:S(2)}) collective-permute-start(bf16[1024,128]{1,0:T(8,128)(2,1)S(1)} %pad_maximum_fusion.1), channel_id=1, source_target_pairs={{0,4},{4,0},{8,12},{12,8},{16,20},{20,16},{24,28},{28,24},{1,5},{5... | collective-permute-start | bytes 786440 | tf_op jit(solution)/shard_map/ppermute | solution.py:1545
  31.6 20.1 %collective-permute-start.2 = (bf16[784,512]{1,0:T(8,128)(2,1)}, bf16[784,512]{1,0:T(8,128)(2,1)S(1)}, u32[]{:S(2)}, u32[]{:S(2)}) collective-permute-start(bf16[784,512]{1,0:T(8,128)(2,1)} %get-tuple-element.142), channel_id=1, source_target_pairs={{0,3},{1,2},{2,1},{3,0},{4,7},{5,6},{6,5},{7,4},{8,11},{9,10},{10,... | collective-permute-start | bytes 2408456 | tf_op jit(solution)/shard_map/ppermute | solution.py:1545
  32.2 11.8 %collective-permute-start.6 = (bf16[2048,128]{1,0:T(8,128)(2,1)S(1)}, bf16[2048,128]{1,0:T(8,128)(2,1)S(1)}, u32[]{:S(2)}, u32[]{:S(2)}) collective-permute-start(bf16[2048,128]{1,0:T(8,128)(2,1)S(1)} %constant_dynamic-update-slice_fusion.own_ref), channel_id=1, source_target_pairs={{0,1},{1,0},{2,3},{3,2},{4,5},{5,4},{6,7},{7,6},{8,9},{9,8},{10,11... | collective-permute-start | bytes 1572872 | tf_op jit(solution)/shard_map/ppermute | solution.py:1545
  33.7 10.2 %collective-permute-start.7 = (f32[24,128]{1,0:T(8,128)S(1)}, f32[24,128]{1,0:T(8,128)S(1)}, u32[]{:S(2)}, u32[]{:S(2)}) collective-permute-start(f32[24,128]{1,0:T(8,128)S(1)} %get-tuple-element.145), channel_id=1, source_target_pairs={{0,1},{1,0},{2,3},{3,2},{4,5},{5,4},{6,7},{7,6},{8,9},{9,8},{10,11... | collective-permute-start | bytes 36872 | tf_op jit(solution)/shard_map/ppermute | solution.py:1545
  56.6 4.5 %collective-permute-start.8 = (f32[32,256]{1,0:T(8,128)S(1)}, f32[32,256]{1,0:T(8,128)S(1)}, u32[]{:S(2)}, u32[]{:S(2)}) collective-permute-start(f32[32,256]{1,0:T(8,128)S(1)} %get-tuple-element.148), channel_id=1, source_target_pairs={{0,2},{1,3},{2,0},{3,1},{4,6},{5,7},{6,4},{7,5},{8,10},{9,11},{10,... | collective-permute-start | bytes 98312 | tf_op jit(solution)/shard_map/ppermute | solution.py:1545
  58.0 3.1 %collective-permute-start.11 = (f32[8,256]{1,0:T(8,128)S(1)}, f32[8,256]{1,0:T(8,128)S(1)}, u32[]{:S(2)}, u32[]{:S(2)}) collective-permute-start(f32[8,256]{1,0:T(8,128)S(1)} %slice.64), channel_id=1, source_target_pairs={{0,3},{1,2},{2,1},{3,0},{4,7},{5,6},{6,5},{7,4},{8,11},{9,10},{10,... | collective-permute-start | bytes 24584 | tf_op jit(solution)/shard_map/ppermute | solution.py:1545
  58.5 2.6 %collective-permute-start.10 = (f32[8,256]{1,0:T(8,128)S(1)}, f32[8,256]{1,0:T(8,128)S(1)}, u32[]{:S(2)}, u32[]{:S(2)}) collective-permute-start(f32[8,256]{1,0:T(8,128)S(1)} %get-tuple-element.150), channel_id=1, source_target_pairs={{0,1},{1,0},{2,3},{3,2},{4,5},{5,4},{6,7},{7,6},{8,9},{9,8},{10,11... | collective-permute-start | bytes 24584 | tf_op jit(solution)/shard_map/ppermute | solution.py:1545
  61.1 3.7 %collective-permute-start.12 = (f32[8,256]{1,0:T(8,128)S(1)}, f32[8,256]{1,0:T(8,128)S(1)}, u32[]{:S(2)}, u32[]{:S(2)}) collective-permute-start(f32[8,256]{1,0:T(8,128)S(1)} %fusion), channel_id=1, source_target_pairs={{0,4},{4,0},{8,12},{12,8},{16,20},{20,16},{24,28},{28,24},{1,5},{5... | collective-permute-start | bytes 24584 | tf_op jit(solution)/shard_map/ppermute | solution.py:1545
  64.8 3.9 %collective-permute-start.14 = (bf16[8,832,128]{2,1,0:T(8,128)(2,1)}, bf16[8,832,128]{2,1,0:T(8,128)(2,1)}, u32[]{:S(2)}, u32[]{:S(2)}) collective-permute-start(bf16[8,832,128]{2,1,0:T(8,128)(2,1)} %bitcast.74), channel_id=1, source_target_pairs={{0,1},{1,0},{2,3},{3,2},{4,5},{5,4},{6,7},{7,6},{8,9},{9,8},{10,11... | collective-permute-start | bytes 5111816 | tf_op jit(solution)/shard_map/ppermute | solution.py:1545
  64.8 12.0 %collective-permute-start.9 = (bf16[784,256]{1,0:T(8,128)(2,1)S(1)}, bf16[784,256]{1,0:T(8,128)(2,1)S(1)}, u32[]{:S(2)}, u32[]{:S(2)}) collective-permute-start(bf16[784,256]{1,0:T(8,128)(2,1)S(1)} %get-tuple-element.149), channel_id=1, source_target_pairs={{0,2},{1,3},{2,0},{3,1},{4,6},{5,7},{6,4},{7,5},{8,10},{9,11},{10,... | collective-permute-start | bytes 1204232 | tf_op jit(solution)/shard_map/ppermute | solution.py:1545
  65.7 4.2 %collective-permute-start.13 = (f32[8,256]{1,0:T(8,128)S(1)}, f32[8,256]{1,0:T(8,128)S(1)}, u32[]{:S(2)}, u32[]{:S(2)}) collective-permute-start(f32[8,256]{1,0:T(8,128)S(1)} %add.116), channel_id=1, source_target_pairs={{0,8},{4,12},{8,0},{12,4},{16,24},{20,28},{24,16},{28,20},{1,9},{5... | collective-permute-start | bytes 24584 | tf_op jit(solution)/shard_map/ppermute | solution.py:1545
  70.0 4.6 %collective-permute-start.15 = (f32[8,256]{1,0:T(8,128)S(1)}, f32[8,256]{1,0:T(8,128)S(1)}, u32[]{:S(2)}, u32[]{:S(2)}) collective-permute-start(f32[8,256]{1,0:T(8,128)S(1)} %add.117.first_ref), channel_id=1, source_target_pairs={{0,16},{4,20},{8,24},{12,28},{16,0},{20,4},{24,8},{28,12},{1,17},{... | collective-permute-start | bytes 24584 | tf_op jit(solution)/shard_map/ppermute | solution.py:1545
  74.6 20.6 %collective-permute-start.20 = (bf16[512,512]{1,0:T(8,128)(2,1)S(1)}, bf16[512,512]{1,0:T(8,128)(2,1)S(1)}, u32[]{:S(2)}, u32[]{:S(2)}) collective-permute-start(bf16[512,512]{1,0:T(8,128)(2,1)S(1)} %pad_maximum_fusion.weight_ref.weights0_ref), channel_id=1, source_target_pairs={{0,2},{1,3},{2,0},{3,1},{4,6},{5,7},{6,4},{7,5},{8,10},{9,11},{10,... | collective-permute-start | bytes 1572872 | tf_op jit(solution)/shard_map/ppermute | solution.py:1545
  85.9 15.2 %collective-permute-start.16 = (bf16[784,256]{1,0:T(8,128)(2,1)S(1)}, bf16[784,256]{1,0:T(8,128)(2,1)S(1)}, u32[]{:S(2)}, u32[]{:S(2)}) collective-permute-start(bf16[784,256]{1,0:T(8,128)(2,1)S(1)} %get-tuple-element.157), channel_id=1, source_target_pairs={{0,2},{1,3},{2,0},{3,1},{4,6},{5,7},{6,4},{7,5},{8,10},{9,11},{10,... | collective-permute-start | bytes 1204232 | tf_op jit(solution)/shard_map/ppermute | solution.py:1545
  87.8 3.8 %collective-permute-start.18 = (f32[8,256]{1,0:T(8,128)S(1)}, f32[8,256]{1,0:T(8,128)S(1)}, u32[]{:S(2)}, u32[]{:S(2)}) collective-permute-start(f32[8,256]{1,0:T(8,128)S(1)} %add.118), channel_id=1, source_target_pairs={{0,4},{4,0},{8,12},{12,8},{16,20},{20,16},{24,28},{28,24},{1,5},{5... | collective-permute-start | bytes 24584 | tf_op jit(solution)/shard_map/ppermute | solution.py:1545
  91.6 3.7 %collective-permute-start.19 = (f32[8,256]{1,0:T(8,128)S(1)}, f32[8,256]{1,0:T(8,128)S(1)}, u32[]{:S(2)}, u32[]{:S(2)}) collective-permute-start(f32[8,256]{1,0:T(8,128)S(1)} %add.120), channel_id=1, source_target_pairs={{0,8},{4,12},{8,0},{12,4},{16,24},{20,28},{24,16},{28,20},{1,9},{5... | collective-permute-start | bytes 24584 | tf_op jit(solution)/shard_map/ppermute | solution.py:1545
  95.2 4.7 %collective-permute-start.21 = (f32[8,256]{1,0:T(8,128)S(1)}, f32[8,256]{1,0:T(8,128)S(1)}, u32[]{:S(2)}, u32[]{:S(2)}) collective-permute-start(f32[8,256]{1,0:T(8,128)S(1)} %add.122), channel_id=1, source_target_pairs={{0,16},{4,20},{8,24},{12,28},{16,0},{20,4},{24,8},{28,12},{1,17},{... | collective-permute-start | bytes 24584 | tf_op jit(solution)/shard_map/ppermute | solution.py:1545
  100.0 3.7 %collective-permute-start.22 = (f32[8,256]{1,0:T(8,128)S(1)}, f32[8,256]{1,0:T(8,128)S(1)}, u32[]{:S(2)}, u32[]{:S(2)}) collective-permute-start(f32[8,256]{1,0:T(8,128)S(1)} %add.123.stats_own_ref.stats_ref), channel_id=1, source_target_pairs={{0,2},{1,3},{2,0},{3,1},{4,6},{5,7},{6,4},{7,5},{8,10},{9,11},{10,... | collective-permute-start | bytes 24584 | tf_op jit(solution)/shard_map/ppermute | solution.py:1545
  105.6 2.4 collective-permute-start.23
  105.7 15.8 %collective-permute-start.27 = (bf16[2304,128]{1,0:T(8,128)(2,1)S(1)}, bf16[2304,128]{1,0:T(8,128)(2,1)}, u32[]{:S(2)}, u32[]{:S(2)}) collective-permute-start(bf16[2304,128]{1,0:T(8,128)(2,1)S(1)} %bitcast.80), channel_id=1, source_target_pairs={{0,2},{1,3},{2,0},{3,1},{4,6},{5,7},{6,4},{7,5},{8,10},{9,11},{10,... | collective-permute-start | bytes 1769480 | tf_op jit(solution)/shard_map/ppermute | solution.py:1545
  109.5 3.8 %collective-permute-start.24 = (f32[8,512]{1,0:T(8,128)S(1)}, f32[8,512]{1,0:T(8,128)S(1)}, u32[]{:S(2)}, u32[]{:S(2)}) collective-permute-start(f32[8,512]{1,0:T(8,128)S(1)} %get-tuple-element.176), channel_id=1, source_target_pairs={{0,4},{4,0},{8,12},{12,8},{16,20},{20,16},{24,28},{28,24},{1,5},{5... | collective-permute-start | bytes 49160 | tf_op jit(solution)/shard_map/ppermute | solution.py:1545
  113.4 3.7 %collective-permute-start.25 = (f32[8,512]{1,0:T(8,128)S(1)}, f32[8,512]{1,0:T(8,128)S(1)}, u32[]{:S(2)}, u32[]{:S(2)}) collective-permute-start(f32[8,512]{1,0:T(8,128)S(1)} %add.124), channel_id=1, source_target_pairs={{0,8},{4,12},{8,0},{12,4},{16,24},{20,28},{24,16},{28,20},{1,9},{5... | collective-permute-start | bytes 49160 | tf_op jit(solution)/shard_map/ppermute | solution.py:1545
  117.1 4.6 %collective-permute-start.26 = (f32[8,512]{1,0:T(8,128)S(1)}, f32[8,512]{1,0:T(8,128)S(1)}, u32[]{:S(2)}, u32[]{:S(2)}) collective-permute-start(f32[8,512]{1,0:T(8,128)S(1)} %add.125.first_ref), channel_id=1, source_target_pairs={{0,16},{4,20},{8,24},{12,28},{16,0},{20,4},{24,8},{28,12},{1,17},{... | collective-permute-start | bytes 49160 | tf_op jit(solution)/shard_map/ppermute | solution.py:1545
  127.7 4.7 %collective-permute-start.28 = (bf16[784,512]{1,0:T(8,128)(2,1)S(1)}, bf16[784,512]{1,0:T(8,128)(2,1)S(1)}, u32[]{:S(2)}, u32[]{:S(2)}) collective-permute-start(bf16[784,512]{1,0:T(8,128)(2,1)S(1)} %get-tuple-element.182), channel_id=1, source_target_pairs={{0,1},{1,0},{2,3},{3,2},{4,5},{5,4},{6,7},{7,6},{8,9},{9,8},{10,11... | collective-permute-start | bytes 2408456 | tf_op jit(solution)/shard_map/ppermute | solution.py:1545
  127.7 16.4 %collective-permute-start.36 = (bf16[512,512]{1,0:T(8,128)(2,1)S(1)}, bf16[512,512]{1,0:T(8,128)(2,1)S(1)}, u32[]{:S(2)}, u32[]{:S(2)}) collective-permute-start(bf16[512,512]{1,0:T(8,128)(2,1)S(1)} %copy-done.15), channel_id=1, source_target_pairs={{0,1},{1,0},{2,3},{3,2},{4,5},{5,4},{6,7},{7,6},{8,9},{9,8},{10,11... | collective-permute-start | bytes 1572872 | tf_op jit(solution)/shard_map/ppermute | solution.py:1545
  128.2 16.5 %collective-permute-start.37 = (bf16[512,512]{1,0:T(8,128)(2,1)S(1)}, bf16[512,512]{1,0:T(8,128)(2,1)S(1)}, u32[]{:S(2)}, u32[]{:S(2)}) collective-permute-start(bf16[512,512]{1,0:T(8,128)(2,1)S(1)} %copy-done.19), channel_id=1, source_target_pairs={{0,1},{1,0},{2,3},{3,2},{4,5},{5,4},{6,7},{7,6},{8,9},{9,8},{10,11... | collective-permute-start | bytes 1572872 | tf_op jit(solution)/shard_map/ppermute | solution.py:1545
  128.3 4.1 %collective-permute-start.29 = (f32[8,512]{1,0:T(8,128)S(1)}, f32[8,512]{1,0:T(8,128)S(1)}, u32[]{:S(2)}, u32[]{:S(2)}) collective-permute-start(f32[8,512]{1,0:T(8,128)S(1)} %get-tuple-element.183.sums_ref), channel_id=1, source_target_pairs={{0,4},{4,0},{8,12},{12,8},{16,20},{20,16},{24,28},{28,24},{1,5},{5... | collective-permute-start | bytes 49160 | tf_op jit(solution)/shard_map/ppermute | solution.py:1545
  133.2 14.2 %collective-permute-start.30 = (bf16[784,256]{1,0:T(8,128)(2,1)S(1)}, bf16[784,256]{1,0:T(8,128)(2,1)S(1)}, u32[]{:S(2)}, u32[]{:S(2)}) collective-permute-start(bf16[784,256]{1,0:T(8,128)(2,1)S(1)} %get-tuple-element.192), channel_id=1, source_target_pairs={{0,2},{1,3},{2,0},{3,1},{4,6},{5,7},{6,4},{7,5},{8,10},{9,11},{10,... | collective-permute-start | bytes 1204232 | tf_op jit(solution)/shard_map/ppermute | solution.py:1545
  134.1 3.7 %collective-permute-start.31 = (f32[8,512]{1,0:T(8,128)S(1)}, f32[8,512]{1,0:T(8,128)S(1)}, u32[]{:S(2)}, u32[]{:S(2)}) collective-permute-start(f32[8,512]{1,0:T(8,128)S(1)} %add.127), channel_id=1, source_target_pairs={{0,8},{4,12},{8,0},{12,4},{16,24},{20,28},{24,16},{28,20},{1,9},{5... | collective-permute-start | bytes 49160 | tf_op jit(solution)/shard_map/ppermute | solution.py:1545
  137.9 4.9 %collective-permute-start.32 = (f32[8,512]{1,0:T(8,128)S(1)}, f32[8,512]{1,0:T(8,128)S(1)}, u32[]{:S(2)}, u32[]{:S(2)}) collective-permute-start(f32[8,512]{1,0:T(8,128)S(1)} %add.128.first_ref), channel_id=1, source_target_pairs={{0,16},{4,20},{8,24},{12,28},{16,0},{20,4},{24,8},{28,12},{1,17},{... | collective-permute-start | bytes 49160 | tf_op jit(solution)/shard_map/ppermute | solution.py:1545
  142.8 2.0 collective-permute-start.33
  142.9 3.8 %collective-permute-start.34 = (f32[8,512]{1,0:T(8,128)S(1)}, f32[8,512]{1,0:T(8,128)S(1)}, u32[]{:S(2)}, u32[]{:S(2)}) collective-permute-start(f32[8,512]{1,0:T(8,128)S(1)} %shard_map.361.deltas0_ref), channel_id=1, source_target_pairs={{0,2},{1,3},{2,0},{3,1},{4,6},{5,7},{6,4},{7,5},{8,10},{9,11},{10,... | collective-permute-start | bytes 49160 | tf_op jit(solution)/shard_map/ppermute | solution.py:1545
  144.1 3.2 %collective-permute-start.35 = (f32[8,512]{1,0:T(8,128)S(1)}, f32[8,512]{1,0:T(8,128)S(1)}, u32[]{:S(2)}, u32[]{:S(2)}) collective-permute-start(f32[8,512]{1,0:T(8,128)S(1)} %shard_map.361.deltas0_ref), channel_id=1, source_target_pairs={{0,3},{1,2},{2,1},{3,0},{4,7},{5,6},{6,5},{7,4},{8,11},{9,10},{10,... | collective-permute-start | bytes 49160 | tf_op jit(solution)/shard_map/ppermute | solution.py:1545
  151.1 20.3 %collective-permute-start.44 = (bf16[2304,128]{1,0:T(8,128)(2,1)}, bf16[2304,128]{1,0:T(8,128)(2,1)}, u32[]{:S(2)}, u32[]{:S(2)}) collective-permute-start(bf16[2304,128]{1,0:T(8,128)(2,1)} %collective-permute-done.27.away_own_ref), channel_id=1, source_target_pairs={{0,1},{1,0},{2,3},{3,2},{4,5},{5,4},{6,7},{7,6},{8,9},{9,8},{10,11... | collective-permute-start | bytes 1769480 | tf_op jit(solution)/shard_map/ppermute | solution.py:1545
  151.3 20.1 %collective-permute-start.42 = (bf16[784,256]{1,0:T(8,128)(2,1)S(1)}, bf16[784,256]{1,0:T(8,128)(2,1)}, u32[]{:S(2)}, u32[]{:S(2)}) collective-permute-start(bf16[784,256]{1,0:T(8,128)(2,1)S(1)} %get-tuple-element.210), channel_id=1, source_target_pairs={{0,2},{1,3},{2,0},{3,1},{4,6},{5,7},{6,4},{7,5},{8,10},{9,11},{10,... | collective-permute-start | bytes 1204232 | tf_op jit(solution)/shard_map/ppermute | solution.py:1545
  153.3 3.7 %collective-permute-start.39 = (f32[8,256]{1,0:T(8,128)S(1)}, f32[8,256]{1,0:T(8,128)S(1)}, u32[]{:S(2)}, u32[]{:S(2)}) collective-permute-start(f32[8,256]{1,0:T(8,128)S(1)} %add.129), channel_id=1, source_target_pairs={{0,4},{4,0},{8,12},{12,8},{16,20},{20,16},{24,28},{28,24},{1,5},{5... | collective-permute-start | bytes 24584 | tf_op jit(solution)/shard_map/ppermute | solution.py:1545
  157.0 4.1 %collective-permute-start.40 = (f32[8,256]{1,0:T(8,128)S(1)}, f32[8,256]{1,0:T(8,128)S(1)}, u32[]{:S(2)}, u32[]{:S(2)}) collective-permute-start(f32[8,256]{1,0:T(8,128)S(1)} %add.131), channel_id=1, source_target_pairs={{0,8},{4,12},{8,0},{12,4},{16,24},{20,28},{24,16},{28,20},{1,9},{5... | collective-permute-start | bytes 24584 | tf_op jit(solution)/shard_map/ppermute | solution.py:1545
  161.1 4.7 %collective-permute-start.41 = (f32[8,256]{1,0:T(8,128)S(1)}, f32[8,256]{1,0:T(8,128)S(1)}, u32[]{:S(2)}, u32[]{:S(2)}) collective-permute-start(f32[8,256]{1,0:T(8,128)S(1)} %add.132), channel_id=1, source_target_pairs={{0,16},{4,20},{8,24},{12,28},{16,0},{20,4},{24,8},{28,12},{1,17},{... | collective-permute-start | bytes 24584 | tf_op jit(solution)/shard_map/ppermute | solution.py:1545
  165.8 5.5 %collective-permute-start.43 = (f32[8,256]{1,0:T(8,128)S(1)}, f32[8,256]{1,0:T(8,128)S(1)}, u32[]{:S(2)}, u32[]{:S(2)}) collective-permute-start(f32[8,256]{1,0:T(8,128)S(1)} %add.133.back_ref), channel_id=1, source_target_pairs={{0,2},{1,3},{2,0},{3,1},{4,6},{5,7},{6,4},{7,5},{8,10},{9,11},{10,... | collective-permute-start | bytes 24584 | tf_op jit(solution)/shard_map/ppermute | solution.py:1545
  189.6 11.8 %collective-permute-start.50 = (bf16[2304,128]{1,0:T(8,128)(2,1)S(1)}, bf16[2304,128]{1,0:T(8,128)(2,1)S(1)}, u32[]{:S(2)}, u32[]{:S(2)}) collective-permute-start(bf16[2304,128]{1,0:T(8,128)(2,1)S(1)} %get-tuple-element.220), channel_id=1, source_target_pairs={{0,1},{1,0},{2,3},{3,2},{4,5},{5,4},{6,7},{7,6},{8,9},{9,8},{10,11... | collective-permute-start | bytes 1769480 | tf_op jit(solution)/shard_map/ppermute | solution.py:1545
  189.8 11.6 %collective-permute-start.51 = (bf16[2304,128]{1,0:T(8,128)(2,1)S(1)}, bf16[2304,128]{1,0:T(8,128)(2,1)S(1)}, u32[]{:S(2)}, u32[]{:S(2)}) collective-permute-start(bf16[2304,128]{1,0:T(8,128)(2,1)S(1)} %get-tuple-element.221), channel_id=1, source_target_pairs={{0,1},{1,0},{2,3},{3,2},{4,5},{5,4},{6,7},{7,6},{8,9},{9,8},{10,11... | collective-permute-start | bytes 1769480 | tf_op jit(solution)/shard_map/ppermute | solution.py:1545
  190.2 14.7 %collective-permute-start.52 = (bf16[784,256]{1,0:T(8,128)(2,1)}, bf16[784,256]{1,0:T(8,128)(2,1)}, u32[]{:S(2)}, u32[]{:S(2)}) collective-permute-start(bf16[784,256]{1,0:T(8,128)(2,1)} %get-tuple-element.228), channel_id=1, source_target_pairs={{0,2},{1,3},{2,0},{3,1},{4,6},{5,7},{6,4},{7,5},{8,10},{9,11},{10,... | collective-permute-start | bytes 1204232 | tf_op jit(solution)/shard_map/ppermute | solution.py:1545
  191.0 4.5 %collective-permute-start.46 = (f32[32,256]{1,0:T(8,128)S(1)}, f32[32,256]{1,0:T(8,128)S(1)}, u32[]{:S(2)}, u32[]{:S(2)}) collective-permute-start(f32[32,256]{1,0:T(8,128)S(1)} %add.134), channel_id=1, source_target_pairs={{0,4},{4,0},{8,12},{12,8},{16,20},{20,16},{24,28},{28,24},{1,5},{5... | collective-permute-start | bytes 98312 | tf_op jit(solution)/shard_map/ppermute | solution.py:1545
  192.4 5.0 %collective-permute-start.48 = (f32[56,256]{1,0:T(8,128)S(1)}, f32[56,256]{1,0:T(8,128)S(1)}, u32[]{:S(2)}, u32[]{:S(2)}) collective-permute-start(f32[56,256]{1,0:T(8,128)S(1)} %shard_map.367), channel_id=1, source_target_pairs={{0,4},{4,0},{8,12},{12,8},{16,20},{20,16},{24,28},{28,24},{1,5},{5... | collective-permute-start | bytes 172040 | tf_op jit(solution)/shard_map/ppermute | solution.py:1545
  195.5 3.9 %collective-permute-start.47 = (f32[32,256]{1,0:T(8,128)S(1)}, f32[32,256]{1,0:T(8,128)S(1)}, u32[]{:S(2)}, u32[]{:S(2)}) collective-permute-start(f32[32,256]{1,0:T(8,128)S(1)} %add.135), channel_id=1, source_target_pairs={{0,8},{4,12},{8,0},{12,4},{16,24},{20,28},{24,16},{28,20},{1,9},{5... | collective-permute-start | bytes 98312 | tf_op jit(solution)/shard_map/ppermute | solution.py:1545
  197.3 26.0 %collective-permute-start.57 = (bf16[512,256]{1,0:T(8,128)(2,1)}, bf16[512,256]{1,0:T(8,128)(2,1)S(1)}, u32[]{:S(2)}, u32[]{:S(2)}) collective-permute-start(bf16[512,256]{1,0:T(8,128)(2,1)} %get-tuple-element.243), channel_id=1, source_target_pairs={{0,2},{1,3},{2,0},{3,1},{4,6},{5,7},{6,4},{7,5},{8,10},{9,11},{10,... | collective-permute-start | bytes 786440 | tf_op jit(solution)/shard_map/ppermute | solution.py:1545
  199.4 5.4 %collective-permute-start.49 = (f32[32,256]{1,0:T(8,128)S(1)}, f32[32,256]{1,0:T(8,128)S(1)}, u32[]{:S(2)}, u32[]{:S(2)}) collective-permute-start(f32[32,256]{1,0:T(8,128)S(1)} %add.137), channel_id=1, source_target_pairs={{0,16},{4,20},{8,24},{12,28},{16,0},{20,4},{24,8},{28,12},{1,17},{... | collective-permute-start | bytes 98312 | tf_op jit(solution)/shard_map/ppermute | solution.py:1545
  203.7 16.6 %collective-permute-start.55 = (bf16[2304,128]{1,0:T(8,128)(2,1)S(1)}, bf16[2304,128]{1,0:T(8,128)(2,1)S(1)}, u32[]{:S(2)}, u32[]{:S(2)}) collective-permute-start(bf16[2304,128]{1,0:T(8,128)(2,1)S(1)} %bitcast.58), channel_id=1, source_target_pairs={{0,4},{4,0},{8,12},{12,8},{16,20},{20,16},{24,28},{28,24},{1,5},{5... | collective-permute-start | bytes 1769480 | tf_op jit(solution)/shard_map/ppermute | solution.py:1545
  204.9 7.2 %collective-permute-start.53 = (f32[32,256]{1,0:T(8,128)S(1)}, f32[32,256]{1,0:T(8,128)S(1)}, u32[]{:S(2)}, u32[]{:S(2)}) collective-permute-start(f32[32,256]{1,0:T(8,128)S(1)} %add.138.back_ref), channel_id=1, source_target_pairs={{0,2},{1,3},{2,0},{3,1},{4,6},{5,7},{6,4},{7,5},{8,10},{9,11},{10,... | collective-permute-start | bytes 98312 | tf_op jit(solution)/shard_map/ppermute | solution.py:1545
  212.0 5.2 %collective-permute-start.56 = (bf16[2048,128]{1,0:T(8,128)(2,1)S(1)}, bf16[2048,128]{1,0:T(8,128)(2,1)S(1)}, u32[]{:S(2)}, u32[]{:S(2)}) collective-permute-start(bf16[2048,128]{1,0:T(8,128)(2,1)S(1)} %get-tuple-element.231), channel_id=1, source_target_pairs={{0,1},{1,0},{2,3},{3,2},{4,5},{5,4},{6,7},{7,6},{8,9},{9,8},{10,11... | collective-permute-start | bytes 1572872 | tf_op jit(solution)/shard_map/ppermute | solution.py:1545
  214.4 8.9 %collective-permute-start.54 = (bf16[784,512]{1,0:T(8,128)(2,1)S(1)}, bf16[784,512]{1,0:T(8,128)(2,1)S(1)}, u32[]{:S(2)}, u32[]{:S(2)}) collective-permute-start(bf16[784,512]{1,0:T(8,128)(2,1)S(1)} %shard_map.372.mine_ref), channel_id=1, source_target_pairs={{0,1},{1,0},{2,3},{3,2},{4,5},{5,4},{6,7},{7,6},{8,9},{9,8},{10,11... | collective-permute-start | bytes 2408456 | tf_op jit(solution)/shard_map/ppermute | solution.py:1545
  216.0 10.0 %collective-permute-start.59 = (f32[56,256]{1,0:T(8,128)S(1)}, f32[56,256]{1,0:T(8,128)S(1)}, u32[]{:S(2)}, u32[]{:S(2)}) collective-permute-start(f32[56,256]{1,0:T(8,128)S(1)} %add.136), channel_id=1, source_target_pairs={{0,8},{4,12},{8,0},{12,4},{16,24},{20,28},{24,16},{28,20},{1,9},{5... | collective-permute-start | bytes 172040 | tf_op jit(solution)/shard_map/ppermute | solution.py:1545
  219.4 8.3 %collective-permute-start.58 = (bf16[1024,128]{1,0:T(8,128)(2,1)S(1)}, bf16[1024,128]{1,0:T(8,128)(2,1)S(1)}, u32[]{:S(2)}, u32[]{:S(2)}) collective-permute-start(bf16[1024,128]{1,0:T(8,128)(2,1)S(1)} %bitcast.60), channel_id=1, source_target_pairs={{0,4},{4,0},{8,12},{12,8},{16,20},{20,16},{24,28},{28,24},{1,5},{5... | collective-permute-start | bytes 786440 | tf_op jit(solution)/shard_map/ppermute | solution.py:1545
  221.0 9.5 %collective-permute-start.61 = (bf16[1152,128]{1,0:T(8,128)(2,1)S(1)}, bf16[1152,128]{1,0:T(8,128)(2,1)S(1)}, u32[]{:S(2)}, u32[]{:S(2)}) collective-permute-start(bf16[1152,128]{1,0:T(8,128)(2,1)S(1)} %bitcast.59), channel_id=1, source_target_pairs={{0,8},{4,12},{8,0},{12,4},{16,24},{20,28},{24,16},{28,20},{1,9},{5... | collective-permute-start | bytes 884744 | tf_op jit(solution)/shard_map/ppermute | solution.py:1545
  226.1 7.2 %collective-permute-start.62 = (f32[56,256]{1,0:T(8,128)S(1)}, f32[56,256]{1,0:T(8,128)S(1)}, u32[]{:S(2)}, u32[]{:S(2)}) collective-permute-start(f32[56,256]{1,0:T(8,128)S(1)} %add.139), channel_id=1, source_target_pairs={{0,16},{4,20},{8,24},{12,28},{16,0},{20,4},{24,8},{28,12},{1,17},{... | collective-permute-start | bytes 172040 | tf_op jit(solution)/shard_map/ppermute | solution.py:1545
  228.3 6.9 %collective-permute-start.60 = (bf16[512,128]{1,0:T(8,128)(2,1)S(1)}, bf16[512,128]{1,0:T(8,128)(2,1)S(1)}, u32[]{:S(2)}, u32[]{:S(2)}) collective-permute-start(bf16[512,128]{1,0:T(8,128)(2,1)S(1)} %bitcast.63), channel_id=1, source_target_pairs={{0,8},{4,12},{8,0},{12,4},{16,24},{20,28},{24,16},{28,20},{1,9},{5... | collective-permute-start | bytes 393224 | tf_op jit(solution)/shard_map/ppermute | solution.py:1545
  231.1 9.6 %collective-permute-start.64 = (bf16[576,128]{1,0:T(8,128)(2,1)S(1)}, bf16[576,128]{1,0:T(8,128)(2,1)S(1)}, u32[]{:S(2)}, u32[]{:S(2)}) collective-permute-start(bf16[576,128]{1,0:T(8,128)(2,1)S(1)} %bitcast.62), channel_id=1, source_target_pairs={{0,16},{4,20},{8,24},{12,28},{16,0},{20,4},{24,8},{28,12},{1,17},{... | collective-permute-start | bytes 442376 | tf_op jit(solution)/shard_map/ppermute | solution.py:1545
  235.8 6.3 %collective-permute-start.63 = (bf16[256,128]{1,0:T(8,128)(2,1)S(1)}, bf16[256,128]{1,0:T(8,128)(2,1)S(1)}, u32[]{:S(2)}, u32[]{:S(2)}) collective-permute-start(bf16[256,128]{1,0:T(8,128)(2,1)S(1)} %bitcast.64), channel_id=1, source_target_pairs={{0,16},{4,20},{8,24},{12,28},{16,0},{20,4},{24,8},{28,12},{1,17},{... | collective-permute-start | bytes 196616 | tf_op jit(solution)/shard_map/ppermute | solution.py:1545
  (43 other events, 642.5 us)
Sparse Core Ops, SparseCore 0:
  10.8 48.4 all-gather.2
  161.2 63.5 reduce-scatter.1

commit v6 on v5

--- a/solution.py
+++ b/solution.py
@@ -321,6 +321,8 @@
             left, weight_ref[tap * depth : (tap + 1) * depth], preferred_element_type=jnp.float32
         )
 
+    first_mid = 5 + len(weight_moves)
+
     def conv_step(clip, _):
         span = PAIRS * SPAN * BLOCK
         total = conv_chunk([mixed_ref], [tap_dot], clip * span, span, 1)
@@ -328,17 +330,23 @@
         for seg in range(SEG):
             value = [total[2 * (SPAN * (seg // 2) + 1 + row) + seg % 2] for row in range(SIDE)]
             store_map(view, seg * PIXELS, slice(None), value)
+        here = row_part(clip, CLIP)
+        move(acc_ref.at[here], mid_ref.at[here], sems, first_mid + clip)
         return 0
 
     lax.fori_loop(0, clips, conv_step, 0)
-    mid_move = move(acc_ref.at[pl.ds(0, rows)], mid_ref, sems, 4)
     result = acc_ref[pl.ds(0, rows), :]
     mid16_ref[...] = result.astype(jnp.bfloat16)
     put_sums(
         sums_ref, jnp.sum(result, 0, keepdims=True), jnp.sum(result * result, 0, keepdims=True)
     )
-    for copy in (gates_move, mixed_move, mid_move):
+    for copy in (gates_move, mixed_move):
         copy.wait()
+    for clip in range(clips):
+        here = pl.ds(clip * CLIP, CLIP)
+        pltpu.make_async_copy(
+            acc_ref.at[here], mid_ref.at[here], sems.at[first_mid + clip]
+        ).wait()
 
 
 def map_rows(rows):
@@ -367,7 +375,7 @@
             pltpu.VMEM((rows, width), own.dtype),
             pltpu.VMEM((spread, 2 * width), jnp.bfloat16),
             pltpu.VMEM(gates, jnp.float32),
-            pltpu.SemaphoreType.DMA((5 + 2 * weights[0].shape[0],)),
+            pltpu.SemaphoreType.DMA((5 + 2 * weights[0].shape[0] + rows // CLIP,)),
         ),
         away=(0, 1, 2),
         lasts=12.0,

time: 250 us -> 250 us (level)
  transfers between devices with their start and end apart: 67 -> 67, of which waited for: 29 -> 27; matrix products, arithmetic and copies ran while one was open for 4% -> 4% of each run, Pallas kernels for 31% -> 31%
where the time goes in v6:
time: 250 us
  Pallas kernels  91.1 us (36%)
  starting transfers between devices  74.7 us (30%)
  waiting for transfers between devices  58.1 us (23%)
  between operations  15 us (6%)
  local copies, waits for them, and re-layouts  9.02 us (4%)
    pallas_call x28, Pallas kernels, run(): call(*[pltpu.with_memory_space_constraint(arg, pltpu.HBM) if spec is remo...  81.7 us
    ppermute x65, starting transfers between devices, swap(): return lax.ppermute(value, axis, [(at, at ^ bit) for at in range(size)])  74.6 us
    ppermute x65, waiting for transfers between devices, swap(): return lax.ppermute(value, axis, [(at, at ^ bit) for at in range(size)])  58.1 us
    pallas_call x4, Pallas kernels, stem_back(): pl.pallas_call(functools.partial(stem_back_body, count, first), grid=(1,)...  9.45 us
  transfers between devices with their start and end apart: 67, of which 27 were waited for; matrix products, arithmetic and copies ran while one was open for 4% of the time, Pallas kernels for 31%

profile of v6, /device:TPU:0, one launch (start us, length us, event | category | flops | bytes accessed | tf_op | source)
XLA Modules:
  0.0 249.8 jit_solution(8476770644474586024)
XLA Ops:
  7.4 3.0 %shard_map.348 = (bf16[784,512]{1,0:T(8,128)(2,1)}, bf16[784,512]{1,0:T(8,128)(2,1)}, bf16[832,128]{1,0:T(8,128)(2,1)}) custom-call(s32[2]{0:T(128)S(1)} %pad_add_fusion.place_ref, bf16[1568,512]{1,0:T(8,128)(2,1)} %block_ref.7, bf16[576,128]{1,0:T(8,128)(2,1)} %mid_ref.1, bf16[64,512]{1,0:T(8,128)(2,1)} %out_ref.1), custom_call_target="tpu_custom_call" | custom-call | flops 300000000 | tf_op jit(solution)/shard_map/pallas_call | solution.py:70
  10.5 3.0 %collective-permute-start.1 = (bf16[784,512]{1,0:T(8,128)(2,1)}, bf16[784,512]{1,0:T(8,128)(2,1)S(1)}, u32[]{:S(2)}, u32[]{:S(2)}) collective-permute-start(bf16[784,512]{1,0:T(8,128)(2,1)} %get-tuple-element.141), channel_id=1, source_target_pairs={{0,2},{1,3},{2,0},{3,1},{4,6},{5,7},{6,4},{7,5},{8,10},{9,11},{10,... | collective-permute-start | bytes 2408456 | tf_op jit(solution)/shard_map/ppermute | solution.py:1553
  13.5 2.6 %collective-permute-start.3 = (bf16[256,128]{1,0:T(8,128)(2,1)S(1)}, bf16[256,128]{1,0:T(8,128)(2,1)S(1)}, u32[]{:S(2)}, u32[]{:S(2)}) collective-permute-start(bf16[256,128]{1,0:T(8,128)(2,1)S(1)} %copy-done.36), channel_id=1, source_target_pairs={{0,16},{4,20},{8,24},{12,28},{16,0},{20,4},{24,8},{28,12},{1,17},{... | collective-permute-start | bytes 196616 | tf_op jit(solution)/shard_map/ppermute | solution.py:1553
  16.1 2.9 %collective-permute-done.3 = bf16[256,128]{1,0:T(8,128)(2,1)S(1)} collective-permute-done((bf16[256,128]{1,0:T(8,128)(2,1)S(1)}, bf16[256,128]{1,0:T(8,128)(2,1)S(1)}, u32[]{:S(2)}, u32[]{:S(2)}) %collective-permute-start.3) | collective-permute-done | bytes 65568 | tf_op jit(solution)/shard_map/ppermute | solution.py:1553
  20.4 4.1 %collective-permute-done.4 = bf16[512,128]{1,0:T(8,128)(2,1)S(1)} collective-permute-done((bf16[512,128]{1,0:T(8,128)(2,1)S(1)}, bf16[512,128]{1,0:T(8,128)(2,1)S(1)}, u32[]{:S(2)}, u32[]{:S(2)}) %collective-permute-start.4) | collective-permute-done | bytes 131104 | tf_op jit(solution)/shard_map/ppermute | solution.py:1553
  25.6 6.0 %collective-permute-done.1.across_ref = bf16[784,512]{1,0:T(8,128)(2,1)S(1)} collective-permute-done((bf16[784,512]{1,0:T(8,128)(2,1)}, bf16[784,512]{1,0:T(8,128)(2,1)S(1)}, u32[]{:S(2)}, u32[]{:S(2)}) %collective-permute-start.1) | collective-permute-done | bytes 802848 | tf_op jit(solution)/shard_map/ppermute | solution.py:1553
  32.2 1.5 collective-permute-start.6
  34.0 1.7 copy.47.video_ref
  36.5 7.4 %shard_map.349 = (f32[32,16,256]{2,1,0:T(8,128)}, bf16[32,112,512]{2,1,0:T(8,128)(2,1)}, bf16[7,512,256]{2,1,0:T(8,128)(2,1)}, f32[8,256]{1,0:T(8,128)S(1)}) custom-call(s32[2]{0:T(128)S(1)} %pad_add_fusion.place_ref, bf16[32,15,1024]{2,1,0:T(8,128)(2,1)S(1)} %copy.47.video_ref, bf16[112,112]{1,0:T(8,128)(2,1)S(1)} %reshape.128.weight_ref), custom_call_target="tpu_custom_call" | custom-call | tf_op jit(solution)/shard_map/pallas_call | solution.py:70
  44.0 7.8 %collective-permute-done.2.corner_ref = bf16[784,512]{1,0:T(8,128)(2,1)S(1)} collective-permute-done((bf16[784,512]{1,0:T(8,128)(2,1)}, bf16[784,512]{1,0:T(8,128)(2,1)S(1)}, u32[]{:S(2)}, u32[]{:S(2)}) %collective-permute-start.2) | collective-permute-done | bytes 802848 | tf_op jit(solution)/shard_map/ppermute | solution.py:1553
  51.8 4.8 %shard_map.351 = (f32[784,256]{1,0:T(8,128)}, bf16[784,256]{1,0:T(8,128)(2,1)S(1)}, f32[8,256]{1,0:T(8,128)S(1)}, f32[32,256]{1,0:T(8,128)S(1)}, bf16[512,256]{1,0:T(8,128)(2,1)}, /*index=5*/bf16[512,256]{1,0:T(8,128)(2,1)}) custom-call(s32[2]{0:T(128)S(1)} %pad_add_fusion.place_ref, bf16[1568,512]{1,0:T(8,128)(2,1)} %block_ref.7, ...), custom_call_target="tpu_custom_call" | custom-call | flops 1200000000 | tf_op jit(solution)/shard_map/pallas_call | solution.py:70
  56.6 1.4 collective-permute-start.8
  58.8 2.3 collective-permute-done.11
  61.1 1.5 collective-permute-start.12
  62.6 2.2 collective-permute-done.12
  65.7 1.8 collective-permute-start.13
  70.0 2.6 %collective-permute-start.15 = (f32[8,256]{1,0:T(8,128)S(1)}, f32[8,256]{1,0:T(8,128)S(1)}, u32[]{:S(2)}, u32[]{:S(2)}) collective-permute-start(f32[8,256]{1,0:T(8,128)S(1)} %add.117.first_ref), channel_id=1, source_target_pairs={{0,16},{4,20},{8,24},{12,28},{16,0},{20,4},{24,8},{28,12},{1,17},{... | collective-permute-start | bytes 24584 | tf_op jit(solution)/shard_map/ppermute | solution.py:1553
  72.6 2.0 collective-permute-done.15.second_ref
  75.4 1.4 collective-permute-done.9.oth_ref.pre_ref
  76.8 9.0 %shard_map.352 = (bf16[1184,512]{1,0:T(8,128)(2,1)}, f32[16,7,8,256]{3,2,1,0:T(8,128)}, f32[784,256]{1,0:T(8,128)}, bf16[784,256]{1,0:T(8,128)(2,1)S(1)}, f32[8,256]{1,0:T(8,128)S(1)}) custom-call(s32[2]{0:T(128)S(1)} %pad_add_fusion.place_ref, s32[2,8]{1,0:T(2,128)S(1)} %pad.4.same_ref, f32[784,256]{1,0:T(8,128)} %get-tuple-element.146.own_ref.pre_ref, ...), custom_call_target="tpu_custom_call" | custom-call | flops 3600000000 | tf_op jit(solution)/shard_map/pallas_call | solution.py:70
  87.6 2.0 collective-permute-start.18
  89.6 1.8 shard_map.353
  91.4 1.9 collective-permute-start.19
  93.5 1.6 collective-permute-done.19
  95.1 3.1 %collective-permute-start.21 = (f32[8,256]{1,0:T(8,128)S(1)}, f32[8,256]{1,0:T(8,128)S(1)}, u32[]{:S(2)}, u32[]{:S(2)}) collective-permute-start(f32[8,256]{1,0:T(8,128)S(1)} %add.122), channel_id=1, source_target_pairs={{0,16},{4,20},{8,24},{12,28},{16,0},{20,4},{24,8},{28,12},{1,17},{... | collective-permute-start | bytes 24584 | tf_op jit(solution)/shard_map/ppermute | solution.py:1553
  98.2 1.6 shard_map.354.turned_ref
  101.0 2.6 %collective-permute-done.22.stats_oth_ref = f32[8,256]{1,0:T(8,128)S(1)} collective-permute-done((f32[8,256]{1,0:T(8,128)S(1)}, f32[8,256]{1,0:T(8,128)S(1)}, u32[]{:S(2)}, u32[]{:S(2)}) %collective-permute-start.22) | collective-permute-done | bytes 8224 | tf_op jit(solution)/shard_map/ppermute | solution.py:1553
  103.6 1.8 shard_map.355.mine_ref.second_ref.rows_ref
  107.8 1.5 shard_map.356
  109.4 1.7 collective-permute-start.24
  111.1 2.1 collective-permute-done.24
  113.2 1.7 collective-permute-start.25
  114.9 2.0 collective-permute-done.25
  116.9 2.8 %collective-permute-start.26 = (f32[8,512]{1,0:T(8,128)S(1)}, f32[8,512]{1,0:T(8,128)S(1)}, u32[]{:S(2)}, u32[]{:S(2)}) collective-permute-start(f32[8,512]{1,0:T(8,128)S(1)} %add.125.first_ref), channel_id=1, source_target_pairs={{0,16},{4,20},{8,24},{12,28},{16,0},{20,4},{24,8},{28,12},{1,17},{... | collective-permute-start | bytes 49160 | tf_op jit(solution)/shard_map/ppermute | solution.py:1553
  119.8 1.6 collective-permute-done.27.away_own_ref
  121.7 5.8 %shard_map.357 = (bf16[1568,512]{1,0:T(8,128)(2,1)}, f32[1568,512]{1,0:T(8,128)}, f32[8,512]{1,0:T(8,128)S(1)}, f32[784,512]{1,0:T(8,128)S(1)}, bf16[784,512]{1,0:T(8,128)(2,1)S(1)}) custom-call(s32[2]{0:T(128)S(1)} %pad_add_fusion.place_ref, f32[1568,512]{1,0:T(8,128)S(1)} %get-tuple-element.175.pre_ref, bf16[1568,512]{1,0:T(8,128)(2,1)S(1)} %copy-done.5, ...), custom_call_target="tpu_custom_call" | custom-call | flops 2249999872 | tf_op jit(solution)/shard_map/pallas_call | solution.py:70
  128.2 1.6 collective-permute-start.29
  129.9 2.4 shard_map.358.start_ref
  134.0 1.6 collective-permute-start.31
  135.6 2.2 collective-permute-done.31
  137.7 2.5 %collective-permute-start.32 = (f32[8,512]{1,0:T(8,128)S(1)}, f32[8,512]{1,0:T(8,128)S(1)}, u32[]{:S(2)}, u32[]{:S(2)}) collective-permute-start(f32[8,512]{1,0:T(8,128)S(1)} %add.128.first_ref), channel_id=1, source_target_pairs={{0,16},{4,20},{8,24},{12,28},{16,0},{20,4},{24,8},{28,12},{1,17},{... | collective-permute-start | bytes 49160 | tf_op jit(solution)/shard_map/ppermute | solution.py:1553
  140.3 2.4 shard_map.360.start_ref
  144.6 1.9 collective-permute-done.34.deltas2_ref
  147.2 3.8 %shard_map.362 = (f32[784,256]{1,0:T(8,128)}, bf16[784,256]{1,0:T(8,128)(2,1)S(1)}, f32[8,256]{1,0:T(8,128)S(1)}) custom-call(s32[2]{0:T(128)S(1)} %pad_add_fusion.place_ref, f32[784,256]{1,0:T(8,128)S(1)} %get-tuple-element.191.keep_ref, bf16[784,256]{1,0:T(8,128)(2,1)S(1)} %collective-permute-done.30.got_ref, ...), custom_call_target="tpu_custom_call" | custom-call | flops 990000000 | tf_op jit(solution)/shard_map/pallas_call | solution.py:70
  154.5 1.4 shard_map.363.refs_0_
  156.9 1.7 collective-permute-start.40
  158.6 2.3 shard_map.364
  161.0 2.3 collective-permute-start.41
  163.3 2.4 shard_map.365.start_ref
  166.9 1.9 shard_map.366.slopes_ref
  168.8 2.4 shard_map.367
  171.3 12.1 %shard_map.368 = (f32[784,256]{1,0:T(8,128)}, bf16[784,256]{1,0:T(8,128)(2,1)}, f32[32,256]{1,0:T(8,128)S(1)}) custom-call(s32[2]{0:T(128)S(1)} %pad_add_fusion.place_ref, s32[2,8]{1,0:T(2,128)S(1)} %pad.4.same_ref, bf16[3,1184,256]{2,1,0:T(8,128)(2,1)S(1)} %shard_map.366.slopes_ref, bf16[784,256]{1,0:T(8,128)(2,1)} %collective-permute-done.42.d_oth_ref, ...), custom_call_target="tpu_custom_call" | custom-call | flops 3449999872 | tf_op jit(solution)/shard_map/pallas_call | solution.py:70
  184.7 4.8 %shard_map.369 = (f32[4608,128]{1,0:T(8,128)}, bf16[2304,128]{1,0:T(8,128)(2,1)S(1)}, bf16[2304,128]{1,0:T(8,128)(2,1)S(1)}) custom-call(s32[2]{0:T(128)S(1)} %pad_add_fusion.place_ref, bf16[512,1152]{1,0:T(8,128)(2,1)S(1)} %copy-done.17, bf16[3,1184,256]{2,1,0:T(8,128)(2,1)S(1)} %shard_map.366.slopes_ref), custom_call_target="tpu_custom_call" | custom-call | flops 1440000000 | tf_op jit(solution)/shard_map/pallas_call | solution.py:70
  192.9 2.5 collective-permute-done.46
  199.3 2.0 collective-permute-start.49
  201.3 2.2 shard_map.370
  206.0 5.8 %shard_map.371 = (bf16[784,256]{1,0:T(8,128)(2,1)S(1)}, f32[2048,128]{1,0:T(8,128)}, bf16[2048,128]{1,0:T(8,128)(2,1)S(1)}) custom-call(s32[2]{0:T(128)S(1)} %pad_add_fusion.place_ref, f32[784,256]{1,0:T(8,128)} %get-tuple-element.215.d_ref, f32[784,256]{1,0:T(8,128)} %get-tuple-element.146.own_ref.pre_ref, f32[8,256]{1,0:T(8,128)S(1)} %add.119.stats_ref.stats_in_ref, ...), custom_call_target="tpu_custom_call" | custom-call | flops 1350000000 | tf_op jit(solution)/shard_map/pallas_call | solution.py:70
  211.9 2.2 shard_map.372.mine_ref
  217.1 2.2 shard_map.373
  223.1 2.7 %shard_map.375 = bf16[1568,512]{1,0:T(8,128)(2,1)} custom-call(s32[2]{0:T(128)S(1)} %pad_add_fusion.place_ref, bf16[784,512]{1,0:T(8,128)(2,1)S(1)} %shard_map.372.mine_ref, bf16[784,512]{1,0:T(8,128)(2,1)S(1)} %collective-permute-done.54.peer_ref, bf16[512,256]{1,0:T(8,128)(2,1)S(1)} %copy-done.20, bf16[512,256]{1,0:T(8,128)(2,1)S(1)} %collective-permute-done.57.far_ref, ...), custom_call_target="tpu_custom_call" | custom-call | flops 840000000 | tf_op jit(solution)/shard_map/pallas_call | solution.py:70
  225.9 1.7 collective-permute-start.62
  228.2 1.6 collective-permute-start.60
  230.8 2.7 %collective-permute-start.64 = (bf16[576,128]{1,0:T(8,128)(2,1)S(1)}, bf16[576,128]{1,0:T(8,128)(2,1)S(1)}, u32[]{:S(2)}, u32[]{:S(2)}) collective-permute-start(bf16[576,128]{1,0:T(8,128)(2,1)S(1)} %bitcast.62), channel_id=1, source_target_pairs={{0,16},{4,20},{8,24},{12,28},{16,0},{20,4},{24,8},{28,12},{1,17},{... | collective-permute-start | bytes 442376 | tf_op jit(solution)/shard_map/ppermute | solution.py:1553
  237.6 3.9 %collective-permute-done.64 = bf16[576,128]{1,0:T(8,128)(2,1)S(1)} collective-permute-done((bf16[576,128]{1,0:T(8,128)(2,1)S(1)}, bf16[576,128]{1,0:T(8,128)(2,1)S(1)}, u32[]{:S(2)}, u32[]{:S(2)}) %collective-permute-start.64) | collective-permute-done | bytes 147488 | tf_op jit(solution)/shard_map/ppermute | solution.py:1553
  (246 shorter events, 50.9 us)
Async XLA Ops:
  7.2 57.6 %all-gather.3.cloned.1.call-start = ((), (), s32[]{:S(2)}) async-start(), calls=%async_computation.2 | async-start | bytes 1916928 | tf_op jit(solution)/shard_map/all_gather | solution.py:1703
  10.5 217.1 %reduce-scatter.2.cloned.1.call-start = ((), (), s32[]{:S(2)}) async-start(), calls=%async_computation.1 | async-start | bytes 1179648 | tf_op jit(solution)/shard_map/reduce_scatter | solution.py:1875
  10.5 21.1 %collective-permute-start.1 = (bf16[784,512]{1,0:T(8,128)(2,1)}, bf16[784,512]{1,0:T(8,128)(2,1)S(1)}, u32[]{:S(2)}, u32[]{:S(2)}) collective-permute-start(bf16[784,512]{1,0:T(8,128)(2,1)} %get-tuple-element.141), channel_id=1, source_target_pairs={{0,2},{1,3},{2,0},{3,1},{4,6},{5,7},{6,4},{7,5},{8,10},{9,11},{10,... | collective-permute-start | bytes 2408456 | tf_op jit(solution)/shard_map/ppermute | solution.py:1553
  13.5 5.5 %collective-permute-start.3 = (bf16[256,128]{1,0:T(8,128)(2,1)S(1)}, bf16[256,128]{1,0:T(8,128)(2,1)S(1)}, u32[]{:S(2)}, u32[]{:S(2)}) collective-permute-start(bf16[256,128]{1,0:T(8,128)(2,1)S(1)} %copy-done.36), channel_id=1, source_target_pairs={{0,16},{4,20},{8,24},{12,28},{16,0},{20,4},{24,8},{28,12},{1,17},{... | collective-permute-start | bytes 196616 | tf_op jit(solution)/shard_map/ppermute | solution.py:1553
  19.0 5.4 %collective-permute-start.4 = (bf16[512,128]{1,0:T(8,128)(2,1)S(1)}, bf16[512,128]{1,0:T(8,128)(2,1)S(1)}, u32[]{:S(2)}, u32[]{:S(2)}) collective-permute-start(bf16[512,128]{1,0:T(8,128)(2,1)S(1)} %pad_maximum_fusion.2), channel_id=1, source_target_pairs={{0,8},{4,12},{8,0},{12,4},{16,24},{20,28},{24,16},{28,20},{1,9},{5... | collective-permute-start | bytes 393224 | tf_op jit(solution)/shard_map/ppermute | solution.py:1553
  20.4 23.6 %collective-permute-start = (bf16[784,512]{1,0:T(8,128)(2,1)}, bf16[784,512]{1,0:T(8,128)(2,1)}, u32[]{:S(2)}, u32[]{:S(2)}) collective-permute-start(bf16[784,512]{1,0:T(8,128)(2,1)} %get-tuple-element.142), channel_id=1, source_target_pairs={{0,1},{1,0},{2,3},{3,2},{4,5},{5,4},{6,7},{7,6},{8,9},{9,8},{10,11... | collective-permute-start | bytes 2408456 | tf_op jit(solution)/shard_map/ppermute | solution.py:1553
  24.4 7.7 %collective-permute-start.5 = (bf16[1024,128]{1,0:T(8,128)(2,1)S(1)}, bf16[1024,128]{1,0:T(8,128)(2,1)S(1)}, u32[]{:S(2)}, u32[]{:S(2)}) collective-permute-start(bf16[1024,128]{1,0:T(8,128)(2,1)S(1)} %pad_maximum_fusion.1), channel_id=1, source_target_pairs={{0,4},{4,0},{8,12},{12,8},{16,20},{20,16},{24,28},{28,24},{1,5},{5... | collective-permute-start | bytes 786440 | tf_op jit(solution)/shard_map/ppermute | solution.py:1553
  31.6 20.1 %collective-permute-start.2 = (bf16[784,512]{1,0:T(8,128)(2,1)}, bf16[784,512]{1,0:T(8,128)(2,1)S(1)}, u32[]{:S(2)}, u32[]{:S(2)}) collective-permute-start(bf16[784,512]{1,0:T(8,128)(2,1)} %get-tuple-element.142), channel_id=1, source_target_pairs={{0,3},{1,2},{2,1},{3,0},{4,7},{5,6},{6,5},{7,4},{8,11},{9,10},{10,... | collective-permute-start | bytes 2408456 | tf_op jit(solution)/shard_map/ppermute | solution.py:1553
  32.2 11.8 %collective-permute-start.6 = (bf16[2048,128]{1,0:T(8,128)(2,1)S(1)}, bf16[2048,128]{1,0:T(8,128)(2,1)S(1)}, u32[]{:S(2)}, u32[]{:S(2)}) collective-permute-start(bf16[2048,128]{1,0:T(8,128)(2,1)S(1)} %constant_dynamic-update-slice_fusion.own_ref), channel_id=1, source_target_pairs={{0,1},{1,0},{2,3},{3,2},{4,5},{5,4},{6,7},{7,6},{8,9},{9,8},{10,11... | collective-permute-start | bytes 1572872 | tf_op jit(solution)/shard_map/ppermute | solution.py:1553
  33.7 10.2 %collective-permute-start.7 = (f32[24,128]{1,0:T(8,128)S(1)}, f32[24,128]{1,0:T(8,128)S(1)}, u32[]{:S(2)}, u32[]{:S(2)}) collective-permute-start(f32[24,128]{1,0:T(8,128)S(1)} %get-tuple-element.145), channel_id=1, source_target_pairs={{0,1},{1,0},{2,3},{3,2},{4,5},{5,4},{6,7},{7,6},{8,9},{9,8},{10,11... | collective-permute-start | bytes 36872 | tf_op jit(solution)/shard_map/ppermute | solution.py:1553
  56.6 4.5 %collective-permute-start.8 = (f32[32,256]{1,0:T(8,128)S(1)}, f32[32,256]{1,0:T(8,128)S(1)}, u32[]{:S(2)}, u32[]{:S(2)}) collective-permute-start(f32[32,256]{1,0:T(8,128)S(1)} %get-tuple-element.148), channel_id=1, source_target_pairs={{0,2},{1,3},{2,0},{3,1},{4,6},{5,7},{6,4},{7,5},{8,10},{9,11},{10,... | collective-permute-start | bytes 98312 | tf_op jit(solution)/shard_map/ppermute | solution.py:1553
  58.0 3.1 %collective-permute-start.11 = (f32[8,256]{1,0:T(8,128)S(1)}, f32[8,256]{1,0:T(8,128)S(1)}, u32[]{:S(2)}, u32[]{:S(2)}) collective-permute-start(f32[8,256]{1,0:T(8,128)S(1)} %slice.64), channel_id=1, source_target_pairs={{0,3},{1,2},{2,1},{3,0},{4,7},{5,6},{6,5},{7,4},{8,11},{9,10},{10,... | collective-permute-start | bytes 24584 | tf_op jit(solution)/shard_map/ppermute | solution.py:1553
  58.5 2.6 %collective-permute-start.10 = (f32[8,256]{1,0:T(8,128)S(1)}, f32[8,256]{1,0:T(8,128)S(1)}, u32[]{:S(2)}, u32[]{:S(2)}) collective-permute-start(f32[8,256]{1,0:T(8,128)S(1)} %get-tuple-element.150), channel_id=1, source_target_pairs={{0,1},{1,0},{2,3},{3,2},{4,5},{5,4},{6,7},{7,6},{8,9},{9,8},{10,11... | collective-permute-start | bytes 24584 | tf_op jit(solution)/shard_map/ppermute | solution.py:1553
  61.1 3.7 %collective-permute-start.12 = (f32[8,256]{1,0:T(8,128)S(1)}, f32[8,256]{1,0:T(8,128)S(1)}, u32[]{:S(2)}, u32[]{:S(2)}) collective-permute-start(f32[8,256]{1,0:T(8,128)S(1)} %fusion), channel_id=1, source_target_pairs={{0,4},{4,0},{8,12},{12,8},{16,20},{20,16},{24,28},{28,24},{1,5},{5... | collective-permute-start | bytes 24584 | tf_op jit(solution)/shard_map/ppermute | solution.py:1553
  64.8 3.9 %collective-permute-start.14 = (bf16[8,832,128]{2,1,0:T(8,128)(2,1)}, bf16[8,832,128]{2,1,0:T(8,128)(2,1)}, u32[]{:S(2)}, u32[]{:S(2)}) collective-permute-start(bf16[8,832,128]{2,1,0:T(8,128)(2,1)} %bitcast.74), channel_id=1, source_target_pairs={{0,1},{1,0},{2,3},{3,2},{4,5},{5,4},{6,7},{7,6},{8,9},{9,8},{10,11... | collective-permute-start | bytes 5111816 | tf_op jit(solution)/shard_map/ppermute | solution.py:1553
  64.8 12.0 %collective-permute-start.9 = (bf16[784,256]{1,0:T(8,128)(2,1)S(1)}, bf16[784,256]{1,0:T(8,128)(2,1)S(1)}, u32[]{:S(2)}, u32[]{:S(2)}) collective-permute-start(bf16[784,256]{1,0:T(8,128)(2,1)S(1)} %get-tuple-element.149), channel_id=1, source_target_pairs={{0,2},{1,3},{2,0},{3,1},{4,6},{5,7},{6,4},{7,5},{8,10},{9,11},{10,... | collective-permute-start | bytes 1204232 | tf_op jit(solution)/shard_map/ppermute | solution.py:1553
  65.7 4.2 %collective-permute-start.13 = (f32[8,256]{1,0:T(8,128)S(1)}, f32[8,256]{1,0:T(8,128)S(1)}, u32[]{:S(2)}, u32[]{:S(2)}) collective-permute-start(f32[8,256]{1,0:T(8,128)S(1)} %add.116), channel_id=1, source_target_pairs={{0,8},{4,12},{8,0},{12,4},{16,24},{20,28},{24,16},{28,20},{1,9},{5... | collective-permute-start | bytes 24584 | tf_op jit(solution)/shard_map/ppermute | solution.py:1553
  70.0 4.6 %collective-permute-start.15 = (f32[8,256]{1,0:T(8,128)S(1)}, f32[8,256]{1,0:T(8,128)S(1)}, u32[]{:S(2)}, u32[]{:S(2)}) collective-permute-start(f32[8,256]{1,0:T(8,128)S(1)} %add.117.first_ref), channel_id=1, source_target_pairs={{0,16},{4,20},{8,24},{12,28},{16,0},{20,4},{24,8},{28,12},{1,17},{... | collective-permute-start | bytes 24584 | tf_op jit(solution)/shard_map/ppermute | solution.py:1553
  74.6 20.5 %collective-permute-start.20 = (bf16[512,512]{1,0:T(8,128)(2,1)S(1)}, bf16[512,512]{1,0:T(8,128)(2,1)S(1)}, u32[]{:S(2)}, u32[]{:S(2)}) collective-permute-start(bf16[512,512]{1,0:T(8,128)(2,1)S(1)} %pad_maximum_fusion.weight_ref.weights0_ref), channel_id=1, source_target_pairs={{0,2},{1,3},{2,0},{3,1},{4,6},{5,7},{6,4},{7,5},{8,10},{9,11},{10,... | collective-permute-start | bytes 1572872 | tf_op jit(solution)/shard_map/ppermute | solution.py:1553
  85.8 15.2 %collective-permute-start.16 = (bf16[784,256]{1,0:T(8,128)(2,1)S(1)}, bf16[784,256]{1,0:T(8,128)(2,1)S(1)}, u32[]{:S(2)}, u32[]{:S(2)}) collective-permute-start(bf16[784,256]{1,0:T(8,128)(2,1)S(1)} %get-tuple-element.157), channel_id=1, source_target_pairs={{0,2},{1,3},{2,0},{3,1},{4,6},{5,7},{6,4},{7,5},{8,10},{9,11},{10,... | collective-permute-start | bytes 1204232 | tf_op jit(solution)/shard_map/ppermute | solution.py:1553
  87.6 3.8 %collective-permute-start.18 = (f32[8,256]{1,0:T(8,128)S(1)}, f32[8,256]{1,0:T(8,128)S(1)}, u32[]{:S(2)}, u32[]{:S(2)}) collective-permute-start(f32[8,256]{1,0:T(8,128)S(1)} %add.118), channel_id=1, source_target_pairs={{0,4},{4,0},{8,12},{12,8},{16,20},{20,16},{24,28},{28,24},{1,5},{5... | collective-permute-start | bytes 24584 | tf_op jit(solution)/shard_map/ppermute | solution.py:1553
  91.4 3.7 %collective-permute-start.19 = (f32[8,256]{1,0:T(8,128)S(1)}, f32[8,256]{1,0:T(8,128)S(1)}, u32[]{:S(2)}, u32[]{:S(2)}) collective-permute-start(f32[8,256]{1,0:T(8,128)S(1)} %add.120), channel_id=1, source_target_pairs={{0,8},{4,12},{8,0},{12,4},{16,24},{20,28},{24,16},{28,20},{1,9},{5... | collective-permute-start | bytes 24584 | tf_op jit(solution)/shard_map/ppermute | solution.py:1553
  95.1 4.7 %collective-permute-start.21 = (f32[8,256]{1,0:T(8,128)S(1)}, f32[8,256]{1,0:T(8,128)S(1)}, u32[]{:S(2)}, u32[]{:S(2)}) collective-permute-start(f32[8,256]{1,0:T(8,128)S(1)} %add.122), channel_id=1, source_target_pairs={{0,16},{4,20},{8,24},{12,28},{16,0},{20,4},{24,8},{28,12},{1,17},{... | collective-permute-start | bytes 24584 | tf_op jit(solution)/shard_map/ppermute | solution.py:1553
  99.8 3.7 %collective-permute-start.22 = (f32[8,256]{1,0:T(8,128)S(1)}, f32[8,256]{1,0:T(8,128)S(1)}, u32[]{:S(2)}, u32[]{:S(2)}) collective-permute-start(f32[8,256]{1,0:T(8,128)S(1)} %add.123.stats_own_ref.stats_ref), channel_id=1, source_target_pairs={{0,2},{1,3},{2,0},{3,1},{4,6},{5,7},{6,4},{7,5},{8,10},{9,11},{10,... | collective-permute-start | bytes 24584 | tf_op jit(solution)/shard_map/ppermute | solution.py:1553
  105.5 2.4 collective-permute-start.23
  105.5 15.8 %collective-permute-start.27 = (bf16[2304,128]{1,0:T(8,128)(2,1)S(1)}, bf16[2304,128]{1,0:T(8,128)(2,1)}, u32[]{:S(2)}, u32[]{:S(2)}) collective-permute-start(bf16[2304,128]{1,0:T(8,128)(2,1)S(1)} %bitcast.80), channel_id=1, source_target_pairs={{0,2},{1,3},{2,0},{3,1},{4,6},{5,7},{6,4},{7,5},{8,10},{9,11},{10,... | collective-permute-start | bytes 1769480 | tf_op jit(solution)/shard_map/ppermute | solution.py:1553
  109.4 3.8 %collective-permute-start.24 = (f32[8,512]{1,0:T(8,128)S(1)}, f32[8,512]{1,0:T(8,128)S(1)}, u32[]{:S(2)}, u32[]{:S(2)}) collective-permute-start(f32[8,512]{1,0:T(8,128)S(1)} %get-tuple-element.176), channel_id=1, source_target_pairs={{0,4},{4,0},{8,12},{12,8},{16,20},{20,16},{24,28},{28,24},{1,5},{5... | collective-permute-start | bytes 49160 | tf_op jit(solution)/shard_map/ppermute | solution.py:1553
  113.2 3.7 %collective-permute-start.25 = (f32[8,512]{1,0:T(8,128)S(1)}, f32[8,512]{1,0:T(8,128)S(1)}, u32[]{:S(2)}, u32[]{:S(2)}) collective-permute-start(f32[8,512]{1,0:T(8,128)S(1)} %add.124), channel_id=1, source_target_pairs={{0,8},{4,12},{8,0},{12,4},{16,24},{20,28},{24,16},{28,20},{1,9},{5... | collective-permute-start | bytes 49160 | tf_op jit(solution)/shard_map/ppermute | solution.py:1553
  116.9 4.6 %collective-permute-start.26 = (f32[8,512]{1,0:T(8,128)S(1)}, f32[8,512]{1,0:T(8,128)S(1)}, u32[]{:S(2)}, u32[]{:S(2)}) collective-permute-start(f32[8,512]{1,0:T(8,128)S(1)} %add.125.first_ref), channel_id=1, source_target_pairs={{0,16},{4,20},{8,24},{12,28},{16,0},{20,4},{24,8},{28,12},{1,17},{... | collective-permute-start | bytes 49160 | tf_op jit(solution)/shard_map/ppermute | solution.py:1553
  127.5 4.7 %collective-permute-start.28 = (bf16[784,512]{1,0:T(8,128)(2,1)S(1)}, bf16[784,512]{1,0:T(8,128)(2,1)S(1)}, u32[]{:S(2)}, u32[]{:S(2)}) collective-permute-start(bf16[784,512]{1,0:T(8,128)(2,1)S(1)} %get-tuple-element.182), channel_id=1, source_target_pairs={{0,1},{1,0},{2,3},{3,2},{4,5},{5,4},{6,7},{7,6},{8,9},{9,8},{10,11... | collective-permute-start | bytes 2408456 | tf_op jit(solution)/shard_map/ppermute | solution.py:1553
  127.6 16.4 %collective-permute-start.36 = (bf16[512,512]{1,0:T(8,128)(2,1)S(1)}, bf16[512,512]{1,0:T(8,128)(2,1)S(1)}, u32[]{:S(2)}, u32[]{:S(2)}) collective-permute-start(bf16[512,512]{1,0:T(8,128)(2,1)S(1)} %copy-done.15), channel_id=1, source_target_pairs={{0,1},{1,0},{2,3},{3,2},{4,5},{5,4},{6,7},{7,6},{8,9},{9,8},{10,11... | collective-permute-start | bytes 1572872 | tf_op jit(solution)/shard_map/ppermute | solution.py:1553
  128.1 16.5 %collective-permute-start.37 = (bf16[512,512]{1,0:T(8,128)(2,1)S(1)}, bf16[512,512]{1,0:T(8,128)(2,1)S(1)}, u32[]{:S(2)}, u32[]{:S(2)}) collective-permute-start(bf16[512,512]{1,0:T(8,128)(2,1)S(1)} %copy-done.19), channel_id=1, source_target_pairs={{0,1},{1,0},{2,3},{3,2},{4,5},{5,4},{6,7},{7,6},{8,9},{9,8},{10,11... | collective-permute-start | bytes 1572872 | tf_op jit(solution)/shard_map/ppermute | solution.py:1553
  128.2 4.1 %collective-permute-start.29 = (f32[8,512]{1,0:T(8,128)S(1)}, f32[8,512]{1,0:T(8,128)S(1)}, u32[]{:S(2)}, u32[]{:S(2)}) collective-permute-start(f32[8,512]{1,0:T(8,128)S(1)} %get-tuple-element.183.sums_ref), channel_id=1, source_target_pairs={{0,4},{4,0},{8,12},{12,8},{16,20},{20,16},{24,28},{28,24},{1,5},{5... | collective-permute-start | bytes 49160 | tf_op jit(solution)/shard_map/ppermute | solution.py:1553
  133.0 14.2 %collective-permute-start.30 = (bf16[784,256]{1,0:T(8,128)(2,1)S(1)}, bf16[784,256]{1,0:T(8,128)(2,1)S(1)}, u32[]{:S(2)}, u32[]{:S(2)}) collective-permute-start(bf16[784,256]{1,0:T(8,128)(2,1)S(1)} %get-tuple-element.192), channel_id=1, source_target_pairs={{0,2},{1,3},{2,0},{3,1},{4,6},{5,7},{6,4},{7,5},{8,10},{9,11},{10,... | collective-permute-start | bytes 1204232 | tf_op jit(solution)/shard_map/ppermute | solution.py:1553
  134.0 3.7 %collective-permute-start.31 = (f32[8,512]{1,0:T(8,128)S(1)}, f32[8,512]{1,0:T(8,128)S(1)}, u32[]{:S(2)}, u32[]{:S(2)}) collective-permute-start(f32[8,512]{1,0:T(8,128)S(1)} %add.127), channel_id=1, source_target_pairs={{0,8},{4,12},{8,0},{12,4},{16,24},{20,28},{24,16},{28,20},{1,9},{5... | collective-permute-start | bytes 49160 | tf_op jit(solution)/shard_map/ppermute | solution.py:1553
  137.7 4.9 %collective-permute-start.32 = (f32[8,512]{1,0:T(8,128)S(1)}, f32[8,512]{1,0:T(8,128)S(1)}, u32[]{:S(2)}, u32[]{:S(2)}) collective-permute-start(f32[8,512]{1,0:T(8,128)S(1)} %add.128.first_ref), channel_id=1, source_target_pairs={{0,16},{4,20},{8,24},{12,28},{16,0},{20,4},{24,8},{28,12},{1,17},{... | collective-permute-start | bytes 49160 | tf_op jit(solution)/shard_map/ppermute | solution.py:1553
  142.7 2.0 collective-permute-start.33
  142.7 3.8 %collective-permute-start.34 = (f32[8,512]{1,0:T(8,128)S(1)}, f32[8,512]{1,0:T(8,128)S(1)}, u32[]{:S(2)}, u32[]{:S(2)}) collective-permute-start(f32[8,512]{1,0:T(8,128)S(1)} %shard_map.361.deltas0_ref), channel_id=1, source_target_pairs={{0,2},{1,3},{2,0},{3,1},{4,6},{5,7},{6,4},{7,5},{8,10},{9,11},{10,... | collective-permute-start | bytes 49160 | tf_op jit(solution)/shard_map/ppermute | solution.py:1553
  144.0 3.2 %collective-permute-start.35 = (f32[8,512]{1,0:T(8,128)S(1)}, f32[8,512]{1,0:T(8,128)S(1)}, u32[]{:S(2)}, u32[]{:S(2)}) collective-permute-start(f32[8,512]{1,0:T(8,128)S(1)} %shard_map.361.deltas0_ref), channel_id=1, source_target_pairs={{0,3},{1,2},{2,1},{3,0},{4,7},{5,6},{6,5},{7,4},{8,11},{9,10},{10,... | collective-permute-start | bytes 49160 | tf_op jit(solution)/shard_map/ppermute | solution.py:1553
  150.9 20.3 %collective-permute-start.44 = (bf16[2304,128]{1,0:T(8,128)(2,1)}, bf16[2304,128]{1,0:T(8,128)(2,1)}, u32[]{:S(2)}, u32[]{:S(2)}) collective-permute-start(bf16[2304,128]{1,0:T(8,128)(2,1)} %collective-permute-done.27.away_own_ref), channel_id=1, source_target_pairs={{0,1},{1,0},{2,3},{3,2},{4,5},{5,4},{6,7},{7,6},{8,9},{9,8},{10,11... | collective-permute-start | bytes 1769480 | tf_op jit(solution)/shard_map/ppermute | solution.py:1553
  151.2 20.1 %collective-permute-start.42 = (bf16[784,256]{1,0:T(8,128)(2,1)S(1)}, bf16[784,256]{1,0:T(8,128)(2,1)}, u32[]{:S(2)}, u32[]{:S(2)}) collective-permute-start(bf16[784,256]{1,0:T(8,128)(2,1)S(1)} %get-tuple-element.210), channel_id=1, source_target_pairs={{0,2},{1,3},{2,0},{3,1},{4,6},{5,7},{6,4},{7,5},{8,10},{9,11},{10,... | collective-permute-start | bytes 1204232 | tf_op jit(solution)/shard_map/ppermute | solution.py:1553
  153.2 3.7 %collective-permute-start.39 = (f32[8,256]{1,0:T(8,128)S(1)}, f32[8,256]{1,0:T(8,128)S(1)}, u32[]{:S(2)}, u32[]{:S(2)}) collective-permute-start(f32[8,256]{1,0:T(8,128)S(1)} %add.129), channel_id=1, source_target_pairs={{0,4},{4,0},{8,12},{12,8},{16,20},{20,16},{24,28},{28,24},{1,5},{5... | collective-permute-start | bytes 24584 | tf_op jit(solution)/shard_map/ppermute | solution.py:1553
  156.9 4.1 %collective-permute-start.40 = (f32[8,256]{1,0:T(8,128)S(1)}, f32[8,256]{1,0:T(8,128)S(1)}, u32[]{:S(2)}, u32[]{:S(2)}) collective-permute-start(f32[8,256]{1,0:T(8,128)S(1)} %add.131), channel_id=1, source_target_pairs={{0,8},{4,12},{8,0},{12,4},{16,24},{20,28},{24,16},{28,20},{1,9},{5... | collective-permute-start | bytes 24584 | tf_op jit(solution)/shard_map/ppermute | solution.py:1553
  161.0 4.7 %collective-permute-start.41 = (f32[8,256]{1,0:T(8,128)S(1)}, f32[8,256]{1,0:T(8,128)S(1)}, u32[]{:S(2)}, u32[]{:S(2)}) collective-permute-start(f32[8,256]{1,0:T(8,128)S(1)} %add.132), channel_id=1, source_target_pairs={{0,16},{4,20},{8,24},{12,28},{16,0},{20,4},{24,8},{28,12},{1,17},{... | collective-permute-start | bytes 24584 | tf_op jit(solution)/shard_map/ppermute | solution.py:1553
  165.7 5.5 %collective-permute-start.43 = (f32[8,256]{1,0:T(8,128)S(1)}, f32[8,256]{1,0:T(8,128)S(1)}, u32[]{:S(2)}, u32[]{:S(2)}) collective-permute-start(f32[8,256]{1,0:T(8,128)S(1)} %add.133.back_ref), channel_id=1, source_target_pairs={{0,2},{1,3},{2,0},{3,1},{4,6},{5,7},{6,4},{7,5},{8,10},{9,11},{10,... | collective-permute-start | bytes 24584 | tf_op jit(solution)/shard_map/ppermute | solution.py:1553
  189.5 11.8 %collective-permute-start.50 = (bf16[2304,128]{1,0:T(8,128)(2,1)S(1)}, bf16[2304,128]{1,0:T(8,128)(2,1)S(1)}, u32[]{:S(2)}, u32[]{:S(2)}) collective-permute-start(bf16[2304,128]{1,0:T(8,128)(2,1)S(1)} %get-tuple-element.220), channel_id=1, source_target_pairs={{0,1},{1,0},{2,3},{3,2},{4,5},{5,4},{6,7},{7,6},{8,9},{9,8},{10,11... | collective-permute-start | bytes 1769480 | tf_op jit(solution)/shard_map/ppermute | solution.py:1553
  189.7 11.6 %collective-permute-start.51 = (bf16[2304,128]{1,0:T(8,128)(2,1)S(1)}, bf16[2304,128]{1,0:T(8,128)(2,1)S(1)}, u32[]{:S(2)}, u32[]{:S(2)}) collective-permute-start(bf16[2304,128]{1,0:T(8,128)(2,1)S(1)} %get-tuple-element.221), channel_id=1, source_target_pairs={{0,1},{1,0},{2,3},{3,2},{4,5},{5,4},{6,7},{7,6},{8,9},{9,8},{10,11... | collective-permute-start | bytes 1769480 | tf_op jit(solution)/shard_map/ppermute | solution.py:1553
  190.0 14.7 %collective-permute-start.52 = (bf16[784,256]{1,0:T(8,128)(2,1)}, bf16[784,256]{1,0:T(8,128)(2,1)}, u32[]{:S(2)}, u32[]{:S(2)}) collective-permute-start(bf16[784,256]{1,0:T(8,128)(2,1)} %get-tuple-element.228), channel_id=1, source_target_pairs={{0,2},{1,3},{2,0},{3,1},{4,6},{5,7},{6,4},{7,5},{8,10},{9,11},{10,... | collective-permute-start | bytes 1204232 | tf_op jit(solution)/shard_map/ppermute | solution.py:1553
  190.8 4.6 %collective-permute-start.46 = (f32[32,256]{1,0:T(8,128)S(1)}, f32[32,256]{1,0:T(8,128)S(1)}, u32[]{:S(2)}, u32[]{:S(2)}) collective-permute-start(f32[32,256]{1,0:T(8,128)S(1)} %add.134), channel_id=1, source_target_pairs={{0,4},{4,0},{8,12},{12,8},{16,20},{20,16},{24,28},{28,24},{1,5},{5... | collective-permute-start | bytes 98312 | tf_op jit(solution)/shard_map/ppermute | solution.py:1553
  192.3 4.9 %collective-permute-start.48 = (f32[56,256]{1,0:T(8,128)S(1)}, f32[56,256]{1,0:T(8,128)S(1)}, u32[]{:S(2)}, u32[]{:S(2)}) collective-permute-start(f32[56,256]{1,0:T(8,128)S(1)} %shard_map.367), channel_id=1, source_target_pairs={{0,4},{4,0},{8,12},{12,8},{16,20},{20,16},{24,28},{28,24},{1,5},{5... | collective-permute-start | bytes 172040 | tf_op jit(solution)/shard_map/ppermute | solution.py:1553
  195.4 3.9 %collective-permute-start.47 = (f32[32,256]{1,0:T(8,128)S(1)}, f32[32,256]{1,0:T(8,128)S(1)}, u32[]{:S(2)}, u32[]{:S(2)}) collective-permute-start(f32[32,256]{1,0:T(8,128)S(1)} %add.135), channel_id=1, source_target_pairs={{0,8},{4,12},{8,0},{12,4},{16,24},{20,28},{24,16},{28,20},{1,9},{5... | collective-permute-start | bytes 98312 | tf_op jit(solution)/shard_map/ppermute | solution.py:1553
  197.1 26.0 %collective-permute-start.57 = (bf16[512,256]{1,0:T(8,128)(2,1)}, bf16[512,256]{1,0:T(8,128)(2,1)S(1)}, u32[]{:S(2)}, u32[]{:S(2)}) collective-permute-start(bf16[512,256]{1,0:T(8,128)(2,1)} %get-tuple-element.243), channel_id=1, source_target_pairs={{0,2},{1,3},{2,0},{3,1},{4,6},{5,7},{6,4},{7,5},{8,10},{9,11},{10,... | collective-permute-start | bytes 786440 | tf_op jit(solution)/shard_map/ppermute | solution.py:1553
  199.3 5.4 %collective-permute-start.49 = (f32[32,256]{1,0:T(8,128)S(1)}, f32[32,256]{1,0:T(8,128)S(1)}, u32[]{:S(2)}, u32[]{:S(2)}) collective-permute-start(f32[32,256]{1,0:T(8,128)S(1)} %add.137), channel_id=1, source_target_pairs={{0,16},{4,20},{8,24},{12,28},{16,0},{20,4},{24,8},{28,12},{1,17},{... | collective-permute-start | bytes 98312 | tf_op jit(solution)/shard_map/ppermute | solution.py:1553
  203.5 16.6 %collective-permute-start.55 = (bf16[2304,128]{1,0:T(8,128)(2,1)S(1)}, bf16[2304,128]{1,0:T(8,128)(2,1)S(1)}, u32[]{:S(2)}, u32[]{:S(2)}) collective-permute-start(bf16[2304,128]{1,0:T(8,128)(2,1)S(1)} %bitcast.58), channel_id=1, source_target_pairs={{0,4},{4,0},{8,12},{12,8},{16,20},{20,16},{24,28},{28,24},{1,5},{5... | collective-permute-start | bytes 1769480 | tf_op jit(solution)/shard_map/ppermute | solution.py:1553
  204.8 7.2 %collective-permute-start.53 = (f32[32,256]{1,0:T(8,128)S(1)}, f32[32,256]{1,0:T(8,128)S(1)}, u32[]{:S(2)}, u32[]{:S(2)}) collective-permute-start(f32[32,256]{1,0:T(8,128)S(1)} %add.138.back_ref), channel_id=1, source_target_pairs={{0,2},{1,3},{2,0},{3,1},{4,6},{5,7},{6,4},{7,5},{8,10},{9,11},{10,... | collective-permute-start | bytes 98312 | tf_op jit(solution)/shard_map/ppermute | solution.py:1553
  211.9 5.3 %collective-permute-start.56 = (bf16[2048,128]{1,0:T(8,128)(2,1)S(1)}, bf16[2048,128]{1,0:T(8,128)(2,1)S(1)}, u32[]{:S(2)}, u32[]{:S(2)}) collective-permute-start(bf16[2048,128]{1,0:T(8,128)(2,1)S(1)} %get-tuple-element.231), channel_id=1, source_target_pairs={{0,1},{1,0},{2,3},{3,2},{4,5},{5,4},{6,7},{7,6},{8,9},{9,8},{10,11... | collective-permute-start | bytes 1572872 | tf_op jit(solution)/shard_map/ppermute | solution.py:1553
  214.2 8.9 %collective-permute-start.54 = (bf16[784,512]{1,0:T(8,128)(2,1)S(1)}, bf16[784,512]{1,0:T(8,128)(2,1)S(1)}, u32[]{:S(2)}, u32[]{:S(2)}) collective-permute-start(bf16[784,512]{1,0:T(8,128)(2,1)S(1)} %shard_map.372.mine_ref), channel_id=1, source_target_pairs={{0,1},{1,0},{2,3},{3,2},{4,5},{5,4},{6,7},{7,6},{8,9},{9,8},{10,11... | collective-permute-start | bytes 2408456 | tf_op jit(solution)/shard_map/ppermute | solution.py:1553
  215.9 10.0 %collective-permute-start.59 = (f32[56,256]{1,0:T(8,128)S(1)}, f32[56,256]{1,0:T(8,128)S(1)}, u32[]{:S(2)}, u32[]{:S(2)}) collective-permute-start(f32[56,256]{1,0:T(8,128)S(1)} %add.136), channel_id=1, source_target_pairs={{0,8},{4,12},{8,0},{12,4},{16,24},{20,28},{24,16},{28,20},{1,9},{5... | collective-permute-start | bytes 172040 | tf_op jit(solution)/shard_map/ppermute | solution.py:1553
  219.3 8.3 %collective-permute-start.58 = (bf16[1024,128]{1,0:T(8,128)(2,1)S(1)}, bf16[1024,128]{1,0:T(8,128)(2,1)S(1)}, u32[]{:S(2)}, u32[]{:S(2)}) collective-permute-start(bf16[1024,128]{1,0:T(8,128)(2,1)S(1)} %bitcast.60), channel_id=1, source_target_pairs={{0,4},{4,0},{8,12},{12,8},{16,20},{20,16},{24,28},{28,24},{1,5},{5... | collective-permute-start | bytes 786440 | tf_op jit(solution)/shard_map/ppermute | solution.py:1553
  220.8 9.4 %collective-permute-start.61 = (bf16[1152,128]{1,0:T(8,128)(2,1)S(1)}, bf16[1152,128]{1,0:T(8,128)(2,1)S(1)}, u32[]{:S(2)}, u32[]{:S(2)}) collective-permute-start(bf16[1152,128]{1,0:T(8,128)(2,1)S(1)} %bitcast.59), channel_id=1, source_target_pairs={{0,8},{4,12},{8,0},{12,4},{16,24},{20,28},{24,16},{28,20},{1,9},{5... | collective-permute-start | bytes 884744 | tf_op jit(solution)/shard_map/ppermute | solution.py:1553
  225.9 8.2 %collective-permute-start.62 = (f32[56,256]{1,0:T(8,128)S(1)}, f32[56,256]{1,0:T(8,128)S(1)}, u32[]{:S(2)}, u32[]{:S(2)}) collective-permute-start(f32[56,256]{1,0:T(8,128)S(1)} %add.139), channel_id=1, source_target_pairs={{0,16},{4,20},{8,24},{12,28},{16,0},{20,4},{24,8},{28,12},{1,17},{... | collective-permute-start | bytes 172040 | tf_op jit(solution)/shard_map/ppermute | solution.py:1553
  228.2 7.5 %collective-permute-start.60 = (bf16[512,128]{1,0:T(8,128)(2,1)S(1)}, bf16[512,128]{1,0:T(8,128)(2,1)S(1)}, u32[]{:S(2)}, u32[]{:S(2)}) collective-permute-start(bf16[512,128]{1,0:T(8,128)(2,1)S(1)} %bitcast.63), channel_id=1, source_target_pairs={{0,8},{4,12},{8,0},{12,4},{16,24},{20,28},{24,16},{28,20},{1,9},{5... | collective-permute-start | bytes 393224 | tf_op jit(solution)/shard_map/ppermute | solution.py:1553
  230.8 10.7 %collective-permute-start.64 = (bf16[576,128]{1,0:T(8,128)(2,1)S(1)}, bf16[576,128]{1,0:T(8,128)(2,1)S(1)}, u32[]{:S(2)}, u32[]{:S(2)}) collective-permute-start(bf16[576,128]{1,0:T(8,128)(2,1)S(1)} %bitcast.62), channel_id=1, source_target_pairs={{0,16},{4,20},{8,24},{12,28},{16,0},{20,4},{24,8},{28,12},{1,17},{... | collective-permute-start | bytes 442376 | tf_op jit(solution)/shard_map/ppermute | solution.py:1553
  236.3 5.9 %collective-permute-start.63 = (bf16[256,128]{1,0:T(8,128)(2,1)S(1)}, bf16[256,128]{1,0:T(8,128)(2,1)S(1)}, u32[]{:S(2)}, u32[]{:S(2)}) collective-permute-start(bf16[256,128]{1,0:T(8,128)(2,1)S(1)} %bitcast.64), channel_id=1, source_target_pairs={{0,16},{4,20},{8,24},{12,28},{16,0},{20,4},{24,8},{28,12},{1,17},{... | collective-permute-start | bytes 196616 | tf_op jit(solution)/shard_map/ppermute | solution.py:1553
  (43 other events, 641.1 us)
Sparse Core Ops, SparseCore 0:
  10.8 48.4 all-gather.2
  161.1 63.4 reduce-scatter.1
